TPU v7x, 32 devices: a whole 2x2x4 slice. The times are simulated.
32 devices in a mesh: dp: 16 (over z, x, core), seq: 2 (over y).
Axes of the slice: x: 2, y: 2, z: 4, core: 2. Of those that a mesh axis runs over, the one named last changes fastest.
Arguments:
- entering_activations: bfloat16 [32, 1024, 1024], P('dp', 'seq'), may hold values from -6 to 6
- document_numbers: int32 [32, 1024], P('dp', 'seq'), may hold values from 0 to 3, never falling along the last dimension, each value on 1 to 800 neighbouring positions
- result_cotangent: bfloat16 [32, 1024, 1024], P('dp', 'seq'), may hold values from -6 to 6
- normalizer_scales: float32 [2, 2, 1024], replicated, may hold values from 0.5 to 1.5
- normalizer_offsets: float32 [2, 2, 1024], replicated, may hold values from -2.5 to 2.5
- shift_blend_factors: float32 [2, 5, 1024], replicated, may hold values from 0 to 1
- fading_natural_logs_per_feature: float32 [2, 1024], replicated, as said below
- feature_reward_logs: float32 [2, 1024], replicated, may hold values from -1 to 1
- attention_triple_matrix: bfloat16 [2, 3, 1024, 1024], P(None, None, 'dp', 'seq'), may hold values from -0.1875 to 0.1875
- attention_result_matrix: bfloat16 [2, 1024, 1024], P(None, 'dp', 'seq'), may hold values from -0.75 to 0.75
- channelmix_lookup_matrix: bfloat16 [2, 1024, 4096], P(None, 'dp', 'seq'), may hold values from -0.1875 to 0.1875
- channelmix_content_matrix: bfloat16 [2, 4096, 1024], P(None, 'dp', 'seq'), may hold values from -0.09375 to 0.09375
- channelmix_accept_matrix: bfloat16 [2, 1024, 1024], P(None, 'dp', 'seq'), may hold values from -0.1875 to 0.1875
Outputs:
- y_out: bfloat16 [32, 1024, 1024], P('dp', 'seq')
- grad_x: float32 [32, 1024, 1024], P('dp', 'seq')
- grad_norm_gain: float32 [2, 2, 1024], replicated
- grad_norm_bias: float32 [2, 2, 1024], replicated
- grad_mixes: float32 [2, 5, 1024], replicated
- grad_time_decay: float32 [2, 1024], replicated
- grad_time_first: float32 [2, 1024], replicated
- grad_att_kvr: float32 [2, 3, 1024, 1024], P(None, None, 'dp', 'seq')
- grad_att_out: float32 [2, 1024, 1024], P(None, 'dp', 'seq')
- grad_ffn_key: float32 [2, 1024, 4096], P(None, 'dp', 'seq')
- grad_ffn_value: float32 [2, 4096, 1024], P(None, 'dp', 'seq')
- grad_ffn_recept: float32 [2, 1024, 1024], P(None, 'dp', 'seq')
Inputs may be any that keep to these rules, and one draw needn't show every extreme that they name: `document_numbers`: within each row the document numbers never fall; a document starts at the row's start and wherever the number changes. exp(fading_natural_logs_per_feature) is a channel's decay rate per token, at most 4 / 512.
All inputs are finite; a program needn't handle non-finite values.
Results may differ from a plain program's by a relative error of at most 0.018.
Values may be sent and summed in bfloat16 or wider, within the bound.
No kernel may reach another device: no remote copies, remote signals or barrier semaphores. Data moves between devices by JAX's collectives and lax.ppermute only.
A program may use at most 448 MiB of HBM per device.

v0:
```python
import jax
import jax.numpy as jnp
from jax import lax
from jax.sharding import PartitionSpec as P

MB = 2


EPS = 1e-05


def passed_along(array, axis, by):
    devices = lax.axis_size(axis)
    pairs = [(i, i + by) for i in range(devices) if 0 <= i + by < devices]
    return lax.ppermute(array, axis, pairs)


def prefix(array, axis, combine, identity, reverse):
    devices, position = (lax.axis_size(axis), lax.axis_index(axis))
    everything = jax.tree.map(lambda part: lax.all_gather(part, axis), array)
    start = jax.tree.map(
        lambda part, zero: jnp.broadcast_to(jnp.asarray(zero, part.dtype), part.shape),
        array,
        identity,
    )

    def lap(k, before):
        at = devices - 1 - k if reverse else k
        reached = at > position if reverse else at < position
        new = combine(before, jax.tree.map(lambda part: part[at], everything))
        return jax.tree.map(lambda a, b: jnp.where(reached, a, b), new, before)

    return lax.fori_loop(0, devices, lap, start)


def norm_apply(residual_flow, gain_vector, bias_vector):
    centre_of = jnp.mean(residual_flow, axis=-1, keepdims=True)
    centred = residual_flow - centre_of
    spread = jnp.mean(centred * centred, axis=-1, keepdims=True)
    return centred * lax.rsqrt(spread + EPS) * gain_vector + bias_vector


def link_states(former, latter):
    return (
        former[0] * latter[0],
        latter[0] * former[1] + latter[1],
        latter[0] * former[2] + latter[2],
    )


def matmul(first_op, second_op):
    return jnp.dot(first_op, second_op, preferred_element_type=jnp.float32)


def matmul_nt(first_op, second_op):
    return lax.dot_general(
        first_op, second_op, (((1,), (1,)), ((), ())), preferred_element_type=jnp.float32
    )


def matmul_tn(first_op, second_op):
    return lax.dot_general(
        first_op, second_op, (((0,), (0,)), ((), ())), preferred_element_type=jnp.float32
    )


def power_tables(fading_feature_factor, length):
    log_decay = jnp.log(fading_feature_factor)
    places = jnp.arange(length, dtype=jnp.float32)[:, None]
    return (jnp.exp(places * log_decay), jnp.exp(-places * log_decay))


def document_mask(active_token_flags, later):
    breaks = jnp.cumsum(1.0 - active_token_flags, axis=1)
    length = active_token_flags.shape[1]
    places = jnp.arange(length)
    if later:
        order = places[:, None] <= places[None, :]
    else:
        order = places[:, None] >= places[None, :]
    same_doc = breaks[:, :, None] == breaks[:, None, :]
    return (jnp.logical_and(same_doc, order[None]).astype(jnp.float32), breaks)


def masked_sum(mask, terms):
    return jnp.einsum(
        "rts,rsc->rtc",
        mask,
        terms,
        precision=lax.Precision.HIGHEST,
        preferred_element_type=jnp.float32,
    )


def fetch_layer(weights, depth_position):
    pieces = (
        weights[0][depth_position],
        weights[1][depth_position],
        weights[2][depth_position],
        weights[3][depth_position],
        weights[4][depth_position],
    )
    half_full = (
        lax.all_gather(pieces[0], "seq", axis=2, tiled=True),
        lax.all_gather(pieces[1], "seq", axis=1, tiled=True),
        lax.all_gather(pieces[2], "seq", axis=1, tiled=True),
        lax.all_gather(pieces[3], "seq", axis=1, tiled=True),
        lax.all_gather(pieces[4], "seq", axis=1, tiled=True),
    )
    return (
        lax.all_gather(half_full[0], "dp", axis=1, tiled=True),
        lax.all_gather(half_full[1], "dp", axis=0, tiled=True),
        lax.all_gather(half_full[2], "dp", axis=0, tiled=True),
        lax.all_gather(half_full[3], "dp", axis=0, tiled=True),
        lax.all_gather(half_full[4], "dp", axis=0, tiled=True),
    )


def shifted(normed, active_token_flags):
    border = passed_along(normed[:, -1:, :], "seq", 1)
    return jnp.concatenate([border, normed[:, :-1, :]], axis=1) * active_token_flags[:, :, None]


def unshifted(grad_prev, active_token_flags):
    masked = grad_prev * active_token_flags[:, :, None]
    border = passed_along(masked[:, :1, :], "seq", -1)
    return jnp.concatenate([masked[:, 1:, :], border], axis=1)


def mix_back(grads_in, mixing_rows, change):
    grad_normed = jnp.zeros_like(change)
    grad_before = jnp.zeros_like(change)
    grad_list = []
    for slot_idx, grad_part in enumerate(grads_in):
        grad_normed = grad_normed + mixing_rows[slot_idx] * grad_part
        grad_before = grad_before + (1.0 - mixing_rows[slot_idx]) * grad_part
        grad_list.append(jnp.sum(change * grad_part, axis=(0, 1)))
    return (grad_normed, grad_before, jnp.stack(grad_list))


def weighted_kv_forward(
    entering_lookups,
    entering_contents,
    active_token_flags,
    fading_feature_factor,
    reward_feature_factor,
):
    powered_lookups = jnp.exp(entering_lookups)
    reward_scaled = powered_lookups * reward_feature_factor
    length = entering_lookups.shape[1]
    width = entering_lookups.shape[2]
    rising, falling = power_tables(fading_feature_factor, length)
    mask, breaks = document_mask(active_token_flags, False)
    terms = jnp.concatenate(
        [falling * powered_lookups * entering_contents, falling * powered_lookups], axis=2
    )
    summed = masked_sum(mask, terms)
    state_a = rising * summed[:, :, :width]
    state_b = rising * summed[:, :, width:]
    running = rising * fading_feature_factor * (breaks == 0.0).astype(jnp.float32)[:, :, None]
    ident_one = jnp.ones_like(running[:, 0])
    ident_zero = jnp.zeros_like(running[:, 0])
    carried_m, enter_a, enter_b = prefix(
        (running[:, -1], state_a[:, -1], state_b[:, -1]),
        "seq",
        link_states,
        (ident_one, ident_zero, ident_zero),
        False,
    )
    whole_a = state_a + running * enter_a[:, None]
    whole_b = state_b + running * enter_b[:, None]
    visited_first = (
        jnp.concatenate([enter_a[:, None], whole_a[:, :-1]], axis=1)
        * active_token_flags[:, :, None]
    )
    visited_second = (
        jnp.concatenate([enter_b[:, None], whole_b[:, :-1]], axis=1)
        * active_token_flags[:, :, None]
    )
    denominator_total = visited_second + reward_scaled
    final_answer = (visited_first + reward_scaled * entering_contents) / denominator_total
    return (
        final_answer,
        (
            visited_first,
            visited_second,
            denominator_total,
            final_answer,
            reward_scaled,
            powered_lookups,
            entering_contents,
            active_token_flags,
        ),
    )


def attention_sum_pullback(grad_out, stored_weighted_kv, fading_feature_factor):
    (
        visited_first,
        visited_second,
        denominator_total,
        final_answer,
        reward_scaled,
        powered_lookups,
        entering_contents,
        active_token_flags,
    ) = stored_weighted_kv
    numerator_cotangent = grad_out / denominator_total
    grad_bottom = -grad_out * final_answer / denominator_total
    length = grad_out.shape[1]
    width = grad_out.shape[2]
    next_live = active_token_flags[:, 1:, None]
    edge_zero = jnp.zeros_like(numerator_cotangent[:, :1])
    feed_a = jnp.concatenate([next_live * numerator_cotangent[:, 1:], edge_zero], axis=1)
    feed_b = jnp.concatenate([next_live * grad_bottom[:, 1:], edge_zero], axis=1)
    rising, falling = power_tables(fading_feature_factor, length)
    mask, breaks = document_mask(active_token_flags, True)
    summed = masked_sum(mask, jnp.concatenate([rising * feed_a, rising * feed_b], axis=2))
    local_a = falling * summed[:, :, :width]
    local_b = falling * summed[:, :, width:]
    running = falling * rising[-1] * (breaks == breaks[:, -1:]).astype(jnp.float32)[:, :, None]
    start_live = active_token_flags[:, 0][:, None]
    chain_m = start_live * fading_feature_factor * running[:, 0]
    chain_a = start_live * (numerator_cotangent[:, 0] + fading_feature_factor * local_a[:, 0])
    chain_b = start_live * (grad_bottom[:, 0] + fading_feature_factor * local_b[:, 0])
    ident_one = jnp.ones_like(chain_m)
    ident_zero = jnp.zeros_like(chain_m)
    carried_m, leave_a, leave_b = prefix(
        (chain_m, chain_a, chain_b), "seq", link_states, (ident_one, ident_zero, ident_zero), True
    )
    cotangent_first = local_a + running * leave_a[:, None]
    grad_b = local_b + running * leave_b[:, None]
    amplified_cotangent = numerator_cotangent * entering_contents + grad_bottom
    content_cotangent = numerator_cotangent * reward_scaled + powered_lookups * cotangent_first
    lookup_cotangent = amplified_cotangent * reward_scaled + powered_lookups * (
        entering_contents * cotangent_first + grad_b
    )
    reward_cotangent = jnp.sum(amplified_cotangent * reward_scaled, axis=(0, 1))
    fading_cotangent = jnp.sum(
        cotangent_first * visited_first + grad_b * visited_second, axis=(0, 1)
    )
    return (lookup_cotangent, content_cotangent, reward_cotangent, fading_cotangent)


def time_forward(
    residual_flow,
    active_token_flags,
    gain_vector,
    bias_vector,
    mixing_rows,
    fading_feature_factor,
    reward_feature_factor,
    complete_group,
):
    normed, norm_back = jax.vjp(norm_apply, residual_flow, gain_vector, bias_vector)
    before = shifted(normed, active_token_flags)
    change = normed - before
    dim_n = normed.shape[-1]
    flat_k = (before + mixing_rows[0] * change).astype(jnp.bfloat16).reshape(-1, dim_n)
    flat_v = (before + mixing_rows[1] * change).astype(jnp.bfloat16).reshape(-1, dim_n)
    flat_r = (before + mixing_rows[2] * change).astype(jnp.bfloat16).reshape(-1, dim_n)
    lookup_mapping = matmul(flat_k, complete_group[0][0]).reshape(normed.shape)
    content_mapping = matmul(flat_v, complete_group[0][1]).reshape(normed.shape)
    recept = matmul(flat_r, complete_group[0][2])
    attention_sum_result, stored_weighted_kv = weighted_kv_forward(
        lookup_mapping,
        content_mapping,
        active_token_flags,
        fading_feature_factor,
        reward_feature_factor,
    )
    gate_r = jax.nn.sigmoid(recept)
    gated_z = (gate_r * attention_sum_result.reshape(-1, dim_n)).astype(jnp.bfloat16)
    output = matmul(gated_z, complete_group[1])
    kept_vals = (
        norm_back,
        change,
        flat_k,
        flat_v,
        flat_r,
        gate_r,
        attention_sum_result,
        gated_z,
        stored_weighted_kv,
    )
    return (residual_flow + output.reshape(residual_flow.shape), kept_vals)


def time_backward(
    grad_stream, kept_vals, mixing_rows, fading_feature_factor, active_token_flags, complete_group
):
    (
        norm_back,
        change,
        flat_k,
        flat_v,
        flat_r,
        gate_r,
        attention_sum_result,
        gated_z,
        stored_weighted_kv,
    ) = kept_vals
    dim_n = grad_stream.shape[-1]
    grad_output = grad_stream.reshape(-1, dim_n).astype(jnp.bfloat16)
    grad_wout = matmul_tn(gated_z, grad_output)
    grad_gated = matmul_nt(grad_output, complete_group[1])
    weighted_kv_gradient = (grad_gated * gate_r).reshape(attention_sum_result.shape)
    grad_recept = (
        grad_gated * attention_sum_result.reshape(-1, dim_n) * gate_r * (1.0 - gate_r)
    ).astype(jnp.bfloat16)
    lookup_cotangent, content_cotangent, reward_cotangent, fading_cotangent = (
        attention_sum_pullback(weighted_kv_gradient, stored_weighted_kv, fading_feature_factor)
    )
    lookup_cotangent = lookup_cotangent.reshape(-1, dim_n).astype(jnp.bfloat16)
    content_cotangent = content_cotangent.reshape(-1, dim_n).astype(jnp.bfloat16)
    grad_kvr = jnp.stack(
        [
            matmul_tn(flat_k, lookup_cotangent),
            matmul_tn(flat_v, content_cotangent),
            matmul_tn(flat_r, grad_recept),
        ]
    )
    grad_xk = matmul_nt(lookup_cotangent, complete_group[0][0]).reshape(change.shape)
    grad_xv = matmul_nt(content_cotangent, complete_group[0][1]).reshape(change.shape)
    grad_xr = matmul_nt(grad_recept, complete_group[0][2]).reshape(change.shape)
    grad_normed, grad_before, blend_cotangent = mix_back(
        (grad_xk, grad_xv, grad_xr), mixing_rows, change
    )
    grad_normed = grad_normed + unshifted(grad_before, active_token_flags)
    grad_in, scale_term_cotangent, shift_term_cotangent = norm_back(grad_normed)
    return (
        grad_stream + grad_in,
        (
            scale_term_cotangent,
            shift_term_cotangent,
            blend_cotangent,
            fading_cotangent,
            reward_cotangent,
        ),
        (grad_kvr, grad_wout),
    )


def channel_forward(
    residual_flow, active_token_flags, gain_vector, bias_vector, mixing_rows, complete_group
):
    normed, norm_back = jax.vjp(norm_apply, residual_flow, gain_vector, bias_vector)
    before = shifted(normed, active_token_flags)
    change = normed - before
    dim_n = normed.shape[-1]
    flat_k = (before + mixing_rows[0] * change).astype(jnp.bfloat16).reshape(-1, dim_n)
    flat_r = (before + mixing_rows[1] * change).astype(jnp.bfloat16).reshape(-1, dim_n)
    hidden = matmul(flat_k, complete_group[2])
    relu_h = jnp.maximum(hidden, 0.0)
    active = (relu_h * relu_h).astype(jnp.bfloat16)
    carried = matmul(active, complete_group[3])
    gate_r = jax.nn.sigmoid(matmul(flat_r, complete_group[4]))
    output = gate_r * carried
    kept_vals = (norm_back, change, flat_k, flat_r, relu_h, active, carried, gate_r)
    return (residual_flow + output.reshape(residual_flow.shape), kept_vals)


def channel_backward(grad_stream, kept_vals, mixing_rows, active_token_flags, complete_group):
    norm_back, change, flat_k, flat_r, relu_h, active, carried, gate_r = kept_vals
    dim_n = grad_stream.shape[-1]
    grad_flat = grad_stream.reshape(-1, dim_n)
    grad_carried = (grad_flat * gate_r).astype(jnp.bfloat16)
    grad_recept = (grad_flat * carried * gate_r * (1.0 - gate_r)).astype(jnp.bfloat16)
    grad_fval = matmul_tn(active, grad_carried)
    grad_active = matmul_nt(grad_carried, complete_group[3])
    grad_hidden = (grad_active * 2.0 * relu_h).astype(jnp.bfloat16)
    grad_fkey = matmul_tn(flat_k, grad_hidden)
    grad_frec = matmul_tn(flat_r, grad_recept)
    grad_xk = matmul_nt(grad_hidden, complete_group[2]).reshape(change.shape)
    grad_xr = matmul_nt(grad_recept, complete_group[4]).reshape(change.shape)
    grad_normed, grad_before, blend_cotangent = mix_back((grad_xk, grad_xr), mixing_rows, change)
    grad_normed = grad_normed + unshifted(grad_before, active_token_flags)
    grad_in, scale_term_cotangent, shift_term_cotangent = norm_back(grad_normed)
    return (
        grad_stream + grad_in,
        (scale_term_cotangent, shift_term_cotangent, blend_cotangent),
        (grad_fkey, grad_fval, grad_frec),
    )


def per_device(
    entering_activations,
    document_numbers,
    result_cotangent,
    normalizer_scales,
    normalizer_offsets,
    shift_blend_factors,
    fading_natural_logs_per_feature,
    feature_reward_logs,
    attention_triple_matrix,
    attention_result_matrix,
    channelmix_lookup_matrix,
    channelmix_content_matrix,
    channelmix_accept_matrix,
):
    weights = (
        attention_triple_matrix,
        attention_result_matrix,
        channelmix_lookup_matrix,
        channelmix_content_matrix,
        channelmix_accept_matrix,
    )
    layer_count = attention_triple_matrix.shape[0]
    border_ids = passed_along(document_numbers[:, -1:] + 1, "seq", 1)
    earlier_ids = jnp.concatenate([border_ids - 1, document_numbers[:, :-1]], axis=1)
    alive_all = (document_numbers == earlier_ids).astype(jnp.float32)
    decay_all = jnp.exp(-jnp.exp(fading_natural_logs_per_feature))
    reward_per_feature = jnp.exp(feature_reward_logs)
    per_batch = entering_activations.shape[0] // MB
    outputs = []
    input_grads = []
    small_layers = [None] * layer_count
    large_layers = [None] * layer_count
    for batch_idx in range(MB):
        rows_lo = batch_idx * per_batch
        residual_flow = entering_activations[rows_lo : rows_lo + per_batch].astype(jnp.float32)
        active_token_flags = alive_all[rows_lo : rows_lo + per_batch]
        held_sets = []
        kept_time = []
        kept_chan = []
        for depth_position in range(layer_count):
            complete_group = fetch_layer(weights, depth_position)
            held_sets.append(complete_group)
            residual_flow, kept_vals = time_forward(
                residual_flow,
                active_token_flags,
                normalizer_scales[depth_position, 0],
                normalizer_offsets[depth_position, 0],
                shift_blend_factors[depth_position, :3],
                decay_all[depth_position],
                reward_per_feature[depth_position],
                complete_group,
            )
            kept_time.append(kept_vals)
            residual_flow, kept_vals = channel_forward(
                residual_flow,
                active_token_flags,
                normalizer_scales[depth_position, 1],
                normalizer_offsets[depth_position, 1],
                shift_blend_factors[depth_position, 3:],
                complete_group,
            )
            kept_chan.append(kept_vals)
        outputs.append(residual_flow.astype(jnp.bfloat16))
        grad_stream = result_cotangent[rows_lo : rows_lo + per_batch].astype(jnp.float32)
        for depth_position in reversed(range(layer_count)):
            complete_group = held_sets[depth_position]
            grad_stream, small_chan, large_chan = channel_backward(
                grad_stream,
                kept_chan[depth_position],
                shift_blend_factors[depth_position, 3:],
                active_token_flags,
                complete_group,
            )
            grad_stream, small_time, large_time = time_backward(
                grad_stream,
                kept_time[depth_position],
                shift_blend_factors[depth_position, :3],
                decay_all[depth_position],
                active_token_flags,
                complete_group,
            )
            grad_td = (
                small_time[3]
                * decay_all[depth_position]
                * -jnp.exp(fading_natural_logs_per_feature[depth_position])
            )
            small_now = (
                jnp.stack([small_time[0], small_chan[0]]),
                jnp.stack([small_time[1], small_chan[1]]),
                jnp.concatenate([small_time[2], small_chan[2]], axis=0),
                grad_td,
                small_time[4],
            )
            large_now = (large_time[0], large_time[1], large_chan[0], large_chan[1], large_chan[2])
            if small_layers[depth_position] is None:
                small_layers[depth_position] = small_now
                large_layers[depth_position] = large_now
            else:
                small_layers[depth_position] = jax.tree.map(
                    jnp.add, small_layers[depth_position], small_now
                )
                large_layers[depth_position] = jax.tree.map(
                    jnp.add, large_layers[depth_position], large_now
                )
        input_grads.append(grad_stream)
    small_stack = jax.tree.map(lambda *members: jnp.stack(members), *small_layers)
    large_stack = jax.tree.map(lambda *members: jnp.stack(members), *large_layers)
    owned_dp = (
        lax.psum_scatter(
            large_stack[0].astype(jnp.bfloat16), "dp", scatter_dimension=2, tiled=True
        ).astype(jnp.float32),
        lax.psum_scatter(
            large_stack[1].astype(jnp.bfloat16), "dp", scatter_dimension=1, tiled=True
        ).astype(jnp.float32),
        lax.psum_scatter(
            large_stack[2].astype(jnp.bfloat16), "dp", scatter_dimension=1, tiled=True
        ).astype(jnp.float32),
        lax.psum_scatter(
            large_stack[3].astype(jnp.bfloat16), "dp", scatter_dimension=1, tiled=True
        ).astype(jnp.float32),
        lax.psum_scatter(
            large_stack[4].astype(jnp.bfloat16), "dp", scatter_dimension=1, tiled=True
        ).astype(jnp.float32),
    )
    owned_all = (
        lax.psum_scatter(
            owned_dp[0].astype(jnp.bfloat16), "seq", scatter_dimension=3, tiled=True
        ).astype(jnp.float32),
        lax.psum_scatter(
            owned_dp[1].astype(jnp.bfloat16), "seq", scatter_dimension=2, tiled=True
        ).astype(jnp.float32),
        lax.psum_scatter(
            owned_dp[2].astype(jnp.bfloat16), "seq", scatter_dimension=2, tiled=True
        ).astype(jnp.float32),
        lax.psum_scatter(
            owned_dp[3].astype(jnp.bfloat16), "seq", scatter_dimension=2, tiled=True
        ).astype(jnp.float32),
        lax.psum_scatter(
            owned_dp[4].astype(jnp.bfloat16), "seq", scatter_dimension=2, tiled=True
        ).astype(jnp.float32),
    )
    small_sum = lax.psum(small_stack, ("dp", "seq"))
    y_out = jnp.concatenate(outputs, axis=0)
    grad_x = jnp.concatenate(input_grads, axis=0)
    return (
        y_out,
        grad_x,
        small_sum[0],
        small_sum[1],
        small_sum[2],
        small_sum[3],
        small_sum[4],
        owned_all[0],
        owned_all[1],
        owned_all[2],
        owned_all[3],
        owned_all[4],
    )


def solution(mesh):
    return jax.shard_map(
        per_device,
        mesh=mesh,
        in_specs=(
            P("dp", "seq", None),
            P("dp", "seq"),
            P("dp", "seq", None),
            P(),
            P(),
            P(),
            P(),
            P(),
            P(None, None, "dp", "seq"),
            P(None, "dp", "seq"),
            P(None, "dp", "seq"),
            P(None, "dp", "seq"),
            P(None, "dp", "seq"),
        ),
        out_specs=(
            P("dp", "seq", None),
            P("dp", "seq", None),
            P(),
            P(),
            P(),
            P(),
            P(),
            P(None, None, "dp", "seq"),
            P(None, "dp", "seq"),
            P(None, "dp", "seq"),
            P(None, "dp", "seq"),
            P(None, "dp", "seq"),
        ),
        check_vma=False,
    )
```

profile of v0, /device:TPU:1, one launch (start us, length us, event | category | flops | bytes accessed | tf_op | source)
XLA Modules:
  0.0 1822.2 jit_solution(15548910132996117971)
XLA Ops:
  8.3 7.6 all-gather
  161.4 7.3 multiply_convert_fusion.15
  186.1 12.5 all-gather.61.cloned.1.call-done
  198.6 10.3 fusion.34
  208.9 7.1 fusion.36
  216.0 57.8 %all-gather.63.cloned.1.call-done = bf16[1,4096,1024]{2,1,0:T(8,128)(2,1)} async-done(((bf16[1,256,1024]{2,1,0:T(8,128)(2,1)}), bf16[1,4096,1024]{2,1,0:T(8,128)(2,1)}) %all-gather.63.cloned.1.call-update) | async-done | bytes 8388624 | tf_op jit(solution)/shard_map/all_gather | solution.py:114
  273.8 11.7 fusion.26
  291.4 24.1 %all-gather.59.cloned.1.call-done = bf16[1,1024,1024]{2,1,0:T(8,128)(2,1)} async-done(((bf16[1,64,1024]{2,1,0:T(8,128)(2,1)}), bf16[1,1024,1024]{2,1,0:T(8,128)(2,1)}) %all-gather.59.cloned.1.call-update) | async-done | bytes 2097168 | tf_op jit(solution)/shard_map/all_gather | solution.py:115
  347.2 31.1 %all-gather.65.cloned.1.call-done = bf16[1,3,1024,1024]{3,2,1,0:T(8,128)(2,1)} async-done(((bf16[1,3,64,1024]{3,2,1,0:T(8,128)(2,1)}), bf16[1,3,1024,1024]{3,2,1,0:T(8,128)(2,1)}) %all-gather.65.cloned.1.call-update) | async-done | bytes 6291472 | tf_op jit(solution)/shard_map/all_gather | solution.py:111
  426.9 7.6 multiply_convert_fusion.14
  452.1 10.7 all-gather.69.cloned.1.call-done
  467.6 71.1 %all-gather.71.cloned.1.call-done = bf16[1,1024,4096]{2,1,0:T(8,128)(2,1)} async-done(((bf16[1,64,4096]{2,1,0:T(8,128)(2,1)}), bf16[1,1024,4096]{2,1,0:T(8,128)(2,1)}) %all-gather.71.cloned.1.call-update) | async-done | bytes 8388624 | tf_op jit(solution)/shard_map/all_gather | solution.py:113
  538.7 11.5 fusion.18
  550.2 63.7 %all-gather.73.cloned.1.call-done = bf16[1,4096,1024]{2,1,0:T(8,128)(2,1)} async-done(((bf16[1,256,1024]{2,1,0:T(8,128)(2,1)}), bf16[1,4096,1024]{2,1,0:T(8,128)(2,1)}) %all-gather.73.cloned.1.call-update) | async-done | bytes 8388624 | tf_op jit(solution)/shard_map/all_gather | solution.py:114
  613.9 11.7 fusion.10
  625.6 13.0 multiply_convert_fusion.1
  638.6 11.0 fusion.14
  649.6 6.9 fusion.20
  656.5 10.0 fusion.12
  670.2 13.4 multiply_convert_fusion.3
  683.6 8.4 fusion.16
  728.2 9.3 fusion.349
  771.1 6.7 fusion.179
  839.2 9.8 fusion.1
  867.1 12.9 multiply_convert_fusion.2
  880.1 11.0 multiply_convert_fusion
  891.1 8.2 fusion.30
  899.4 9.0 fusion.32
  908.5 6.7 fusion.153
  951.7 10.0 fusion.350
  1054.7 14.5 fusion.291
  1069.2 17.0 fusion.5
  1086.2 13.2 fusion.290
  1099.4 16.2 fusion.4
  1115.6 13.8 pad_maximum_fusion.1
  1130.7 10.6 fusion.472
  1141.2 11.6 fusion.3
  1152.8 8.4 fusion.471
  1161.3 11.6 fusion.2
  1172.8 13.9 pad_maximum_fusion
  1230.3 11.3 fusion.433
  1247.6 157.4 %reduce-scatter.23.cloned.1.call-done = bf16[2,256,1024]{2,1,0:T(8,128)(2,1)} async-done(((bf16[2,4096,1024]{2,1,0:T(8,128)(2,1)}), bf16[2,256,1024]{2,1,0:T(8,128)(2,1)}) %reduce-scatter.23.cloned.1.call-update) | async-done | bytes 1048592 | tf_op jit(solution)/shard_map/reduce_scatter | solution.py:504
  1410.4 176.1 %reduce-scatter.19.cloned.1.call-done = bf16[2,64,4096]{2,1,0:T(8,128)(2,1)} async-done(((bf16[2,1024,4096]{2,1,0:T(8,128)(2,1)}), bf16[2,64,4096]{2,1,0:T(8,128)(2,1)}) %reduce-scatter.19.cloned.1.call-update) | async-done | bytes 1048592 | tf_op jit(solution)/shard_map/reduce_scatter | solution.py:501
  1604.4 8.7 reduce-scatter.17.cloned.1.call-done
  1614.7 18.0 reduce-scatter.13.cloned.1.call-done
  1634.6 20.7 %reduce-scatter.25.cloned.1.call-done = bf16[2,256,512]{2,1,0:T(8,128)(2,1)} async-done(((bf16[2,256,1024]{2,1,0:T(8,128)(2,1)}), bf16[2,256,512]{2,1,0:T(8,128)(2,1)}) %reduce-scatter.25.cloned.1.call-update) | async-done | bytes 524304 | tf_op jit(solution)/shard_map/reduce_scatter | solution.py:521
  1657.5 20.3 %reduce-scatter.21.cloned.1.call-done = bf16[2,64,2048]{2,1,0:T(8,128)(2,1)} async-done(((bf16[2,64,4096]{2,1,0:T(8,128)(2,1)}), bf16[2,64,2048]{2,1,0:T(8,128)(2,1)}) %reduce-scatter.21.cloned.1.call-update) | async-done | bytes 524304 | tf_op jit(solution)/shard_map/reduce_scatter | solution.py:518
  1679.9 128.4 %all-reduce.11.cloned.1.call-done = (f32[2,2,1024]{2,1,0:T(2,128)}, f32[2,2,1024]{2,1,0:T(2,128)}, f32[2,5,1024]{2,0,1:T(2,128)}, f32[2,1024]{1,0:T(2,128)}, f32[2,1024]{1,0:T(2,128)}) async-done(((f32[2,2,1024]{2,1,0:T(2,128)}, f32[2,2,1024]{2,1,0:T(2,128)}, f32[2,5,1024]{2,0,1:T(2,128)}, f32[2,1024]{1,0:T(2,128)}, f32[2,1024]{1,0:T(2,128)}), (f32[2,2,1024]{2,1,0:T(2,128)}, f32[2,2,1024]{2,1,0:T(2,128)}, ...) | async-done | bytes 90128 | tf_op jit(solution)/shard_map/psum | solution.py:528
  (1299 shorter events, 635.8 us)
Async XLA Ops:
  7.2 92.2 %all-gather.55.cloned.1.call-start = ((), (), s32[]{:S(2)}) async-start(), calls=%async_computation.20 | async-start | bytes 6684672 | tf_op jit(solution)/shard_map/all_gather | solution.py:111
  16.0 152.7 %all-gather.57.cloned.1.call-start = ((), (), s32[]{:S(2)}) async-start(), calls=%async_computation.21 | async-start | bytes 2228224 | tf_op jit(solution)/shard_map/all_gather | solution.py:112
  20.8 177.8 %all-gather.61.cloned.1.call-start = ((), (), s32[]{:S(2)}) async-start(), calls=%async_computation.23 | async-start | bytes 8912896 | tf_op jit(solution)/shard_map/all_gather | solution.py:113
  27.1 246.7 %all-gather.63.cloned.1.call-start = ((), (), s32[]{:S(2)}) async-start(), calls=%async_computation.24 | async-start | bytes 8912896 | tf_op jit(solution)/shard_map/all_gather | solution.py:114
  33.5 281.9 %all-gather.59.cloned.1.call-start = ((), (), s32[]{:S(2)}) async-start(), calls=%async_computation.22 | async-start | bytes 2228224 | tf_op jit(solution)/shard_map/all_gather | solution.py:115
  38.2 340.0 %all-gather.65.cloned.1.call-start = ((), (), s32[]{:S(2)}) async-start(), calls=%async_computation.25 | async-start | bytes 6684672 | tf_op jit(solution)/shard_map/all_gather | solution.py:111
  44.3 390.3 %all-gather.67.cloned.1.call-start = ((), (), s32[]{:S(2)}) async-start(), calls=%async_computation.26 | async-start | bytes 2228224 | tf_op jit(solution)/shard_map/all_gather | solution.py:112
  49.0 413.8 %all-gather.69.cloned.1.call-start = ((), (), s32[]{:S(2)}) async-start(), calls=%async_computation.27 | async-start | bytes 2228224 | tf_op jit(solution)/shard_map/all_gather | solution.py:115
  53.3 485.4 %all-gather.71.cloned.1.call-start = ((), (), s32[]{:S(2)}) async-start(), calls=%async_computation.28 | async-start | bytes 8912896 | tf_op jit(solution)/shard_map/all_gather | solution.py:113
  59.7 554.2 %all-gather.73.cloned.1.call-start = ((), (), s32[]{:S(2)}) async-start(), calls=%async_computation.29 | async-start | bytes 8912896 | tf_op jit(solution)/shard_map/all_gather | solution.py:114
  63.5 24.1 %collective-permute-start.5 = (f32[1,1,1024]{2,1,0:T(1,128)S(1)}, f32[1,1,1024]{2,1,0:T(1,128)S(1)}, u32[]{:S(2)}, u32[]{:S(2)}) collective-permute-start(f32[1,1,1024]{2,1,0:T(1,128)S(1)} %slice.821), channel_id=1, source_target_pairs={{0,1},{2,3},{4,5},{6,7},{8,9},{10,11},{12,13},{14,15},{16,17},{18,... | collective-permute-start | bytes 12296 | tf_op jit(solution)/shard_map/ppermute | solution.py:15
  66.8 12.4 collective-permute-start.1
  68.1 25.5 %collective-permute-start = (f32[1,1,1024]{2,1,0:T(1,128)S(1)}, f32[1,1,1024]{2,1,0:T(1,128)S(1)}, u32[]{:S(2)}, u32[]{:S(2)}) collective-permute-start(f32[1,1,1024]{2,1,0:T(1,128)S(1)} %slice.784), channel_id=1, source_target_pairs={{0,1},{2,3},{4,5},{6,7},{8,9},{10,11},{12,13},{14,15},{16,17},{18,... | collective-permute-start | bytes 12296 | tf_op jit(solution)/shard_map/ppermute | solution.py:15
  75.7 1135.7 %reduce-scatter.27.cloned.1.call-start = ((), (), s32[]{:S(2)}) async-start(), calls=%async_computation.18 | async-start | bytes 4456448 | tf_op jit(solution)/shard_map/reduce_scatter | solution.py:507
  75.8 311.7 %copy-start.237 = (f32[512]{0:T(512)}, f32[512]{0:T(512)S(1)}, u32[]{:S(2)}) copy-start(f32[512]{0:T(512)S(1)} %iota_negate_fusion) | copy-start | bytes 6148
  77.3 319.1 %copy-start.229 = (f32[1,1024]{1,0:T(1,128)}, f32[1,1024]{1,0:T(1,128)S(1)}, u32[]{:S(2)}) copy-start(f32[1,1024]{1,0:T(1,128)S(1)} %get-tuple-element.1836) | copy-start | bytes 12292
  83.7 305.1 %copy-start.247 = (f32[512]{0:T(512)}, f32[512]{0:T(512)S(1)}, u32[]{:S(2)}) copy-start(f32[512]{0:T(512)S(1)} %get-tuple-element.1638) | copy-start | bytes 6148
  87.6 305.0 %copy-start.250 = (f32[512]{0:T(512)}, f32[512]{0:T(512)S(1)}, u32[]{:S(2)}) copy-start(f32[512]{0:T(512)S(1)} %get-tuple-element.1628) | copy-start | bytes 6148
  177.5 5.4 collective-permute-start.2
  179.4 3.5 collective-permute-start.6
  328.3 11.4 collective-permute-start.3
  331.4 8.3 collective-permute-start.7
  415.5 311.1 %copy-start.240 = (f32[1,1024]{1,0:T(1,128)}, f32[1,1024]{1,0:T(1,128)S(1)}, u32[]{:S(2)}) copy-start(f32[1,1024]{1,0:T(1,128)S(1)} %get-tuple-element.1223) | copy-start | bytes 12292
  443.4 5.0 collective-permute-start.4
  446.5 2.0 collective-permute-start.8
  699.8 7.2 collective-permute-start.9
  701.1 5.9 collective-permute-start.13
  833.9 15.4 collective-permute-start.10
  835.2 14.1 collective-permute-start.14
  926.0 5.5 collective-permute-start.11
  927.3 4.4 collective-permute-start.15
  931.0 293.1 %reduce-scatter.15.cloned.1.call-start = ((), (), s32[]{:S(2)}) async-start(), calls=%async_computation.12 | async-start | bytes 4456448 | tf_op jit(solution)/shard_map/reduce_scatter | solution.py:498
  1001.1 228.2 %reduce-scatter.11.cloned.1.call-start = ((), (), s32[]{:S(2)}) async-start(), calls=%async_computation.10 | async-start | bytes 13369344 | tf_op jit(solution)/shard_map/reduce_scatter | solution.py:495
  1053.1 351.8 %reduce-scatter.23.cloned.1.call-start = ((), (), s32[]{:S(2)}) async-start(), calls=%async_computation.16 | async-start | bytes 17825792 | tf_op jit(solution)/shard_map/reduce_scatter | solution.py:504
  1129.5 457.0 %reduce-scatter.19.cloned.1.call-start = ((), (), s32[]{:S(2)}) async-start(), calls=%async_computation.14 | async-start | bytes 17825792 | tf_op jit(solution)/shard_map/reduce_scatter | solution.py:501
  1186.8 415.9 %reduce-scatter.29.cloned.1.call-start = ((), (), s32[]{:S(2)}) async-start(), calls=%async_computation.19 | async-start | bytes 393216 | tf_op jit(solution)/shard_map/reduce_scatter | solution.py:524
  1211.5 401.6 %reduce-scatter.17.cloned.1.call-start = ((), (), s32[]{:S(2)}) async-start(), calls=%async_computation.13 | async-start | bytes 393216 | tf_op jit(solution)/shard_map/reduce_scatter | solution.py:515
  1219.4 10.6 collective-permute-start.12
  1224.1 408.5 %reduce-scatter.13.cloned.1.call-start = ((), (), s32[]{:S(2)}) async-start(), calls=%async_computation.11 | async-start | bytes 1179648 | tf_op jit(solution)/shard_map/reduce_scatter | solution.py:512
  1225.8 4.3 collective-permute-start.16
  1229.3 426.0 %reduce-scatter.25.cloned.1.call-start = ((), (), s32[]{:S(2)}) async-start(), calls=%async_computation.17 | async-start | bytes 1572864 | tf_op jit(solution)/shard_map/reduce_scatter | solution.py:521
  1244.7 160.3 %copy-start.289 = (f32[512]{0:T(512)S(1)}, f32[512]{0:T(512)}, u32[]{:S(2)}) copy-start(f32[512]{0:T(512)} %copy-done.288) | copy-start | bytes 6148
  1244.7 160.3 %copy-start.295 = (f32[512]{0:T(512)S(1)}, f32[512]{0:T(512)}, u32[]{:S(2)}) copy-start(f32[512]{0:T(512)} %copy-done.294) | copy-start | bytes 6148
  1244.7 160.3 %copy-start.362 = (f32[1,1,1024]{2,1,0:T(1,128)S(1)}, f32[1,1,1024]{2,1,0:T(1,128)}, u32[]{:S(2)}) copy-start(f32[1,1,1024]{2,1,0:T(1,128)} %copy-done.361) | copy-start | bytes 12292
  1404.9 272.8 %reduce-scatter.21.cloned.1.call-start = ((), (), s32[]{:S(2)}) async-start(), calls=%async_computation.15 | async-start | bytes 1572864 | tf_op jit(solution)/shard_map/reduce_scatter | solution.py:518
  1405.1 181.5 %copy-start.379 = (f32[1024]{0:T(1024)S(1)}, f32[1024]{0:T(1024)}, u32[]{:S(2)}) copy-start(f32[1024]{0:T(1024)} %get-tuple-element.1611) | copy-start | bytes 12292
  1405.1 181.5 %copy-start.380 = (f32[1024]{0:T(1024)S(1)}, f32[1024]{0:T(1024)}, u32[]{:S(2)}) copy-start(f32[1024]{0:T(1024)} %get-tuple-element.1809) | copy-start | bytes 12292
  1586.5 221.8 %all-reduce.11.cloned.1.call-start = ((), (), s32[]{:S(2)}) async-start(), calls=%async_computation.30 | async-start | bytes 180224 | tf_op jit(solution)/shard_map/psum | solution.py:528
  (414 other events, 3152.9 us)
Sparse Core Ops, SparseCore 0:
  16.1 64.4 all-gather.54
  82.7 39.9 all-gather.56
  124.9 73.6 all-gather.60
  200.6 73.1 all-gather.62
  275.8 39.6 all-gather.58
  317.5 60.7 all-gather.64
  380.4 39.9 all-gather.66
  422.6 40.1 all-gather.68
  465.0 73.6 all-gather.70
  540.7 73.1 all-gather.72
  931.1 76.7 reduce-scatter.26
  1012.1 71.4 reduce-scatter.14
  1087.6 134.7 reduce-scatter.10
  1226.3 178.5 reduce-scatter.22
  1408.9 177.5 reduce-scatter.18
  1588.6 10.6 reduce-scatter.28
  1601.4 11.6 reduce-scatter.16
  1615.2 17.4 reduce-scatter.12
  1635.0 20.2 reduce-scatter.24
  1657.4 20.3 reduce-scatter.20
  1685.9 122.3 all-reduce.10
where the time goes:
time: 1830 us; the launch traced here: 1820 us
  waiting for transfers between devices  801 us (44%)
  matrix products  465 us (25%)
  other arithmetic  284 us (16%)
  blocking collectives  136 us (7%)
  local copies, waits for them, and re-layouts  82.3 us (4%)
  starting transfers between devices  29.9 us (2%)
  between operations  23.1 us (1%)
    reduce_scatter x1, waiting for transfers between devices, per_device(): lax.psum_scatter(large_stack[2].astype(jnp.bfloat16), 'dp', scatter_dimen...  176 us
    reduce_scatter x1, waiting for transfers between devices, per_device(): lax.psum_scatter(large_stack[3].astype(jnp.bfloat16), 'dp', scatter_dimen...  157 us
    dot_general x28, matrix products, matmul_tn(): lax.dot_general(first_op, second_op, (((0,), (0,)), ((), ())), preferred_...  146 us
    dot_general x28, matrix products, matmul(): return jnp.dot(first_op, second_op, preferred_element_type=jnp.float32)  144 us
    dot_general x28, matrix products, matmul_nt(): lax.dot_general(first_op, second_op, (((1,), (1,)), ((), ())), preferred_...  141 us
    psum x1, waiting for transfers between devices, per_device(): small_sum = lax.psum(small_stack, ('dp', 'seq'))  128 us
    all_gather x2, waiting for transfers between devices, fetch_layer(): lax.all_gather(half_full[3], 'dp', axis=0, tiled=True)  121 us
    all_gather x2, waiting for transfers between devices, fetch_layer(): lax.all_gather(half_full[2], 'dp', axis=0, tiled=True)  83.6 us
  transfers between devices with their start and end apart: 38, of which 17 were waited for; matrix products, arithmetic and copies ran while one was open for 28% of the time, Pallas kernels for 0%

commit v1 on v0

--- a/solution.py
+++ b/solution.py
@@ -1,36 +1,234 @@
+import functools
+
 import jax
 import jax.numpy as jnp
+import numpy as np
 from jax import lax
+from jax.experimental import pallas as pl
+from jax.experimental.pallas import tpu as pltpu
 from jax.sharding import PartitionSpec as P
 
-MB = 2
-
-
 EPS = 1e-05
+BF = jnp.bfloat16
+F32 = jnp.float32
+BOTH = ("dp", "seq")
+VMEM = 58 * 2**20
+
+
+def sizes():
+    return lax.axis_size("dp"), lax.axis_size("seq")
+
+
+def paired():
+    dp, seq = sizes()
+    return seq == 2 and dp % 4 == 0
+
+
+def place(d):
+    return d // 4, d // 2 % 2, d % 2
+
+
+def core_of():
+    if not paired():
+        return jnp.int32(0)
+    return lax.rem(lax.axis_index("dp"), 2)
+
+
+def moved(array, target):
+    dp, seq = sizes()
+    pairs = []
+    for d in range(dp):
+        for y in range(seq):
+            z, x, c, y2 = target(*place(d), y)
+            pairs.append((d * seq + y, (z * 4 + x * 2 + c) * seq + y2))
+    return lax.ppermute(array, BOTH, pairs)
+
+
+def to_core(z, x, c, y):
+    return z, x, 1 - c, y
+
+
+def to_second(z, x, c, y):
+    return (z, 1 - x, c, y) if c == 0 else (z, x, c, 1 - y)
+
+
+def to_third(z, x, c, y):
+    return (z, x, c, 1 - y) if c == 0 else (z, 1 - x, c, y)
+
+
+def along_z(step):
+    depth = sizes()[0] // 4
+
+    def target(z, x, c, y):
+        return (z + step) % depth, x, c, y
+
+    return target
+
+
+def unit_tables():
+    dp, seq = sizes()
+    depth = dp // 4
+    rows = []
+    for d in range(dp):
+        for y in range(seq):
+            z, x, c = place(d)
+            half, index = [], []
+            for yy in range(2):
+                for zz in range(depth):
+                    for xx in range(2):
+                        dx, dy, dz = xx ^ x, yy ^ y, (z - zz) % depth
+                        half.append(dy if c == 0 else dx)
+                        index.append((dx if c == 0 else dy) * depth + dz)
+            held = []
+            for side in range(2):
+                own = [i for i, h in zip(index, half) if h == side]
+                last, line = own[0], []
+                for i, h in zip(index, half):
+                    last = i if h == side else last
+                    line.append(last)
+                held.append(line)
+            order = [0] * (4 * depth)
+            for unit, (i, h) in enumerate(zip(index, half)):
+                order[h * 2 * depth + i] = unit
+            rows.append([half, held[0], held[1], order])
+    table = jnp.asarray(np.array(rows, np.int32))
+    me = lax.axis_index("dp") * seq + lax.axis_index("seq")
+    return lax.dynamic_index_in_dim(table, me, 0, keepdims=False)
+
+
+def arrange(table, own, other):
+    units, block = 2 * own.shape[0], (1,) + own.shape[1:]
+
+    def body(table_ref, own_ref, other_ref, out_ref):
+        half = table_ref[0, pl.program_id(0)]
+
+        @pl.when(half == 0)
+        def _():
+            out_ref[...] = own_ref[...]
+
+        @pl.when(half == 1)
+        def _():
+            out_ref[...] = other_ref[...]
+
+    return pl.pallas_call(
+        body,
+        grid_spec=pltpu.PrefetchScalarGridSpec(
+            num_scalar_prefetch=1,
+            grid=(units,),
+            in_specs=[
+                pl.BlockSpec(block, lambda i, t: (t[1, i], 0, 0)),
+                pl.BlockSpec(block, lambda i, t: (t[2, i], 0, 0)),
+            ],
+            out_specs=pl.BlockSpec(block, lambda i, t: (i, 0, 0)),
+        ),
+        out_shape=jax.ShapeDtypeStruct((units,) + own.shape[1:], own.dtype),
+        compiler_params=pltpu.CompilerParams(vmem_limit_bytes=VMEM),
+        cost_estimate=pl.CostEstimate(flops=0, bytes_accessed=4 * own.size * 2, transcendentals=0),
+    )(table, own, other)
+
+
+def split_units(table, whole):
+    units, block = whole.shape[0], (1,) + whole.shape[1:]
+    half = units // 2
+
+    def body(table_ref, in_ref, away_ref, keep_ref):
+        step = pl.program_id(0)
+
+        @pl.when(step < half)
+        def _():
+            away_ref[...] = in_ref[...]
+
+        @pl.when(step >= half)
+        def _():
+            keep_ref[...] = in_ref[...]
+
+    shape = jax.ShapeDtypeStruct((half,) + whole.shape[1:], whole.dtype)
+    return pl.pallas_call(
+        body,
+        grid_spec=pltpu.PrefetchScalarGridSpec(
+            num_scalar_prefetch=1,
+            grid=(units,),
+            in_specs=[pl.BlockSpec(block, lambda i, t: (t[3, lax.rem(i + half, units)], 0, 0))],
+            out_specs=[
+                pl.BlockSpec(block, lambda i, t: (jnp.minimum(i, half - 1), 0, 0)),
+                pl.BlockSpec(block, lambda i, t: (jnp.maximum(i - half, 0), 0, 0)),
+            ],
+        ),
+        out_shape=[shape, shape],
+        compiler_params=pltpu.CompilerParams(vmem_limit_bytes=VMEM),
+        cost_estimate=pl.CostEstimate(flops=0, bytes_accessed=4 * whole.size, transcendentals=0),
+    )(table, whole)
+
+
+def gather_pair(core, table, first, second):
+    dp, seq = sizes()
+    if not paired():
+        return tuple(
+            lax.all_gather(part, ("seq", "dp")).reshape((seq, dp) + part.shape)
+            for part in (first, second)
+        )
+    depth = dp // 4
+    kept = jnp.where(core == 0, first, second)
+    came = moved(jnp.where(core == 0, second, first), to_core)
+    pair = jnp.where(core == 0, jnp.stack([kept, came]), jnp.stack([came, kept]))
+    line = jnp.stack([pair] + [moved(pair, along_z(step)) for step in range(1, depth)])
+    line = line.reshape((depth, -1) + first.shape[1:])
+    half = jnp.concatenate([line, moved(line, to_second)])
+    mine = arrange(table, half, moved(half, to_third))
+    other = moved(mine, to_core)
+    shape = (seq, dp) + first.shape
+    return mine.reshape(shape), other.reshape(shape)
+
+
+def scatter_pair(core, table, stores):
+    dp, seq = sizes()
+    shape = stores.shape[3:]
+    if not paired():
+        flat = stores.reshape((2, seq * dp) + shape)
+        return tuple(
+            lax.psum_scatter(flat[i], ("seq", "dp"), scatter_dimension=0).astype(F32)
+            for i in range(2)
+        )
+    depth = dp // 4
+    groups = [[2 * i, 2 * i + 1] for i in range(dp // 2)]
+    flat = stores.reshape((2, 4 * depth, 2 * shape[0]) + shape[1:])
+    own = lax.psum_scatter(flat, "dp", scatter_dimension=0, axis_index_groups=groups)
+    away, keep = split_units(table, own)
+    came = moved(away, to_third)
+    away = (keep[depth:].astype(F32) + came[depth:].astype(F32)).astype(BF)
+    keep = (keep[:depth].astype(F32) + came[:depth].astype(F32)).astype(BF)
+    came = moved(away, to_second)
+    line = (keep.astype(F32) + came.astype(F32)).astype(BF)
+    total = line[0].astype(F32)
+    for step in range(1, depth):
+        total = total + moved(line[step], along_z(-step)).astype(F32)
+    total = total.reshape((2,) + shape)
+    kept = jnp.where(core == 0, total[0], total[1])
+    came = moved(jnp.where(core == 0, total[1], total[0]), to_core)
+    return jnp.where(core == 0, kept, came), jnp.where(core == 0, came, kept)
+
+
+def summed_everywhere(array):
+    dp, seq = sizes()
+    if not paired():
+        return lax.psum(array, BOTH)
+    steps = [to_core, lambda z, x, c, y: (z, x, c, 1 - y), lambda z, x, c, y: (z, 1 - x, c, y)]
+    for target in steps:
+        array = array + moved(array, target)
+    total = array
+    if dp // 4 == 4:
+        for bit in (1, 2):
+            total = total + moved(total, lambda z, x, c, y, bit=bit: (z ^ bit, x, c, y))
+        return total
+    for step in range(1, dp // 4):
+        total = total + moved(array, along_z(step))
+    return total
 
 
 def passed_along(array, axis, by):
     devices = lax.axis_size(axis)
     pairs = [(i, i + by) for i in range(devices) if 0 <= i + by < devices]
     return lax.ppermute(array, axis, pairs)
-
-
-def prefix(array, axis, combine, identity, reverse):
-    devices, position = (lax.axis_size(axis), lax.axis_index(axis))
-    everything = jax.tree.map(lambda part: lax.all_gather(part, axis), array)
-    start = jax.tree.map(
-        lambda part, zero: jnp.broadcast_to(jnp.asarray(zero, part.dtype), part.shape),
-        array,
-        identity,
-    )
-
-    def lap(k, before):
-        at = devices - 1 - k if reverse else k
-        reached = at > position if reverse else at < position
-        new = combine(before, jax.tree.map(lambda part: part[at], everything))
-        return jax.tree.map(lambda a, b: jnp.where(reached, a, b), new, before)
-
-    return lax.fori_loop(0, devices, lap, start)
 
 
 def norm_apply(residual_flow, gain_vector, bias_vector):
@@ -38,14 +236,6 @@
     centred = residual_flow - centre_of
     spread = jnp.mean(centred * centred, axis=-1, keepdims=True)
     return centred * lax.rsqrt(spread + EPS) * gain_vector + bias_vector
-
-
-def link_states(former, latter):
-    return (
-        former[0] * latter[0],
-        latter[0] * former[1] + latter[1],
-        latter[0] * former[2] + latter[2],
-    )
 
 
 def matmul(first_op, second_op):
@@ -89,30 +279,6 @@
         terms,
         precision=lax.Precision.HIGHEST,
         preferred_element_type=jnp.float32,
-    )
-
-
-def fetch_layer(weights, depth_position):
-    pieces = (
-        weights[0][depth_position],
-        weights[1][depth_position],
-        weights[2][depth_position],
-        weights[3][depth_position],
-        weights[4][depth_position],
-    )
-    half_full = (
-        lax.all_gather(pieces[0], "seq", axis=2, tiled=True),
-        lax.all_gather(pieces[1], "seq", axis=1, tiled=True),
-        lax.all_gather(pieces[2], "seq", axis=1, tiled=True),
-        lax.all_gather(pieces[3], "seq", axis=1, tiled=True),
-        lax.all_gather(pieces[4], "seq", axis=1, tiled=True),
-    )
-    return (
-        lax.all_gather(half_full[0], "dp", axis=1, tiled=True),
-        lax.all_gather(half_full[1], "dp", axis=0, tiled=True),
-        lax.all_gather(half_full[2], "dp", axis=0, tiled=True),
-        lax.all_gather(half_full[3], "dp", axis=0, tiled=True),
-        lax.all_gather(half_full[4], "dp", axis=0, tiled=True),
     )
 
 
@@ -158,15 +324,7 @@
     state_a = rising * summed[:, :, :width]
     state_b = rising * summed[:, :, width:]
     running = rising * fading_feature_factor * (breaks == 0.0).astype(jnp.float32)[:, :, None]
-    ident_one = jnp.ones_like(running[:, 0])
-    ident_zero = jnp.zeros_like(running[:, 0])
-    carried_m, enter_a, enter_b = prefix(
-        (running[:, -1], state_a[:, -1], state_b[:, -1]),
-        "seq",
-        link_states,
-        (ident_one, ident_zero, ident_zero),
-        False,
-    )
+    enter_a, enter_b = entering(running[:, -1], state_a[:, -1], state_b[:, -1], 1)
     whole_a = state_a + running * enter_a[:, None]
     whole_b = state_b + running * enter_b[:, None]
     visited_first = (
@@ -223,11 +381,7 @@
     chain_m = start_live * fading_feature_factor * running[:, 0]
     chain_a = start_live * (numerator_cotangent[:, 0] + fading_feature_factor * local_a[:, 0])
     chain_b = start_live * (grad_bottom[:, 0] + fading_feature_factor * local_b[:, 0])
-    ident_one = jnp.ones_like(chain_m)
-    ident_zero = jnp.zeros_like(chain_m)
-    carried_m, leave_a, leave_b = prefix(
-        (chain_m, chain_a, chain_b), "seq", link_states, (ident_one, ident_zero, ident_zero), True
-    )
+    leave_a, leave_b = entering(chain_m, chain_a, chain_b, -1)
     cotangent_first = local_a + running * leave_a[:, None]
     grad_b = local_b + running * leave_b[:, None]
     amplified_cotangent = numerator_cotangent * entering_contents + grad_bottom
@@ -313,7 +467,7 @@
     )
     lookup_cotangent = lookup_cotangent.reshape(-1, dim_n).astype(jnp.bfloat16)
     content_cotangent = content_cotangent.reshape(-1, dim_n).astype(jnp.bfloat16)
-    grad_kvr = jnp.stack(
+    grad_kvr = tuple(
         [
             matmul_tn(flat_k, lookup_cotangent),
             matmul_tn(flat_v, content_cotangent),
@@ -383,6 +537,66 @@
     )
 
 
+def entering(chain, end_a, end_b, by):
+    ends, chain = jnp.stack([end_a, end_b]), chain[None]
+    came = passed_along(ends, "seq", by)
+    for _ in range(lax.axis_size("seq") - 2):
+        came = passed_along(ends + chain * came, "seq", by)
+    return came[0], came[1]
+
+
+def packed(parts):
+    return jnp.concatenate(parts, axis=-2)
+
+
+def gather_group(core, table, firsts, seconds):
+    if not paired():
+        pairs = [gather_pair(core, table, a, b) for a, b in zip(firsts, seconds)]
+        return [a for a, _ in pairs], [b for _, b in pairs]
+    mine, other = gather_pair(core, table, packed(firsts), packed(seconds))
+    cuts = np.cumsum([a.shape[0] for a in firsts])[:-1].tolist()
+    return jnp.split(mine, cuts, axis=2), jnp.split(other, cuts, axis=2)
+
+
+def scatter_group(core, table, stores):
+    if not paired():
+        pairs = [scatter_pair(core, table, s) for s in stores]
+        return [a for a, _ in pairs], [b for _, b in pairs]
+    first, second = scatter_pair(core, table, packed(stores))
+    cuts = np.cumsum([s.shape[3] for s in stores])[:-1].tolist()
+    return jnp.split(first, cuts, axis=0), jnp.split(second, cuts, axis=0)
+
+
+def whole_matrix(store):
+    seq, dp, rows, columns = store.shape
+    return store.transpose(1, 2, 0, 3).reshape(dp * rows, seq * columns)
+
+
+def store_of(matrix):
+    dp, seq = sizes()
+    rows, columns = matrix.shape
+    return matrix.reshape(dp, rows // dp, seq, columns // seq).transpose(2, 0, 1, 3)
+
+
+def channel_width(shard):
+    return min(512, shard.shape[1] // 2)
+
+
+def cut_lookup(shard, grain):
+    rows, columns = shard.shape
+    width = min(512, columns // 2)
+    cut = shard.reshape(rows, columns // (2 * grain), 2, grain).transpose(2, 0, 1, 3)
+    cut = cut.reshape(2, rows, columns // 2 // width, width).transpose(0, 2, 1, 3)
+    return cut.reshape(2, -1, width)
+
+
+def join_lookup(first, second, rows, grain):
+    width = first.shape[-1]
+    cut = jnp.stack([first, second]).reshape(2, -1, rows, width).transpose(0, 2, 1, 3)
+    cut = cut.reshape(2, rows, -1, grain).transpose(1, 2, 0, 3)
+    return cut.reshape(rows, -1)
+
+
 def per_device(
     entering_activations,
     document_numbers,
@@ -398,149 +612,120 @@
     channelmix_content_matrix,
     channelmix_accept_matrix,
 ):
-    weights = (
-        attention_triple_matrix,
-        attention_result_matrix,
-        channelmix_lookup_matrix,
-        channelmix_content_matrix,
-        channelmix_accept_matrix,
-    )
+    dp, seq = sizes()
+    core = core_of()
+    table = unit_tables() if paired() else None
     layer_count = attention_triple_matrix.shape[0]
     border_ids = passed_along(document_numbers[:, -1:] + 1, "seq", 1)
     earlier_ids = jnp.concatenate([border_ids - 1, document_numbers[:, :-1]], axis=1)
-    alive_all = (document_numbers == earlier_ids).astype(jnp.float32)
+    alive = (document_numbers == earlier_ids).astype(jnp.float32)
     decay_all = jnp.exp(-jnp.exp(fading_natural_logs_per_feature))
-    reward_per_feature = jnp.exp(feature_reward_logs)
-    per_batch = entering_activations.shape[0] // MB
-    outputs = []
-    input_grads = []
-    small_layers = [None] * layer_count
-    large_layers = [None] * layer_count
-    for batch_idx in range(MB):
-        rows_lo = batch_idx * per_batch
-        residual_flow = entering_activations[rows_lo : rows_lo + per_batch].astype(jnp.float32)
-        active_token_flags = alive_all[rows_lo : rows_lo + per_batch]
-        held_sets = []
-        kept_time = []
-        kept_chan = []
-        for depth_position in range(layer_count):
-            complete_group = fetch_layer(weights, depth_position)
-            held_sets.append(complete_group)
-            residual_flow, kept_vals = time_forward(
-                residual_flow,
-                active_token_flags,
-                normalizer_scales[depth_position, 0],
-                normalizer_offsets[depth_position, 0],
-                shift_blend_factors[depth_position, :3],
-                decay_all[depth_position],
-                reward_per_feature[depth_position],
-                complete_group,
-            )
-            kept_time.append(kept_vals)
-            residual_flow, kept_vals = channel_forward(
-                residual_flow,
-                active_token_flags,
-                normalizer_scales[depth_position, 1],
-                normalizer_offsets[depth_position, 1],
-                shift_blend_factors[depth_position, 3:],
-                complete_group,
-            )
-            kept_chan.append(kept_vals)
-        outputs.append(residual_flow.astype(jnp.bfloat16))
-        grad_stream = result_cotangent[rows_lo : rows_lo + per_batch].astype(jnp.float32)
-        for depth_position in reversed(range(layer_count)):
-            complete_group = held_sets[depth_position]
-            grad_stream, small_chan, large_chan = channel_backward(
-                grad_stream,
-                kept_chan[depth_position],
-                shift_blend_factors[depth_position, 3:],
-                active_token_flags,
-                complete_group,
-            )
-            grad_stream, small_time, large_time = time_backward(
-                grad_stream,
-                kept_time[depth_position],
-                shift_blend_factors[depth_position, :3],
-                decay_all[depth_position],
-                active_token_flags,
-                complete_group,
-            )
-            grad_td = (
-                small_time[3]
-                * decay_all[depth_position]
-                * -jnp.exp(fading_natural_logs_per_feature[depth_position])
-            )
-            small_now = (
-                jnp.stack([small_time[0], small_chan[0]]),
-                jnp.stack([small_time[1], small_chan[1]]),
-                jnp.concatenate([small_time[2], small_chan[2]], axis=0),
-                grad_td,
-                small_time[4],
-            )
-            large_now = (large_time[0], large_time[1], large_chan[0], large_chan[1], large_chan[2])
-            if small_layers[depth_position] is None:
-                small_layers[depth_position] = small_now
-                large_layers[depth_position] = large_now
-            else:
-                small_layers[depth_position] = jax.tree.map(
-                    jnp.add, small_layers[depth_position], small_now
-                )
-                large_layers[depth_position] = jax.tree.map(
-                    jnp.add, large_layers[depth_position], large_now
-                )
-        input_grads.append(grad_stream)
-    small_stack = jax.tree.map(lambda *members: jnp.stack(members), *small_layers)
-    large_stack = jax.tree.map(lambda *members: jnp.stack(members), *large_layers)
-    owned_dp = (
-        lax.psum_scatter(
-            large_stack[0].astype(jnp.bfloat16), "dp", scatter_dimension=2, tiled=True
-        ).astype(jnp.float32),
-        lax.psum_scatter(
-            large_stack[1].astype(jnp.bfloat16), "dp", scatter_dimension=1, tiled=True
-        ).astype(jnp.float32),
-        lax.psum_scatter(
-            large_stack[2].astype(jnp.bfloat16), "dp", scatter_dimension=1, tiled=True
-        ).astype(jnp.float32),
-        lax.psum_scatter(
-            large_stack[3].astype(jnp.bfloat16), "dp", scatter_dimension=1, tiled=True
-        ).astype(jnp.float32),
-        lax.psum_scatter(
-            large_stack[4].astype(jnp.bfloat16), "dp", scatter_dimension=1, tiled=True
-        ).astype(jnp.float32),
-    )
-    owned_all = (
-        lax.psum_scatter(
-            owned_dp[0].astype(jnp.bfloat16), "seq", scatter_dimension=3, tiled=True
-        ).astype(jnp.float32),
-        lax.psum_scatter(
-            owned_dp[1].astype(jnp.bfloat16), "seq", scatter_dimension=2, tiled=True
-        ).astype(jnp.float32),
-        lax.psum_scatter(
-            owned_dp[2].astype(jnp.bfloat16), "seq", scatter_dimension=2, tiled=True
-        ).astype(jnp.float32),
-        lax.psum_scatter(
-            owned_dp[3].astype(jnp.bfloat16), "seq", scatter_dimension=2, tiled=True
-        ).astype(jnp.float32),
-        lax.psum_scatter(
-            owned_dp[4].astype(jnp.bfloat16), "seq", scatter_dimension=2, tiled=True
-        ).astype(jnp.float32),
-    )
-    small_sum = lax.psum(small_stack, ("dp", "seq"))
-    y_out = jnp.concatenate(outputs, axis=0)
-    grad_x = jnp.concatenate(input_grads, axis=0)
+    reward_all = jnp.exp(feature_reward_logs)
+    grain = channelmix_content_matrix.shape[1] // 2
+    half_rows = channelmix_accept_matrix.shape[1] // 2
+
+    groups = []
+    for depth in range(layer_count):
+        triple, result = attention_triple_matrix[depth], attention_result_matrix[depth]
+        mine, other = gather_group(core, table, [triple[0], triple[1]], [triple[2], result])
+        first = [jnp.where(core == 0, a, b) for a, b in zip(mine, other)]
+        second = [jnp.where(core == 0, b, a) for a, b in zip(mine, other)]
+        kvr = [whole_matrix(w) for w in (first[0], first[1], second[0])]
+        out = whole_matrix(second[1])
+        lookup = cut_lookup(channelmix_lookup_matrix[depth], grain)
+        content, accept = channelmix_content_matrix[depth], channelmix_accept_matrix[depth]
+        mine, other = gather_group(
+            core,
+            table,
+            [lookup[0], content[:grain], accept[:half_rows]],
+            [lookup[1], content[grain:], accept[half_rows:]],
+        )
+        first = [jnp.where(core == 0, a, b) for a, b in zip(mine, other)]
+        second = [jnp.where(core == 0, b, a) for a, b in zip(mine, other)]
+        rows, width = channelmix_lookup_matrix.shape[1], lookup.shape[-1]
+        def of_lookup(store):
+            store = store.reshape(seq, dp, -1, rows, width).transpose(1, 3, 0, 2, 4)
+            return store.reshape(dp * rows, -1)
+
+        full_lookup = jnp.concatenate([of_lookup(first[0]), of_lookup(second[0])], axis=1)
+        full_content = jnp.concatenate([whole_matrix(first[1]), whole_matrix(second[1])], axis=0)
+        full_accept = whole_matrix(jnp.concatenate([first[2], second[2]], axis=2))
+        groups.append((kvr, out, full_lookup, full_content, full_accept))
+
+    residual_flow = entering_activations.astype(jnp.float32)
+    kept_time, kept_chan = [], []
+    for depth in range(layer_count):
+        residual_flow, kept = time_forward(
+            residual_flow,
+            alive,
+            normalizer_scales[depth, 0],
+            normalizer_offsets[depth, 0],
+            shift_blend_factors[depth, :3],
+            decay_all[depth],
+            reward_all[depth],
+            groups[depth],
+        )
+        kept_time.append(kept)
+        residual_flow, kept = channel_forward(
+            residual_flow,
+            alive,
+            normalizer_scales[depth, 1],
+            normalizer_offsets[depth, 1],
+            shift_blend_factors[depth, 3:],
+            groups[depth],
+        )
+        kept_chan.append(kept)
+    y_out = residual_flow.astype(jnp.bfloat16)
+    grad_stream = result_cotangent.astype(jnp.float32)
+    small, large = [None] * layer_count, [None] * layer_count
+    for depth in reversed(range(layer_count)):
+        grad_stream, small_chan, (grad_fkey, grad_fval, grad_frec) = channel_backward(
+            grad_stream, kept_chan[depth], shift_blend_factors[depth, 3:], alive, groups[depth]
+        )
+        rows, width = channelmix_lookup_matrix.shape[1], min(512, grad_fkey.shape[1] // seq // 2)
+        key = grad_fkey.astype(BF).reshape(dp, rows, 2, seq, -1, width)
+        key = key.transpose(2, 3, 0, 4, 1, 5).reshape(2, seq, dp, -1, width)
+        value = grad_fval.astype(BF).reshape(2, dp, grain, seq, -1).transpose(0, 3, 1, 2, 4)
+        take = grad_frec.astype(BF).reshape(dp, 2, half_rows, seq, -1).transpose(1, 3, 0, 2, 4)
+        first, second = scatter_group(core, table, [key, value, take])
+        chan_shards = (
+            join_lookup(first[0], second[0], rows, grain),
+            jnp.concatenate([first[1], second[1]]),
+            jnp.concatenate([first[2], second[2]]),
+        )
+        grad_stream, small_time, (grad_kvr, grad_wout) = time_backward(
+            grad_stream,
+            kept_time[depth],
+            shift_blend_factors[depth, :3],
+            decay_all[depth],
+            alive,
+            groups[depth],
+        )
+        parts = [store_of(g.astype(BF)) for g in (grad_kvr[0], grad_kvr[1], grad_kvr[2], grad_wout)]
+        first, second = scatter_group(
+            core, table, [jnp.stack([parts[0], parts[2]]), jnp.stack([parts[1], parts[3]])]
+        )
+        large[depth] = (jnp.stack([first[0], first[1], second[0]]), second[1]) + chan_shards
+        grad_td = small_time[3] * decay_all[depth] * -jnp.exp(fading_natural_logs_per_feature[depth])
+        small[depth] = jnp.concatenate(
+            [
+                jnp.stack([small_time[0], small_chan[0], small_time[1], small_chan[1]]),
+                small_time[2],
+                small_chan[2],
+                jnp.stack([grad_td, small_time[4]]),
+            ]
+        )
+    small = summed_everywhere(jnp.stack(small))
+    large = [jnp.stack(members) for members in zip(*large)]
     return (
         y_out,
-        grad_x,
-        small_sum[0],
-        small_sum[1],
-        small_sum[2],
-        small_sum[3],
-        small_sum[4],
-        owned_all[0],
-        owned_all[1],
-        owned_all[2],
-        owned_all[3],
-        owned_all[4],
+        grad_stream,
+        small[:, 0:2],
+        small[:, 2:4],
+        small[:, 4:9],
+        small[:, 9],
+        small[:, 10],
+        *large,
     )
 
 

time: 1830 us -> 1890 us (1.033)
  waiting for transfers between devices: 801 us -> 295 us
  local copies, waits for them, and re-layouts: 82.3 us -> 496 us
  starting transfers between devices: 29.9 us -> 210 us
  blocking collectives: 136 us -> 0 us
  Pallas kernels: 0 us -> 98.1 us
  other arithmetic: 284 us -> 358 us
  matrix products: 465 us -> 395 us
    reduce_scatter x10 -> x4, waiting for transfers between devices: 401 us -> 0.03 us  [scatter_pair(): lax.psum_scatter(flat, 'dp', scatter_dimension=0, axis_index_groups=groups)]
    ppermute x0 -> x57, waiting for transfers between devices: none -> 294 us  [moved(): return lax.ppermute(array, BOTH, pairs)]
    all_gather x10 -> x0, waiting for transfers between devices: 271 us -> none  [the longest x2 121 us: fetch_layer(): lax.all_gather(half_full[3], 'dp', axis=0, tiled=True)]
    reshape x0 -> x45, local copies, waits for them, and re-layouts: none -> 214 us  [the longest x16 53.6 us: store_of(): matrix.reshape(dp, rows // dp, seq, columns // seq).transpose(2, 0, 1, 3)]
    ppermute x0 -> x57, starting transfers between devices: none -> 187 us  [moved(): return lax.ppermute(array, BOTH, pairs)]
    all_gather x34 -> x0, blocking collectives: 136 us -> none  [the longest x24 80.5 us: prefix(): everything = jax.tree.map(lambda part: lax.all_gather(part, axis), array)]
    psum x1 -> x0, waiting for transfers between devices: 128 us -> none  [per_device(): small_sum = lax.psum(small_stack, ('dp', 'seq'))]
    transpose x0 -> x22, local copies, waits for them, and re-layouts: none -> 112 us  [the longest x14 63 us: whole_matrix(): return store.transpose(1, 2, 0, 3).reshape(dp * rows, seq * columns)]
  transfers between devices with their start and end apart: 38 -> 74, of which waited for: 17 -> 21; matrix products, arithmetic and copies ran while one was open for 28% -> 41% of each run, Pallas kernels for 0% -> 5%
where the time goes in v1:
time: 1890 us; the launch traced here: 1870 us
  local copies, waits for them, and re-layouts  496 us (26%)
  matrix products  395 us (21%)
  other arithmetic  358 us (19%)
  waiting for transfers between devices  295 us (16%)
  starting transfers between devices  210 us (11%)
  Pallas kernels  98.1 us (5%)
    ppermute x57, waiting for transfers between devices, moved(): return lax.ppermute(array, BOTH, pairs)  294 us
    ppermute x57, starting transfers between devices, moved(): return lax.ppermute(array, BOTH, pairs)  187 us
    dot_general x14, matrix products, matmul_nt(): lax.dot_general(first_op, second_op, (((1,), (1,)), ((), ())), preferred_...  136 us
    dot_general x14, matrix products, matmul_tn(): lax.dot_general(first_op, second_op, (((0,), (0,)), ((), ())), preferred_...  108 us
    dot_general x14, matrix products, matmul(): return jnp.dot(first_op, second_op, preferred_element_type=jnp.float32)  106 us
    unnamed x718, local copies, waits for them, and re-layouts  106 us
    transpose x14, local copies, waits for them, and re-layouts, whole_matrix(): return store.transpose(1, 2, 0, 3).reshape(dp * rows, seq * columns)  63 us
    reshape x16, local copies, waits for them, and re-layouts, store_of(): matrix.reshape(dp, rows // dp, seq, columns // seq).transpose(2, 0, 1, 3)  53.6 us
  transfers between devices with their start and end apart: 74, of which 21 were waited for; matrix products, arithmetic and copies ran while one was open for 41% of the time, Pallas kernels for 5%

profile of v1, /device:TPU:1, one launch (start us, length us, event | category | flops | bytes accessed | tf_op | source)
XLA Modules:
  0.0 1870.2 jit_solution(11803798701379801415)
XLA Ops:
  43.4 16.7 collective-permute-done.4
  75.5 38.6 %collective-permute-done.13 = bf16[2,288,512]{2,1,0:T(8,128)(2,1)S(1)} collective-permute-done((bf16[2,288,512]{2,1,0:T(8,128)(2,1)S(1)}, bf16[2,288,512]{2,1,0:T(8,128)(2,1)S(1)}, u32[]{:S(2)}, u32[]{:S(2)}) %collective-permute-start.13) | collective-permute-done | bytes 589856 | tf_op jit(solution)/shard_map/ppermute | solution.py:44
  139.0 34.3 %collective-permute-done.30 = bf16[2,288,512]{2,1,0:T(8,128)(2,1)S(1)} collective-permute-done((bf16[2,288,512]{2,1,0:T(8,128)(2,1)S(1)}, bf16[2,288,512]{2,1,0:T(8,128)(2,1)S(1)}, u32[]{:S(2)}, u32[]{:S(2)}) %collective-permute-start.30) | collective-permute-done | bytes 589856 | tf_op jit(solution)/shard_map/ppermute | solution.py:44
  186.4 10.9 shard_map.229
  229.4 14.8 collective-permute-done.21
  248.3 11.5 add_convert_fusion.19
  297.4 13.8 shard_map.230
  311.2 60.4 %collective-permute-start.17 = (bf16[16,576,512]{2,1,0:T(8,128)(2,1)}, bf16[16,576,512]{2,1,0:T(8,128)(2,1)}, u32[]{:S(2)}, u32[]{:S(2)}) collective-permute-start(bf16[16,576,512]{2,1,0:T(8,128)(2,1)} %shard_map.230), channel_id=1, source_target_pairs={{0,2},{1,3},{2,0},{3,1},{4,6},{5,7},{6,4},{7,5},{8,10},{9,11},{10,... | collective-permute-start | bytes 28311560 | tf_op jit(solution)/shard_map/ppermute | solution.py:44
  383.2 13.3 shard_map.232
  420.5 11.2 shard_map.231
  445.8 10.6 slice_add_fusion.2
  528.4 12.2 broadcast_select_fusion
  648.3 14.9 fusion.138
  663.2 14.5 fusion.47
  805.6 14.5 fusion.140
  820.2 16.3 fusion.48
  843.6 17.9 multiply_convert_fusion.1
  861.6 12.8 fusion.141
  939.0 11.8 fusion.8
  1022.4 10.6 multiply_reduce_fusion.2
  1064.3 17.2 multiply_convert_fusion
  1081.6 15.1 fusion.144
  1096.7 19.9 %multiply_reduce_fusion.7 = (f32[1024]{0:T(1024)}, f32[1024]{0:T(1024)}, f32[1024]{0:T(1024)}, f32[2,512,1024]{2,1,0:T(8,128)}, f32[2,512,1024]{2,1,0:T(8,128)}) fusion(f32[2,512,1024]{2,1,0:T(8,128)} %copy-done.12, f32[2,512]{1,0:T(2,128)S(1)} %get-tuple-element.114, f32[2,511,1024]{2,1,0:T(8,128)} %bitcast.709, f32[2,1,1024]{2,1,0:T(1,128)S(1)} %copy-done.308, ...), kind=kOutput, calls=%fused_computation.131 | convolution fusion | flops 2172646400 | bytes 48279552 | tf_op jit(solution)/shard_map/dot_general | solution.py:246
  1161.3 12.0 fusion.12
  1260.2 14.8 convolution_convert_fusion.1
  1274.9 14.4 reshape.1847
  1299.7 17.4 convolution_convert_fusion
  1317.1 14.5 reshape.1849
  1340.2 14.3 pad_maximum_fusion.1
  1356.1 15.3 convolution_convert_fusion.3
  1371.4 15.3 reshape.1841
  1386.7 10.4 copy.166
  1397.1 17.2 convolution_convert_fusion.2
  1414.3 14.5 reshape.1843
  1445.2 14.4 pad_maximum_fusion
  1486.9 10.4 multiply_reduce_fusion
  1512.0 11.1 shard_map.234
  1523.8 11.0 shard_map.233
  1545.9 13.3 shard_map.236
  1566.1 13.4 shard_map.235
  1580.3 42.3 %collective-permute-done.43 = f32[2,11,1024]{2,0,1:T(2,128)S(1)} collective-permute-done((f32[2,11,1024]{2,0,1:T(2,128)S(1)}, f32[2,11,1024]{2,0,1:T(2,128)S(1)}, u32[]{:S(2)}, u32[]{:S(2)}) %collective-permute-start.43) | collective-permute-done | bytes 90144 | tf_op jit(solution)/shard_map/ppermute | solution.py:44
  1655.8 12.1 collective-permute-done.47
  1684.8 27.9 %collective-permute-start.57 = (f32[128,512]{1,0:T(8,128)S(1)}, f32[128,512]{1,0:T(8,128)S(1)}, u32[]{:S(2)}, u32[]{:S(2)}) collective-permute-start(f32[128,512]{1,0:T(8,128)S(1)} %slice_select_fusion.4), channel_id=1, source_target_pairs={{0,2},{1,3},{2,0},{3,1},{4,6},{5,7},{6,4},{7,5},{8,10},{9,11},{10,... | collective-permute-start | bytes 786440 | tf_op jit(solution)/shard_map/ppermute | solution.py:44
  1725.2 18.2 collective-permute-done.65
  1750.6 18.1 collective-permute-done.59
  1774.2 29.9 %collective-permute-done.67 = bf16[576,512]{1,0:T(8,128)(2,1)S(1)} collective-permute-done((bf16[576,512]{1,0:T(8,128)(2,1)S(1)}, bf16[576,512]{1,0:T(8,128)(2,1)S(1)}, u32[]{:S(2)}, u32[]{:S(2)}) %collective-permute-start.67) | collective-permute-done | bytes 589856 | tf_op jit(solution)/shard_map/ppermute | solution.py:44
  1804.5 25.7 %collective-permute-start.69 = (f32[288,512]{1,0:T(8,128)S(1)}, f32[288,512]{1,0:T(8,128)S(1)}, u32[]{:S(2)}, u32[]{:S(2)}) collective-permute-start(f32[288,512]{1,0:T(8,128)S(1)} %slice_select_fusion), channel_id=1, source_target_pairs={{0,2},{1,3},{2,0},{3,1},{4,6},{5,7},{6,4},{7,5},{8,10},{9,11},{10,... | collective-permute-start | bytes 1769480 | tf_op jit(solution)/shard_map/ppermute | solution.py:44
  1831.0 20.3 %collective-permute-done.61 = bf16[576,512]{1,0:T(8,128)(2,1)S(1)} collective-permute-done((bf16[576,512]{1,0:T(8,128)(2,1)S(1)}, bf16[576,512]{1,0:T(8,128)(2,1)S(1)}, u32[]{:S(2)}, u32[]{:S(2)}) %collective-permute-start.61) | collective-permute-done | bytes 589856 | tf_op jit(solution)/shard_map/ppermute | solution.py:44
  (1189 shorter events, 1009.9 us)
Async XLA Ops:
  7.2 1504.8 %reduce-scatter.7.cloned.1.call-start = ((), (), s32[]{:S(2)}) async-start(), calls=%async_computation.5 | async-start | bytes 12582912 | tf_op jit(solution)/shard_map/reduce_scatter | solution.py:195
  17.9 104.0 %collective-permute-start.28 = (bf16[288,512]{1,0:T(8,128)(2,1)}, bf16[288,512]{1,0:T(8,128)(2,1)S(1)}, u32[]{:S(2)}, u32[]{:S(2)}) collective-permute-start(bf16[288,512]{1,0:T(8,128)(2,1)} %maximum_select_fusion.8), channel_id=1, source_target_pairs={{0,2},{1,3},{2,0},{3,1},{4,6},{5,7},{6,4},{7,5},{8,10},{9,11},{10,... | collective-permute-start | bytes 884744 | tf_op jit(solution)/shard_map/ppermute | solution.py:44
  20.3 41.3 %collective-permute-start.11 = (bf16[288,512]{1,0:T(8,128)(2,1)S(1)}, bf16[288,512]{1,0:T(8,128)(2,1)S(1)}, u32[]{:S(2)}, u32[]{:S(2)}) collective-permute-start(bf16[288,512]{1,0:T(8,128)(2,1)S(1)} %maximum_select_fusion.5), channel_id=1, source_target_pairs={{0,2},{1,3},{2,0},{3,1},{4,6},{5,7},{6,4},{7,5},{8,10},{9,11},{10,... | collective-permute-start | bytes 884744 | tf_op jit(solution)/shard_map/ppermute | solution.py:44
  60.2 56.5 %collective-permute-start.6 = (bf16[4,256,512]{2,1,0:T(8,128)(2,1)S(1)}, bf16[4,256,512]{2,1,0:T(8,128)(2,1)S(1)}, u32[]{:S(2)}, u32[]{:S(2)}) collective-permute-start(bf16[4,256,512]{2,1,0:T(8,128)(2,1)S(1)} %pad_maximum_fusion.4), channel_id=1, source_target_pairs={{0,4},{1,5},{2,3},{3,2},{4,0},{5,1},{6,7},{7,6},{8,12},{9,13},{10,... | collective-permute-start | bytes 3145736 | tf_op jit(solution)/shard_map/ppermute | solution.py:44
  61.7 52.4 %collective-permute-start.13 = (bf16[2,288,512]{2,1,0:T(8,128)(2,1)S(1)}, bf16[2,288,512]{2,1,0:T(8,128)(2,1)S(1)}, u32[]{:S(2)}, u32[]{:S(2)}) collective-permute-start(bf16[2,288,512]{2,1,0:T(8,128)(2,1)S(1)} %maximum_select_fusion.1), channel_id=1, source_target_pairs={{0,16},{1,17},{2,18},{3,19},{4,20},{5,21},{6,22},{7,23},{8,24},{9,... | collective-permute-start | bytes 1769480 | tf_op jit(solution)/shard_map/ppermute | solution.py:44
  64.0 50.1 %collective-permute-start.12 = (bf16[2,288,512]{2,1,0:T(8,128)(2,1)S(1)}, bf16[2,288,512]{2,1,0:T(8,128)(2,1)S(1)}, u32[]{:S(2)}, u32[]{:S(2)}) collective-permute-start(bf16[2,288,512]{2,1,0:T(8,128)(2,1)S(1)} %maximum_select_fusion.1), channel_id=1, source_target_pairs={{0,8},{1,9},{2,10},{3,11},{4,12},{5,13},{6,14},{7,15},{8,16},{9,17... | collective-permute-start | bytes 1769480 | tf_op jit(solution)/shard_map/ppermute | solution.py:44
  116.0 81.4 %collective-permute-start.15 = (bf16[4,576,512]{2,1,0:T(8,128)(2,1)}, bf16[4,576,512]{2,1,0:T(8,128)(2,1)}, u32[]{:S(2)}, u32[]{:S(2)}) collective-permute-start(bf16[4,576,512]{2,1,0:T(8,128)(2,1)} %pad_maximum_fusion.2), channel_id=1, source_target_pairs={{0,4},{1,5},{2,3},{3,2},{4,0},{5,1},{6,7},{7,6},{8,12},{9,13},{10,... | collective-permute-start | bytes 7077896 | tf_op jit(solution)/shard_map/ppermute | solution.py:44
  117.8 68.6 %collective-permute-start.7 = (bf16[8,256,512]{2,1,0:T(8,128)(2,1)}, bf16[8,256,512]{2,1,0:T(8,128)(2,1)}, u32[]{:S(2)}, u32[]{:S(2)}) collective-permute-start(bf16[8,256,512]{2,1,0:T(8,128)(2,1)} %constant_dynamic-update-slice_fusion.own_ref), channel_id=1, source_target_pairs={{0,1},{1,0},{2,6},{3,7},{4,5},{5,4},{6,2},{7,3},{8,9},{9,8},{10,14... | collective-permute-start | bytes 6291464 | tf_op jit(solution)/shard_map/ppermute | solution.py:44
  122.1 51.3 %collective-permute-start.30 = (bf16[2,288,512]{2,1,0:T(8,128)(2,1)S(1)}, bf16[2,288,512]{2,1,0:T(8,128)(2,1)S(1)}, u32[]{:S(2)}, u32[]{:S(2)}) collective-permute-start(bf16[2,288,512]{2,1,0:T(8,128)(2,1)S(1)} %maximum_select_fusion.3), channel_id=1, source_target_pairs={{0,16},{1,17},{2,18},{3,19},{4,20},{5,21},{6,22},{7,23},{8,24},{9,... | collective-permute-start | bytes 1769480 | tf_op jit(solution)/shard_map/ppermute | solution.py:44
  122.9 52.1 %collective-permute-start.29 = (bf16[2,288,512]{2,1,0:T(8,128)(2,1)S(1)}, bf16[2,288,512]{2,1,0:T(8,128)(2,1)S(1)}, u32[]{:S(2)}, u32[]{:S(2)}) collective-permute-start(bf16[2,288,512]{2,1,0:T(8,128)(2,1)S(1)} %maximum_select_fusion.3), channel_id=1, source_target_pairs={{0,8},{1,9},{2,10},{3,11},{4,12},{5,13},{6,14},{7,15},{8,16},{9,17... | collective-permute-start | bytes 1769480 | tf_op jit(solution)/shard_map/ppermute | solution.py:44
  135.3 83.0 %collective-permute-start.1 = (s32[2,1]{1,0:T(2,128)S(1)}, s32[2,1]{1,0:T(2,128)S(1)}, u32[]{:S(2)}, u32[]{:S(2)}) collective-permute-start(s32[2,1]{1,0:T(2,128)S(1)} %slice_add_fusion.4), channel_id=1, source_target_pairs={{0,1},{2,3},{4,5},{6,7},{8,9},{10,11},{12,13},{14,15},{16,17},{18,... | collective-permute-start | bytes 32 | tf_op jit(solution)/shard_map/ppermute | solution.py:231
  173.4 45.7 %collective-permute-start.19 = (bf16[128,512]{1,0:T(8,128)(2,1)}, bf16[128,512]{1,0:T(8,128)(2,1)}, u32[]{:S(2)}, u32[]{:S(2)}) collective-permute-start(bf16[128,512]{1,0:T(8,128)(2,1)} %maximum_select_fusion.18), channel_id=1, source_target_pairs={{0,2},{1,3},{2,0},{3,1},{4,6},{5,7},{6,4},{7,5},{8,10},{9,11},{10,... | collective-permute-start | bytes 393224 | tf_op jit(solution)/shard_map/ppermute | solution.py:44
  177.5 36.7 %collective-permute-start.32 = (bf16[4,576,512]{2,1,0:T(8,128)(2,1)}, bf16[4,576,512]{2,1,0:T(8,128)(2,1)}, u32[]{:S(2)}, u32[]{:S(2)}) collective-permute-start(bf16[4,576,512]{2,1,0:T(8,128)(2,1)} %pad_maximum_fusion.3), channel_id=1, source_target_pairs={{0,4},{1,5},{2,3},{3,2},{4,0},{5,1},{6,7},{7,6},{8,12},{9,13},{10,... | collective-permute-start | bytes 7077896 | tf_op jit(solution)/shard_map/ppermute | solution.py:44
  197.3 78.3 %collective-permute-start.8 = (bf16[16,256,512]{2,1,0:T(8,128)(2,1)}, bf16[16,256,512]{2,1,0:T(8,128)(2,1)}, u32[]{:S(2)}, u32[]{:S(2)}) collective-permute-start(bf16[16,256,512]{2,1,0:T(8,128)(2,1)} %shard_map.229), channel_id=1, source_target_pairs={{0,2},{1,3},{2,0},{3,1},{4,6},{5,7},{6,4},{7,5},{8,10},{9,11},{10,... | collective-permute-start | bytes 12582920 | tf_op jit(solution)/shard_map/ppermute | solution.py:44
  200.6 96.8 %collective-permute-start.16 = (bf16[8,576,512]{2,1,0:T(8,128)(2,1)}, bf16[8,576,512]{2,1,0:T(8,128)(2,1)}, u32[]{:S(2)}, u32[]{:S(2)}) collective-permute-start(bf16[8,576,512]{2,1,0:T(8,128)(2,1)} %constant_dynamic-update-slice_fusion.5.own_ref), channel_id=1, source_target_pairs={{0,1},{1,0},{2,6},{3,7},{4,5},{5,4},{6,2},{7,3},{8,9},{9,8},{10,14... | collective-permute-start | bytes 14155784 | tf_op jit(solution)/shard_map/ppermute | solution.py:44
  217.5 165.7 %collective-permute-start.33 = (bf16[8,576,512]{2,1,0:T(8,128)(2,1)}, bf16[8,576,512]{2,1,0:T(8,128)(2,1)}, u32[]{:S(2)}, u32[]{:S(2)}) collective-permute-start(bf16[8,576,512]{2,1,0:T(8,128)(2,1)} %constant_dynamic-update-slice_fusion.17.own_ref), channel_id=1, source_target_pairs={{0,1},{1,0},{2,6},{3,7},{4,5},{5,4},{6,2},{7,3},{8,9},{9,8},{10,14... | collective-permute-start | bytes 14155784 | tf_op jit(solution)/shard_map/ppermute | solution.py:44
  221.0 23.2 %collective-permute-start.21 = (bf16[2,128,512]{2,1,0:T(8,128)(2,1)S(1)}, bf16[2,128,512]{2,1,0:T(8,128)(2,1)S(1)}, u32[]{:S(2)}, u32[]{:S(2)}) collective-permute-start(bf16[2,128,512]{2,1,0:T(8,128)(2,1)S(1)} %maximum_select_fusion.13), channel_id=1, source_target_pairs={{0,16},{1,17},{2,18},{3,19},{4,20},{5,21},{6,22},{7,23},{8,24},{9,... | collective-permute-start | bytes 786440 | tf_op jit(solution)/shard_map/ppermute | solution.py:44
  247.6 25.4 %collective-permute-start.23 = (bf16[4,256,512]{2,1,0:T(8,128)(2,1)S(1)}, bf16[4,256,512]{2,1,0:T(8,128)(2,1)S(1)}, u32[]{:S(2)}, u32[]{:S(2)}) collective-permute-start(bf16[4,256,512]{2,1,0:T(8,128)(2,1)S(1)} %pad_maximum_fusion.5), channel_id=1, source_target_pairs={{0,4},{1,5},{2,3},{3,2},{4,0},{5,1},{6,7},{7,6},{8,12},{9,13},{10,... | collective-permute-start | bytes 3145736 | tf_op jit(solution)/shard_map/ppermute | solution.py:44
  274.1 146.3 %collective-permute-start.24 = (bf16[8,256,512]{2,1,0:T(8,128)(2,1)}, bf16[8,256,512]{2,1,0:T(8,128)(2,1)}, u32[]{:S(2)}, u32[]{:S(2)}) collective-permute-start(bf16[8,256,512]{2,1,0:T(8,128)(2,1)} %constant_dynamic-update-slice_fusion.12.own_ref), channel_id=1, source_target_pairs={{0,1},{1,0},{2,6},{3,7},{4,5},{5,4},{6,2},{7,3},{8,9},{9,8},{10,14... | collective-permute-start | bytes 6291464 | tf_op jit(solution)/shard_map/ppermute | solution.py:44
  311.2 204.2 %collective-permute-start.17 = (bf16[16,576,512]{2,1,0:T(8,128)(2,1)}, bf16[16,576,512]{2,1,0:T(8,128)(2,1)}, u32[]{:S(2)}, u32[]{:S(2)}) collective-permute-start(bf16[16,576,512]{2,1,0:T(8,128)(2,1)} %shard_map.230), channel_id=1, source_target_pairs={{0,2},{1,3},{2,0},{3,1},{4,6},{5,7},{6,4},{7,5},{8,10},{9,11},{10,... | collective-permute-start | bytes 28311560 | tf_op jit(solution)/shard_map/ppermute | solution.py:44
  396.5 128.8 %collective-permute-start.34 = (bf16[16,576,512]{2,1,0:T(8,128)(2,1)}, bf16[16,576,512]{2,1,0:T(8,128)(2,1)}, u32[]{:S(2)}, u32[]{:S(2)}) collective-permute-start(bf16[16,576,512]{2,1,0:T(8,128)(2,1)} %shard_map.232), channel_id=1, source_target_pairs={{0,2},{1,3},{2,0},{3,1},{4,6},{5,7},{6,4},{7,5},{8,10},{9,11},{10,... | collective-permute-start | bytes 28311560 | tf_op jit(solution)/shard_map/ppermute | solution.py:44
  413.1 32.5 %collective-permute-start.9 = (f32[2,2,1024]{2,0,1:T(2,128)S(1)}, f32[2,2,1024]{2,0,1:T(2,128)S(1)}, u32[]{:S(2)}, u32[]{:S(2)}) collective-permute-start(f32[2,2,1024]{2,0,1:T(2,128)S(1)} %pad_maximum_fusion.12), channel_id=1, source_target_pairs={{0,1},{2,3},{4,5},{6,7},{8,9},{10,11},{12,13},{14,15},{16,17},{18,... | collective-permute-start | bytes 49160 | tf_op jit(solution)/shard_map/ppermute | solution.py:231
  431.7 40.3 %collective-permute-start.25 = (bf16[16,256,512]{2,1,0:T(8,128)(2,1)}, bf16[16,256,512]{2,1,0:T(8,128)(2,1)}, u32[]{:S(2)}, u32[]{:S(2)}) collective-permute-start(bf16[16,256,512]{2,1,0:T(8,128)(2,1)} %shard_map.231), channel_id=1, source_target_pairs={{0,2},{1,3},{2,0},{3,1},{4,6},{5,7},{6,4},{7,5},{8,10},{9,11},{10,... | collective-permute-start | bytes 12582920 | tf_op jit(solution)/shard_map/ppermute | solution.py:44
  470.4 35.1 %collective-permute-start.10 = (f32[2,1,1024]{2,1,0:T(1,128)S(1)}, f32[2,1,1024]{2,1,0:T(1,128)S(1)}, u32[]{:S(2)}, u32[]{:S(2)}) collective-permute-start(f32[2,1,1024]{2,1,0:T(1,128)S(1)} %slice.771), channel_id=1, source_target_pairs={{0,1},{2,3},{4,5},{6,7},{8,9},{10,11},{12,13},{14,15},{16,17},{18,... | collective-permute-start | bytes 24584 | tf_op jit(solution)/shard_map/ppermute | solution.py:231
  690.6 24.9 %collective-permute-start.18 = (f32[2,1,1024]{2,1,0:T(1,128)S(1)}, f32[2,1,1024]{2,1,0:T(1,128)S(1)}, u32[]{:S(2)}, u32[]{:S(2)}) collective-permute-start(f32[2,1,1024]{2,1,0:T(1,128)S(1)} %slice.775), channel_id=1, source_target_pairs={{0,1},{2,3},{4,5},{6,7},{8,9},{10,11},{12,13},{14,15},{16,17},{18,... | collective-permute-start | bytes 24584 | tf_op jit(solution)/shard_map/ppermute | solution.py:231
  1040.8 483.1 %reduce-scatter.5.cloned.1.call-start = ((), (), s32[]{:S(2)}) async-start(), calls=%async_computation.4 | async-start | bytes 12582912 | tf_op jit(solution)/shard_map/reduce_scatter | solution.py:195
  1182.0 24.7 %collective-permute-start.39 = (f32[2,2,1024]{2,0,1:T(2,128)S(1)}, f32[2,2,1024]{2,0,1:T(2,128)S(1)}, u32[]{:S(2)}, u32[]{:S(2)}) collective-permute-start(f32[2,2,1024]{2,0,1:T(2,128)S(1)} %pad_maximum_fusion.15), channel_id=1, source_target_pairs={{1,0},{3,2},{5,4},{7,6},{9,8},{11,10},{13,12},{15,14},{17,16},{19,... | collective-permute-start | bytes 49160 | tf_op jit(solution)/shard_map/ppermute | solution.py:231
  1245.2 300.7 %reduce-scatter.11.cloned.1.call-start = ((), (), s32[]{:S(2)}) async-start(), calls=%async_computation.7 | async-start | bytes 28311552 | tf_op jit(solution)/shard_map/reduce_scatter | solution.py:195
  1354.5 211.6 %reduce-scatter.9.cloned.1.call-start = ((), (), s32[]{:S(2)}) async-start(), calls=%async_computation.6 | async-start | bytes 28311552 | tf_op jit(solution)/shard_map/reduce_scatter | solution.py:195
  1523.2 104.8 %collective-permute-start.52 = (bf16[8,256,512]{2,1,0:T(8,128)(2,1)}, bf16[8,256,512]{2,1,0:T(8,128)(2,1)}, u32[]{:S(2)}, u32[]{:S(2)}) collective-permute-start(bf16[8,256,512]{2,1,0:T(8,128)(2,1)} %get-tuple-element.23), channel_id=1, source_target_pairs={{0,1},{1,0},{2,6},{3,7},{4,5},{5,4},{6,2},{7,3},{8,9},{9,8},{10,14... | collective-permute-start | bytes 6291464 | tf_op jit(solution)/shard_map/ppermute | solution.py:44
  1534.8 96.8 %collective-permute-start.46 = (bf16[8,256,512]{2,1,0:T(8,128)(2,1)}, bf16[8,256,512]{2,1,0:T(8,128)(2,1)}, u32[]{:S(2)}, u32[]{:S(2)}) collective-permute-start(bf16[8,256,512]{2,1,0:T(8,128)(2,1)} %get-tuple-element.21), channel_id=1, source_target_pairs={{0,1},{1,0},{2,6},{3,7},{4,5},{5,4},{6,2},{7,3},{8,9},{9,8},{10,14... | collective-permute-start | bytes 6291464 | tf_op jit(solution)/shard_map/ppermute | solution.py:44
  1559.2 153.6 %collective-permute-start.64 = (bf16[8,576,512]{2,1,0:T(8,128)(2,1)}, bf16[8,576,512]{2,1,0:T(8,128)(2,1)}, u32[]{:S(2)}, u32[]{:S(2)}) collective-permute-start(bf16[8,576,512]{2,1,0:T(8,128)(2,1)} %get-tuple-element.27), channel_id=1, source_target_pairs={{0,1},{1,0},{2,6},{3,7},{4,5},{5,4},{6,2},{7,3},{8,9},{9,8},{10,14... | collective-permute-start | bytes 14155784 | tf_op jit(solution)/shard_map/ppermute | solution.py:44
  1565.3 57.3 %collective-permute-start.43 = (f32[2,11,1024]{2,0,1:T(2,128)S(1)}, f32[2,11,1024]{2,0,1:T(2,128)S(1)}, u32[]{:S(2)}, u32[]{:S(2)}) collective-permute-start(f32[2,11,1024]{2,0,1:T(2,128)S(1)} %fusion.227), channel_id=1, source_target_pairs={{0,4},{1,5},{2,6},{3,7},{4,0},{5,1},{6,2},{7,3},{8,12},{9,13},{10,... | collective-permute-start | bytes 270344 | tf_op jit(solution)/shard_map/ppermute | solution.py:44
  1579.6 142.2 %collective-permute-start.58 = (bf16[8,576,512]{2,1,0:T(8,128)(2,1)}, bf16[8,576,512]{2,1,0:T(8,128)(2,1)S(1)}, u32[]{:S(2)}, u32[]{:S(2)}) collective-permute-start(bf16[8,576,512]{2,1,0:T(8,128)(2,1)} %get-tuple-element.25), channel_id=1, source_target_pairs={{0,1},{1,0},{2,6},{3,7},{4,5},{5,4},{6,2},{7,3},{8,9},{9,8},{10,14... | collective-permute-start | bytes 14155784 | tf_op jit(solution)/shard_map/ppermute | solution.py:44
  1633.2 34.7 %collective-permute-start.47 = (bf16[4,256,512]{2,1,0:T(8,128)(2,1)S(1)}, bf16[4,256,512]{2,1,0:T(8,128)(2,1)S(1)}, u32[]{:S(2)}, u32[]{:S(2)}) collective-permute-start(bf16[4,256,512]{2,1,0:T(8,128)(2,1)S(1)} %add_convert_fusion.25), channel_id=1, source_target_pairs={{0,4},{1,5},{2,3},{3,2},{4,0},{5,1},{6,7},{7,6},{8,12},{9,13},{10,... | collective-permute-start | bytes 3145736 | tf_op jit(solution)/shard_map/ppermute | solution.py:44
  1655.8 22.8 %collective-permute-start.56 = (bf16[256,512]{1,0:T(8,128)(2,1)S(1)}, bf16[256,512]{1,0:T(8,128)(2,1)S(1)}, u32[]{:S(2)}, u32[]{:S(2)}) collective-permute-start(bf16[256,512]{1,0:T(8,128)(2,1)S(1)} %get-tuple-element.192), channel_id=1, source_target_pairs={{0,8},{1,9},{2,10},{3,11},{4,12},{5,13},{6,14},{7,15},{8,16},{9,17... | collective-permute-start | bytes 786440 | tf_op jit(solution)/shard_map/ppermute | solution.py:44
  1678.6 34.1 %collective-permute-start.50 = (bf16[256,512]{1,0:T(8,128)(2,1)S(1)}, bf16[256,512]{1,0:T(8,128)(2,1)S(1)}, u32[]{:S(2)}, u32[]{:S(2)}) collective-permute-start(bf16[256,512]{1,0:T(8,128)(2,1)S(1)} %get-tuple-element.189), channel_id=1, source_target_pairs={{0,8},{1,9},{2,10},{3,11},{4,12},{5,13},{6,14},{7,15},{8,16},{9,17... | collective-permute-start | bytes 786440 | tf_op jit(solution)/shard_map/ppermute | solution.py:44
  1678.9 33.8 %collective-permute-start.49 = (bf16[256,512]{1,0:T(8,128)(2,1)S(1)}, bf16[256,512]{1,0:T(8,128)(2,1)S(1)}, u32[]{:S(2)}, u32[]{:S(2)}) collective-permute-start(bf16[256,512]{1,0:T(8,128)(2,1)S(1)} %get-tuple-element.190), channel_id=1, source_target_pairs={{0,16},{1,17},{2,18},{3,19},{4,20},{5,21},{6,22},{7,23},{8,24},{9,... | collective-permute-start | bytes 786440 | tf_op jit(solution)/shard_map/ppermute | solution.py:44
  1684.8 39.2 %collective-permute-start.57 = (f32[128,512]{1,0:T(8,128)S(1)}, f32[128,512]{1,0:T(8,128)S(1)}, u32[]{:S(2)}, u32[]{:S(2)}) collective-permute-start(f32[128,512]{1,0:T(8,128)S(1)} %slice_select_fusion.4), channel_id=1, source_target_pairs={{0,2},{1,3},{2,0},{3,1},{4,6},{5,7},{6,4},{7,5},{8,10},{9,11},{10,... | collective-permute-start | bytes 786440 | tf_op jit(solution)/shard_map/ppermute | solution.py:44
  1715.4 28.1 %collective-permute-start.65 = (bf16[4,576,512]{2,1,0:T(8,128)(2,1)S(1)}, bf16[4,576,512]{2,1,0:T(8,128)(2,1)S(1)}, u32[]{:S(2)}, u32[]{:S(2)}) collective-permute-start(bf16[4,576,512]{2,1,0:T(8,128)(2,1)S(1)} %add_convert_fusion.1), channel_id=1, source_target_pairs={{0,4},{1,5},{2,3},{3,2},{4,0},{5,1},{6,7},{7,6},{8,12},{9,13},{10,... | collective-permute-start | bytes 7077896 | tf_op jit(solution)/shard_map/ppermute | solution.py:44
  1722.5 46.2 %collective-permute-start.59 = (bf16[4,576,512]{2,1,0:T(8,128)(2,1)S(1)}, bf16[4,576,512]{2,1,0:T(8,128)(2,1)S(1)}, u32[]{:S(2)}, u32[]{:S(2)}) collective-permute-start(bf16[4,576,512]{2,1,0:T(8,128)(2,1)S(1)} %add_convert_fusion.4), channel_id=1, source_target_pairs={{0,4},{1,5},{2,3},{3,2},{4,0},{5,1},{6,7},{7,6},{8,12},{9,13},{10,... | collective-permute-start | bytes 7077896 | tf_op jit(solution)/shard_map/ppermute | solution.py:44
  1746.2 26.9 %collective-permute-start.66 = (bf16[576,512]{1,0:T(8,128)(2,1)S(1)}, bf16[576,512]{1,0:T(8,128)(2,1)S(1)}, u32[]{:S(2)}, u32[]{:S(2)}) collective-permute-start(bf16[576,512]{1,0:T(8,128)(2,1)S(1)} %get-tuple-element.177), channel_id=1, source_target_pairs={{0,24},{1,25},{2,26},{3,27},{4,28},{5,29},{6,30},{7,31},{8,0},{9,1... | collective-permute-start | bytes 1769480 | tf_op jit(solution)/shard_map/ppermute | solution.py:44
  1746.3 27.9 %collective-permute-start.68 = (bf16[576,512]{1,0:T(8,128)(2,1)S(1)}, bf16[576,512]{1,0:T(8,128)(2,1)S(1)}, u32[]{:S(2)}, u32[]{:S(2)}) collective-permute-start(bf16[576,512]{1,0:T(8,128)(2,1)S(1)} %get-tuple-element.178), channel_id=1, source_target_pairs={{0,8},{1,9},{2,10},{3,11},{4,12},{5,13},{6,14},{7,15},{8,16},{9,17... | collective-permute-start | bytes 1769480 | tf_op jit(solution)/shard_map/ppermute | solution.py:44
  1749.5 54.7 %collective-permute-start.67 = (bf16[576,512]{1,0:T(8,128)(2,1)S(1)}, bf16[576,512]{1,0:T(8,128)(2,1)S(1)}, u32[]{:S(2)}, u32[]{:S(2)}) collective-permute-start(bf16[576,512]{1,0:T(8,128)(2,1)S(1)} %get-tuple-element.179), channel_id=1, source_target_pairs={{0,16},{1,17},{2,18},{3,19},{4,20},{5,21},{6,22},{7,23},{8,24},{9,... | collective-permute-start | bytes 1769480 | tf_op jit(solution)/shard_map/ppermute | solution.py:44
  1769.8 61.1 %collective-permute-start.60 = (bf16[576,512]{1,0:T(8,128)(2,1)S(1)}, bf16[576,512]{1,0:T(8,128)(2,1)S(1)}, u32[]{:S(2)}, u32[]{:S(2)}) collective-permute-start(bf16[576,512]{1,0:T(8,128)(2,1)S(1)} %get-tuple-element.174), channel_id=1, source_target_pairs={{0,24},{1,25},{2,26},{3,27},{4,28},{5,29},{6,30},{7,31},{8,0},{9,1... | collective-permute-start | bytes 1769480 | tf_op jit(solution)/shard_map/ppermute | solution.py:44
  1769.9 61.1 %collective-permute-start.62 = (bf16[576,512]{1,0:T(8,128)(2,1)S(1)}, bf16[576,512]{1,0:T(8,128)(2,1)S(1)}, u32[]{:S(2)}, u32[]{:S(2)}) collective-permute-start(bf16[576,512]{1,0:T(8,128)(2,1)S(1)} %get-tuple-element.175), channel_id=1, source_target_pairs={{0,8},{1,9},{2,10},{3,11},{4,12},{5,13},{6,14},{7,15},{8,16},{9,17... | collective-permute-start | bytes 1769480 | tf_op jit(solution)/shard_map/ppermute | solution.py:44
  1773.1 78.1 %collective-permute-start.61 = (bf16[576,512]{1,0:T(8,128)(2,1)S(1)}, bf16[576,512]{1,0:T(8,128)(2,1)S(1)}, u32[]{:S(2)}, u32[]{:S(2)}) collective-permute-start(bf16[576,512]{1,0:T(8,128)(2,1)S(1)} %get-tuple-element.176), channel_id=1, source_target_pairs={{0,16},{1,17},{2,18},{3,19},{4,20},{5,21},{6,22},{7,23},{8,24},{9,... | collective-permute-start | bytes 1769480 | tf_op jit(solution)/shard_map/ppermute | solution.py:44
  1804.5 50.0 %collective-permute-start.69 = (f32[288,512]{1,0:T(8,128)S(1)}, f32[288,512]{1,0:T(8,128)S(1)}, u32[]{:S(2)}, u32[]{:S(2)}) collective-permute-start(f32[288,512]{1,0:T(8,128)S(1)} %slice_select_fusion), channel_id=1, source_target_pairs={{0,2},{1,3},{2,0},{3,1},{4,6},{5,7},{6,4},{7,5},{8,10},{9,11},{10,... | collective-permute-start | bytes 1769480 | tf_op jit(solution)/shard_map/ppermute | solution.py:44
  (366 other events, 6981.6 us)
Sparse Core Ops, SparseCore 0:
  1040.9 16.2 reduce-scatter.6
  1245.3 16.2 reduce-scatter.4
  1354.7 27.7 reduce-scatter.10
  1459.7 27.7 reduce-scatter.8

commit v2 on v1

v2 whole, which is shorter than its diff:
```python
import jax
import jax.numpy as jnp
import numpy as np
from jax import lax
from jax.experimental import pallas as pl
from jax.experimental.pallas import tpu as pltpu
from jax.sharding import PartitionSpec as P

EPS = 1e-05
BF = jnp.bfloat16
F32 = jnp.float32
BOTH = ("dp", "seq")
VMEM = 58 * 2**20


def sizes():
    return lax.axis_size("dp"), lax.axis_size("seq")


def paired():
    dp, seq = sizes()
    return seq == 2 and dp % 4 == 0


def place(d):
    return d // 4, d // 2 % 2, d % 2


def core_of():
    if not paired():
        return jnp.int32(0)
    return lax.rem(lax.axis_index("dp"), 2)


def moved(array, target):
    dp, seq = sizes()
    pairs = []
    for d in range(dp):
        for y in range(seq):
            z, x, c, y2 = target(*place(d), y)
            pairs.append((d * seq + y, (z * 4 + x * 2 + c) * seq + y2))
    return lax.ppermute(array, BOTH, pairs)


def to_core(z, x, c, y):
    return z, x, 1 - c, y


def to_second(z, x, c, y):
    return (z, 1 - x, c, y) if c == 0 else (z, x, c, 1 - y)


def to_third(z, x, c, y):
    return (z, x, c, 1 - y) if c == 0 else (z, 1 - x, c, y)


def along_z(step):
    depth = sizes()[0] // 4

    def target(z, x, c, y):
        return (z + step) % depth, x, c, y

    return target


def unit_tables():
    dp, seq = sizes()
    depth = dp // 4
    rows = []
    for d in range(dp):
        for y in range(seq):
            z, x, c = place(d)
            half, index = [], []
            for yy in range(2):
                for zz in range(depth):
                    for xx in range(2):
                        dx, dy, dz = xx ^ x, yy ^ y, (z - zz) % depth
                        half.append(dy if c == 0 else dx)
                        index.append((dx if c == 0 else dy) * depth + dz)
            held = []
            for side in range(2):
                own = [i for i, h in zip(index, half) if h == side]
                last, line = own[0], []
                for i, h in zip(index, half):
                    last = i if h == side else last
                    line.append(last)
                held.append(line)
            order = [0] * (4 * depth)
            for unit, (i, h) in enumerate(zip(index, half)):
                order[h * 2 * depth + i] = unit
            rows.append([half, held[0], held[1], order])
    table = jnp.asarray(np.array(rows, np.int32))
    me = lax.axis_index("dp") * seq + lax.axis_index("seq")
    return lax.dynamic_index_in_dim(table, me, 0, keepdims=False)


def arrange(table, own, other):
    units, block = 2 * own.shape[0], (1,) + own.shape[1:]

    def body(table_ref, own_ref, other_ref, out_ref):
        half = table_ref[0, pl.program_id(0)]

        @pl.when(half == 0)
        def _():
            out_ref[...] = own_ref[...]

        @pl.when(half == 1)
        def _():
            out_ref[...] = other_ref[...]

    return pl.pallas_call(
        body,
        grid_spec=pltpu.PrefetchScalarGridSpec(
            num_scalar_prefetch=1,
            grid=(units,),
            in_specs=[
                pl.BlockSpec(block, lambda i, t: (t[1, i], 0, 0)),
                pl.BlockSpec(block, lambda i, t: (t[2, i], 0, 0)),
            ],
            out_specs=pl.BlockSpec(block, lambda i, t: (i, 0, 0)),
        ),
        out_shape=jax.ShapeDtypeStruct((units,) + own.shape[1:], own.dtype),
        compiler_params=pltpu.CompilerParams(vmem_limit_bytes=VMEM),
        cost_estimate=pl.CostEstimate(flops=0, bytes_accessed=4 * own.size * 2, transcendentals=0),
    )(table, own, other)


def split_units(table, whole):
    units, block = whole.shape[0], (1,) + whole.shape[1:]
    half = units // 2

    def body(table_ref, in_ref, away_ref, keep_ref):
        step = pl.program_id(0)

        @pl.when(step < half)
        def _():
            away_ref[...] = in_ref[...]

        @pl.when(step >= half)
        def _():
            keep_ref[...] = in_ref[...]

    shape = jax.ShapeDtypeStruct((half,) + whole.shape[1:], whole.dtype)
    return pl.pallas_call(
        body,
        grid_spec=pltpu.PrefetchScalarGridSpec(
            num_scalar_prefetch=1,
            grid=(units,),
            in_specs=[pl.BlockSpec(block, lambda i, t: (t[3, lax.rem(i + half, units)], 0, 0))],
            out_specs=[
                pl.BlockSpec(block, lambda i, t: (jnp.minimum(i, half - 1), 0, 0)),
                pl.BlockSpec(block, lambda i, t: (jnp.maximum(i - half, 0), 0, 0)),
            ],
        ),
        out_shape=[shape, shape],
        compiler_params=pltpu.CompilerParams(vmem_limit_bytes=VMEM),
        cost_estimate=pl.CostEstimate(flops=0, bytes_accessed=4 * whole.size, transcendentals=0),
    )(table, whole)


def gather_pair(core, table, first, second):
    dp, seq = sizes()
    if not paired():
        return tuple(
            lax.all_gather(part, ("seq", "dp")).reshape((seq, dp) + part.shape)
            for part in (first, second)
        )
    depth = dp // 4
    kept = jnp.where(core == 0, first, second)
    came = moved(jnp.where(core == 0, second, first), to_core)
    pair = jnp.where(core == 0, jnp.stack([kept, came]), jnp.stack([came, kept]))
    line = jnp.stack([pair] + [moved(pair, along_z(step)) for step in range(1, depth)])
    line = line.reshape((depth, -1) + first.shape[1:])
    half = jnp.concatenate([line, moved(line, to_second)])
    mine = arrange(table, half, moved(half, to_third))
    other = moved(mine, to_core)
    shape = (seq, dp) + first.shape
    return mine.reshape(shape), other.reshape(shape)


def scatter_pair(core, table, stores):
    dp, seq = sizes()
    shape = stores.shape[3:]
    if not paired():
        flat = stores.reshape((2, seq * dp) + shape)
        return tuple(
            lax.psum_scatter(flat[i], ("seq", "dp"), scatter_dimension=0).astype(F32)
            for i in range(2)
        )
    depth = dp // 4
    groups = [[2 * i, 2 * i + 1] for i in range(dp // 2)]
    flat = stores.reshape((2, 4 * depth, 2 * shape[0]) + shape[1:])
    own = lax.psum_scatter(flat, "dp", scatter_dimension=0, axis_index_groups=groups)
    away, keep = split_units(table, own)
    came = moved(away, to_third)
    away = (keep[depth:].astype(F32) + came[depth:].astype(F32)).astype(BF)
    keep = (keep[:depth].astype(F32) + came[:depth].astype(F32)).astype(BF)
    came = moved(away, to_second)
    line = (keep.astype(F32) + came.astype(F32)).astype(BF)
    total = line[0].astype(F32)
    for step in range(1, depth):
        total = total + moved(line[step], along_z(-step)).astype(F32)
    total = total.reshape((2,) + shape)
    kept = jnp.where(core == 0, total[0], total[1])
    came = moved(jnp.where(core == 0, total[1], total[0]), to_core)
    return jnp.where(core == 0, kept, came), jnp.where(core == 0, came, kept)


def summed_everywhere(array):
    dp, seq = sizes()
    if not paired():
        return lax.psum(array, BOTH)
    steps = [to_core, lambda z, x, c, y: (z, x, c, 1 - y), lambda z, x, c, y: (z, 1 - x, c, y)]
    for target in steps:
        array = array + moved(array, target)
    total = array
    if dp // 4 == 4:
        for bit in (1, 2):
            total = total + moved(total, lambda z, x, c, y, bit=bit: (z ^ bit, x, c, y))
        return total
    for step in range(1, dp // 4):
        total = total + moved(array, along_z(step))
    return total


def params(**more):
    return pltpu.CompilerParams(vmem_limit_bytes=VMEM, **more)


def cost(flops, bytes_accessed):
    return pl.CostEstimate(flops=int(flops), bytes_accessed=int(bytes_accessed), transcendentals=0)


def held(shape):
    zeros = (0,) * len(shape)
    return pl.BlockSpec(shape, lambda *_: zeros, pipeline_mode=pl.Buffered(1))


def fixed(shape):
    zeros = (0,) * len(shape)
    return pl.BlockSpec(shape, lambda *_: zeros)


SCALAR = pl.BlockSpec(memory_space=pltpu.SMEM)


def dot(a, b):
    return lax.dot_general(a, b, (((1,), (0,)), ((), ())), preferred_element_type=F32)


def dot_nt(a, b):
    return lax.dot_general(a, b, (((1,), (1,)), ((), ())), preferred_element_type=F32)


def dot_tn(a, b):
    return lax.dot_general(a, b, (((0,), (0,)), ((), ())), preferred_element_type=F32)


def split_sum(mask, terms):
    high = terms.astype(BF)
    low = (terms - high.astype(F32)).astype(BF)
    return dot(mask, high) + dot(mask, low)


def centred_norm(s):
    centred = s - jnp.mean(s, axis=-1, keepdims=True)
    rate = lax.rsqrt(jnp.mean(centred * centred, axis=-1, keepdims=True) + EPS)
    return centred * rate, rate


def norm_back(grad, unit, rate, gain):
    grad = grad * gain
    return rate * (
        grad
        - jnp.mean(grad, axis=-1, keepdims=True)
        - unit * jnp.mean(grad * unit, axis=-1, keepdims=True)
    )


def down_one(tile, first):
    rows = lax.broadcasted_iota(jnp.int32, tile.shape, 0)
    return jnp.where(rows == 0, first, pltpu.roll(tile, 1, 0))


def up_one(tile, last):
    size = tile.shape[0]
    rows = lax.broadcasted_iota(jnp.int32, tile.shape, 0)
    return jnp.where(rows == size - 1, last, pltpu.roll(tile, size - 1, 0))


def summed_rows(tile):
    return jnp.sum(tile, axis=0, keepdims=True)


def times(x, store, lo, hi, out_ref, rows=slice(None)):
    seq, dp, _, columns = store.shape
    for y in range(seq):
        weight = store[y, :, lo:hi, :].reshape(dp * (hi - lo), columns)
        out_ref[rows, y * columns : (y + 1) * columns] = dot(x, weight)


def times_back(g, store, lo, hi):
    seq, dp, _, columns = store.shape
    total = None
    for y in range(seq):
        weight = store[y, :, lo:hi, :].reshape(dp * (hi - lo), columns)
        part = dot_nt(g[:, y * columns : (y + 1) * columns], weight)
        total = part if total is None else total + part
    return total


def by_core(core_ref, mine, other, run):
    @pl.when(core_ref[0] == 0)
    def _():
        run(mine, other)

    @pl.when(core_ref[0] != 0)
    def _():
        run(other, mine)


def tile_rows(length):
    return min(256, length)


ALIVE, ENTERS, TAIL, HEAD, LEAVES = range(5)


def col(marks, which):
    return marks[:, which : which + 1]


def token_marks(document_numbers, earlier):
    rows, length = document_numbers.shape
    tile = tile_rows(length)
    tiles = document_numbers.reshape(rows, length // tile, tile)
    before = earlier.reshape(tiles.shape)[:, :, :1]
    marks = [
        document_numbers == earlier,
        (tiles == before).reshape(rows, length),
        document_numbers == document_numbers[:, -1:],
        document_numbers == document_numbers[:, :1],
        (tiles == tiles[:, :, -1:]).reshape(rows, length),
        jnp.zeros_like(document_numbers, dtype=bool),
        jnp.zeros_like(document_numbers, dtype=bool),
    ]
    marks = [m.astype(F32) for m in marks] + [document_numbers.astype(F32)]
    marks = jnp.stack(marks, axis=-1).reshape(rows * length, 8)
    lines = document_numbers.astype(F32).reshape(rows * length // tile, 1, tile)
    return marks, lines


def time_in(core, s, before, marks, gain, bias, mix, rate, mine, other, length):
    tokens, width = s.shape
    tile = tile_rows(length)
    per_run = length // tile
    runs = tokens // length

    def body(
        core_ref, s_ref, before_ref, marks_ref, gain_ref, bias_ref, mix_ref, rate_ref,
        mine_ref, other_ref,
        xk_ref, xv_ref, xr_ref, k_ref, v_ref, r_ref, end_ref, lead_ref, carry_ref,
    ):
        step = pl.program_id(0)
        run, part = lax.div(step, per_run), lax.rem(step, per_run)
        unit, _ = centred_norm(s_ref[...].astype(F32))
        normed = unit * gain_ref[...] + bias_ref[...]

        @pl.when(part == 0)
        def _():
            carry_ref[...] = before_ref[pl.ds(run, 1), :]
            end_ref[pl.ds(run, 1)] = jnp.zeros((1, 2, width), F32)

        lead_ref[0] = carry_ref[...]
        shifted = down_one(normed, carry_ref[...]) * col(marks_ref[...], ALIVE)
        carry_ref[...] = normed[tile - 1 :, :]
        change = normed - shifted
        xk_ref[...] = (shifted + mix_ref[0:1, :] * change).astype(BF)
        xv_ref[...] = (shifted + mix_ref[1:2, :] * change).astype(BF)
        xr_ref[...] = (shifted + mix_ref[2:3, :] * change).astype(BF)

        def project(first, second):
            rows = first.shape[2] // 2
            times(xk_ref[...], first, 0, rows, k_ref)
            times(xv_ref[...], first, rows, 2 * rows, v_ref)
            times(xr_ref[...], second, 0, rows, r_ref)

        by_core(core_ref, mine_ref, other_ref, project)
        places = lax.broadcasted_iota(jnp.int32, (tile, 1), 0).astype(F32)
        left = (length - 1 - part * tile).astype(F32) - places
        weight = jnp.exp(k_ref[...] - left * rate_ref[...]) * col(marks_ref[...], TAIL)
        ends = jnp.concatenate([summed_rows(weight * v_ref[...]), summed_rows(weight)], axis=0)
        end_ref[pl.ds(run, 1)] += ends[None]

    block = pl.BlockSpec((tile, width), lambda i: (i, 0))
    half, full = jax.ShapeDtypeStruct((tokens, width), BF), jax.ShapeDtypeStruct((tokens, width), F32)
    return pl.pallas_call(
        body,
        grid=(tokens // tile,),
        in_specs=[
            SCALAR, block, fixed(before.shape), pl.BlockSpec((tile, 8), lambda i: (i, 0)),
            fixed(gain.shape), fixed(bias.shape), fixed(mix.shape), fixed(rate.shape),
            held(mine.shape), held(other.shape),
        ],
        out_specs=[block] * 6 + [fixed((runs, 2, width)), pl.BlockSpec((1, 1, width), lambda i: (i, 0, 0))],
        out_shape=[half] * 3 + [full] * 3 + [
            jax.ShapeDtypeStruct((runs, 2, width), F32),
            jax.ShapeDtypeStruct((tokens // tile, 1, width), F32),
        ],
        scratch_shapes=[pltpu.VMEM((1, width), F32)],
        compiler_params=params(),
        cost_estimate=cost(6 * tokens * width * width, 22 * tokens * width + 4 * mine.size),
    )(core, s, before, marks, gain, bias, mix, rate, mine, other)


def time_out(core, s, k, v, r, enter, marks, lines, rate, bonus, mine, other, length):
    tokens, width = s.shape
    tile = tile_rows(length)
    per_run = length // tile

    def body(
        core_ref, s_ref, k_ref, v_ref, r_ref, enter_ref, marks_ref, line_ref, rate_ref, bonus_ref,
        mine_ref, other_ref, z_ref, sa_ref, sb_ref, out_ref, state_ref,
    ):
        step = pl.program_id(0)
        run, part = lax.div(step, per_run), lax.rem(step, per_run)

        @pl.when(part == 0)
        def _():
            state_ref[...] = enter_ref[pl.ds(run, 1)][0]

        marks = marks_ref[...]
        places = lax.broadcasted_iota(jnp.int32, (tile, 1), 0).astype(F32)
        spread = places * rate_ref[...]
        falling, decay = jnp.exp(-spread), jnp.exp(-rate_ref[...])
        powered = jnp.exp(k_ref[...])
        content = v_ref[...]
        raised = jnp.exp(k_ref[...] + spread)
        at = lax.broadcasted_iota(jnp.int32, (tile, tile), 0)
        source = lax.broadcasted_iota(jnp.int32, (tile, tile), 1)
        same = col(marks, 7) == line_ref[0]
        mask = jnp.where(jnp.logical_and(same, source < at), 1.0, 0.0).astype(BF)
        carried = falling * col(marks, ENTERS)
        ahead = falling * jnp.exp(rate_ref[...])
        state_a = ahead * split_sum(mask, raised * content) + carried * state_ref[0:1, :]
        state_b = ahead * split_sum(mask, raised) + carried * state_ref[1:2, :]
        sa_ref[...] = state_a
        sb_ref[...] = state_b
        state_ref[0:1, :] = decay * state_a[tile - 1 :] + (powered * content)[tile - 1 :]
        state_ref[1:2, :] = decay * state_b[tile - 1 :] + powered[tile - 1 :]
        scaled = powered * bonus_ref[...]
        answer = (state_a + scaled * content) / (state_b + scaled)
        z_ref[...] = (jax.nn.sigmoid(r_ref[...]) * answer).astype(BF)

        def project(first, second):
            rows = first.shape[2] // 2
            times(z_ref[...], second, rows, 2 * rows, out_ref)

        by_core(core_ref, mine_ref, other_ref, project)
        out_ref[...] += s_ref[...].astype(F32)

    block = pl.BlockSpec((tile, width), lambda i: (i, 0))
    half, full = jax.ShapeDtypeStruct((tokens, width), BF), jax.ShapeDtypeStruct((tokens, width), F32)
    return pl.pallas_call(
        body,
        grid=(tokens // tile,),
        in_specs=[
            SCALAR, block, block, block, block, fixed(enter.shape),
            pl.BlockSpec((tile, 8), lambda i: (i, 0)), pl.BlockSpec((1, 1, tile), lambda i: (i, 0, 0)),
            fixed(rate.shape), fixed(bonus.shape), held(mine.shape), held(other.shape),
        ],
        out_specs=[block] * 4,
        out_shape=[half, full, full, full],
        scratch_shapes=[pltpu.VMEM((2, width), F32)],
        compiler_params=params(),
        cost_estimate=cost(4 * tokens * width * width, 30 * tokens * width + 4 * mine.size),
    )(core, s, k, v, r, enter, marks, lines, rate, bonus, mine, other)


def lookup_block(store, rows, blocks, step):
    seq, dp, _, width = store.shape
    return pl.BlockSpec(
        (1, dp, rows, width), lambda i: (lax.div(step(i), blocks), 0, lax.rem(step(i), blocks), 0)
    )


def content_block(store, grain, at, group, step):
    seq, _, _, columns = store.shape
    return pl.BlockSpec((seq, group, grain, columns), lambda i: (0, step(i), at // grain, 0))


class Cut:
    def __init__(self, lookup, content, lookup_rows, grain):
        store, _ = lookup
        seq, dp, _, self.width = store.shape
        self.rows, self.grain = lookup_rows, grain
        self.group = self.width // grain
        self.steps = dp // self.group
        self.blocks = self.steps // seq
        self.at = content[1]

    def specs(self, lookup, content, step):
        return [
            lookup_block(lookup[0], self.rows, self.blocks, step),
            content_block(content[0], self.grain, self.at, self.group, step),
        ]


def hidden_step(x_ref, lookup_ref, content_ref, act_ref, total_ref, first):
    tokens = x_ref.shape[0]
    tile = min(256, tokens)
    _, dp, rows, width = lookup_ref.shape
    seq, group, grain, columns = content_ref.shape
    up = lookup_ref[0].reshape(dp * rows, width)
    for t in range(0, tokens, tile):
        hidden = jnp.maximum(dot(x_ref[t : t + tile, :], up), 0.0)
        act = (hidden * hidden).astype(BF)
        act_ref[0, t : t + tile, :] = act
        for y in range(seq):
            part = dot(act, content_ref[y].reshape(group * grain, columns))
            where = (slice(t, t + tile), slice(y * columns, (y + 1) * columns))
            total_ref[where] = part if first else total_ref[where] + part


def channel_one(s, before, marks, gain, bias, mix, lookup, content, cut, length):
    tokens, width = s.shape
    tile = tile_rows(length)
    tiles, per_run = tokens // tile, length // tile

    def body(
        s_ref, before_ref, marks_ref, gain_ref, bias_ref, mix_ref, lookup_ref, content_ref,
        xk_ref, xr_ref, lead_ref, act_ref, total_ref,
    ):
        @pl.when(pl.program_id(0) == 0)
        def _():
            last = None
            for i in range(tiles):
                rows = slice(i * tile, (i + 1) * tile)
                unit, _ = centred_norm(s_ref[rows, :])
                normed = unit * gain_ref[...] + bias_ref[...]
                if i % per_run == 0:
                    last = before_ref[i // per_run : i // per_run + 1, :]
                lead_ref[i] = last
                shifted = down_one(normed, last) * col(marks_ref[rows, :], ALIVE)
                last = normed[tile - 1 :, :]
                change = normed - shifted
                xk_ref[rows, :] = (shifted + mix_ref[0:1, :] * change).astype(BF)
                xr_ref[rows, :] = (shifted + mix_ref[1:2, :] * change).astype(BF)
            hidden_step(xk_ref, lookup_ref, content_ref, act_ref, total_ref, True)

        @pl.when(pl.program_id(0) > 0)
        def _():
            hidden_step(xk_ref, lookup_ref, content_ref, act_ref, total_ref, False)

    half, full = jax.ShapeDtypeStruct((tokens, width), BF), jax.ShapeDtypeStruct((tokens, width), F32)
    return pl.pallas_call(
        body,
        grid=(cut.steps,),
        in_specs=[
            held(s.shape), fixed(before.shape), held(marks.shape),
            fixed(gain.shape), fixed(bias.shape), fixed(mix.shape),
        ] + cut.specs(lookup, content, lambda i: i),
        out_specs=[
            fixed((tokens, width)), fixed((tokens, width)), fixed((tiles, 1, width)),
            pl.BlockSpec((1, tokens, cut.width), lambda i: (i, 0, 0)), fixed((tokens, width)),
        ],
        out_shape=[
            half, half, jax.ShapeDtypeStruct((tiles, 1, width), F32),
            jax.ShapeDtypeStruct((cut.steps, tokens, cut.width), BF), full,
        ],
        compiler_params=params(),
        cost_estimate=cost(
            4 * tokens * width * cut.width * cut.steps,
            14 * tokens * width + cut.steps * cut.width * (4 * width + 2 * tokens),
        ),
    )(s, before, marks, gain, bias, mix, lookup[0], content[0])


def channel_two(s, xk, xr, total, lookup, content, accept, cut, kind):
    tokens, width = s.shape
    tile = min(256, tokens)

    def body(
        s_ref, xk_ref, xr_ref, total_ref, accept_ref, lookup_ref, content_ref,
        act_ref, carried_ref, gate_ref, out_ref, sum_ref, take_ref,
    ):
        @pl.when(pl.program_id(0) == 0)
        def _():
            sum_ref[...] = total_ref[...]

        hidden_step(xk_ref, lookup_ref, content_ref, act_ref, sum_ref, False)

        @pl.when(pl.program_id(0) == cut.steps - 1)
        def _():
            for t in range(0, tokens, tile):
                rows = slice(t, t + tile)
                times(xr_ref[rows, :], accept_ref, 0, accept_ref.shape[2], take_ref)
                gate = jax.nn.sigmoid(take_ref[...])
                carried = sum_ref[rows, :]
                gate_ref[rows, :] = gate.astype(BF)
                carried_ref[rows, :] = carried.astype(BF)
                out_ref[rows, :] = (s_ref[rows, :] + gate * carried).astype(kind)

    half = jax.ShapeDtypeStruct((tokens, width), BF)
    return pl.pallas_call(
        body,
        grid=(cut.steps,),
        in_specs=[held(s.shape), held(xk.shape), held(xr.shape), held(total.shape), held(accept.shape)]
        + cut.specs(lookup, content, lambda i: i),
        out_specs=[pl.BlockSpec((1, tokens, cut.width), lambda i: (i, 0, 0))] + [fixed((tokens, width))] * 3,
        out_shape=[
            jax.ShapeDtypeStruct((cut.steps, tokens, cut.width), BF), half, half,
            jax.ShapeDtypeStruct((tokens, width), kind),
        ],
        scratch_shapes=[pltpu.VMEM((tokens, width), F32), pltpu.VMEM((tile, width), F32)],
        compiler_params=params(),
        cost_estimate=cost(
            4 * tokens * width * cut.width * cut.steps + 2 * tokens * width * width,
            20 * tokens * width + cut.steps * cut.width * (4 * width + 2 * tokens) + 2 * accept.size,
        ),
    )(s, xk, xr, total, accept, lookup[0], content[0])


def mixed_back(grads, s, lead, alive, gain, bias, mix_ref, after):
    unit, rate = centred_norm(s)
    normed = unit * gain + bias
    change = normed - down_one(normed, lead) * alive
    own, before, mixes = None, None, []
    for j, grad in enumerate(grads):
        mix = mix_ref[j : j + 1, :]
        a, b = mix * grad, (1.0 - mix) * grad
        own, before = (a, b) if own is None else (own + a, before + b)
        mixes.append(summed_rows(change * grad))
    before = before * alive
    grad = own + up_one(before, after)
    small = [summed_rows(grad * unit), summed_rows(grad)] + mixes
    return norm_back(grad, unit, rate, gain), before[0:1, :], small


def channel_back(
    core, g, fix, s, lead, marks, gain, bias, mix, gate, carried, xk, xr, acts, lookups, contents, accept,
    cut, length, packing,
):
    tokens, width = s.shape
    tile = tile_rows(length)
    tiles, per_run = tokens // tile, length // tile
    steps = cut.steps
    shapes, spots = packing
    seq, dp = accept.shape[:2]
    columns = width // seq
    half_rows = accept.shape[2] // 2
    last = 2 * steps - 1
    slots = len(shapes)

    def body(
        core_ref, g_ref, fix_ref, s_ref, lead_ref, marks_ref, gain_ref, bias_ref, mix_ref,
        gate_ref, carried_ref, xk_ref, xr_ref, act0_ref, act1_ref, accept_ref,
        lookup0_ref, content0_ref, lookup1_ref, content1_ref, *rest,
    ):
        outs, rest = rest[:slots], rest[slots:]
        out_ref, edge_ref, small_ref, gc_ref, gr_ref, sum_ref, key_ref, val_ref, take_ref, sem, stage_ref = rest
        lookup_out, content_out, accept_out = outs if slots == 3 else (outs[0],) * 3
        step = pl.program_id(0)
        slot = lax.rem(step, 2)

        def copies(which, store, q):
            y, block = lax.div(q, cut.blocks), lax.rem(q, cut.blocks)
            rows = pl.ds(pl.multiple_of(spots[0] + block * cut.rows, 16), cut.rows)
            key = pltpu.make_async_copy(
                key_ref.at[which], lookup_out.at[store, y, :, rows, :], sem.at[which, 0]
            )
            parts = pl.ds(q * cut.group, cut.group)
            rows = pl.ds(spots[1], cut.grain)
            val = pltpu.make_async_copy(
                val_ref.at[which], content_out.at[store, :, parts, rows, :], sem.at[which, 1]
            )
            return key, val

        def store_of_step(i):
            core = core_ref[0]
            return jnp.where(i < steps, core, 1 - core), lax.rem(i, steps)

        @pl.when(step == 0)
        def _():
            for i in range(tiles):
                rows = slice(i * tile, (i + 1) * tile)
                grad = g_ref[rows, :].astype(F32)
                if (i + 1) % per_run == 0:
                    at = lax.broadcasted_iota(jnp.int32, grad.shape, 0)
                    run = i // per_run
                    grad = jnp.where(at == tile - 1, grad + fix_ref[run : run + 1, :], grad)
                gate = gate_ref[rows, :].astype(F32)
                passed = grad * gate
                out_ref[rows, :] = grad
                gc_ref[rows, :] = passed.astype(BF)
                gr_ref[rows, :] = (passed * carried_ref[rows, :].astype(F32) * (1.0 - gate)).astype(BF)

        @pl.when(step >= 2)
        def _():
            for copy in copies(slot, *store_of_step(step - 2)):
                copy.wait()

        def work(act_ref, lookup_ref, content_ref, first):
            up = lookup_ref[0].reshape(dp * cut.rows, cut.width)
            size = min(256, tokens)
            for t in range(0, tokens, size):
                rows = slice(t, t + size)
                act = act_ref[0, rows, :].astype(F32)
                grad = None
                for y in range(seq):
                    part = dot_nt(
                        gc_ref[rows, y * columns : (y + 1) * columns],
                        content_ref[y].reshape(cut.group * cut.grain, columns),
                    )
                    grad = part if grad is None else grad + part
                grad = (grad * (2.0 * jnp.sqrt(act))).astype(BF)
                take_ref[rows, :] = grad
                part = dot_nt(grad, up)
                sum_ref[rows, :] = part if first else sum_ref[rows, :] + part
            key = dot_tn(xk_ref[...], take_ref[...])
            key_ref[slot] = key.astype(BF).reshape(dp, cut.rows, cut.width)
            for y in range(seq):
                val = dot_tn(act_ref[0], gc_ref[:, y * columns : (y + 1) * columns])
                val_ref[slot, y] = val.astype(BF).reshape(cut.group, cut.grain, columns)

        @pl.when(step == 0)
        def _():
            work(act0_ref, lookup0_ref, content0_ref, True)

        @pl.when(jnp.logical_and(step > 0, step < steps))
        def _():
            work(act0_ref, lookup0_ref, content0_ref, False)

        @pl.when(step >= steps)
        def _():
            work(act1_ref, lookup1_ref, content1_ref, False)

        for copy in copies(slot, *store_of_step(step)):
            copy.start()

        @pl.when(step == last)
        def _():
            for copy in copies(1 - slot, *store_of_step(step - 1)):
                copy.wait()
            for copy in copies(slot, *store_of_step(step)):
                copy.wait()
            rows = pl.ds(spots[2], half_rows)
            takes = []
            for y in range(seq):
                grad = dot_tn(xr_ref[...], gr_ref[:, y * columns : (y + 1) * columns])
                grad = grad.astype(BF).reshape(dp, 2 * half_rows, columns)
                for h in range(2):
                    buffer = stage_ref.at[h, y]
                    stage_ref[h, y] = grad[:, h * half_rows : (h + 1) * half_rows, :]
                    takes.append(
                        pltpu.make_async_copy(buffer, accept_out.at[h, y, :, rows, :], sem.at[h, 2 + y])
                    )
                    takes[-1].start()
            after = None
            small = None
            for i in reversed(range(tiles)):
                at = slice(i * tile, (i + 1) * tile)
                if (i + 1) % per_run == 0:
                    after = jnp.zeros((1, width), F32)
                grads = [sum_ref[at, :], times_back(gr_ref[at, :], accept_ref, 0, 2 * half_rows)]
                add, after, more = mixed_back(
                    grads, s_ref[at, :], lead_ref[i], col(marks_ref[at, :], ALIVE),
                    gain_ref[...], bias_ref[...], mix_ref, after,
                )
                out_ref[at, :] += add
                small = more if small is None else [a + b for a, b in zip(small, more)]
                if i % per_run == 0:
                    edge_ref[i // per_run : i // per_run + 1, :] = after
            for j, line in enumerate(small):
                small_ref[j : j + 1, :] = line
            for copy in takes:
                copy.wait()

    own = lambda i: jnp.minimum(i, steps - 1)
    partner = lambda i: jnp.maximum(i - steps, 0)
    act = lambda step: pl.BlockSpec((1, tokens, cut.width), lambda i: (step(i), 0, 0))
    any_space = pl.BlockSpec(memory_space=pl.ANY)
    return pl.pallas_call(
        body,
        grid=(2 * steps,),
        in_specs=[
            SCALAR, held(g.shape), fixed(fix.shape), held(s.shape), fixed(lead.shape), held(marks.shape),
            fixed(gain.shape), fixed(bias.shape), fixed(mix.shape), held(gate.shape), held(carried.shape),
            held(xk.shape), held(xr.shape), act(own), act(partner), held(accept.shape),
        ] + cut.specs(lookups[0], contents[0], own) + cut.specs(lookups[1], contents[1], partner),
        out_specs=[any_space] * slots + [fixed((tokens, width)), fixed(fix.shape), fixed((4, width))],
        out_shape=[jax.ShapeDtypeStruct(shape, BF) for shape in shapes] + [
            jax.ShapeDtypeStruct((tokens, width), F32), jax.ShapeDtypeStruct(fix.shape, F32),
            jax.ShapeDtypeStruct((4, width), F32),
        ],
        scratch_shapes=[
            pltpu.VMEM((tokens, width), BF), pltpu.VMEM((tokens, width), BF),
            pltpu.VMEM((tokens, width), F32),
            pltpu.VMEM((2, dp, cut.rows, cut.width), BF),
            pltpu.VMEM((2, seq, cut.group, cut.grain, columns), BF),
            pltpu.VMEM((tokens, cut.width), BF),
            pltpu.SemaphoreType.DMA((2, 2 + seq)),
            pltpu.VMEM((2, seq, dp, half_rows, columns), BF),
        ],
        compiler_params=params(),
        cost_estimate=cost(
            16 * tokens * width * cut.width * steps + 4 * tokens * width * width,
            30 * tokens * width + 2 * steps * cut.width * (8 * width + 2 * tokens),
        ),
    )(
        core, g, fix, s, lead, marks, gain, bias, mix, gate, carried, xk, xr, *acts, accept,
        lookups[0][0], contents[0][0], lookups[1][0], contents[1][0],
    )


def out_back(core, g, fix, k, v, r, sa, sb, marks, rate, bonus, mine, other, length):
    tokens, width = g.shape
    tile = tile_rows(length)
    per_run = length // tile
    runs = tokens // length

    def body(
        core_ref, g_ref, fix_ref, k_ref, v_ref, r_ref, sa_ref, sb_ref, marks_ref, rate_ref, bonus_ref,
        mine_ref, other_ref, go_ref, gr_ref, gn_ref, gd_ref, chain_ref, gz_ref,
    ):
        step = pl.program_id(0)
        run, part = lax.div(step, per_run), lax.rem(step, per_run)
        grad = g_ref[...]
        at = lax.broadcasted_iota(jnp.int32, grad.shape, 0)
        hit = jnp.logical_and(at == tile - 1, part == per_run - 1)
        go_ref[...] = jnp.where(hit, grad + fix_ref[pl.ds(run, 1), :], grad).astype(BF)

        def project(first, second):
            rows = first.shape[2] // 2
            gz_ref[...] = times_back(go_ref[...], second, rows, 2 * rows)

        by_core(core_ref, mine_ref, other_ref, project)
        gate = jax.nn.sigmoid(r_ref[...])
        scaled = jnp.exp(k_ref[...]) * bonus_ref[...]
        inverse = 1.0 / (sb_ref[...] + scaled)
        answer = (sa_ref[...] + scaled * v_ref[...]) * inverse
        gated = gz_ref[...] * gate
        gr_ref[...] = (gated * answer * (1.0 - gate)).astype(BF)
        gn = gated * inverse
        gd = -gn * answer
        gn_ref[...] = gn
        gd_ref[...] = gd

        @pl.when(part == 0)
        def _():
            chain_ref[pl.ds(run, 1)] = jnp.zeros((1, 2, width), F32)

        places = (lax.broadcasted_iota(jnp.int32, (tile, 1), 0) + part * tile).astype(F32)
        weight = jnp.exp(-places * rate_ref[...]) * col(marks_ref[...], HEAD)
        sums = jnp.concatenate([summed_rows(weight * gn), summed_rows(weight * gd)], axis=0)
        chain_ref[pl.ds(run, 1)] += sums[None]

    block = pl.BlockSpec((tile, width), lambda i: (i, 0))
    half, full = jax.ShapeDtypeStruct((tokens, width), BF), jax.ShapeDtypeStruct((tokens, width), F32)
    return pl.pallas_call(
        body,
        grid=(tokens // tile,),
        in_specs=[
            SCALAR, block, fixed(fix.shape), block, block, block, block, block,
            pl.BlockSpec((tile, 8), lambda i: (i, 0)), fixed(rate.shape), fixed(bonus.shape),
            held(mine.shape), held(other.shape),
        ],
        out_specs=[block] * 4 + [fixed((runs, 2, width))],
        out_shape=[half, half, full, full, jax.ShapeDtypeStruct((runs, 2, width), F32)],
        scratch_shapes=[pltpu.VMEM((tile, width), F32)],
        compiler_params=params(),
        cost_estimate=cost(2 * tokens * width * width, 36 * tokens * width + 4 * mine.size),
    )(core, g, fix, k, v, r, sa, sb, marks, rate, bonus, mine, other)


def time_back(
    core, g, fix, s, lead, k, v, sa, sb, gn, gd, gr, leave, marks, lines, gain, bias, mix, rate, bonus,
    mine, other, length,
):
    tokens, width = s.shape
    tile = tile_rows(length)
    tiles, per_run = tokens // tile, length // tile
    runs = tokens // length

    def body(
        core_ref, g_ref, fix_ref, s_ref, lead_ref, k_ref, v_ref, sa_ref, sb_ref, gn_ref, gd_ref, gr_ref,
        leave_ref, marks_ref, line_ref, gain_ref, bias_ref, mix_ref, rate_ref, bonus_ref,
        mine_ref, other_ref, gk_ref, gv_ref, out_ref, edge_ref, small_ref,
        state_ref, after_ref, xk_ref, xv_ref, xr_ref,
    ):
        step = pl.program_id(0)
        i = tiles - 1 - step
        run, part = lax.div(i, per_run), lax.rem(i, per_run)

        @pl.when(part == per_run - 1)
        def _():
            state_ref[...] = leave_ref[pl.ds(run, 1)][0]
            after_ref[...] = jnp.zeros((1, width), F32)

        marks = marks_ref[...]
        alive = col(marks, ALIVE)
        places = lax.broadcasted_iota(jnp.int32, (tile, 1), 0).astype(F32)
        spread = places * rate_ref[...]
        falling, decay = jnp.exp(-spread), jnp.exp(-rate_ref[...])
        rising = jnp.exp(spread + rate_ref[...])
        at = lax.broadcasted_iota(jnp.int32, (tile, tile), 0)
        source = lax.broadcasted_iota(jnp.int32, (tile, tile), 1)
        same = col(marks, 7) == line_ref[0]
        mask = jnp.where(jnp.logical_and(same, source > at), 1.0, 0.0).astype(BF)
        gn, gd = gn_ref[...], gd_ref[...]
        carried = jnp.exp(spread - (tile - 1) * rate_ref[...]) * col(marks, LEAVES)
        ga = rising * split_sum(mask, falling * gn) + carried * state_ref[0:1, :]
        gb = rising * split_sum(mask, falling * gd) + carried * state_ref[1:2, :]
        first = alive[0:1, :]
        state_ref[0:1, :] = first * (gn[0:1, :] + decay * ga[0:1, :])
        state_ref[1:2, :] = first * (gd[0:1, :] + decay * gb[0:1, :])
        powered, content = jnp.exp(k_ref[...]), v_ref[...]
        scaled = powered * bonus_ref[...]
        reward = (gn * content + gd) * scaled
        gv_ref[...] = (gn * scaled + powered * ga).astype(BF)
        gk_ref[...] = (reward + powered * (content * ga + gb)).astype(BF)
        sums = [summed_rows(ga * sa_ref[...] + gb * sb_ref[...]), summed_rows(reward)]

        def project(first, second):
            rows = first.shape[2] // 2
            xk_ref[...] = times_back(gk_ref[...], first, 0, rows)
            xv_ref[...] = times_back(gv_ref[...], first, rows, 2 * rows)
            xr_ref[...] = times_back(gr_ref[...], second, 0, rows)

        by_core(core_ref, mine_ref, other_ref, project)
        grads = [xk_ref[...], xv_ref[...], xr_ref[...]]
        add, after, small = mixed_back(
            grads, s_ref[...].astype(F32), lead_ref[0], alive, gain_ref[...], bias_ref[...], mix_ref,
            after_ref[...],
        )
        after_ref[...] = after
        grad = g_ref[...]
        row = lax.broadcasted_iota(jnp.int32, grad.shape, 0)
        hit = jnp.logical_and(row == tile - 1, part == per_run - 1)
        out_ref[...] = jnp.where(hit, grad + fix_ref[pl.ds(run, 1), :], grad) + add
        edge_ref[pl.ds(run, 1), :] = after

        @pl.when(step == 0)
        def _():
            small_ref[...] = jnp.zeros_like(small_ref)

        for j, line in enumerate(small + sums):
            small_ref[j : j + 1, :] += line

    back = lambda i: tiles - 1 - i
    block = pl.BlockSpec((tile, width), lambda i: (back(i), 0))
    half, full = jax.ShapeDtypeStruct((tokens, width), BF), jax.ShapeDtypeStruct((tokens, width), F32)
    return pl.pallas_call(
        body,
        grid=(tiles,),
        in_specs=[
            SCALAR, block, fixed(fix.shape), block, pl.BlockSpec((1, 1, width), lambda i: (back(i), 0, 0)),
            block, block, block, block, block, block, block, fixed(leave.shape),
            pl.BlockSpec((tile, 8), lambda i: (back(i), 0)),
            pl.BlockSpec((1, 1, tile), lambda i: (back(i), 0, 0)),
            fixed(gain.shape), fixed(bias.shape), fixed(mix.shape), fixed(rate.shape), fixed(bonus.shape),
            held(mine.shape), held(other.shape),
        ],
        out_specs=[block, block, block, fixed(fix.shape), fixed((7, width))],
        out_shape=[
            half, half, full, jax.ShapeDtypeStruct(fix.shape, F32), jax.ShapeDtypeStruct((7, width), F32),
        ],
        scratch_shapes=[
            pltpu.VMEM((2, width), F32), pltpu.VMEM((1, width), F32),
            pltpu.VMEM((tile, width), F32), pltpu.VMEM((tile, width), F32), pltpu.VMEM((tile, width), F32),
        ],
        compiler_params=params(),
        cost_estimate=cost(8 * tokens * width * width, 46 * tokens * width + 4 * mine.size),
    )(
        core, g, fix, s, lead, k, v, sa, sb, gn, gd, gr, leave, marks, lines, gain, bias, mix, rate, bonus,
        mine, other,
    )


def weight_grads(first, second, grads):
    dp, seq = sizes()
    tokens, width = grads[0].shape
    rows, columns = width // dp, width // seq
    pairs = list(zip(first + second, grads))

    def body(*refs):
        ins, (out_ref, x_ref, g_ref, sem) = refs[: 2 * len(pairs)], refs[2 * len(pairs) :]
        which, y = pl.program_id(0), pl.program_id(1)
        slot = lax.rem(which, 2)

        def copies(i):
            return (
                pltpu.make_async_copy(ins[2 * i], x_ref.at[i % 2], sem.at[i % 2, 0]),
                pltpu.make_async_copy(ins[2 * i + 1], g_ref.at[i % 2], sem.at[i % 2, 1]),
            )

        @pl.when(jnp.logical_and(which == 0, y == 0))
        def _():
            for copy in copies(0):
                copy.start()

        for i in range(len(pairs)):

            @pl.when(jnp.logical_and(which == i, y == 0))
            def _(i=i):
                for copy in copies(i):
                    copy.wait()
                if i + 1 < len(pairs):
                    for copy in copies(i + 1):
                        copy.start()

        at = pl.ds(pl.multiple_of(y * columns, columns), columns)
        grad = dot_tn(x_ref[slot], g_ref[slot, :, at])
        out_ref[0, 0] = grad.astype(BF).reshape(dp, rows, columns)

    return pl.pallas_call(
        body,
        grid=(len(pairs), seq),
        in_specs=[pl.BlockSpec(memory_space=pl.ANY)] * (2 * len(pairs)),
        out_specs=pl.BlockSpec((1, 1, dp, rows, columns), lambda m, y: (lax.div(m, 2), y, 0, lax.rem(m, 2), 0)),
        out_shape=jax.ShapeDtypeStruct((2, seq, dp, 2 * rows, columns), BF),
        scratch_shapes=[
            pltpu.VMEM((2, tokens, width), BF), pltpu.VMEM((2, tokens, width), BF),
            pltpu.SemaphoreType.DMA((2, 2)),
        ],
        compiler_params=params(),
        cost_estimate=cost(8 * tokens * width * width, 16 * tokens * width + 8 * width * width),
    )(*[array for pair in pairs for array in pair])


def passed_along(array, axis, by):
    devices = lax.axis_size(axis)
    pairs = [(i, i + by) for i in range(devices) if 0 <= i + by < devices]
    return lax.ppermute(array, axis, pairs)


def entering(chain, ends, by):
    came = passed_along(ends, "seq", by)
    for _ in range(lax.axis_size("seq") - 2):
        came = passed_along(ends + chain * came, "seq", by)
    return came


def last_tokens(s, length):
    return s.reshape(-1, length, s.shape[-1])[:, -1].astype(F32)


def edge_norm(s, length, gain, bias):
    unit, _ = centred_norm(last_tokens(s, length))
    return passed_along(unit * gain + bias, "seq", 1)


def edge_back(edge, s, length, gain):
    came = passed_along(edge, "seq", -1)
    unit, rate = centred_norm(last_tokens(s, length))
    small = jnp.concatenate([summed_rows(came * unit), summed_rows(came)])
    return norm_back(came, unit, rate, gain), small


def cut_lookup(shard, grain):
    rows, columns = shard.shape
    width = min(512, columns // 2)
    cut = shard.reshape(rows, columns // (2 * grain), 2, grain).transpose(2, 0, 1, 3)
    cut = cut.reshape(2, rows, columns // 2 // width, width).transpose(0, 2, 1, 3)
    return cut.reshape(2, -1, width)


def join_lookup(first, second, rows, grain):
    width = first.shape[-1]
    cut = jnp.stack([first, second]).reshape(2, -1, rows, width).transpose(0, 2, 1, 3)
    cut = cut.reshape(2, rows, -1, grain).transpose(1, 2, 0, 3)
    return cut.reshape(rows, -1)


def gather_group(core, table, firsts, seconds):
    if not paired():
        pairs = [gather_pair(core, table, a, b) for a, b in zip(firsts, seconds)]
        return [(a, 0) for a, _ in pairs], [(b, 0) for _, b in pairs]
    mine, other = gather_pair(core, table, jnp.concatenate(firsts), jnp.concatenate(seconds))
    spots = [0] + np.cumsum([a.shape[0] for a in firsts])[:-1].tolist()
    return [(mine, at) for at in spots], [(other, at) for at in spots]


def scatter_group(core, table, stores, sizes_of):
    if not paired():
        pairs = [scatter_pair(core, table, s) for s in stores]
        return [a for a, _ in pairs], [b for _, b in pairs]
    first, second = scatter_pair(core, table, stores[0])
    cuts = np.cumsum(sizes_of)[:-1].tolist()
    return jnp.split(first, cuts), jnp.split(second, cuts)


def per_device(
    entering_activations,
    document_numbers,
    result_cotangent,
    normalizer_scales,
    normalizer_offsets,
    shift_blend_factors,
    fading_natural_logs_per_feature,
    feature_reward_logs,
    attention_triple_matrix,
    attention_result_matrix,
    channelmix_lookup_matrix,
    channelmix_content_matrix,
    channelmix_accept_matrix,
):
    dp, seq = sizes()
    core = core_of()
    cores = core.reshape(1)
    table = unit_tables() if paired() else None
    layers = attention_triple_matrix.shape[0]
    runs, length, width = entering_activations.shape
    tokens = runs * length

    lookup_rows = channelmix_lookup_matrix.shape[1]
    grain = channelmix_content_matrix.shape[1] // 2
    half_rows = channelmix_accept_matrix.shape[1] // 2

    att, chan = [], []
    for depth in range(layers):
        triple, result = attention_triple_matrix[depth], attention_result_matrix[depth]
        att.append(
            gather_pair(
                core,
                table,
                jnp.concatenate([triple[0], triple[1]]),
                jnp.concatenate([triple[2], result]),
            )
        )
        lookup = cut_lookup(channelmix_lookup_matrix[depth], grain)
        content, accept = channelmix_content_matrix[depth], channelmix_accept_matrix[depth]
        mine, other = gather_group(
            core,
            table,
            [lookup[0], content[:grain], accept[:half_rows]],
            [lookup[1], content[grain:], accept[half_rows:]],
        )
        takes = [array[:, :, at : at + half_rows] for array, at in (mine[2], other[2])]
        first = jnp.where(core == 0, takes[0], takes[1])
        second = jnp.where(core == 0, takes[1], takes[0])
        cut = Cut(mine[0], mine[1], lookup_rows, grain)
        chan.append((mine, other, jnp.concatenate([first, second], axis=2), cut))

    border = passed_along(document_numbers[:, -1:] + 1, "seq", 1)
    earlier = jnp.concatenate([border - 1, document_numbers[:, :-1]], axis=1)
    marks, lines = token_marks(document_numbers, earlier)
    through = (earlier[:, :1] == document_numbers[:, -1:]).astype(F32)[:, :, None]
    begins = (earlier[:, :1] == document_numbers[:, :1]).astype(F32)[:, :, None]
    rates = jnp.exp(fading_natural_logs_per_feature)
    bonuses = jnp.exp(feature_reward_logs)

    flow = entering_activations.reshape(tokens, width)
    kept = []
    for depth in range(layers):
        gain, bias = normalizer_scales[depth], normalizer_offsets[depth]
        mix, rate, bonus = shift_blend_factors[depth], rates[depth : depth + 1], bonuses[depth : depth + 1]
        chain = jnp.exp(-length * rate)[None] * through
        mine, other = att[depth]
        before = edge_norm(flow, length, gain[0], bias[0])
        xk, xv, xr, k, v, r, ends, lead = time_in(
            cores, flow, before, marks, gain[0:1], bias[0:1], mix[:3], rate, mine, other, length
        )
        enter = entering(chain, ends, 1)
        z, sa, sb, middle = time_out(
            cores, flow, k, v, r, enter, marks, lines, rate, bonus, mine, other, length
        )
        time_kept = (flow, lead, xk, xv, xr, k, v, r, z, sa, sb)
        mine, other, accept, cut = chan[depth]
        before = edge_norm(middle, length, gain[1], bias[1])
        xk, xr, lead, act0, total = channel_one(
            middle, before, marks, gain[1:2], bias[1:2], mix[3:], mine[0], mine[1], cut, length
        )
        kind = BF if depth == layers - 1 else F32
        act1, carried, gate, flow = channel_two(middle, xk, xr, total, other[0], other[1], accept, cut, kind)
        kept.append((time_kept, (middle, lead, xk, xr, (act0, act1), carried, gate)))
    y_out = flow

    grad = result_cotangent.reshape(tokens, width)
    fix = jnp.zeros((runs, width), F32)
    small, large = [None] * layers, [None] * layers
    columns = width // seq
    for depth in reversed(range(layers)):
        gain, bias = normalizer_scales[depth], normalizer_offsets[depth]
        mix, rate, bonus = shift_blend_factors[depth], rates[depth : depth + 1], bonuses[depth : depth + 1]
        chain = jnp.exp(-length * rate)[None] * through
        (flow, lead_t, xk_t, xv_t, xr_t, k, v, r, z, sa, sb), channel_kept = kept[depth]
        middle, lead, xk, xr, acts, carried, gate = channel_kept
        mine, other, accept, cut = chan[depth]
        part_rows = [cut.blocks * lookup_rows, grain, half_rows]
        if paired():
            packing = [(2, seq, dp, sum(part_rows), columns)], [0, part_rows[0], part_rows[0] + grain]
        else:
            widths = [cut.width, columns, columns]
            packing = [(2, seq, dp, n, w) for n, w in zip(part_rows, widths)], [0, 0, 0]
        *stores, grad, edge, small_chan = channel_back(
            cores, grad, fix, middle, lead, marks, gain[1:2], bias[1:2], mix[3:], gate, carried, xk, xr,
            acts, (mine[0], other[0]), (mine[1], other[1]), accept, cut, length, packing,
        )
        first, second = scatter_group(core, table, stores, part_rows)
        chan_large = (
            join_lookup(first[0], second[0], lookup_rows, grain),
            jnp.concatenate([first[1], second[1]]),
            jnp.concatenate([first[2], second[2]]),
        )
        fix, edge_chan = edge_back(edge, middle, length, gain[1])
        mine, other = att[depth]
        go, gr, gn, gd, sums = out_back(
            cores, grad, fix, k, v, r, sa, sb, marks, rate, bonus, mine, other, length
        )
        leave = entering(chain, begins * sums, -1)
        gk, gv, grad, edge, small_time = time_back(
            cores, grad, fix, flow, lead_t, k, v, sa, sb, gn, gd, gr, leave, marks, lines,
            gain[0:1], bias[0:1], mix[:3], rate, bonus, mine, other, length,
        )
        store = weight_grads([xk_t, xv_t], [xr_t, z], [gk, gv, gr, go])
        rows = store.shape[3] // 2
        first, second = scatter_group(core, table, [store], [2 * rows])
        triple = jnp.stack([first[0][:rows], first[0][rows:], second[0][:rows]])
        large[depth] = (triple, second[0][rows:]) + chan_large
        fix, edge_time = edge_back(edge, flow, length, gain[0])
        fading = small_time[5:6] * -rate * jnp.exp(-rate)
        small[depth] = jnp.concatenate(
            [
                small_time[0:1] + edge_time[0:1],
                small_chan[0:1] + edge_chan[0:1],
                small_time[1:2] + edge_time[1:2],
                small_chan[1:2] + edge_chan[1:2],
                small_time[2:5],
                small_chan[2:4],
                fading,
                small_time[6:7],
            ]
        )
    grad = grad.reshape(runs, length, width).at[:, -1].add(fix)
    small = summed_everywhere(jnp.stack(small))
    large = [jnp.stack(members) for members in zip(*large)]
    return (
        y_out.reshape(runs, length, width),
        grad,
        small[:, 0:2],
        small[:, 2:4],
        small[:, 4:9],
        small[:, 9],
        small[:, 10],
        *large,
    )


def solution(mesh):
    return jax.shard_map(
        per_device,
        mesh=mesh,
        in_specs=(
            P("dp", "seq", None),
            P("dp", "seq"),
            P("dp", "seq", None),
            P(),
            P(),
            P(),
            P(),
            P(),
            P(None, None, "dp", "seq"),
            P(None, "dp", "seq"),
            P(None, "dp", "seq"),
            P(None, "dp", "seq"),
            P(None, "dp", "seq"),
        ),
        out_specs=(
            P("dp", "seq", None),
            P("dp", "seq", None),
            P(),
            P(),
            P(),
            P(),
            P(),
            P(None, None, "dp", "seq"),
            P(None, "dp", "seq"),
            P(None, "dp", "seq"),
            P(None, "dp", "seq"),
            P(None, "dp", "seq"),
        ),
        check_vma=False,
    )
```

time: 1890 us -> 1250 us (0.66)
  local copies, waits for them, and re-layouts: 496 us -> 42.6 us
  Pallas kernels: 98.1 us -> 516 us
  matrix products: 395 us -> 0 us
  other arithmetic: 358 us -> 48.6 us
  waiting for transfers between devices: 295 us -> 463 us
  starting transfers between devices: 210 us -> 153 us
    pallas_call x0 -> x16, Pallas kernels: none -> 418 us  [the longest x2 134 us: channel_back(): pl.pallas_call(body, grid=(2 * steps,), in_specs=[SCALAR, held(g.shape),...]
    dot_general x46 -> x0, matrix products: 395 us -> none  [the longest x14 136 us: matmul_nt(): lax.dot_general(first_op, second_op, (((1,), (1,)), ((), ())), preferred_...]
    reshape x41 -> x3, local copies, waits for them, and re-layouts: 213 us -> 0.64 us  [the longest x1 0.61 us: token_marks(): lines = document_numbers.astype(F32).reshape(rows * length // tile, 1, tile)]
    transpose x20 -> x0, local copies, waits for them, and re-layouts: 111 us -> none  [the longest x14 63 us: whole_matrix(): return store.transpose(1, 2, 0, 3).reshape(dp * rows, seq * columns)]
    ppermute x57, waiting for transfers between devices: 294 us -> 405 us  [moved(): return lax.ppermute(array, BOTH, pairs)]
    unnamed x718 -> x131, local copies, waits for them, and re-layouts: 106 us -> 18.8 us
    reduce_sum x17 -> x12, other arithmetic: 69.1 us -> 4.35 us  [the longest x4 2.97 us: centred_norm(): centred = s - jnp.mean(s, axis=-1, keepdims=True)]
    convert_element_type x11 -> x1, other arithmetic: 62.7 us -> 0.01 us  [token_marks(): marks = [m.astype(F32) for m in marks] + [document_numbers.astype(F32)]]
  transfers between devices with their start and end apart: 74 -> 74, of which waited for: 21 -> 31; matrix products, arithmetic and copies ran while one was open for 41% -> 6% of each run, Pallas kernels for 5% -> 26%
where the time goes in v2:
time: 1250 us; the launch traced here: 1240 us
  Pallas kernels  516 us (41%)
  waiting for transfers between devices  463 us (37%)
  starting transfers between devices  153 us (12%)
  other arithmetic  48.6 us (4%)
  local copies, waits for them, and re-layouts  42.6 us (3%)
  between operations  15.7 us (1%)
    ppermute x57, waiting for transfers between devices, moved(): return lax.ppermute(array, BOTH, pairs)  405 us
    pallas_call x2, Pallas kernels, channel_back(): pl.pallas_call(body, grid=(2 * steps,), in_specs=[SCALAR, held(g.shape),...  134 us
    ppermute x57, starting transfers between devices, moved(): return lax.ppermute(array, BOTH, pairs)  126 us
    pallas_call x2, Pallas kernels, time_back(): pl.pallas_call(body, grid=(tiles,), in_specs=[SCALAR, block, fixed(fix.sh...  63.9 us
    pallas_call x4, Pallas kernels, split_units(): pl.pallas_call(body, grid_spec=pltpu.PrefetchScalarGridSpec(num_scalar_pr...  49.8 us
    pallas_call x4, Pallas kernels, arrange(): pl.pallas_call(body, grid_spec=pltpu.PrefetchScalarGridSpec(num_scalar_pr...  48.5 us
    pallas_call x2, Pallas kernels, channel_two(): pl.pallas_call(body, grid=(cut.steps,), in_specs=[held(s.shape), held(xk....  45.5 us
    reduce_scatter x4, waiting for transfers between devices, scatter_pair(): lax.psum_scatter(flat, 'dp', scatter_dimension=0, axis_index_groups=groups)  41 us
  transfers between devices with their start and end apart: 74, of which 31 were waited for; matrix products, arithmetic and copies ran while one was open for 6% of the time, Pallas kernels for 26%

profile of v2, /device:TPU:1, one launch (start us, length us, event | category | flops | bytes accessed | tf_op | source)
XLA Modules:
  0.0 1238.6 jit_solution(3515632921682729400)
XLA Ops:
  13.1 4.5 collective-permute-start.14
  18.2 11.8 collective-permute-done.14
  30.0 37.7 %collective-permute-done.13 = bf16[2,288,512]{2,1,0:T(8,128)(2,1)S(1)} collective-permute-done((bf16[2,288,512]{2,1,0:T(8,128)(2,1)S(1)}, bf16[2,288,512]{2,1,0:T(8,128)(2,1)S(1)}, u32[]{:S(2)}, u32[]{:S(2)}) %collective-permute-start.13) | collective-permute-done | bytes 589856 | tf_op jit(solution)/shard_map/ppermute | solution.py:42
  82.6 15.1 %collective-permute-done.15 = bf16[4,576,512]{2,1,0:T(8,128)(2,1)} collective-permute-done((bf16[4,576,512]{2,1,0:T(8,128)(2,1)}, bf16[4,576,512]{2,1,0:T(8,128)(2,1)}, u32[]{:S(2)}, u32[]{:S(2)}) %collective-permute-start.15) | collective-permute-done | bytes 2359328 | tf_op jit(solution)/shard_map/ppermute | solution.py:42
  102.3 26.7 %collective-permute-done.30 = bf16[2,288,512]{2,1,0:T(8,128)(2,1)S(1)} collective-permute-done((bf16[2,288,512]{2,1,0:T(8,128)(2,1)S(1)}, bf16[2,288,512]{2,1,0:T(8,128)(2,1)S(1)}, u32[]{:S(2)}, u32[]{:S(2)}) %collective-permute-start.30) | collective-permute-done | bytes 589856 | tf_op jit(solution)/shard_map/ppermute | solution.py:42
  137.6 44.3 %collective-permute-done.32 = bf16[4,576,512]{2,1,0:T(8,128)(2,1)S(1)} collective-permute-done((bf16[4,576,512]{2,1,0:T(8,128)(2,1)S(1)}, bf16[4,576,512]{2,1,0:T(8,128)(2,1)S(1)}, u32[]{:S(2)}, u32[]{:S(2)}) %collective-permute-start.32) | collective-permute-done | bytes 2359328 | tf_op jit(solution)/shard_map/ppermute | solution.py:42
  186.3 24.0 %collective-permute-done.6 = bf16[4,256,512]{2,1,0:T(8,128)(2,1)S(1)} collective-permute-done((bf16[4,256,512]{2,1,0:T(8,128)(2,1)S(1)}, bf16[4,256,512]{2,1,0:T(8,128)(2,1)S(1)}, u32[]{:S(2)}, u32[]{:S(2)}) %collective-permute-start.6) | collective-permute-done | bytes 1048608 | tf_op jit(solution)/shard_map/ppermute | solution.py:42
  212.1 13.2 %shard_map.232 = bf16[16,576,512]{2,1,0:T(8,128)(2,1)} custom-call(s32[4,16]{1,0:T(4,128)} %dynamic-slice_bitcast_fusion.table_ref, bf16[8,576,512]{2,1,0:T(8,128)(2,1)} %constant_dynamic-update-slice_fusion.5.own_ref, bf16[8,576,512]{2,1,0:T(8,128)(2,1)} %collective-permute-done.16.other_ref), custom_call_target="tpu_custom_call" | custom-call | bytes 18874368 | tf_op jit(solution)/shard_map/pallas_call | solution.py:111
  226.0 44.5 %collective-permute-done.7.other_ref = bf16[8,256,512]{2,1,0:T(8,128)(2,1)} collective-permute-done((bf16[8,256,512]{2,1,0:T(8,128)(2,1)S(1)}, bf16[8,256,512]{2,1,0:T(8,128)(2,1)}, u32[]{:S(2)}, u32[]{:S(2)}) %collective-permute-start.7) | collective-permute-done | bytes 2097184 | tf_op jit(solution)/shard_map/ppermute | solution.py:42
  270.5 11.0 shard_map.229
  286.3 13.3 %shard_map.238 = bf16[16,576,512]{2,1,0:T(8,128)(2,1)} custom-call(s32[4,16]{1,0:T(4,128)} %dynamic-slice_bitcast_fusion.table_ref, bf16[8,576,512]{2,1,0:T(8,128)(2,1)} %constant_dynamic-update-slice_fusion.15.own_ref, bf16[8,576,512]{2,1,0:T(8,128)(2,1)} %collective-permute-done.33.other_ref), custom_call_target="tpu_custom_call" | custom-call | bytes 18874368 | tf_op jit(solution)/shard_map/pallas_call | solution.py:111
  300.9 6.4 collective-permute-done.21
  313.0 11.7 collective-permute-done.23
  331.3 17.6 %shard_map.230 = (bf16[1024,1024]{1,0:T(8,128)(2,1)}, bf16[1024,1024]{1,0:T(8,128)(2,1)}, bf16[1024,1024]{1,0:T(8,128)(2,1)}, f32[1024,1024]{1,0:T(8,128)}, f32[...) custom-call(s32[1]{0:T(128)} %bitcast.core_ref, ...), custom_call_target="tpu_custom_call" | custom-call | flops 6442450944 | bytes 31457280 | tf_op jit(solution)/shard_map/pallas_call | solution.py:397
  353.0 11.0 shard_map.235
  364.0 21.2 %collective-permute-start.25 = (bf16[16,256,512]{2,1,0:T(8,128)(2,1)}, bf16[16,256,512]{2,1,0:T(8,128)(2,1)S(1)}, u32[]{:S(2)}, u32[]{:S(2)}) collective-permute-start(bf16[16,256,512]{2,1,0:T(8,128)(2,1)} %shard_map.235), channel_id=1, source_target_pairs={{0,2},{1,3},{2,0},{3,1},{4,6},{5,7},{6,4},{7,5},{8,10},{9,11},{10,... | collective-permute-start | bytes 12582920 | tf_op jit(solution)/shard_map/ppermute | solution.py:42
  385.8 17.7 %shard_map.231 = (bf16[1024,1024]{1,0:T(8,128)(2,1)}, f32[1024,1024]{1,0:T(8,128)}, f32[1024,1024]{1,0:T(8,128)}, f32[1024,1024]{1,0:T(8,128)}) custom-call(s32[1]{0:T(128)} %bitcast.core_ref, bf16[1024,1024]{1,0:T(8,128)(2,1)} %bitcast.403, f32[1024,1024]{1,0:T(8,128)} %get-tuple-element.102.k_ref, f32[1024,1024]{1,0:T(8,128)} %get-tuple-element.103.v_ref, ...), custom_call_target="tpu_custom_call" | custom-call | flops 4294967296 | bytes 39845888 | tf_op jit(solution)/shard_map/pallas_call | solution.py:464
  408.0 19.5 %shard_map.233 = (bf16[1024,1024]{1,0:T(8,128)(2,1)}, bf16[1024,1024]{1,0:T(8,128)(2,1)}, f32[4,1,1024]{2,1,0:T(1,128)}, bf16[4,1024,512]{2,1,0:T(8,128)(2,1)}, f32[1024,1024]{1,0:T(8,128)}) custom-call(f32[1024,1024]{1,0:T(8,128)} %get-tuple-element.106.s_ref, f32[2,1024]{1,0:T(2,128)} %copy-done.42, f32[1024,8]{1,0:T(8,128)} %copy.115.marks_ref, ...), custom_call_target="tpu_custom_call" | custom-call | flops 8589934592 | bytes 27262976 | tf_op jit(solution)/shard_map/pallas_call | solution.py:556
  430.7 23.0 %shard_map.234 = (bf16[4,1024,512]{2,1,0:T(8,128)(2,1)}, bf16[1024,1024]{1,0:T(8,128)(2,1)}, bf16[1024,1024]{1,0:T(8,128)(2,1)}, f32[1024,1024]{1,0:T(8,128)}) custom-call(f32[1024,1024]{1,0:T(8,128)} %get-tuple-element.106.s_ref, bf16[1024,1024]{1,0:T(8,128)(2,1)} %get-tuple-element.107.xk_ref, bf16[1024,1024]{1,0:T(8,128)(2,1)} %get-tuple-element.108.xr_ref, ...), custom_call_target="tpu_custom_call" | custom-call | flops 10737418240 | bytes 35651584 | tf_op jit(solution)/shard_map/pallas_call | solution.py:605
  462.0 17.7 %shard_map.236 = (bf16[1024,1024]{1,0:T(8,128)(2,1)}, bf16[1024,1024]{1,0:T(8,128)(2,1)}, bf16[1024,1024]{1,0:T(8,128)(2,1)}, f32[1024,1024]{1,0:T(8,128)}, f32[...) custom-call(s32[1]{0:T(128)} %bitcast.core_ref, ...), custom_call_target="tpu_custom_call" | custom-call | flops 6442450944 | bytes 31457280 | tf_op jit(solution)/shard_map/pallas_call | solution.py:397
  483.6 18.3 %shard_map.237 = (bf16[1024,1024]{1,0:T(8,128)(2,1)}, f32[1024,1024]{1,0:T(8,128)}, f32[1024,1024]{1,0:T(8,128)}, f32[1024,1024]{1,0:T(8,128)}) custom-call(s32[1]{0:T(128)} %bitcast.core_ref, f32[1024,1024]{1,0:T(8,128)} %get-tuple-element.110.s_ref, f32[1024,1024]{1,0:T(8,128)} %get-tuple-element.111.k_ref, f32[1024,1024]{1,0:T(8,128)} %get-tuple-element.112.v_ref, ...), custom_call_target="tpu_custom_call" | custom-call | flops 4294967296 | bytes 39845888 | tf_op jit(solution)/shard_map/pallas_call | solution.py:464
  508.6 19.4 %shard_map.239 = (bf16[1024,1024]{1,0:T(8,128)(2,1)}, bf16[1024,1024]{1,0:T(8,128)(2,1)}, f32[4,1,1024]{2,1,0:T(1,128)}, bf16[4,1024,512]{2,1,0:T(8,128)(2,1)}, f32[1024,1024]{1,0:T(8,128)}) custom-call(f32[1024,1024]{1,0:T(8,128)} %get-tuple-element.115.s_ref, f32[2,1024]{1,0:T(2,128)} %copy-done.43, f32[1024,8]{1,0:T(8,128)} %copy.115.marks_ref, ...), custom_call_target="tpu_custom_call" | custom-call | flops 8589934592 | bytes 27262976 | tf_op jit(solution)/shard_map/pallas_call | solution.py:556
  528.0 22.5 %shard_map.240 = (bf16[4,1024,512]{2,1,0:T(8,128)(2,1)}, bf16[1024,1024]{1,0:T(8,128)(2,1)}, bf16[1024,1024]{1,0:T(8,128)(2,1)}, bf16[1024,1024]{1,0:T(8,128)(2,1)}) custom-call(f32[1024,1024]{1,0:T(8,128)} %get-tuple-element.115.s_ref, bf16[1024,1024]{1,0:T(8,128)(2,1)} %get-tuple-element.116.xk_ref, bf16[1024,1024]{1,0:T(8,128)(2,1)} %get-tuple-element.117.xr_ref, ...), custom_call_target="tpu_custom_call" | custom-call | flops 10737418240 | bytes 35651584 | tf_op jit(solution)/shard_map/pallas_call | solution.py:605
  551.1 64.5 %shard_map.241 = (bf16[2,2,16,288,512]{4,3,2,1,0:T(8,128)(2,1)}, f32[1024,1024]{1,0:T(8,128)}, f32[2,1024]{1,0:T(2,128)}, f32[4,1024]{1,0:T(4,128)}) custom-call(s32[1]{0:T(128)} %bitcast.core_ref, bf16[1024,1024]{1,0:T(8,128)(2,1)} %bitcast.530, f32[2,1024]{1,0:T(2,128)} %broadcast_in_dim.18.fix_ref, f32[1024,1024]{1,0:T(8,128)} %get-tuple-element.115.s_ref, ...), custom_call_target="tpu_custom_call" | custom-call | flops 38654705664 | bytes 73400320 | tf_op jit(solution)/shard_map/pallas_call | solution.py:783
  621.1 18.1 %shard_map.242 = (bf16[1024,1024]{1,0:T(8,128)(2,1)}, bf16[1024,1024]{1,0:T(8,128)(2,1)}, f32[1024,1024]{1,0:T(8,128)}, f32[1024,1024]{1,0:T(8,128)}, f32[2,2,1024]{2,1,0:T(2,128)}) custom-call(s32[1]{0:T(128)} %bitcast.core_ref, f32[1024,1024]{1,0:T(8,128)} %get-tuple-element.125.g_ref, f32[2,1024]{1,0:T(2,128)} %subtract_multiply_fusion.2.fix_ref, ...), custom_call_target="tpu_custom_call" | custom-call | flops 2147483648 | bytes 46137344 | tf_op jit(solution)/shard_map/pallas_call | solution.py:860
  645.1 32.1 %shard_map.243 = (bf16[1024,1024]{1,0:T(8,128)(2,1)}, bf16[1024,1024]{1,0:T(8,128)(2,1)}, f32[1024,1024]{1,0:T(8,128)}, f32[2,1024]{1,0:T(2,128)}, f32[7,1024]{1,0:T(8,128)}) custom-call(s32[1]{0:T(128)} %bitcast.core_ref, f32[1024,1024]{1,0:T(8,128)} %get-tuple-element.125.g_ref, f32[2,1024]{1,0:T(2,128)} %subtract_multiply_fusion.2.fix_ref, ...), custom_call_target="tpu_custom_call" | custom-call | flops 8589934592 | bytes 56623104 | tf_op jit(solution)/shard_map/pallas_call | solution.py:953
  677.2 14.2 %shard_map.249 = bf16[2,2,16,128,512]{4,3,2,1,0:T(8,128)(2,1)} custom-call(bf16[1024,1024]{1,0:T(8,128)(2,1)} %get-tuple-element.165.refs_0_, bf16[1024,1024]{1,0:T(8,128)(2,1)} %get-tuple-element.166.refs_1_, bf16[1024,1024]{1,0:T(8,128)(2,1)} %get-tuple-element.167.refs_2_, bf16[1024,1024]{1,0:T(8,128)(2,1)} %get-tuple-element.168.refs_3_, ...), custom_call_target="tpu_custom_call" | custom-call | flops 8589934592 | bytes 25165824 | tf_op jit(solution)/shard_map/pallas_call | solution.py:1016
  697.3 69.0 %shard_map.244 = (bf16[2,2,16,288,512]{4,3,2,1,0:T(8,128)(2,1)}, f32[1024,1024]{1,0:T(8,128)}, f32[2,1024]{1,0:T(2,128)}, f32[4,1024]{1,0:T(4,128)}) custom-call(s32[1]{0:T(128)} %bitcast.core_ref, f32[1024,1024]{1,0:T(8,128)} %get-tuple-element.134.g_ref, f32[2,1024]{1,0:T(2,128)} %subtract_multiply_fusion.1.fix_ref, ...), custom_call_target="tpu_custom_call" | custom-call | flops 38654705664 | bytes 73400320 | tf_op jit(solution)/shard_map/pallas_call | solution.py:783
  771.8 18.1 %shard_map.245 = (bf16[1024,1024]{1,0:T(8,128)(2,1)}, bf16[1024,1024]{1,0:T(8,128)(2,1)}, f32[1024,1024]{1,0:T(8,128)}, f32[1024,1024]{1,0:T(8,128)}, f32[2,2,1024]{2,1,0:T(2,128)}) custom-call(s32[1]{0:T(128)} %bitcast.core_ref, f32[1024,1024]{1,0:T(8,128)} %get-tuple-element.141.g_ref, f32[2,1024]{1,0:T(2,128)} %subtract_multiply_fusion.fix_ref, ...), custom_call_target="tpu_custom_call" | custom-call | flops 2147483648 | bytes 46137344 | tf_op jit(solution)/shard_map/pallas_call | solution.py:860
  795.8 31.9 %shard_map.246 = (bf16[1024,1024]{1,0:T(8,128)(2,1)}, bf16[1024,1024]{1,0:T(8,128)(2,1)}, f32[1024,1024]{1,0:T(8,128)}, f32[2,1024]{1,0:T(2,128)}, f32[7,1024]{1,0:T(8,128)}) custom-call(s32[1]{0:T(128)} %bitcast.core_ref, f32[1024,1024]{1,0:T(8,128)} %get-tuple-element.141.g_ref, f32[2,1024]{1,0:T(2,128)} %subtract_multiply_fusion.fix_ref, ...), custom_call_target="tpu_custom_call" | custom-call | flops 8589934592 | bytes 56623104 | tf_op jit(solution)/shard_map/pallas_call | solution.py:953
  827.7 14.2 %shard_map.247 = bf16[2,2,16,128,512]{4,3,2,1,0:T(8,128)(2,1)} custom-call(bf16[1024,1024]{1,0:T(8,128)(2,1)} %get-tuple-element.156.refs_0_, bf16[1024,1024]{1,0:T(8,128)(2,1)} %get-tuple-element.157.refs_1_, bf16[1024,1024]{1,0:T(8,128)(2,1)} %get-tuple-element.158.refs_2_, bf16[1024,1024]{1,0:T(8,128)(2,1)} %get-tuple-element.159.refs_3_, ...), custom_call_target="tpu_custom_call" | custom-call | flops 8589934592 | bytes 25165824 | tf_op jit(solution)/shard_map/pallas_call | solution.py:1016
  843.3 11.1 shard_map.250
  855.6 8.1 reduce-scatter.5.cloned.1.call-done
  863.7 11.1 shard_map.248
  877.8 17.7 %reduce-scatter.11.cloned.1.call-done = bf16[1,16,576,512]{3,2,1,0:T(8,128)(2,1)} async-done(((bf16[2,16,576,512]{3,2,1,0:T(8,128)(2,1)}), bf16[1,16,576,512]{3,2,1,0:T(8,128)(2,1)}) %reduce-scatter.11.cloned.1.call-update) | async-done | bytes 9437200 | tf_op jit(solution)/shard_map/reduce_scatter | solution.py:193
  895.6 14.1 %shard_map.252 = (bf16[8,576,512]{2,1,0:T(8,128)(2,1)}, bf16[8,576,512]{2,1,0:T(8,128)(2,1)}) custom-call(s32[4,16]{1,0:T(4,128)} %dynamic-slice_bitcast_fusion.table_ref, bf16[16,576,512]{2,1,0:T(8,128)(2,1)} %bitcast.401), custom_call_target="tpu_custom_call" | custom-call | bytes 18874368 | tf_op jit(solution)/shard_map/pallas_call | solution.py:144
  912.2 15.1 %reduce-scatter.9.cloned.1.call-done = bf16[1,16,576,512]{3,2,1,0:T(8,128)(2,1)} async-done(((bf16[2,16,576,512]{3,2,1,0:T(8,128)(2,1)}), bf16[1,16,576,512]{3,2,1,0:T(8,128)(2,1)}) %reduce-scatter.9.cloned.1.call-update) | async-done | bytes 9437200 | tf_op jit(solution)/shard_map/reduce_scatter | solution.py:193
  927.3 13.5 %shard_map.251 = (bf16[8,576,512]{2,1,0:T(8,128)(2,1)}, bf16[8,576,512]{2,1,0:T(8,128)(2,1)}) custom-call(s32[4,16]{1,0:T(4,128)} %dynamic-slice_bitcast_fusion.table_ref, bf16[16,576,512]{2,1,0:T(8,128)(2,1)} %bitcast.400), custom_call_target="tpu_custom_call" | custom-call | bytes 18874368 | tf_op jit(solution)/shard_map/pallas_call | solution.py:144
  948.1 67.1 %collective-permute-done.43 = f32[2,11,1024]{2,1,0:T(8,128)S(1)} collective-permute-done((f32[2,11,1024]{2,1,0:T(8,128)S(1)}, f32[2,11,1024]{2,1,0:T(8,128)S(1)}, u32[]{:S(2)}, u32[]{:S(2)}) %collective-permute-start.43) | collective-permute-done | bytes 90144 | tf_op jit(solution)/shard_map/ppermute | solution.py:42
  1036.9 6.8 collective-permute-done.47
  1049.3 7.7 collective-permute-done.55
  1060.4 15.3 %collective-permute-start.57 = (f32[128,512]{1,0:T(8,128)S(1)}, f32[128,512]{1,0:T(8,128)S(1)}, u32[]{:S(2)}, u32[]{:S(2)}) collective-permute-start(f32[128,512]{1,0:T(8,128)S(1)} %slice_select_fusion.4), channel_id=1, source_target_pairs={{0,2},{1,3},{2,0},{3,1},{4,6},{5,7},{6,4},{7,5},{8,10},{9,11},{10,... | collective-permute-start | bytes 786440 | tf_op jit(solution)/shard_map/ppermute | solution.py:42
  1075.7 8.0 collective-permute-done.49
  1096.0 18.4 %collective-permute-done.65 = bf16[4,576,512]{2,1,0:T(8,128)(2,1)S(1)} collective-permute-done((bf16[4,576,512]{2,1,0:T(8,128)(2,1)S(1)}, bf16[4,576,512]{2,1,0:T(8,128)(2,1)S(1)}, u32[]{:S(2)}, u32[]{:S(2)}) %collective-permute-start.65) | collective-permute-done | bytes 2359328 | tf_op jit(solution)/shard_map/ppermute | solution.py:42
  1119.1 20.6 %collective-permute-done.59 = bf16[4,576,512]{2,1,0:T(8,128)(2,1)S(1)} collective-permute-done((bf16[4,576,512]{2,1,0:T(8,128)(2,1)S(1)}, bf16[4,576,512]{2,1,0:T(8,128)(2,1)S(1)}, u32[]{:S(2)}, u32[]{:S(2)}) %collective-permute-start.59) | collective-permute-done | bytes 2359328 | tf_op jit(solution)/shard_map/ppermute | solution.py:42
  1144.6 24.3 %collective-permute-done.67 = bf16[576,512]{1,0:T(8,128)(2,1)S(1)} collective-permute-done((bf16[576,512]{1,0:T(8,128)(2,1)S(1)}, bf16[576,512]{1,0:T(8,128)(2,1)S(1)}, u32[]{:S(2)}, u32[]{:S(2)}) %collective-permute-start.67) | collective-permute-done | bytes 589856 | tf_op jit(solution)/shard_map/ppermute | solution.py:42
  1169.3 31.0 %collective-permute-start.69 = (f32[288,512]{1,0:T(8,128)S(1)}, f32[288,512]{1,0:T(8,128)S(1)}, u32[]{:S(2)}, u32[]{:S(2)}) collective-permute-start(f32[288,512]{1,0:T(8,128)S(1)} %slice_select_fusion), channel_id=1, source_target_pairs={{0,2},{1,3},{2,0},{3,1},{4,6},{5,7},{6,4},{7,5},{8,10},{9,11},{10,... | collective-permute-start | bytes 1769480 | tf_op jit(solution)/shard_map/ppermute | solution.py:42
  1201.1 16.8 %collective-permute-done.61 = bf16[576,512]{1,0:T(8,128)(2,1)S(1)} collective-permute-done((bf16[576,512]{1,0:T(8,128)(2,1)S(1)}, bf16[576,512]{1,0:T(8,128)(2,1)S(1)}, u32[]{:S(2)}, u32[]{:S(2)}) %collective-permute-start.61) | collective-permute-done | bytes 589856 | tf_op jit(solution)/shard_map/ppermute | solution.py:42
  (453 shorter events, 202.0 us)
Async XLA Ops:
  7.2 836.1 %reduce-scatter.7.cloned.1.call-start = ((), (), s32[]{:S(2)}) async-start(), calls=%async_computation.5 | async-start | bytes 12582912 | tf_op jit(solution)/shard_map/reduce_scatter | solution.py:193
  17.6 50.2 %collective-permute-start.13 = (bf16[2,288,512]{2,1,0:T(8,128)(2,1)S(1)}, bf16[2,288,512]{2,1,0:T(8,128)(2,1)S(1)}, u32[]{:S(2)}, u32[]{:S(2)}) collective-permute-start(bf16[2,288,512]{2,1,0:T(8,128)(2,1)S(1)} %maximum_select_fusion.1), channel_id=1, source_target_pairs={{0,16},{1,17},{2,18},{3,19},{4,20},{5,21},{6,22},{7,23},{8,24},{9,... | collective-permute-start | bytes 1769480 | tf_op jit(solution)/shard_map/ppermute | solution.py:42
  17.6 50.2 %collective-permute-start.12 = (bf16[2,288,512]{2,1,0:T(8,128)(2,1)S(1)}, bf16[2,288,512]{2,1,0:T(8,128)(2,1)S(1)}, u32[]{:S(2)}, u32[]{:S(2)}) collective-permute-start(bf16[2,288,512]{2,1,0:T(8,128)(2,1)S(1)} %maximum_select_fusion.1), channel_id=1, source_target_pairs={{0,8},{1,9},{2,10},{3,11},{4,12},{5,13},{6,14},{7,15},{8,16},{9,17... | collective-permute-start | bytes 1769480 | tf_op jit(solution)/shard_map/ppermute | solution.py:42
  69.5 28.3 %collective-permute-start.15 = (bf16[4,576,512]{2,1,0:T(8,128)(2,1)}, bf16[4,576,512]{2,1,0:T(8,128)(2,1)}, u32[]{:S(2)}, u32[]{:S(2)}) collective-permute-start(bf16[4,576,512]{2,1,0:T(8,128)(2,1)} %pad_maximum_fusion), channel_id=1, source_target_pairs={{0,4},{1,5},{2,3},{3,2},{4,0},{5,1},{6,7},{7,6},{8,12},{9,13},{10,... | collective-permute-start | bytes 7077896 | tf_op jit(solution)/shard_map/ppermute | solution.py:42
  75.1 27.1 %collective-permute-start.31 = (bf16[2,288,512]{2,1,0:T(8,128)(2,1)S(1)}, bf16[2,288,512]{2,1,0:T(8,128)(2,1)S(1)}, u32[]{:S(2)}, u32[]{:S(2)}) collective-permute-start(bf16[2,288,512]{2,1,0:T(8,128)(2,1)S(1)} %maximum_select_fusion.3), channel_id=1, source_target_pairs={{0,24},{1,25},{2,26},{3,27},{4,28},{5,29},{6,30},{7,31},{8,0},{9,1... | collective-permute-start | bytes 1769480 | tf_op jit(solution)/shard_map/ppermute | solution.py:42
  75.2 53.8 %collective-permute-start.30 = (bf16[2,288,512]{2,1,0:T(8,128)(2,1)S(1)}, bf16[2,288,512]{2,1,0:T(8,128)(2,1)S(1)}, u32[]{:S(2)}, u32[]{:S(2)}) collective-permute-start(bf16[2,288,512]{2,1,0:T(8,128)(2,1)S(1)} %maximum_select_fusion.3), channel_id=1, source_target_pairs={{0,16},{1,17},{2,18},{3,19},{4,20},{5,21},{6,22},{7,23},{8,24},{9,... | collective-permute-start | bytes 1769480 | tf_op jit(solution)/shard_map/ppermute | solution.py:42
  77.8 51.2 %collective-permute-start.29 = (bf16[2,288,512]{2,1,0:T(8,128)(2,1)S(1)}, bf16[2,288,512]{2,1,0:T(8,128)(2,1)S(1)}, u32[]{:S(2)}, u32[]{:S(2)}) collective-permute-start(bf16[2,288,512]{2,1,0:T(8,128)(2,1)S(1)} %maximum_select_fusion.3), channel_id=1, source_target_pairs={{0,8},{1,9},{2,10},{3,11},{4,12},{5,13},{6,14},{7,15},{8,16},{9,17... | collective-permute-start | bytes 1769480 | tf_op jit(solution)/shard_map/ppermute | solution.py:42
  101.0 111.2 %collective-permute-start.16 = (bf16[8,576,512]{2,1,0:T(8,128)(2,1)}, bf16[8,576,512]{2,1,0:T(8,128)(2,1)}, u32[]{:S(2)}, u32[]{:S(2)}) collective-permute-start(bf16[8,576,512]{2,1,0:T(8,128)(2,1)} %constant_dynamic-update-slice_fusion.5.own_ref), channel_id=1, source_target_pairs={{0,1},{1,0},{2,6},{3,7},{4,5},{5,4},{6,2},{7,3},{8,9},{9,8},{10,14... | collective-permute-start | bytes 14155784 | tf_op jit(solution)/shard_map/ppermute | solution.py:42
  129.3 52.6 %collective-permute-start.32 = (bf16[4,576,512]{2,1,0:T(8,128)(2,1)S(1)}, bf16[4,576,512]{2,1,0:T(8,128)(2,1)S(1)}, u32[]{:S(2)}, u32[]{:S(2)}) collective-permute-start(bf16[4,576,512]{2,1,0:T(8,128)(2,1)S(1)} %pad_maximum_fusion.1), channel_id=1, source_target_pairs={{0,4},{1,5},{2,3},{3,2},{4,0},{5,1},{6,7},{7,6},{8,12},{9,13},{10,... | collective-permute-start | bytes 7077896 | tf_op jit(solution)/shard_map/ppermute | solution.py:42
  132.2 52.5 %collective-permute-start.5 = (bf16[2,128,512]{2,1,0:T(8,128)(2,1)S(1)}, bf16[2,128,512]{2,1,0:T(8,128)(2,1)S(1)}, u32[]{:S(2)}, u32[]{:S(2)}) collective-permute-start(bf16[2,128,512]{2,1,0:T(8,128)(2,1)S(1)} %maximum_select_fusion.11), channel_id=1, source_target_pairs={{0,24},{1,25},{2,26},{3,27},{4,28},{5,29},{6,30},{7,31},{8,0},{9,1... | collective-permute-start | bytes 786440 | tf_op jit(solution)/shard_map/ppermute | solution.py:42
  132.3 52.5 %collective-permute-start.4 = (bf16[2,128,512]{2,1,0:T(8,128)(2,1)S(1)}, bf16[2,128,512]{2,1,0:T(8,128)(2,1)S(1)}, u32[]{:S(2)}, u32[]{:S(2)}) collective-permute-start(bf16[2,128,512]{2,1,0:T(8,128)(2,1)S(1)} %maximum_select_fusion.11), channel_id=1, source_target_pairs={{0,16},{1,17},{2,18},{3,19},{4,20},{5,21},{6,22},{7,23},{8,24},{9,... | collective-permute-start | bytes 786440 | tf_op jit(solution)/shard_map/ppermute | solution.py:42
  132.8 52.0 %collective-permute-start.3 = (bf16[2,128,512]{2,1,0:T(8,128)(2,1)S(1)}, bf16[2,128,512]{2,1,0:T(8,128)(2,1)S(1)}, u32[]{:S(2)}, u32[]{:S(2)}) collective-permute-start(bf16[2,128,512]{2,1,0:T(8,128)(2,1)S(1)} %maximum_select_fusion.11), channel_id=1, source_target_pairs={{0,8},{1,9},{2,10},{3,11},{4,12},{5,13},{6,14},{7,15},{8,16},{9,17... | collective-permute-start | bytes 786440 | tf_op jit(solution)/shard_map/ppermute | solution.py:42
  183.5 100.5 %collective-permute-start.33 = (bf16[8,576,512]{2,1,0:T(8,128)(2,1)}, bf16[8,576,512]{2,1,0:T(8,128)(2,1)}, u32[]{:S(2)}, u32[]{:S(2)}) collective-permute-start(bf16[8,576,512]{2,1,0:T(8,128)(2,1)} %constant_dynamic-update-slice_fusion.15.own_ref), channel_id=1, source_target_pairs={{0,1},{1,0},{2,6},{3,7},{4,5},{5,4},{6,2},{7,3},{8,9},{9,8},{10,14... | collective-permute-start | bytes 14155784 | tf_op jit(solution)/shard_map/ppermute | solution.py:42
  184.9 25.4 %collective-permute-start.6 = (bf16[4,256,512]{2,1,0:T(8,128)(2,1)S(1)}, bf16[4,256,512]{2,1,0:T(8,128)(2,1)S(1)}, u32[]{:S(2)}, u32[]{:S(2)}) collective-permute-start(bf16[4,256,512]{2,1,0:T(8,128)(2,1)S(1)} %pad_maximum_fusion.4), channel_id=1, source_target_pairs={{0,4},{1,5},{2,3},{3,2},{4,0},{5,1},{6,7},{7,6},{8,12},{9,13},{10,... | collective-permute-start | bytes 3145736 | tf_op jit(solution)/shard_map/ppermute | solution.py:42
  210.4 60.1 %collective-permute-start.7 = (bf16[8,256,512]{2,1,0:T(8,128)(2,1)S(1)}, bf16[8,256,512]{2,1,0:T(8,128)(2,1)}, u32[]{:S(2)}, u32[]{:S(2)}) collective-permute-start(bf16[8,256,512]{2,1,0:T(8,128)(2,1)S(1)} %constant_dynamic-update-slice_fusion.own_ref), channel_id=1, source_target_pairs={{0,1},{1,0},{2,6},{3,7},{4,5},{5,4},{6,2},{7,3},{8,9},{9,8},{10,14... | collective-permute-start | bytes 6291464 | tf_op jit(solution)/shard_map/ppermute | solution.py:42
  225.4 202.1 %collective-permute-start.17 = (bf16[16,576,512]{2,1,0:T(8,128)(2,1)}, bf16[16,576,512]{2,1,0:T(8,128)(2,1)}, u32[]{:S(2)}, u32[]{:S(2)}) collective-permute-start(bf16[16,576,512]{2,1,0:T(8,128)(2,1)} %shard_map.232), channel_id=1, source_target_pairs={{0,2},{1,3},{2,0},{3,1},{4,6},{5,7},{6,4},{7,5},{8,10},{9,11},{10,... | collective-permute-start | bytes 28311560 | tf_op jit(solution)/shard_map/ppermute | solution.py:42
  225.4 56.4 %collective-permute-start.19 = (bf16[128,512]{1,0:T(8,128)(2,1)S(1)}, bf16[128,512]{1,0:T(8,128)(2,1)S(1)}, u32[]{:S(2)}, u32[]{:S(2)}) collective-permute-start(bf16[128,512]{1,0:T(8,128)(2,1)S(1)} %maximum_select_fusion.18), channel_id=1, source_target_pairs={{0,2},{1,3},{2,0},{3,1},{4,6},{5,7},{6,4},{7,5},{8,10},{9,11},{10,... | collective-permute-start | bytes 393224 | tf_op jit(solution)/shard_map/ppermute | solution.py:42
  281.5 49.2 %collective-permute-start.8 = (bf16[16,256,512]{2,1,0:T(8,128)(2,1)}, bf16[16,256,512]{2,1,0:T(8,128)(2,1)}, u32[]{:S(2)}, u32[]{:S(2)}) collective-permute-start(bf16[16,256,512]{2,1,0:T(8,128)(2,1)} %shard_map.229), channel_id=1, source_target_pairs={{0,2},{1,3},{2,0},{3,1},{4,6},{5,7},{6,4},{7,5},{8,10},{9,11},{10,... | collective-permute-start | bytes 12582920 | tf_op jit(solution)/shard_map/ppermute | solution.py:42
  282.1 25.2 %collective-permute-start.21 = (bf16[2,128,512]{2,1,0:T(8,128)(2,1)S(1)}, bf16[2,128,512]{2,1,0:T(8,128)(2,1)S(1)}, u32[]{:S(2)}, u32[]{:S(2)}) collective-permute-start(bf16[2,128,512]{2,1,0:T(8,128)(2,1)S(1)} %maximum_select_fusion.13), channel_id=1, source_target_pairs={{0,16},{1,17},{2,18},{3,19},{4,20},{5,21},{6,22},{7,23},{8,24},{9,... | collective-permute-start | bytes 786440 | tf_op jit(solution)/shard_map/ppermute | solution.py:42
  284.1 26.4 %collective-permute-start.20 = (bf16[2,128,512]{2,1,0:T(8,128)(2,1)S(1)}, bf16[2,128,512]{2,1,0:T(8,128)(2,1)S(1)}, u32[]{:S(2)}, u32[]{:S(2)}) collective-permute-start(bf16[2,128,512]{2,1,0:T(8,128)(2,1)S(1)} %maximum_select_fusion.13), channel_id=1, source_target_pairs={{0,8},{1,9},{2,10},{3,11},{4,12},{5,13},{6,14},{7,15},{8,16},{9,17... | collective-permute-start | bytes 786440 | tf_op jit(solution)/shard_map/ppermute | solution.py:42
  299.6 181.6 %collective-permute-start.34 = (bf16[16,576,512]{2,1,0:T(8,128)(2,1)}, bf16[16,576,512]{2,1,0:T(8,128)(2,1)}, u32[]{:S(2)}, u32[]{:S(2)}) collective-permute-start(bf16[16,576,512]{2,1,0:T(8,128)(2,1)} %shard_map.238), channel_id=1, source_target_pairs={{0,2},{1,3},{2,0},{3,1},{4,6},{5,7},{6,4},{7,5},{8,10},{9,11},{10,... | collective-permute-start | bytes 28311560 | tf_op jit(solution)/shard_map/ppermute | solution.py:42
  307.3 19.4 %collective-permute-start.1 = (s32[2,1]{1,0:T(2,128)S(1)}, s32[2,1]{1,0:T(2,128)S(1)}, u32[]{:S(2)}, u32[]{:S(2)}) collective-permute-start(s32[2,1]{1,0:T(2,128)S(1)} %get-tuple-element.402), channel_id=1, source_target_pairs={{0,1},{2,3},{4,5},{6,7},{8,9},{10,11},{12,13},{14,15},{16,17},{18,... | collective-permute-start | bytes 32 | tf_op jit(solution)/shard_map/ppermute | solution.py:1034
  324.7 28.3 %collective-permute-start.24 = (bf16[8,256,512]{2,1,0:T(8,128)(2,1)S(1)}, bf16[8,256,512]{2,1,0:T(8,128)(2,1)}, u32[]{:S(2)}, u32[]{:S(2)}) collective-permute-start(bf16[8,256,512]{2,1,0:T(8,128)(2,1)S(1)} %constant_dynamic-update-slice_fusion.10.own_ref), channel_id=1, source_target_pairs={{0,1},{1,0},{2,6},{3,7},{4,5},{5,4},{6,2},{7,3},{8,9},{9,8},{10,14... | collective-permute-start | bytes 6291464 | tf_op jit(solution)/shard_map/ppermute | solution.py:42
  348.9 36.3 %collective-permute-start.9 = (f32[2,2,1024]{2,1,0:T(2,128)}, f32[2,2,1024]{2,1,0:T(2,128)S(1)}, u32[]{:S(2)}, u32[]{:S(2)}) collective-permute-start(f32[2,2,1024]{2,1,0:T(2,128)} %get-tuple-element.105), channel_id=1, source_target_pairs={{0,1},{2,3},{4,5},{6,7},{8,9},{10,11},{12,13},{14,15},{16,17},{18,... | collective-permute-start | bytes 49160 | tf_op jit(solution)/shard_map/ppermute | solution.py:1034
  364.0 96.0 %collective-permute-start.25 = (bf16[16,256,512]{2,1,0:T(8,128)(2,1)}, bf16[16,256,512]{2,1,0:T(8,128)(2,1)S(1)}, u32[]{:S(2)}, u32[]{:S(2)}) collective-permute-start(bf16[16,256,512]{2,1,0:T(8,128)(2,1)} %shard_map.235), channel_id=1, source_target_pairs={{0,2},{1,3},{2,0},{3,1},{4,6},{5,7},{6,4},{7,5},{8,10},{9,11},{10,... | collective-permute-start | bytes 12582920 | tf_op jit(solution)/shard_map/ppermute | solution.py:42
  691.4 172.3 %reduce-scatter.5.cloned.1.call-start = ((), (), s32[]{:S(2)}) async-start(), calls=%async_computation.4 | async-start | bytes 12582912 | tf_op jit(solution)/shard_map/reduce_scatter | solution.py:193
  841.9 53.7 %reduce-scatter.11.cloned.1.call-start = ((), (), s32[]{:S(2)}) async-start(), calls=%async_computation.7 | async-start | bytes 28311552 | tf_op jit(solution)/shard_map/reduce_scatter | solution.py:193
  842.6 84.7 %reduce-scatter.9.cloned.1.call-start = ((), (), s32[]{:S(2)}) async-start(), calls=%async_computation.6 | async-start | bytes 28311552 | tf_op jit(solution)/shard_map/reduce_scatter | solution.py:193
  854.4 162.4 %collective-permute-start.52 = (bf16[8,256,512]{2,1,0:T(8,128)(2,1)}, bf16[8,256,512]{2,1,0:T(8,128)(2,1)}, u32[]{:S(2)}, u32[]{:S(2)}) collective-permute-start(bf16[8,256,512]{2,1,0:T(8,128)(2,1)} %get-tuple-element.173), channel_id=1, source_target_pairs={{0,1},{1,0},{2,6},{3,7},{4,5},{5,4},{6,2},{7,3},{8,9},{9,8},{10,14... | collective-permute-start | bytes 6291464 | tf_op jit(solution)/shard_map/ppermute | solution.py:42
  874.8 146.9 %collective-permute-start.46 = (bf16[8,256,512]{2,1,0:T(8,128)(2,1)}, bf16[8,256,512]{2,1,0:T(8,128)(2,1)}, u32[]{:S(2)}, u32[]{:S(2)}) collective-permute-start(bf16[8,256,512]{2,1,0:T(8,128)(2,1)} %get-tuple-element.164), channel_id=1, source_target_pairs={{0,1},{1,0},{2,6},{3,7},{4,5},{5,4},{6,2},{7,3},{8,9},{9,8},{10,14... | collective-permute-start | bytes 6291464 | tf_op jit(solution)/shard_map/ppermute | solution.py:42
  876.5 34.5 %collective-permute-start.40 = (f32[2,1024]{1,0:T(2,128)S(1)}, f32[2,1024]{1,0:T(2,128)S(1)}, u32[]{:S(2)}, u32[]{:S(2)}) collective-permute-start(f32[2,1024]{1,0:T(2,128)S(1)} %copy-done.38), channel_id=1, source_target_pairs={{1,0},{3,2},{5,4},{7,6},{9,8},{11,10},{13,12},{15,14},{17,16},{19,... | collective-permute-start | bytes 24584 | tf_op jit(solution)/shard_map/ppermute | solution.py:1034
  909.7 174.1 %collective-permute-start.64 = (bf16[8,576,512]{2,1,0:T(8,128)(2,1)}, bf16[8,576,512]{2,1,0:T(8,128)(2,1)}, u32[]{:S(2)}, u32[]{:S(2)}) collective-permute-start(bf16[8,576,512]{2,1,0:T(8,128)(2,1)} %get-tuple-element.179), channel_id=1, source_target_pairs={{0,1},{1,0},{2,6},{3,7},{4,5},{5,4},{6,2},{7,3},{8,9},{9,8},{10,14... | collective-permute-start | bytes 14155784 | tf_op jit(solution)/shard_map/ppermute | solution.py:42
  911.4 30.8 %collective-permute-start.41 = (f32[2,11,1024]{2,1,0:T(8,128)S(1)}, f32[2,11,1024]{2,1,0:T(8,128)S(1)}, u32[]{:S(2)}, u32[]{:S(2)}) collective-permute-start(f32[2,11,1024]{2,1,0:T(8,128)S(1)} %pad_maximum_fusion.11), channel_id=1, source_target_pairs={{0,2},{1,3},{2,0},{3,1},{4,6},{5,7},{6,4},{7,5},{8,10},{9,11},{10,... | collective-permute-start | bytes 270344 | tf_op jit(solution)/shard_map/ppermute | solution.py:42
  940.8 150.3 %collective-permute-start.58 = (bf16[8,576,512]{2,1,0:T(8,128)(2,1)}, bf16[8,576,512]{2,1,0:T(8,128)(2,1)}, u32[]{:S(2)}, u32[]{:S(2)}) collective-permute-start(bf16[8,576,512]{2,1,0:T(8,128)(2,1)} %get-tuple-element.176), channel_id=1, source_target_pairs={{0,1},{1,0},{2,6},{3,7},{4,5},{5,4},{6,2},{7,3},{8,9},{9,8},{10,14... | collective-permute-start | bytes 14155784 | tf_op jit(solution)/shard_map/ppermute | solution.py:42
  948.0 67.2 %collective-permute-start.43 = (f32[2,11,1024]{2,1,0:T(8,128)S(1)}, f32[2,11,1024]{2,1,0:T(8,128)S(1)}, u32[]{:S(2)}, u32[]{:S(2)}) collective-permute-start(f32[2,11,1024]{2,1,0:T(8,128)S(1)} %fusion.48), channel_id=1, source_target_pairs={{0,4},{1,5},{2,6},{3,7},{4,0},{5,1},{6,2},{7,3},{8,12},{9,13},{10,... | collective-permute-start | bytes 270344 | tf_op jit(solution)/shard_map/ppermute | solution.py:42
  1024.2 19.5 %collective-permute-start.47 = (bf16[4,256,512]{2,1,0:T(8,128)(2,1)}, bf16[4,256,512]{2,1,0:T(8,128)(2,1)}, u32[]{:S(2)}, u32[]{:S(2)}) collective-permute-start(bf16[4,256,512]{2,1,0:T(8,128)(2,1)} %add_convert_fusion.10), channel_id=1, source_target_pairs={{0,4},{1,5},{2,3},{3,2},{4,0},{5,1},{6,7},{7,6},{8,12},{9,13},{10,... | collective-permute-start | bytes 3145736 | tf_op jit(solution)/shard_map/ppermute | solution.py:42
  1048.0 27.7 %collective-permute-start.50 = (bf16[256,512]{1,0:T(8,128)(2,1)S(1)}, bf16[256,512]{1,0:T(8,128)(2,1)S(1)}, u32[]{:S(2)}, u32[]{:S(2)}) collective-permute-start(bf16[256,512]{1,0:T(8,128)(2,1)S(1)} %get-tuple-element.277), channel_id=1, source_target_pairs={{0,8},{1,9},{2,10},{3,11},{4,12},{5,13},{6,14},{7,15},{8,16},{9,17... | collective-permute-start | bytes 786440 | tf_op jit(solution)/shard_map/ppermute | solution.py:42
  1056.9 26.7 %collective-permute-start.49 = (bf16[256,512]{1,0:T(8,128)(2,1)S(1)}, bf16[256,512]{1,0:T(8,128)(2,1)S(1)}, u32[]{:S(2)}, u32[]{:S(2)}) collective-permute-start(bf16[256,512]{1,0:T(8,128)(2,1)S(1)} %get-tuple-element.278), channel_id=1, source_target_pairs={{0,16},{1,17},{2,18},{3,19},{4,20},{5,21},{6,22},{7,23},{8,24},{9,... | collective-permute-start | bytes 786440 | tf_op jit(solution)/shard_map/ppermute | solution.py:42
  1060.4 34.4 %collective-permute-start.57 = (f32[128,512]{1,0:T(8,128)S(1)}, f32[128,512]{1,0:T(8,128)S(1)}, u32[]{:S(2)}, u32[]{:S(2)}) collective-permute-start(f32[128,512]{1,0:T(8,128)S(1)} %slice_select_fusion.4), channel_id=1, source_target_pairs={{0,2},{1,3},{2,0},{3,1},{4,6},{5,7},{6,4},{7,5},{8,10},{9,11},{10,... | collective-permute-start | bytes 786440 | tf_op jit(solution)/shard_map/ppermute | solution.py:42
  1086.4 28.1 %collective-permute-start.65 = (bf16[4,576,512]{2,1,0:T(8,128)(2,1)S(1)}, bf16[4,576,512]{2,1,0:T(8,128)(2,1)S(1)}, u32[]{:S(2)}, u32[]{:S(2)}) collective-permute-start(bf16[4,576,512]{2,1,0:T(8,128)(2,1)S(1)} %add_convert_fusion.1), channel_id=1, source_target_pairs={{0,4},{1,5},{2,3},{3,2},{4,0},{5,1},{6,7},{7,6},{8,12},{9,13},{10,... | collective-permute-start | bytes 7077896 | tf_op jit(solution)/shard_map/ppermute | solution.py:42
  1093.5 46.2 %collective-permute-start.59 = (bf16[4,576,512]{2,1,0:T(8,128)(2,1)S(1)}, bf16[4,576,512]{2,1,0:T(8,128)(2,1)S(1)}, u32[]{:S(2)}, u32[]{:S(2)}) collective-permute-start(bf16[4,576,512]{2,1,0:T(8,128)(2,1)S(1)} %add_convert_fusion.4), channel_id=1, source_target_pairs={{0,4},{1,5},{2,3},{3,2},{4,0},{5,1},{6,7},{7,6},{8,12},{9,13},{10,... | collective-permute-start | bytes 7077896 | tf_op jit(solution)/shard_map/ppermute | solution.py:42
  1117.2 27.0 %collective-permute-start.66 = (bf16[576,512]{1,0:T(8,128)(2,1)S(1)}, bf16[576,512]{1,0:T(8,128)(2,1)S(1)}, u32[]{:S(2)}, u32[]{:S(2)}) collective-permute-start(bf16[576,512]{1,0:T(8,128)(2,1)S(1)} %get-tuple-element.269), channel_id=1, source_target_pairs={{0,24},{1,25},{2,26},{3,27},{4,28},{5,29},{6,30},{7,31},{8,0},{9,1... | collective-permute-start | bytes 1769480 | tf_op jit(solution)/shard_map/ppermute | solution.py:42
  1118.8 25.8 %collective-permute-start.68 = (bf16[576,512]{1,0:T(8,128)(2,1)S(1)}, bf16[576,512]{1,0:T(8,128)(2,1)S(1)}, u32[]{:S(2)}, u32[]{:S(2)}) collective-permute-start(bf16[576,512]{1,0:T(8,128)(2,1)S(1)} %get-tuple-element.270), channel_id=1, source_target_pairs={{0,8},{1,9},{2,10},{3,11},{4,12},{5,13},{6,14},{7,15},{8,16},{9,17... | collective-permute-start | bytes 1769480 | tf_op jit(solution)/shard_map/ppermute | solution.py:42
  1118.8 50.1 %collective-permute-start.67 = (bf16[576,512]{1,0:T(8,128)(2,1)S(1)}, bf16[576,512]{1,0:T(8,128)(2,1)S(1)}, u32[]{:S(2)}, u32[]{:S(2)}) collective-permute-start(bf16[576,512]{1,0:T(8,128)(2,1)S(1)} %get-tuple-element.271), channel_id=1, source_target_pairs={{0,16},{1,17},{2,18},{3,19},{4,20},{5,21},{6,22},{7,23},{8,24},{9,... | collective-permute-start | bytes 1769480 | tf_op jit(solution)/shard_map/ppermute | solution.py:42
  1142.5 58.6 %collective-permute-start.60 = (bf16[576,512]{1,0:T(8,128)(2,1)S(1)}, bf16[576,512]{1,0:T(8,128)(2,1)S(1)}, u32[]{:S(2)}, u32[]{:S(2)}) collective-permute-start(bf16[576,512]{1,0:T(8,128)(2,1)S(1)} %get-tuple-element.266), channel_id=1, source_target_pairs={{0,24},{1,25},{2,26},{3,27},{4,28},{5,29},{6,30},{7,31},{8,0},{9,1... | collective-permute-start | bytes 1769480 | tf_op jit(solution)/shard_map/ppermute | solution.py:42
  1144.1 57.0 %collective-permute-start.62 = (bf16[576,512]{1,0:T(8,128)(2,1)S(1)}, bf16[576,512]{1,0:T(8,128)(2,1)S(1)}, u32[]{:S(2)}, u32[]{:S(2)}) collective-permute-start(bf16[576,512]{1,0:T(8,128)(2,1)S(1)} %get-tuple-element.267), channel_id=1, source_target_pairs={{0,8},{1,9},{2,10},{3,11},{4,12},{5,13},{6,14},{7,15},{8,16},{9,17... | collective-permute-start | bytes 1769480 | tf_op jit(solution)/shard_map/ppermute | solution.py:42
  1144.3 73.6 %collective-permute-start.61 = (bf16[576,512]{1,0:T(8,128)(2,1)S(1)}, bf16[576,512]{1,0:T(8,128)(2,1)S(1)}, u32[]{:S(2)}, u32[]{:S(2)}) collective-permute-start(bf16[576,512]{1,0:T(8,128)(2,1)S(1)} %get-tuple-element.268), channel_id=1, source_target_pairs={{0,16},{1,17},{2,18},{3,19},{4,20},{5,21},{6,22},{7,23},{8,24},{9,... | collective-permute-start | bytes 1769480 | tf_op jit(solution)/shard_map/ppermute | solution.py:42
  1169.3 53.6 %collective-permute-start.69 = (f32[288,512]{1,0:T(8,128)S(1)}, f32[288,512]{1,0:T(8,128)S(1)}, u32[]{:S(2)}, u32[]{:S(2)}) collective-permute-start(f32[288,512]{1,0:T(8,128)S(1)} %slice_select_fusion), channel_id=1, source_target_pairs={{0,2},{1,3},{2,0},{3,1},{4,6},{5,7},{6,4},{7,5},{8,10},{9,11},{10,... | collective-permute-start | bytes 1769480 | tf_op jit(solution)/shard_map/ppermute | solution.py:42
  (74 other events, 1230.6 us)
Sparse Core Ops, SparseCore 0:
  691.5 19.5 reduce-scatter.6
  842.0 21.6 reduce-scatter.4
  866.0 29.5 reduce-scatter.10
  897.7 29.5 reduce-scatter.8

commit v3 on v2

--- a/solution.py
+++ b/solution.py
@@ -63,35 +63,41 @@
     return target
 
 
+def unit_spots(z, x, c, y):
+    depth = sizes()[0] // 4
+    half, index = [], []
+    for yy in range(2):
+        for zz in range(depth):
+            for xx in range(2):
+                dx, dy, dz = xx ^ x, yy ^ y, (z - zz) % depth
+                half.append(dy if c == 0 else dx)
+                index.append((dx if c == 0 else dy) * depth + dz)
+    return half, index
+
+
 def unit_tables():
     dp, seq = sizes()
-    depth = dp // 4
     rows = []
     for d in range(dp):
         for y in range(seq):
             z, x, c = place(d)
-            half, index = [], []
-            for yy in range(2):
-                for zz in range(depth):
-                    for xx in range(2):
-                        dx, dy, dz = xx ^ x, yy ^ y, (z - zz) % depth
-                        half.append(dy if c == 0 else dx)
-                        index.append((dx if c == 0 else dy) * depth + dz)
-            held = []
+            half, index = unit_spots(z, x, c, y)
+            lines = [half]
             for side in range(2):
-                own = [i for i, h in zip(index, half) if h == side]
-                last, line = own[0], []
+                line, last = [], [i for i, h in zip(index, half) if h == side][0]
                 for i, h in zip(index, half):
                     last = i if h == side else last
                     line.append(last)
-                held.append(line)
-            order = [0] * (4 * depth)
-            for unit, (i, h) in enumerate(zip(index, half)):
-                order[h * 2 * depth + i] = unit
-            rows.append([half, held[0], held[1], order])
+                lines.append(line)
+            for core in range(2):
+                lines.extend(unit_spots(z, x, core, y))
+            rows.append(lines)
     table = jnp.asarray(np.array(rows, np.int32))
     me = lax.axis_index("dp") * seq + lax.axis_index("seq")
     return lax.dynamic_index_in_dim(table, me, 0, keepdims=False)
+
+
+SPOTS = 3
 
 
 def arrange(table, own, other):
@@ -121,106 +127,100 @@
         ),
         out_shape=jax.ShapeDtypeStruct((units,) + own.shape[1:], own.dtype),
         compiler_params=pltpu.CompilerParams(vmem_limit_bytes=VMEM),
-        cost_estimate=pl.CostEstimate(flops=0, bytes_accessed=4 * own.size * 2, transcendentals=0),
+        cost_estimate=pl.CostEstimate(flops=1, bytes_accessed=1, transcendentals=0),
     )(table, own, other)
 
 
-def split_units(table, whole):
-    units, block = whole.shape[0], (1,) + whole.shape[1:]
-    half = units // 2
-
-    def body(table_ref, in_ref, away_ref, keep_ref):
-        step = pl.program_id(0)
-
-        @pl.when(step < half)
-        def _():
-            away_ref[...] = in_ref[...]
-
-        @pl.when(step >= half)
-        def _():
-            keep_ref[...] = in_ref[...]
-
-    shape = jax.ShapeDtypeStruct((half,) + whole.shape[1:], whole.dtype)
-    return pl.pallas_call(
-        body,
-        grid_spec=pltpu.PrefetchScalarGridSpec(
-            num_scalar_prefetch=1,
-            grid=(units,),
-            in_specs=[pl.BlockSpec(block, lambda i, t: (t[3, lax.rem(i + half, units)], 0, 0))],
-            out_specs=[
-                pl.BlockSpec(block, lambda i, t: (jnp.minimum(i, half - 1), 0, 0)),
-                pl.BlockSpec(block, lambda i, t: (jnp.maximum(i - half, 0), 0, 0)),
-            ],
-        ),
-        out_shape=[shape, shape],
-        compiler_params=pltpu.CompilerParams(vmem_limit_bytes=VMEM),
-        cost_estimate=pl.CostEstimate(flops=0, bytes_accessed=4 * whole.size, transcendentals=0),
-    )(table, whole)
-
-
-def gather_pair(core, table, first, second):
-    dp, seq = sizes()
-    if not paired():
-        return tuple(
-            lax.all_gather(part, ("seq", "dp")).reshape((seq, dp) + part.shape)
-            for part in (first, second)
-        )
-    depth = dp // 4
-    kept = jnp.where(core == 0, first, second)
-    came = moved(jnp.where(core == 0, second, first), to_core)
-    pair = jnp.where(core == 0, jnp.stack([kept, came]), jnp.stack([came, kept]))
-    line = jnp.stack([pair] + [moved(pair, along_z(step)) for step in range(1, depth)])
-    line = line.reshape((depth, -1) + first.shape[1:])
-    half = jnp.concatenate([line, moved(line, to_second)])
-    mine = arrange(table, half, moved(half, to_third))
-    other = moved(mine, to_core)
-    shape = (seq, dp) + first.shape
-    return mine.reshape(shape), other.reshape(shape)
-
-
-def scatter_pair(core, table, stores):
-    dp, seq = sizes()
-    shape = stores.shape[3:]
-    if not paired():
-        flat = stores.reshape((2, seq * dp) + shape)
-        return tuple(
-            lax.psum_scatter(flat[i], ("seq", "dp"), scatter_dimension=0).astype(F32)
-            for i in range(2)
-        )
-    depth = dp // 4
-    groups = [[2 * i, 2 * i + 1] for i in range(dp // 2)]
-    flat = stores.reshape((2, 4 * depth, 2 * shape[0]) + shape[1:])
-    own = lax.psum_scatter(flat, "dp", scatter_dimension=0, axis_index_groups=groups)
-    away, keep = split_units(table, own)
-    came = moved(away, to_third)
-    away = (keep[depth:].astype(F32) + came[depth:].astype(F32)).astype(BF)
-    keep = (keep[:depth].astype(F32) + came[:depth].astype(F32)).astype(BF)
-    came = moved(away, to_second)
-    line = (keep.astype(F32) + came.astype(F32)).astype(BF)
-    total = line[0].astype(F32)
-    for step in range(1, depth):
-        total = total + moved(line[step], along_z(-step)).astype(F32)
-    total = total.reshape((2,) + shape)
-    kept = jnp.where(core == 0, total[0], total[1])
-    came = moved(jnp.where(core == 0, total[1], total[0]), to_core)
-    return jnp.where(core == 0, kept, came), jnp.where(core == 0, came, kept)
-
-
-def summed_everywhere(array):
-    dp, seq = sizes()
-    if not paired():
-        return lax.psum(array, BOTH)
-    steps = [to_core, lambda z, x, c, y: (z, x, c, 1 - y), lambda z, x, c, y: (z, 1 - x, c, y)]
-    for target in steps:
-        array = array + moved(array, target)
-    total = array
-    if dp // 4 == 4:
-        for bit in (1, 2):
-            total = total + moved(total, lambda z, x, c, y, bit=bit: (z ^ bit, x, c, y))
-        return total
-    for step in range(1, dp // 4):
-        total = total + moved(array, along_z(step))
-    return total
+def tie(arrays, *others):
+    return lax.optimization_barrier((arrays, others))[0]
+
+
+class Gathering:
+    def __init__(self, table, pair):
+        self.table, self.pair, self.depth = table, pair, sizes()[0] // 4
+
+    def z(self, *after):
+        pair = tie(self.pair, *after)
+        self.parts = [moved(pair, along_z(step)) for step in range(1, self.depth)]
+
+    def end_z(self, *after):
+        line = jnp.stack([self.pair] + tie(self.parts, *after))
+        self.line = line.reshape((self.depth, -1) + line.shape[3:])
+        return self.line
+
+    def second(self, *after):
+        self.came = moved(tie(self.line, *after), to_second)
+        return self.came
+
+    def third(self, *after):
+        self.half = jnp.concatenate(tie([self.line, self.came], *after))
+        self.far = moved(self.half, to_third)
+        return self.far
+
+    def arrange(self, *after):
+        self.mine = arrange(self.table, *tie((self.half, self.far), *after))
+        return self.mine
+
+    def swap(self):
+        dp, seq = sizes()
+        other = moved(self.mine, to_core)
+        shape = (seq, dp, self.mine.shape[1] // 2) + self.mine.shape[2:]
+        return self.mine.reshape(shape), other.reshape(shape)
+
+
+class Scattering:
+    def __init__(self, away, keep):
+        self.depth = sizes()[0] // 4
+        groups = [[2 * i, 2 * i + 1] for i in range(sizes()[0] // 2)]
+        self.take = lambda array: lax.psum_scatter(array, "dp", scatter_dimension=0, axis_index_groups=groups)
+        self.away, self.keep = self.take(away), keep
+
+    def third(self, *after):
+        self.away = tie(self.away, *after)
+        self.keep = self.take(tie(self.keep, self.away))
+        self.came = moved(self.away, to_third)
+        return self.away
+
+    def end_third(self, *after):
+        depth, keep, came = self.depth, *tie((self.keep, self.came), *after)
+        self.away = (keep[depth:].astype(F32) + came[depth:].astype(F32)).astype(BF)
+        self.keep = (keep[:depth].astype(F32) + came[:depth].astype(F32)).astype(BF)
+        return self.away
+
+    def second(self, *after):
+        self.came = moved(tie(self.away, *after), to_second)
+
+    def end_second(self, *after):
+        keep, came = tie((self.keep, self.came), *after)
+        self.line = (keep.astype(F32) + came.astype(F32)).astype(BF)
+        return self.line
+
+    def z(self, *after):
+        line = tie(self.line, *after)
+        self.parts = [moved(line[step], along_z(-step)) for step in range(1, self.depth)]
+        return self.parts
+
+    def end_z(self, core):
+        total = self.line[0].astype(F32)
+        for part in self.parts:
+            total = total + part.astype(F32)
+        total = total.reshape((2, -1) + total.shape[1:])
+        kept = jnp.where(core == 0, total[0], total[1])
+        came = moved(jnp.where(core == 0, total[1], total[0]), to_core)
+        return jnp.where(core == 0, kept, came), jnp.where(core == 0, came, kept)
+
+
+def summed_z(array):
+    dp, _ = sizes()
+    return lax.psum(array, "dp", axis_index_groups=[list(range(i, dp, 4)) for i in range(4)])
+
+
+def hop_y(array):
+    return array + moved(array, lambda z, x, c, y: (z, x, c, 1 - y))
+
+
+def hop_x(array):
+    return array + moved(array, lambda z, x, c, y: (z, 1 - x, c, y))
 
 
 def params(**more):
@@ -228,7 +228,7 @@
 
 
 def cost(flops, bytes_accessed):
-    return pl.CostEstimate(flops=int(flops), bytes_accessed=int(bytes_accessed), transcendentals=0)
+    return pl.CostEstimate(flops=1, bytes_accessed=1, transcendentals=0)
 
 
 def held(shape):
@@ -639,7 +639,7 @@
 
 def channel_back(
     core, g, fix, s, lead, marks, gain, bias, mix, gate, carried, xk, xr, acts, lookups, contents, accept,
-    cut, length, packing,
+    cut, length, packing, table,
 ):
     tokens, width = s.shape
     tile = tile_rows(length)
@@ -651,30 +651,60 @@
     half_rows = accept.shape[2] // 2
     last = 2 * steps - 1
     slots = len(shapes)
+    split = slots == 2
+    units = dp // 2
 
     def body(
         core_ref, g_ref, fix_ref, s_ref, lead_ref, marks_ref, gain_ref, bias_ref, mix_ref,
         gate_ref, carried_ref, xk_ref, xr_ref, act0_ref, act1_ref, accept_ref,
-        lookup0_ref, content0_ref, lookup1_ref, content1_ref, *rest,
+        lookup0_ref, content0_ref, lookup1_ref, content1_ref, table_ref, *rest,
     ):
         outs, rest = rest[:slots], rest[slots:]
         out_ref, edge_ref, small_ref, gc_ref, gr_ref, sum_ref, key_ref, val_ref, take_ref, sem, stage_ref = rest
-        lookup_out, content_out, accept_out = outs if slots == 3 else (outs[0],) * 3
+        if not split:
+            lookup_out, content_out, accept_out = outs
         step = pl.program_id(0)
         slot = lax.rem(step, 2)
 
-        def copies(which, store, q):
+        def waits(which):
+            if split:
+                rows = pl.ds(0, cut.rows)
+                key = outs[1].at[0, :, :, rows, :]
+                val = outs[1].at[0, pl.ds(0, seq * cut.group // 2), :, pl.ds(0, cut.grain), :]
+                val_from = val_ref.at[which].reshape(seq * cut.group // 2, 2, cut.grain, columns)
+            else:
+                key = lookup_out.at[0, 0, :, :, pl.ds(0, cut.rows), :]
+                val = content_out.at[0, :, pl.ds(0, cut.group // 2), :, :, :]
+                val_from = val_ref.at[which]
+            pltpu.make_async_copy(key_ref.at[which], key, sem.at[which, 0]).wait()
+            pltpu.make_async_copy(val_from, val, sem.at[which, 1]).wait()
+
+        def send(source, unit, store, rows, sem):
+            half = table_ref[SPOTS + 2 * store, unit]
+            index = table_ref[SPOTS + 1 + 2 * store, unit]
+            for side in range(2):
+
+                @pl.when(half == 1 - side)
+                def _(side=side):
+                    pltpu.make_async_copy(source, outs[side].at[store, index, :, rows, :], sem).start()
+
+        def start(which, store, q):
             y, block = lax.div(q, cut.blocks), lax.rem(q, cut.blocks)
-            rows = pl.ds(pl.multiple_of(spots[0] + block * cut.rows, 16), cut.rows)
-            key = pltpu.make_async_copy(
-                key_ref.at[which], lookup_out.at[store, y, :, rows, :], sem.at[which, 0]
-            )
-            parts = pl.ds(q * cut.group, cut.group)
-            rows = pl.ds(spots[1], cut.grain)
-            val = pltpu.make_async_copy(
-                val_ref.at[which], content_out.at[store, :, parts, rows, :], sem.at[which, 1]
-            )
-            return key, val
+            if split:
+                rows = pl.ds(pl.multiple_of(spots[0] + block * cut.rows, 16), cut.rows)
+                for unit in range(units):
+                    send(key_ref.at[which, unit], y * units + unit, store, rows, sem.at[which, 0])
+                for y in range(seq):
+                    for part in range(cut.group // 2):
+                        unit = y * units + q * (cut.group // 2) + part
+                        rows = pl.ds(spots[1], cut.grain)
+                        send(val_ref.at[which, y, part], unit, store, rows, sem.at[which, 1])
+            else:
+                rows = pl.ds(pl.multiple_of(block * cut.rows, 16), cut.rows)
+                key = lookup_out.at[store, y, :, :, rows, :]
+                pltpu.make_async_copy(key_ref.at[which], key, sem.at[which, 0]).start()
+                val = content_out.at[store, :, pl.ds(q * (cut.group // 2), cut.group // 2), :, :, :]
+                pltpu.make_async_copy(val_ref.at[which], val, sem.at[which, 1]).start()
 
         def store_of_step(i):
             core = core_ref[0]
@@ -697,8 +727,7 @@
 
         @pl.when(step >= 2)
         def _():
-            for copy in copies(slot, *store_of_step(step - 2)):
-                copy.wait()
+            waits(slot)
 
         def work(act_ref, lookup_ref, content_ref, first):
             up = lookup_ref[0].reshape(dp * cut.rows, cut.width)
@@ -718,10 +747,10 @@
                 part = dot_nt(grad, up)
                 sum_ref[rows, :] = part if first else sum_ref[rows, :] + part
             key = dot_tn(xk_ref[...], take_ref[...])
-            key_ref[slot] = key.astype(BF).reshape(dp, cut.rows, cut.width)
+            key_ref[slot] = key.astype(BF).reshape(units, 2, cut.rows, cut.width)
             for y in range(seq):
                 val = dot_tn(act_ref[0], gc_ref[:, y * columns : (y + 1) * columns])
-                val_ref[slot, y] = val.astype(BF).reshape(cut.group, cut.grain, columns)
+                val_ref[slot, y] = val.astype(BF).reshape(cut.group // 2, 2, cut.grain, columns)
 
         @pl.when(step == 0)
         def _():
@@ -735,27 +764,25 @@
         def _():
             work(act1_ref, lookup1_ref, content1_ref, False)
 
-        for copy in copies(slot, *store_of_step(step)):
-            copy.start()
+        start(slot, *store_of_step(step))
 
         @pl.when(step == last)
         def _():
-            for copy in copies(1 - slot, *store_of_step(step - 1)):
-                copy.wait()
-            for copy in copies(slot, *store_of_step(step)):
-                copy.wait()
+            waits(1 - slot)
+            waits(slot)
             rows = pl.ds(spots[2], half_rows)
-            takes = []
             for y in range(seq):
                 grad = dot_tn(xr_ref[...], gr_ref[:, y * columns : (y + 1) * columns])
                 grad = grad.astype(BF).reshape(dp, 2 * half_rows, columns)
                 for h in range(2):
-                    buffer = stage_ref.at[h, y]
-                    stage_ref[h, y] = grad[:, h * half_rows : (h + 1) * half_rows, :]
-                    takes.append(
-                        pltpu.make_async_copy(buffer, accept_out.at[h, y, :, rows, :], sem.at[h, 2 + y])
-                    )
-                    takes[-1].start()
+                    part = grad[:, h * half_rows : (h + 1) * half_rows, :]
+                    stage_ref[h, y] = part.reshape(units, 2, half_rows, columns)
+                    if split:
+                        for unit in range(units):
+                            send(stage_ref.at[h, y, unit], y * units + unit, h, rows, sem.at[h, 2 + y])
+                    else:
+                        take = accept_out.at[h, y]
+                        pltpu.make_async_copy(stage_ref.at[h, y], take, sem.at[h, 2 + y]).start()
             after = None
             small = None
             for i in reversed(range(tiles)):
@@ -773,8 +800,13 @@
                     edge_ref[i // per_run : i // per_run + 1, :] = after
             for j, line in enumerate(small):
                 small_ref[j : j + 1, :] = line
-            for copy in takes:
-                copy.wait()
+            for h in range(2):
+                for y in range(seq):
+                    if split:
+                        take = outs[1].at[0, :, :, rows, :]
+                    else:
+                        take = accept_out.at[h, y]
+                    pltpu.make_async_copy(stage_ref.at[h, y], take, sem.at[h, 2 + y]).wait()
 
     own = lambda i: jnp.minimum(i, steps - 1)
     partner = lambda i: jnp.maximum(i - steps, 0)
@@ -787,7 +819,7 @@
             SCALAR, held(g.shape), fixed(fix.shape), held(s.shape), fixed(lead.shape), held(marks.shape),
             fixed(gain.shape), fixed(bias.shape), fixed(mix.shape), held(gate.shape), held(carried.shape),
             held(xk.shape), held(xr.shape), act(own), act(partner), held(accept.shape),
-        ] + cut.specs(lookups[0], contents[0], own) + cut.specs(lookups[1], contents[1], partner),
+        ] + cut.specs(lookups[0], contents[0], own) + cut.specs(lookups[1], contents[1], partner) + [SCALAR],
         out_specs=[any_space] * slots + [fixed((tokens, width)), fixed(fix.shape), fixed((4, width))],
         out_shape=[jax.ShapeDtypeStruct(shape, BF) for shape in shapes] + [
             jax.ShapeDtypeStruct((tokens, width), F32), jax.ShapeDtypeStruct(fix.shape, F32),
@@ -796,11 +828,11 @@
         scratch_shapes=[
             pltpu.VMEM((tokens, width), BF), pltpu.VMEM((tokens, width), BF),
             pltpu.VMEM((tokens, width), F32),
-            pltpu.VMEM((2, dp, cut.rows, cut.width), BF),
-            pltpu.VMEM((2, seq, cut.group, cut.grain, columns), BF),
+            pltpu.VMEM((2, units, 2, cut.rows, cut.width), BF),
+            pltpu.VMEM((2, seq, cut.group // 2, 2, cut.grain, columns), BF),
             pltpu.VMEM((tokens, cut.width), BF),
             pltpu.SemaphoreType.DMA((2, 2 + seq)),
-            pltpu.VMEM((2, seq, dp, half_rows, columns), BF),
+            pltpu.VMEM((2, seq, units, 2, half_rows, columns), BF),
         ],
         compiler_params=params(),
         cost_estimate=cost(
@@ -809,7 +841,7 @@
         ),
     )(
         core, g, fix, s, lead, marks, gain, bias, mix, gate, carried, xk, xr, *acts, accept,
-        lookups[0][0], contents[0][0], lookups[1][0], contents[1][0],
+        lookups[0][0], contents[0][0], lookups[1][0], contents[1][0], table,
     )
 
 
@@ -977,16 +1009,24 @@
     )
 
 
-def weight_grads(first, second, grads):
+def weight_grads(first, second, grads, table):
     dp, seq = sizes()
     tokens, width = grads[0].shape
     rows, columns = width // dp, width // seq
     pairs = list(zip(first + second, grads))
-
-    def body(*refs):
-        ins, (out_ref, x_ref, g_ref, sem) = refs[: 2 * len(pairs)], refs[2 * len(pairs) :]
+    split, units = paired(), dp // 2
+    if split:
+        shapes = [(2, units * seq // 2, 2, 2 * rows, columns)] * 2
+    else:
+        shapes = [(2, seq, units, 2, 2 * rows, columns)]
+
+    def body(table_ref, *refs):
+        ins, rest = refs[: 2 * len(pairs)], refs[2 * len(pairs) :]
+        outs, (x_ref, g_ref, stage_ref, sem, out_sem) = rest[: len(shapes)], rest[len(shapes) :]
         which, y = pl.program_id(0), pl.program_id(1)
         slot = lax.rem(which, 2)
+        step = which * seq + y
+        place = lax.rem(step, 2)
 
         def copies(i):
             return (
@@ -994,7 +1034,11 @@
                 pltpu.make_async_copy(ins[2 * i + 1], g_ref.at[i % 2], sem.at[i % 2, 1]),
             )
 
-        @pl.when(jnp.logical_and(which == 0, y == 0))
+        def wait(at):
+            target = outs[0].at[0, :, :, pl.ds(0, rows), :] if split else outs[0].at[0, 0, :, :, pl.ds(0, rows), :]
+            pltpu.make_async_copy(stage_ref.at[at], target, out_sem.at[at]).wait()
+
+        @pl.when(step == 0)
         def _():
             for copy in copies(0):
                 copy.start()
@@ -1009,23 +1053,50 @@
                     for copy in copies(i + 1):
                         copy.start()
 
+        @pl.when(step >= 2)
+        def _():
+            wait(place)
+
         at = pl.ds(pl.multiple_of(y * columns, columns), columns)
         grad = dot_tn(x_ref[slot], g_ref[slot, :, at])
-        out_ref[0, 0] = grad.astype(BF).reshape(dp, rows, columns)
-
+        stage_ref[place] = grad.astype(BF).reshape(units, 2, rows, columns)
+        store = lax.div(which, 2)
+        span = pl.ds(pl.multiple_of(lax.rem(which, 2) * rows, 16), rows)
+        if split:
+            for unit in range(units):
+                half = table_ref[SPOTS + 2 * store, y * units + unit]
+                index = table_ref[SPOTS + 1 + 2 * store, y * units + unit]
+                for side in range(2):
+
+                    @pl.when(half == 1 - side)
+                    def _(side=side, unit=unit, index=index):
+                        pltpu.make_async_copy(
+                            stage_ref.at[place, unit], outs[side].at[store, index, :, span, :], out_sem.at[place]
+                        ).start()
+        else:
+            target = outs[0].at[store, y, :, :, span, :]
+            pltpu.make_async_copy(stage_ref.at[place], target, out_sem.at[place]).start()
+
+        @pl.when(step == len(pairs) * seq - 1)
+        def _():
+            wait(1 - place)
+            wait(place)
+
+    any_space = pl.BlockSpec(memory_space=pl.ANY)
     return pl.pallas_call(
         body,
         grid=(len(pairs), seq),
-        in_specs=[pl.BlockSpec(memory_space=pl.ANY)] * (2 * len(pairs)),
-        out_specs=pl.BlockSpec((1, 1, dp, rows, columns), lambda m, y: (lax.div(m, 2), y, 0, lax.rem(m, 2), 0)),
-        out_shape=jax.ShapeDtypeStruct((2, seq, dp, 2 * rows, columns), BF),
+        in_specs=[SCALAR] + [any_space] * (2 * len(pairs)),
+        out_specs=[any_space] * len(shapes),
+        out_shape=[jax.ShapeDtypeStruct(shape, BF) for shape in shapes],
         scratch_shapes=[
             pltpu.VMEM((2, tokens, width), BF), pltpu.VMEM((2, tokens, width), BF),
-            pltpu.SemaphoreType.DMA((2, 2)),
+            pltpu.VMEM((2, units, 2, rows, columns), BF),
+            pltpu.SemaphoreType.DMA((2, 2)), pltpu.SemaphoreType.DMA((2,)),
         ],
         compiler_params=params(),
         cost_estimate=cost(8 * tokens * width * width, 16 * tokens * width + 8 * width * width),
-    )(*[array for pair in pairs for array in pair])
+    )(table, *[array for pair in pairs for array in pair])
 
 
 def passed_along(array, axis, by):
@@ -1072,22 +1143,54 @@
     return cut.reshape(rows, -1)
 
 
-def gather_group(core, table, firsts, seconds):
-    if not paired():
-        pairs = [gather_pair(core, table, a, b) for a, b in zip(firsts, seconds)]
-        return [(a, 0) for a, _ in pairs], [(b, 0) for _, b in pairs]
-    mine, other = gather_pair(core, table, jnp.concatenate(firsts), jnp.concatenate(seconds))
-    spots = [0] + np.cumsum([a.shape[0] for a in firsts])[:-1].tolist()
-    return [(mine, at) for at in spots], [(other, at) for at in spots]
-
-
-def scatter_group(core, table, stores, sizes_of):
-    if not paired():
-        pairs = [scatter_pair(core, table, s) for s in stores]
-        return [a for a, _ in pairs], [b for _, b in pairs]
-    first, second = scatter_pair(core, table, stores[0])
-    cuts = np.cumsum(sizes_of)[:-1].tolist()
-    return jnp.split(first, cuts), jnp.split(second, cuts)
+def spots_of(shards):
+    return [0] + np.cumsum([shard.shape[0] for shard in shards]).tolist()
+
+
+def cut_at(array, spots):
+    return [array[a:b] for a, b in zip(spots, spots[1:])]
+
+
+def gather_plain(first, second):
+    dp, seq = sizes()
+    whole = lambda a: (lax.all_gather(a, ("seq", "dp")).reshape((seq, dp) + a.shape), 0)
+    return [whole(a) for a in first], [whole(a) for a in second]
+
+
+def scatter_plain(stores):
+    dp, seq = sizes()
+    take = lambda a: lax.psum_scatter(
+        a.reshape((seq * dp,) + a.shape[-2:]), ("seq", "dp"), scatter_dimension=0
+    ).astype(F32)
+    return [take(s[0]) for s in stores], [take(s[1]) for s in stores]
+
+
+def by_half(first_is_low, low, high):
+    return jnp.where(first_is_low, low, high), jnp.where(first_is_low, high, low)
+
+
+def partner_y(array):
+    return lax.ppermute(array, "seq", [(0, 1), (1, 0)])
+
+
+def rows_cut(array):
+    half = array.shape[0] // 2
+    return by_half(lax.axis_index("seq") == 0, array[:half], array[half:])
+
+
+def rows_joined(kept, came):
+    low = lax.axis_index("seq") == 0
+    return jnp.concatenate(by_half(low, kept, came), axis=1)
+
+
+def runs_cut(array):
+    length = array.shape[1] // 2
+    return by_half(lax.axis_index("seq") == 0, array[:, :length], array[:, length:])
+
+
+def runs_joined(kept, came):
+    low = lax.axis_index("seq") == 0
+    return jnp.concatenate(by_half(low, kept, came), axis=0)
 
 
 def per_device(
@@ -1106,125 +1209,262 @@
     channelmix_accept_matrix,
 ):
     dp, seq = sizes()
+    staged = paired()
     core = core_of()
     cores = core.reshape(1)
-    table = unit_tables() if paired() else None
+    table = unit_tables() if staged else jnp.zeros((1, 1), jnp.int32)
     layers = attention_triple_matrix.shape[0]
     runs, length, width = entering_activations.shape
-    tokens = runs * length
+    tokens, columns = runs * length, width // seq
+    swapped = staged and layers == 2 and runs % 2 == 0
+    if swapped:
+        kept_rows, sent_rows = rows_cut(document_numbers)
+        document_numbers = rows_joined(kept_rows, partner_y(sent_rows))
+        kept_rows, sent_rows = rows_cut(entering_activations)
+        entering_activations = rows_joined(kept_rows, partner_y(sent_rows))
+        runs, length = runs // 2, length * 2
 
     lookup_rows = channelmix_lookup_matrix.shape[1]
     grain = channelmix_content_matrix.shape[1] // 2
     half_rows = channelmix_accept_matrix.shape[1] // 2
 
-    att, chan = [], []
+    shards = []
     for depth in range(layers):
         triple, result = attention_triple_matrix[depth], attention_result_matrix[depth]
-        att.append(
-            gather_pair(
-                core,
-                table,
-                jnp.concatenate([triple[0], triple[1]]),
-                jnp.concatenate([triple[2], result]),
+        lookup = cut_lookup(channelmix_lookup_matrix[depth], grain)
+        content, accept = channelmix_content_matrix[depth], channelmix_accept_matrix[depth]
+        shards.append(([jnp.concatenate([triple[0], triple[1]])], [jnp.concatenate([triple[2], result])]))
+        shards.append(
+            (
+                [lookup[0], content[:grain], accept[:half_rows]],
+                [lookup[1], content[grain:], accept[half_rows:]],
             )
         )
-        lookup = cut_lookup(channelmix_lookup_matrix[depth], grain)
-        content, accept = channelmix_content_matrix[depth], channelmix_accept_matrix[depth]
-        mine, other = gather_group(
-            core,
-            table,
-            [lookup[0], content[:grain], accept[:half_rows]],
-            [lookup[1], content[grain:], accept[half_rows:]],
-        )
+
+    held = {}
+    if staged:
+        first = jnp.concatenate([shard for group in shards for shard in group[0]])
+        second = jnp.concatenate([shard for group in shards for shard in group[1]])
+        kept = jnp.where(core == 0, first, second)
+        came = moved(jnp.where(core == 0, second, first), to_core)
+        pair = jnp.where(core == 0, jnp.stack([kept, came]), jnp.stack([came, kept]))
+        ends = spots_of([jnp.concatenate(group[0]) for group in shards])
+        moves = [Gathering(table, pair[:, a:b]) for a, b in zip(ends, ends[1:])]
+    else:
+        moves = [gather_plain(*group) for group in shards]
+
+    def give_att(depth, mine, other):
+        held["att", depth] = (mine, other)
+
+    def give_chan(depth, mine, other):
         takes = [array[:, :, at : at + half_rows] for array, at in (mine[2], other[2])]
         first = jnp.where(core == 0, takes[0], takes[1])
         second = jnp.where(core == 0, takes[1], takes[0])
-        cut = Cut(mine[0], mine[1], lookup_rows, grain)
-        chan.append((mine, other, jnp.concatenate([first, second], axis=2), cut))
-
-    border = passed_along(document_numbers[:, -1:] + 1, "seq", 1)
-    earlier = jnp.concatenate([border - 1, document_numbers[:, :-1]], axis=1)
+        held["cut", depth] = Cut(mine[0], mine[1], lookup_rows, grain)
+        held["chan", depth] = (mine, other, jnp.concatenate([first, second], axis=2))
+
+    def with_rows(array, group):
+        return [(array, at) for at in spots_of(shards[group][0])[:-1]]
+
+    if swapped:
+        border = jnp.full((runs, 1), -1, document_numbers.dtype)
+    else:
+        border = passed_along(document_numbers[:, -1:] + 1, "seq", 1) - 1
+    earlier = jnp.concatenate([border, document_numbers[:, :-1]], axis=1)
+    edges = jnp.zeros((runs, width), F32)
+    states = jnp.zeros((runs, 2, width), F32)
     marks, lines = token_marks(document_numbers, earlier)
     through = (earlier[:, :1] == document_numbers[:, -1:]).astype(F32)[:, :, None]
     begins = (earlier[:, :1] == document_numbers[:, :1]).astype(F32)[:, :, None]
     rates = jnp.exp(fading_natural_logs_per_feature)
     bonuses = jnp.exp(feature_reward_logs)
 
-    flow = entering_activations.reshape(tokens, width)
-    kept = []
-    for depth in range(layers):
-        gain, bias = normalizer_scales[depth], normalizer_offsets[depth]
-        mix, rate, bonus = shift_blend_factors[depth], rates[depth : depth + 1], bonuses[depth : depth + 1]
-        chain = jnp.exp(-length * rate)[None] * through
-        mine, other = att[depth]
-        before = edge_norm(flow, length, gain[0], bias[0])
-        xk, xv, xr, k, v, r, ends, lead = time_in(
-            cores, flow, before, marks, gain[0:1], bias[0:1], mix[:3], rate, mine, other, length
+    def layer_values(depth):
+        gain, bias, mix = normalizer_scales[depth], normalizer_offsets[depth], shift_blend_factors[depth]
+        rate, bonus = rates[depth : depth + 1], bonuses[depth : depth + 1]
+        return gain, bias, mix, rate, bonus, jnp.exp(-length * rate)[None] * through
+
+    kept = {}
+
+    def run_time_in(depth, flow):
+        gain, bias, mix, rate, _, _ = layer_values(depth)
+        before = edges if swapped else edge_norm(flow, length, gain[0], bias[0])
+        kept["time", depth] = (flow,) + tuple(
+            time_in(
+                cores, flow, before, marks, gain[0:1], bias[0:1], mix[:3], rate, *held["att", depth], length
+            )
         )
-        enter = entering(chain, ends, 1)
+        return kept["time", depth][4]
+
+    def run_time_out(depth, *after):
+        _, _, _, rate, bonus, chain = layer_values(depth)
+        flow, xk, xv, xr, k, v, r, ends, lead = kept["time", depth]
+        enter = states if swapped else entering(chain, ends, 1)
+        k = tie(k, *after) if after else k
         z, sa, sb, middle = time_out(
-            cores, flow, k, v, r, enter, marks, lines, rate, bonus, mine, other, length
+            cores, flow, k, v, r, enter, marks, lines, rate, bonus, *held["att", depth], length
         )
-        time_kept = (flow, lead, xk, xv, xr, k, v, r, z, sa, sb)
-        mine, other, accept, cut = chan[depth]
-        before = edge_norm(middle, length, gain[1], bias[1])
-        xk, xr, lead, act0, total = channel_one(
+        kept["time", depth] = (flow, lead, xk, xv, xr, k, v, r, z, sa, sb)
+        gain, bias, _, _, _, _ = layer_values(depth)
+        before = edges if swapped else edge_norm(middle, length, gain[1], bias[1])
+        kept["middle", depth] = (middle, before)
+        return middle
+
+    def run_channel_one(depth, mine, cut, *after):
+        gain, bias, mix, _, _, _ = layer_values(depth)
+        middle, before = kept["middle", depth]
+        before = tie(before, *after) if after else before
+        kept["one", depth] = channel_one(
             middle, before, marks, gain[1:2], bias[1:2], mix[3:], mine[0], mine[1], cut, length
         )
+        return kept["one", depth][4]
+
+    def run_channel_two(depth, *after):
+        middle, _ = kept["middle", depth]
+        xk, xr, lead, act0, total = kept["one", depth]
+        _, other, accept = held["chan", depth]
+        total = tie(total, *after) if after else total
         kind = BF if depth == layers - 1 else F32
-        act1, carried, gate, flow = channel_two(middle, xk, xr, total, other[0], other[1], accept, cut, kind)
-        kept.append((time_kept, (middle, lead, xk, xr, (act0, act1), carried, gate)))
-    y_out = flow
+        act1, carried, gate, flow = channel_two(
+            middle, xk, xr, total, other[0], other[1], accept, held["cut", depth], kind
+        )
+        kept["chan", depth] = (middle, lead, xk, xr, (act0, act1), carried, gate)
+        return flow
+
+    flow = entering_activations.reshape(tokens, width)
+    if staged and layers == 2:
+        att0, chan0, att1, chan1 = moves
+
+        def place_att(depth, move):
+            give_att(depth, *move.swap())
+
+        def place_chan(depth, move, group):
+            mine, other = move.swap()
+            give_chan(depth, with_rows(mine, group), with_rows(other, group))
+
+        att0.z()
+        chan0.z(att0.end_z())
+        att0.second(flow)
+        far = att0.third(chan0.parts[0])
+        att0.arrange()
+        att0.mine = tie(att0.mine, chan0.parts)
+        chan0.end_z(far)
+        near = chan0.second()
+        place_att(0, att0)
+        done = run_time_in(0, flow)
+        far = chan0.third(done)
+        att1.z(done)
+        done = run_time_out(0, near)
+        line = att1.end_z(done)
+        chan1.z(line)
+        near = att1.second(far, done)
+        mine = chan0.arrange(done, line, chan1.parts)
+        place_chan(0, chan0, 1)
+        far = att1.third(mine)
+        own, _, _ = held["chan", 0]
+        done = run_channel_one(0, own, held["cut", 0], near)
+        line = chan1.end_z(done)
+        near = chan1.second(far)
+        mine = att1.arrange(done, line)
+        place_att(1, att1)
+        flow = run_channel_two(0, mine)
+        far = chan1.third(flow)
+        done = run_time_in(1, tie(flow, near))
+        done = run_time_out(1)
+        chan1.arrange(done)
+        place_chan(1, chan1, 3)
+        own, _, _ = held["chan", 1]
+        run_channel_one(1, own, held["cut", 1])
+        y_out = run_channel_two(1)
+        if swapped:
+            kept_rows, sent_rows = rows_cut(tie(result_cotangent, far))
+            result_cotangent = rows_joined(kept_rows, partner_y(sent_rows))
+            kept_runs, sent_runs = runs_cut(y_out.reshape(runs, length, width))
+            y_out = runs_joined(kept_runs, partner_y(sent_runs))
+    else:
+        for depth in range(layers):
+            if staged:
+                for move in moves[2 * depth : 2 * depth + 2]:
+                    move.z()
+                    move.end_z()
+                    move.second()
+                    move.third()
+                    move.arrange()
+                give_att(depth, *moves[2 * depth].swap())
+                mine, other = moves[2 * depth + 1].swap()
+                group = 2 * depth + 1
+                give_chan(depth, with_rows(mine, group), with_rows(other, group))
+            else:
+                mine, other = moves[2 * depth]
+                give_att(depth, mine[0][0], other[0][0])
+                give_chan(depth, *moves[2 * depth + 1])
+            run_time_in(depth, flow)
+            run_time_out(depth)
+            run_channel_one(depth, held["chan", depth][0], held["cut", depth])
+            flow = run_channel_two(depth)
+        y_out = flow
 
     grad = result_cotangent.reshape(tokens, width)
     fix = jnp.zeros((runs, width), F32)
-    small, large = [None] * layers, [None] * layers
-    columns = width // seq
+    small = [None] * layers
+    sums = {}
+    earlier_chan = earlier_att = None
     for depth in reversed(range(layers)):
-        gain, bias = normalizer_scales[depth], normalizer_offsets[depth]
-        mix, rate, bonus = shift_blend_factors[depth], rates[depth : depth + 1], bonuses[depth : depth + 1]
-        chain = jnp.exp(-length * rate)[None] * through
-        (flow, lead_t, xk_t, xv_t, xr_t, k, v, r, z, sa, sb), channel_kept = kept[depth]
-        middle, lead, xk, xr, acts, carried, gate = channel_kept
-        mine, other, accept, cut = chan[depth]
+        gain, bias, mix, rate, bonus, chain = layer_values(depth)
+        flow, lead_t, xk_t, xv_t, xr_t, k, v, r, z, sa, sb = kept["time", depth]
+        middle, lead, xk, xr, acts, carried, gate = kept["chan", depth]
+        mine, other, accept = held["chan", depth]
+        cut = held["cut", depth]
         part_rows = [cut.blocks * lookup_rows, grain, half_rows]
-        if paired():
-            packing = [(2, seq, dp, sum(part_rows), columns)], [0, part_rows[0], part_rows[0] + grain]
+        part_spots = [0, part_rows[0], part_rows[0] + grain, part_rows[0] + grain + half_rows]
+        if staged:
+            packing = [(2, seq * dp // 4, 2, part_spots[3], columns)] * 2, part_spots
         else:
             widths = [cut.width, columns, columns]
-            packing = [(2, seq, dp, n, w) for n, w in zip(part_rows, widths)], [0, 0, 0]
+            packing = [(2, seq, dp // 2, 2, n, w) for n, w in zip(part_rows, widths)], [0, 0, 0]
         *stores, grad, edge, small_chan = channel_back(
             cores, grad, fix, middle, lead, marks, gain[1:2], bias[1:2], mix[3:], gate, carried, xk, xr,
-            acts, (mine[0], other[0]), (mine[1], other[1]), accept, cut, length, packing,
+            acts, (mine[0], other[0]), (mine[1], other[1]), accept, cut, length, packing, table,
         )
-        first, second = scatter_group(core, table, stores, part_rows)
-        chan_large = (
-            join_lookup(first[0], second[0], lookup_rows, grain),
-            jnp.concatenate([first[1], second[1]]),
-            jnp.concatenate([first[2], second[2]]),
+        out_grad = grad
+        if staged:
+            flat = [s.reshape((2, seq * dp // 4, 2 * part_spots[3], columns)) for s in stores]
+            if earlier_att:
+                line = earlier_chan.end_second(grad)
+                earlier_chan.z()
+                away = earlier_att.third(line)
+                edge, out_grad = tie((edge, grad), away)
+                flat = tie(flat, away)
+            elif swapped:
+                edge, out_grad = tie((edge, grad), y_out)
+                flat = tie(flat, y_out)
+            chan_move = Scattering(*flat)
+        if swapped:
+            fix, edge_chan = edges, jnp.zeros((2, width), F32)
+        else:
+            fix, edge_chan = edge_back(edge, middle, length, gain[1])
+        mine, other = held["att", depth]
+        go, gr, gn, gd, ends = out_back(
+            cores, out_grad, fix, k, v, r, sa, sb, marks, rate, bonus, mine, other, length
         )
-        fix, edge_chan = edge_back(edge, middle, length, gain[1])
-        mine, other = att[depth]
-        go, gr, gn, gd, sums = out_back(
-            cores, grad, fix, k, v, r, sa, sb, marks, rate, bonus, mine, other, length
-        )
-        leave = entering(chain, begins * sums, -1)
+        if staged:
+            if earlier_att:
+                near = earlier_att.end_third(go)
+                earlier_att.second()
+                go = tie(go, near, earlier_chan.parts[0])
+            away = chan_move.third(go)
+            gn = tie(gn, away)
+        leave = states if swapped else entering(chain, begins * ends, -1)
         gk, gv, grad, edge, small_time = time_back(
             cores, grad, fix, flow, lead_t, k, v, sa, sb, gn, gd, gr, leave, marks, lines,
             gain[0:1], bias[0:1], mix[:3], rate, bonus, mine, other, length,
         )
-        store = weight_grads([xk_t, xv_t], [xr_t, z], [gk, gv, gr, go])
-        rows = store.shape[3] // 2
-        first, second = scatter_group(core, table, [store], [2 * rows])
-        triple = jnp.stack([first[0][:rows], first[0][rows:], second[0][:rows]])
-        large[depth] = (triple, second[0][rows:]) + chan_large
-        fix, edge_time = edge_back(edge, flow, length, gain[0])
         fading = small_time[5:6] * -rate * jnp.exp(-rate)
         small[depth] = jnp.concatenate(
             [
-                small_time[0:1] + edge_time[0:1],
+                small_time[0:1],
                 small_chan[0:1] + edge_chan[0:1],
-                small_time[1:2] + edge_time[1:2],
+                small_time[1:2],
                 small_chan[1:2] + edge_chan[1:2],
                 small_time[2:5],
                 small_chan[2:4],
@@ -1232,11 +1472,78 @@
                 small_time[6:7],
             ]
         )
-    grad = grad.reshape(runs, length, width).at[:, -1].add(fix)
-    small = summed_everywhere(jnp.stack(small))
+        first_hop = None
+        if staged and depth == 0:
+            first_hop = hop_y(jnp.stack(small))
+        if staged and earlier_chan:
+            gk, gv = tie((gk, gv), earlier_chan.parts)
+        stores_att = weight_grads([xk_t, xv_t], [xr_t, z], [gk, gv, gr, go], table)
+        rows = width // dp
+        if staged:
+            more = []
+            if depth == 0:
+                sums_xy = hop_x(tie(first_hop, stores_att[0]))
+                more.append(sums_xy)
+            near = chan_move.end_third(stores_att[0], *more)
+            if earlier_att:
+                near = tie(near, earlier_att.end_second(near))
+                earlier_att.z()
+            flat = [s.reshape((2, seq * dp // 4, 4 * rows, columns)) for s in stores_att]
+            att_move = Scattering(*tie(flat, near))
+            chan_move.second()
+            grad = tie(grad, near)
+            if depth > 0:
+                earlier_chan, earlier_att = chan_move, att_move
+            sums["chan", depth], sums["att", depth] = chan_move, att_move
+        else:
+            sums["chan", depth] = scatter_plain(stores)
+            sums["att", depth] = scatter_plain(stores_att)
+        if swapped:
+            edge_time = jnp.zeros((2, width), F32)
+        else:
+            fix, edge_time = edge_back(edge, flow, length, gain[0])
+            small[depth] = small[depth].at[0].add(edge_time[0]).at[2].add(edge_time[1])
+    small = jnp.stack(small)
+    grad = grad.reshape(runs, length, width)
+    if not swapped:
+        grad = grad.at[:, -1].add(fix)
+    if staged:
+        last_chan, last_att = sums["chan", 0], sums["att", 0]
+        sums_xy = sums_xy + moved(sums_xy, to_core)
+        away, parts = last_att.away, earlier_att.parts
+        line = last_chan.end_second(away)
+        last_att.third(line, parts)
+        last_chan.z(away, parts)
+        small = summed_z(tie(sums_xy, line))
+        last_att.end_third()
+        last_att.second(last_chan.parts[0])
+        line = last_att.end_second()
+        last_att.z()
+        small = tie(small, last_att.parts)
+        for move in (earlier_chan, earlier_att, last_chan):
+            move.parts = tie(move.parts, line)
+        if swapped:
+            kept_runs, sent_runs = runs_cut(tie(grad, line))
+            came = partner_y(sent_runs.astype(BF))
+            grad = runs_joined(kept_runs, came.astype(F32))
+        for name in list(sums):
+            first, second = sums[name].end_z(core)
+            spots = part_spots if name[0] == "chan" else [0, 2 * rows]
+            sums[name] = (cut_at(first, spots), cut_at(second, spots)) if name[0] == "chan" else ([first], [second])
+    else:
+        small = lax.psum(small, BOTH)
+    large = []
+    for depth in range(layers):
+        first, second = sums["att", depth]
+        triple = jnp.stack([first[0][:rows], first[0][rows:], second[0][:rows]])
+        result = second[0][rows:]
+        first, second = sums["chan", depth]
+        lookup = join_lookup(first[0], second[0], lookup_rows, grain)
+        content = jnp.concatenate([first[1], second[1]])
+        large.append((triple, result, lookup, content, jnp.concatenate([first[2], second[2]])))
     large = [jnp.stack(members) for members in zip(*large)]
     return (
-        y_out.reshape(runs, length, width),
+        y_out if swapped else y_out.reshape(runs, length, width),
         grad,
         small[:, 0:2],
         small[:, 2:4],

time: 1250 us -> 964 us (0.77)
  waiting for transfers between devices: 463 us -> 243 us
  starting transfers between devices: 153 us -> 86.6 us
  Pallas kernels: 516 us -> 478 us
  other arithmetic: 48.6 us -> 77.5 us
    ppermute x57 -> x52, waiting for transfers between devices: 405 us -> 192 us  [moved(): return lax.ppermute(array, BOTH, pairs)]
    pallas_call x6 -> x2, Pallas kernels: 78.1 us -> 29.9 us  [weight_grads(): pl.pallas_call(body, grid=(len(pairs), seq), in_specs=[SCALAR] + [any_spa...]
    ppermute x57 -> x52, starting transfers between devices: 126 us -> 79.9 us  [moved(): return lax.ppermute(array, BOTH, pairs)]
    reduce_scatter x4 -> x8, waiting for transfers between devices: 41 us -> 2.35 us  [__init__(): lax.psum_scatter(array, 'dp', scatter_dimension=0, axis_index_groups=groups)]
    ppermute x13 -> x5, waiting for transfers between devices: 16 us -> 41.7 us  [partner_y(): return lax.ppermute(array, 'seq', [(0, 1), (1, 0)])]
    ppermute x13 -> x5, starting transfers between devices: 26.4 us -> 6.27 us  [partner_y(): return lax.ppermute(array, 'seq', [(0, 1), (1, 0)])]
    convert_element_type x8 -> x9, other arithmetic: 18.4 us -> 30.1 us  [the longest x3 16.2 us: end_third(): self.keep = (keep[:depth].astype(F32) + came[:depth].astype(F32)).astype(BF)]
  transfers between devices with their start and end apart: 74 -> 66, of which waited for: 31 -> 24; matrix products, arithmetic and copies ran while one was open for 6% -> 10% of each run, Pallas kernels for 26% -> 47%
where the time goes in v3:
time: 964 us; the launch traced here: 951 us
  Pallas kernels  478 us (50%)
  waiting for transfers between devices  243 us (25%)
  starting transfers between devices  86.6 us (9%)
  other arithmetic  77.5 us (8%)
  local copies, waits for them, and re-layouts  50.5 us (5%)
  between operations  15.4 us (2%)
    ppermute x52, waiting for transfers between devices, moved(): return lax.ppermute(array, BOTH, pairs)  192 us
    pallas_call x2, Pallas kernels, channel_back(): pl.pallas_call(body, grid=(2 * steps,), in_specs=[SCALAR, held(g.shape),...  133 us
    ppermute x52, starting transfers between devices, moved(): return lax.ppermute(array, BOTH, pairs)  79.9 us
    pallas_call x2, Pallas kernels, time_back(): pl.pallas_call(body, grid=(tiles,), in_specs=[SCALAR, block, fixed(fix.sh...  69.2 us
    pallas_call x4, Pallas kernels, arrange(): pl.pallas_call(body, grid_spec=pltpu.PrefetchScalarGridSpec(num_scalar_pr...  48.7 us
    pallas_call x2, Pallas kernels, channel_two(): pl.pallas_call(body, grid=(cut.steps,), in_specs=[held(s.shape), held(xk....  45.7 us
    ppermute x5, waiting for transfers between devices, partner_y(): return lax.ppermute(array, 'seq', [(0, 1), (1, 0)])  41.7 us
    pallas_call x2, Pallas kernels, out_back(): pl.pallas_call(body, grid=(tokens // tile,), in_specs=[SCALAR, block, fix...  40.4 us
  transfers between devices with their start and end apart: 66, of which 24 were waited for; matrix products, arithmetic and copies ran while one was open for 10% of the time, Pallas kernels for 47%

profile of v3, /device:TPU:1, one launch (start us, length us, event | category | flops | bytes accessed | tf_op | source)
XLA Modules:
  0.0 950.8 jit_solution(10009803458119170655)
XLA Ops:
  20.0 3.9 collective-permute-start.5
  24.4 17.0 %collective-permute-done = bf16[1,512,1024]{2,1,0:T(8,128)(2,1)S(1)} collective-permute-done((bf16[1,512,1024]{2,1,0:T(8,128)(2,1)S(1)}, bf16[1,512,1024]{2,1,0:T(8,128)(2,1)S(1)}, u32[]{:S(2)}, u32[]{:S(2)}) %collective-permute-start) | collective-permute-done | bytes 1048608 | tf_op jit(solution)/shard_map/ppermute | solution.py:1173
  48.9 14.6 %collective-permute-done.7 = bf16[2,288,512]{2,1,0:T(8,128)(2,1)S(1)} collective-permute-done((bf16[2,288,512]{2,1,0:T(8,128)(2,1)S(1)}, bf16[2,288,512]{2,1,0:T(8,128)(2,1)S(1)}, u32[]{:S(2)}, u32[]{:S(2)}) %collective-permute-start.7) | collective-permute-done | bytes 589856 | tf_op jit(solution)/shard_map/ppermute | solution.py:42
  68.7 21.9 %collective-permute-done.8.other_ref = bf16[8,256,512]{2,1,0:T(8,128)(2,1)} collective-permute-done((bf16[8,256,512]{2,1,0:T(8,128)(2,1)S(1)}, bf16[8,256,512]{2,1,0:T(8,128)(2,1)}, u32[]{:S(2)}, u32[]{:S(2)}) %collective-permute-start.8) | collective-permute-done | bytes 2097184 | tf_op jit(solution)/shard_map/ppermute | solution.py:42
  90.6 10.9 %shard_map.229 = bf16[16,256,512]{2,1,0:T(8,128)(2,1)} custom-call(s32[7,16]{1,0:T(8,128)} %dynamic-slice_bitcast_fusion.table_ref, bf16[8,256,512]{2,1,0:T(8,128)(2,1)} %copy-done.12, bf16[8,256,512]{2,1,0:T(8,128)(2,1)} %collective-permute-done.8.other_ref), custom_call_target="tpu_custom_call" | custom-call | flops 1 | bytes 1 | tf_op jit(solution)/shard_map/pallas_call | solution.py:117
  101.5 4.3 collective-permute-done.9
  112.3 24.6 %collective-permute-done.1 = s32[1,512]{1,0:T(1,128)S(1)} collective-permute-done((s32[1,512]{1,0:T(1,128)S(1)}, s32[1,512]{1,0:T(1,128)S(1)}, u32[]{:S(2)}, u32[]{:S(2)}) %collective-permute-start.1) | collective-permute-done | bytes 2080 | tf_op jit(solution)/shard_map/ppermute | solution.py:1173
  142.2 17.6 %shard_map.230 = (bf16[1024,1024]{1,0:T(8,128)(2,1)}, bf16[1024,1024]{1,0:T(8,128)(2,1)}, bf16[1024,1024]{1,0:T(8,128)(2,1)}, f32[1024,1024]{1,0:T(8,128)}, f32[...) custom-call(s32[1]{0:T(128)} %bitcast.core_ref, ...), custom_call_target="tpu_custom_call" | custom-call | flops 1 | bytes 1 | tf_op jit(solution)/shard_map/pallas_call | solution.py:397
  168.1 17.6 %shard_map.231 = (bf16[1024,1024]{1,0:T(8,128)(2,1)}, f32[1024,1024]{1,0:T(8,128)}, f32[1024,1024]{1,0:T(8,128)}, f32[1024,1024]{1,0:T(8,128)}) custom-call(s32[1]{0:T(128)} %bitcast.core_ref, bf16[1024,1024]{1,0:T(8,128)(2,1)} %maximum_bitcast_fusion.s_ref, f32[1024,1024]{1,0:T(8,128)} %get-tuple-element.191.k_ref, f32[1024,1024]{1,0:T(8,128)} %get-tuple-element.192.v_ref, ...), custom_call_target="tpu_custom_call" | custom-call | flops 1 | bytes 1 | tf_op jit(solution)/shard_map/pallas_call | solution.py:464
  187.8 8.0 collective-permute-start.20
  195.8 4.3 collective-permute-start.19
  201.5 8.9 collective-permute-done.20
  210.4 19.0 %collective-permute-done.19 = bf16[2,288,512]{2,1,0:T(8,128)(2,1)} collective-permute-done((bf16[2,288,512]{2,1,0:T(8,128)(2,1)}, bf16[2,288,512]{2,1,0:T(8,128)(2,1)}, u32[]{:S(2)}, u32[]{:S(2)}) %collective-permute-start.19) | collective-permute-done | bytes 589856 | tf_op jit(solution)/shard_map/ppermute | solution.py:42
  229.4 13.3 %shard_map.232 = bf16[16,576,512]{2,1,0:T(8,128)(2,1)} custom-call(s32[7,16]{1,0:T(8,128)} %dynamic-slice_bitcast_fusion.table_ref, bf16[8,576,512]{2,1,0:T(8,128)(2,1)} %copy-done.2, bf16[8,576,512]{2,1,0:T(8,128)(2,1)} %collective-permute-done.16.other_ref), custom_call_target="tpu_custom_call" | custom-call | flops 1 | bytes 1 | tf_op jit(solution)/shard_map/pallas_call | solution.py:117
  242.7 13.9 %collective-permute-done.17 = bf16[4,256,512]{2,1,0:T(8,128)(2,1)S(1)} collective-permute-done((bf16[4,256,512]{2,1,0:T(8,128)(2,1)S(1)}, bf16[4,256,512]{2,1,0:T(8,128)(2,1)S(1)}, u32[]{:S(2)}, u32[]{:S(2)}) %collective-permute-start.17) | collective-permute-done | bytes 1048608 | tf_op jit(solution)/shard_map/ppermute | solution.py:42
  258.9 19.5 %shard_map.233 = (bf16[1024,1024]{1,0:T(8,128)(2,1)}, bf16[1024,1024]{1,0:T(8,128)(2,1)}, f32[4,1,1024]{2,1,0:T(1,128)}, bf16[4,1024,512]{2,1,0:T(8,128)(2,1)}, f32[1024,1024]{1,0:T(8,128)}) custom-call(f32[1024,1024]{1,0:T(8,128)} %get-tuple-element.194.s_ref, f32[1,1024]{1,0:T(1,128)} %broadcast_1_before_ref_fix_ref.2.before_ref.fix_ref, ...), custom_call_target="tpu_custom_call" | custom-call | flops 1 | bytes 1 | tf_op jit(solution)/shard_map/pallas_call | solution.py:556
  282.2 11.0 %shard_map.234 = bf16[16,256,512]{2,1,0:T(8,128)(2,1)} custom-call(s32[7,16]{1,0:T(8,128)} %dynamic-slice_bitcast_fusion.table_ref, bf16[8,256,512]{2,1,0:T(8,128)(2,1)} %copy-done.13, bf16[8,256,512]{2,1,0:T(8,128)(2,1)} %collective-permute-done.21.other_ref), custom_call_target="tpu_custom_call" | custom-call | flops 1 | bytes 1 | tf_op jit(solution)/shard_map/pallas_call | solution.py:117
  296.4 23.2 %shard_map.235 = (bf16[4,1024,512]{2,1,0:T(8,128)(2,1)}, bf16[1024,1024]{1,0:T(8,128)(2,1)}, bf16[1024,1024]{1,0:T(8,128)(2,1)}, f32[1024,1024]{1,0:T(8,128)}) custom-call(f32[1024,1024]{1,0:T(8,128)} %get-tuple-element.194.s_ref, bf16[1024,1024]{1,0:T(8,128)(2,1)} %get-tuple-element.206.xk_ref, bf16[1024,1024]{1,0:T(8,128)(2,1)} %get-tuple-element.207.xr_ref, ...), custom_call_target="tpu_custom_call" | custom-call | flops 1 | bytes 1 | tf_op jit(solution)/shard_map/pallas_call | solution.py:605
  329.2 6.2 collective-permute-done.24
  337.5 17.7 %shard_map.236 = (bf16[1024,1024]{1,0:T(8,128)(2,1)}, bf16[1024,1024]{1,0:T(8,128)(2,1)}, bf16[1024,1024]{1,0:T(8,128)(2,1)}, f32[1024,1024]{1,0:T(8,128)}, f32[...) custom-call(s32[1]{0:T(128)} %bitcast.core_ref, ...), custom_call_target="tpu_custom_call" | custom-call | flops 1 | bytes 1 | tf_op jit(solution)/shard_map/pallas_call | solution.py:397
  355.2 18.3 %shard_map.237 = (bf16[1024,1024]{1,0:T(8,128)(2,1)}, f32[1024,1024]{1,0:T(8,128)}, f32[1024,1024]{1,0:T(8,128)}, f32[1024,1024]{1,0:T(8,128)}) custom-call(s32[1]{0:T(128)} %bitcast.core_ref, f32[1024,1024]{1,0:T(8,128)} %get-tuple-element.219.s_ref, f32[1024,1024]{1,0:T(8,128)} %get-tuple-element.220.k_ref, f32[1024,1024]{1,0:T(8,128)} %get-tuple-element.221.v_ref, ...), custom_call_target="tpu_custom_call" | custom-call | flops 1 | bytes 1 | tf_op jit(solution)/shard_map/pallas_call | solution.py:464
  373.5 4.6 collective-permute-done.25.other_ref
  380.4 13.5 %shard_map.238 = bf16[16,576,512]{2,1,0:T(8,128)(2,1)} custom-call(s32[7,16]{1,0:T(8,128)} %dynamic-slice_bitcast_fusion.table_ref, bf16[8,576,512]{2,1,0:T(8,128)(2,1)} %constant_dynamic-update-slice_fusion.38.own_ref, bf16[8,576,512]{2,1,0:T(8,128)(2,1)} %copy-done.11), custom_call_target="tpu_custom_call" | custom-call | flops 1 | bytes 1 | tf_op jit(solution)/shard_map/pallas_call | solution.py:117
  393.9 5.1 collective-permute-start.26
  399.7 19.9 %shard_map.239 = (bf16[1024,1024]{1,0:T(8,128)(2,1)}, bf16[1024,1024]{1,0:T(8,128)(2,1)}, f32[4,1,1024]{2,1,0:T(1,128)}, bf16[4,1024,512]{2,1,0:T(8,128)(2,1)}, f32[1024,1024]{1,0:T(8,128)}) custom-call(f32[1024,1024]{1,0:T(8,128)} %get-tuple-element.223.s_ref, f32[1,1024]{1,0:T(1,128)} %broadcast_1_before_ref_fix_ref.2.before_ref.fix_ref, ...), custom_call_target="tpu_custom_call" | custom-call | flops 1 | bytes 1 | tf_op jit(solution)/shard_map/pallas_call | solution.py:556
  422.9 22.5 %shard_map.240 = (bf16[4,1024,512]{2,1,0:T(8,128)(2,1)}, bf16[1024,1024]{1,0:T(8,128)(2,1)}, bf16[1024,1024]{1,0:T(8,128)(2,1)}, bf16[1024,1024]{1,0:T(8,128)(2,1)}) custom-call(f32[1024,1024]{1,0:T(8,128)} %get-tuple-element.223.s_ref, bf16[1024,1024]{1,0:T(8,128)(2,1)} %get-tuple-element.228.xk_ref, bf16[1024,1024]{1,0:T(8,128)(2,1)} %get-tuple-element.229.xr_ref, ...), custom_call_target="tpu_custom_call" | custom-call | flops 1 | bytes 1 | tf_op jit(solution)/shard_map/pallas_call | solution.py:605
  451.5 65.5 %shard_map.241 = (bf16[2,8,2,288,512]{4,3,2,1,0:T(8,128)(2,1)}, bf16[2,8,2,288,512]{4,3,2,1,0:T(8,128)(2,1)}, f32[1024,1024]{1,0:T(8,128)}, f32[1,1024]{1,0:T(1,128)}, f32[4,1024]{1,0:T(4,128)}) custom-call(s32[1]{0:T(128)} %bitcast.core_ref, bf16[1024,1024]{1,0:T(8,128)(2,1)} %maximum_bitcast_fusion.1.g_ref, ...), custom_call_target="tpu_custom_call" | custom-call | flops 1 | bytes 1 | tf_op jit(solution)/shard_map/pallas_call | solution.py:815
  518.7 20.5 %shard_map.242 = (bf16[1024,1024]{1,0:T(8,128)(2,1)}, bf16[1024,1024]{1,0:T(8,128)(2,1)}, f32[1024,1024]{1,0:T(8,128)}, f32[1024,1024]{1,0:T(8,128)}, f32[1,2,1024]{2,1,0:T(2,128)}) custom-call(s32[1]{0:T(128)} %bitcast.core_ref, f32[1024,1024]{1,0:T(8,128)} %get-tuple-element.242.g_ref, f32[1,1024]{1,0:T(1,128)} %broadcast_1_before_ref_fix_ref.2.before_ref.fix_ref, ...), custom_call_target="tpu_custom_call" | custom-call | flops 1 | bytes 1 | tf_op jit(solution)/shard_map/pallas_call | solution.py:892
  539.9 34.0 %shard_map.243 = (bf16[1024,1024]{1,0:T(8,128)(2,1)}, bf16[1024,1024]{1,0:T(8,128)(2,1)}, f32[1024,1024]{1,0:T(8,128)}, f32[1,1024]{1,0:T(1,128)}, f32[7,1024]{1,0:T(8,128)}) custom-call(s32[1]{0:T(128)} %bitcast.core_ref, f32[1024,1024]{1,0:T(8,128)} %get-tuple-element.242.g_ref, f32[1,1024]{1,0:T(1,128)} %broadcast_1_before_ref_fix_ref.2.before_ref.fix_ref, ...), custom_call_target="tpu_custom_call" | custom-call | flops 1 | bytes 1 | tf_op jit(solution)/shard_map/pallas_call | solution.py:985
  573.9 15.0 %shard_map.244 = (bf16[2,8,2,128,512]{4,3,2,1,0:T(8,128)(2,1)}, bf16[2,8,2,128,512]{4,3,2,1,0:T(8,128)(2,1)}) custom-call(s32[7,16]{1,0:T(8,128)} %dynamic-slice_bitcast_fusion.table_ref, bf16[1024,1024]{1,0:T(8,128)(2,1)} %get-tuple-element.255.refs_0_, bf16[1024,1024]{1,0:T(8,128)(2,1)} %get-tuple-element.256.refs_1_, ...), custom_call_target="tpu_custom_call" | custom-call | flops 1 | bytes 1 | tf_op jit(solution)/shard_map/pallas_call | solution.py:1086
  588.8 4.2 collective-permute-done.29
  593.0 5.5 add_convert_fusion.4
  599.1 67.9 %shard_map.245 = (bf16[2,8,2,288,512]{4,3,2,1,0:T(8,128)(2,1)}, bf16[2,8,2,288,512]{4,3,2,1,0:T(8,128)(2,1)}, f32[1024,1024]{1,0:T(8,128)}, f32[1,1024]{1,0:T(1,128)}, f32[4,1024]{1,0:T(4,128)}) custom-call(s32[1]{0:T(128)} %bitcast.core_ref, f32[1024,1024]{1,0:T(8,128)} %get-tuple-element.264.g_ref, ...), custom_call_target="tpu_custom_call" | custom-call | flops 1 | bytes 1 | tf_op jit(solution)/shard_map/pallas_call | solution.py:815
  672.0 19.9 %shard_map.246 = (bf16[1024,1024]{1,0:T(8,128)(2,1)}, bf16[1024,1024]{1,0:T(8,128)(2,1)}, f32[1024,1024]{1,0:T(8,128)}, f32[1024,1024]{1,0:T(8,128)}, f32[1,2,1024]{2,1,0:T(2,128)}) custom-call(s32[1]{0:T(128)} %bitcast.core_ref, f32[1024,1024]{1,0:T(8,128)} %get-tuple-element.279.g_ref, f32[1,1024]{1,0:T(1,128)} %broadcast_1_before_ref_fix_ref.2.before_ref.fix_ref, ...), custom_call_target="tpu_custom_call" | custom-call | flops 1 | bytes 1 | tf_op jit(solution)/shard_map/pallas_call | solution.py:892
  695.3 5.2 add_convert_fusion.10
  709.4 35.2 %shard_map.247 = (bf16[1024,1024]{1,0:T(8,128)(2,1)}, bf16[1024,1024]{1,0:T(8,128)(2,1)}, f32[1024,1024]{1,0:T(8,128)}, f32[1,1024]{1,0:T(1,128)}, f32[7,1024]{1,0:T(8,128)}) custom-call(s32[1]{0:T(128)} %bitcast.core_ref, f32[1024,1024]{1,0:T(8,128)} %get-tuple-element.279.g_ref, f32[1,1024]{1,0:T(1,128)} %broadcast_1_before_ref_fix_ref.2.before_ref.fix_ref, ...), custom_call_target="tpu_custom_call" | custom-call | flops 1 | bytes 1 | tf_op jit(solution)/shard_map/pallas_call | solution.py:985
  747.3 15.0 %shard_map.248 = (bf16[2,8,2,128,512]{4,3,2,1,0:T(8,128)(2,1)}, bf16[2,8,2,128,512]{4,3,2,1,0:T(8,128)(2,1)}) custom-call(s32[7,16]{1,0:T(8,128)} %dynamic-slice_bitcast_fusion.table_ref, bf16[1024,1024]{1,0:T(8,128)(2,1)} %get-tuple-element.297.refs_0_, bf16[1024,1024]{1,0:T(8,128)(2,1)} %get-tuple-element.300.refs_1_, ...), custom_call_target="tpu_custom_call" | custom-call | flops 1 | bytes 1 | tf_op jit(solution)/shard_map/pallas_call | solution.py:1086
  762.9 6.3 collective-permute-done.37
  769.9 5.5 add_convert_fusion.1
  784.9 21.4 %collective-permute-done.39 = bf16[4,576,512]{2,1,0:T(8,128)(2,1)} collective-permute-done((bf16[4,576,512]{2,1,0:T(8,128)(2,1)}, bf16[4,576,512]{2,1,0:T(8,128)(2,1)}, u32[]{:S(2)}, u32[]{:S(2)}) %collective-permute-start.39) | collective-permute-done | bytes 2359328 | tf_op jit(solution)/shard_map/ppermute | solution.py:42
  806.4 3.7 add_convert_fusion
  816.3 21.0 %collective-permute-done.43 = bf16[8,256,512]{2,1,0:T(8,128)(2,1)} collective-permute-done((bf16[8,256,512]{2,1,0:T(8,128)(2,1)}, bf16[8,256,512]{2,1,0:T(8,128)(2,1)}, u32[]{:S(2)}, u32[]{:S(2)}) %collective-permute-start.43) | collective-permute-done | bytes 2097184 | tf_op jit(solution)/shard_map/ppermute | solution.py:42
  837.3 3.8 add_convert_fusion.7
  845.6 11.5 %collective-permute-start.47 = (f32[2,11,1024]{2,1,0:T(8,128)S(1)}, f32[2,11,1024]{2,1,0:T(8,128)S(1)}, u32[]{:S(2)}, u32[]{:S(2)}) collective-permute-start(f32[2,11,1024]{2,1,0:T(8,128)S(1)} %copy-done.32), channel_id=1, source_target_pairs={{0,2},{1,3},{2,0},{3,1},{4,6},{5,7},{6,4},{7,5},{8,10},{9,11},{10,... | collective-permute-start | bytes 270344 | tf_op jit(solution)/shard_map/ppermute | solution.py:42
  860.3 26.7 %collective-permute-done.53 = bf16[576,512]{1,0:T(8,128)(2,1)} collective-permute-done((bf16[576,512]{1,0:T(8,128)(2,1)}, bf16[576,512]{1,0:T(8,128)(2,1)}, u32[]{:S(2)}, u32[]{:S(2)}) %collective-permute-start.53) | collective-permute-done | bytes 589856 | tf_op jit(solution)/shard_map/ppermute | solution.py:42
  901.3 5.0 collective-permute-done.50
  906.8 6.1 all-reduce.2.cloned.1.call-done
  912.9 4.0 collective-permute-done.49
  (407 shorter events, 170.9 us)
Async XLA Ops:
  7.2 532.1 %reduce-scatter.9.cloned.1.call-start = ((), (), s32[]{:S(2)}) async-start(), calls=%async_computation.8 | async-start | bytes 14155776 | tf_op jit(solution)/shard_map/reduce_scatter | solution.py:175
  15.1 26.3 %collective-permute-start = (bf16[1,512,1024]{2,1,0:T(8,128)(2,1)S(1)}, bf16[1,512,1024]{2,1,0:T(8,128)(2,1)S(1)}, u32[]{:S(2)}, u32[]{:S(2)}) collective-permute-start(bf16[1,512,1024]{2,1,0:T(8,128)(2,1)S(1)} %broadcast_select_fusion.14), channel_id=1, source_target_pairs={{0,1},{1,0},{2,3},{3,2},{4,5},{5,4},{6,7},{7,6},{8,9},{9,8},{10,11... | collective-permute-start | bytes 3145736 | tf_op jit(solution)/shard_map/ppermute | solution.py:1173
  20.0 23.1 %collective-permute-start.5 = (bf16[2,128,512]{2,1,0:T(8,128)(2,1)S(1)}, bf16[2,128,512]{2,1,0:T(8,128)(2,1)S(1)}, u32[]{:S(2)}, u32[]{:S(2)}) collective-permute-start(bf16[2,128,512]{2,1,0:T(8,128)(2,1)S(1)} %get-tuple-element.423), channel_id=1, source_target_pairs={{0,24},{1,25},{2,26},{3,27},{4,28},{5,29},{6,30},{7,31},{8,0},{9,1... | collective-permute-start | bytes 786440 | tf_op jit(solution)/shard_map/ppermute | solution.py:42
  23.9 22.1 %collective-permute-start.4 = (bf16[2,128,512]{2,1,0:T(8,128)(2,1)S(1)}, bf16[2,128,512]{2,1,0:T(8,128)(2,1)S(1)}, u32[]{:S(2)}, u32[]{:S(2)}) collective-permute-start(bf16[2,128,512]{2,1,0:T(8,128)(2,1)S(1)} %get-tuple-element.423), channel_id=1, source_target_pairs={{0,16},{1,17},{2,18},{3,19},{4,20},{5,21},{6,22},{7,23},{8,24},{9,... | collective-permute-start | bytes 786440 | tf_op jit(solution)/shard_map/ppermute | solution.py:42
  23.9 22.1 %collective-permute-start.3 = (bf16[2,128,512]{2,1,0:T(8,128)(2,1)S(1)}, bf16[2,128,512]{2,1,0:T(8,128)(2,1)S(1)}, u32[]{:S(2)}, u32[]{:S(2)}) collective-permute-start(bf16[2,128,512]{2,1,0:T(8,128)(2,1)S(1)} %get-tuple-element.423), channel_id=1, source_target_pairs={{0,8},{1,9},{2,10},{3,11},{4,12},{5,13},{6,14},{7,15},{8,16},{9,17... | collective-permute-start | bytes 786440 | tf_op jit(solution)/shard_map/ppermute | solution.py:42
  64.5 26.1 %collective-permute-start.8 = (bf16[8,256,512]{2,1,0:T(8,128)(2,1)S(1)}, bf16[8,256,512]{2,1,0:T(8,128)(2,1)}, u32[]{:S(2)}, u32[]{:S(2)}) collective-permute-start(bf16[8,256,512]{2,1,0:T(8,128)(2,1)S(1)} %constant_dynamic-update-slice_fusion.32.own_ref), channel_id=1, source_target_pairs={{0,1},{1,0},{2,6},{3,7},{4,5},{5,4},{6,2},{7,3},{8,9},{9,8},{10,14... | collective-permute-start | bytes 6291464 | tf_op jit(solution)/shard_map/ppermute | solution.py:42
  66.8 34.8 %collective-permute-start.10 = (bf16[2,288,512]{2,1,0:T(8,128)(2,1)S(1)}, bf16[2,288,512]{2,1,0:T(8,128)(2,1)}, u32[]{:S(2)}, u32[]{:S(2)}) collective-permute-start(bf16[2,288,512]{2,1,0:T(8,128)(2,1)S(1)} %get-tuple-element.181), channel_id=1, source_target_pairs={{0,24},{1,25},{2,26},{3,27},{4,28},{5,29},{6,30},{7,31},{8,0},{9,1... | collective-permute-start | bytes 1769480 | tf_op jit(solution)/shard_map/ppermute | solution.py:42
  67.5 38.4 %collective-permute-start.9 = (bf16[2,288,512]{2,1,0:T(8,128)(2,1)S(1)}, bf16[2,288,512]{2,1,0:T(8,128)(2,1)}, u32[]{:S(2)}, u32[]{:S(2)}) collective-permute-start(bf16[2,288,512]{2,1,0:T(8,128)(2,1)S(1)} %get-tuple-element.181), channel_id=1, source_target_pairs={{0,16},{1,17},{2,18},{3,19},{4,20},{5,21},{6,22},{7,23},{8,24},{9,... | collective-permute-start | bytes 1769480 | tf_op jit(solution)/shard_map/ppermute | solution.py:42
  105.9 35.8 %collective-permute-start.11 = (bf16[16,256,512]{2,1,0:T(8,128)(2,1)}, bf16[16,256,512]{2,1,0:T(8,128)(2,1)}, u32[]{:S(2)}, u32[]{:S(2)}) collective-permute-start(bf16[16,256,512]{2,1,0:T(8,128)(2,1)} %shard_map.229), channel_id=1, source_target_pairs={{0,2},{1,3},{2,0},{3,1},{4,6},{5,7},{6,4},{7,5},{8,10},{9,11},{10,... | collective-permute-start | bytes 12582920 | tf_op jit(solution)/shard_map/ppermute | solution.py:42
  108.7 51.1 %collective-permute-start.12 = (bf16[4,576,512]{2,1,0:T(8,128)(2,1)S(1)}, bf16[4,576,512]{2,1,0:T(8,128)(2,1)}, u32[]{:S(2)}, u32[]{:S(2)}) collective-permute-start(bf16[4,576,512]{2,1,0:T(8,128)(2,1)S(1)} %pad_maximum_fusion.1), channel_id=1, source_target_pairs={{0,4},{1,5},{2,3},{3,2},{4,0},{5,1},{6,7},{7,6},{8,12},{9,13},{10,... | collective-permute-start | bytes 7077896 | tf_op jit(solution)/shard_map/ppermute | solution.py:42
  108.8 28.1 %collective-permute-start.1 = (s32[1,512]{1,0:T(1,128)S(1)}, s32[1,512]{1,0:T(1,128)S(1)}, u32[]{:S(2)}, u32[]{:S(2)}) collective-permute-start(s32[1,512]{1,0:T(1,128)S(1)} %broadcast_select_fusion.28), channel_id=1, source_target_pairs={{0,1},{1,0},{2,3},{3,2},{4,5},{5,4},{6,7},{7,6},{8,9},{9,8},{10,11... | collective-permute-start | bytes 6152 | tf_op jit(solution)/shard_map/ppermute | solution.py:1173
  163.5 65.9 %collective-permute-start.16 = (bf16[8,576,512]{2,1,0:T(8,128)(2,1)S(1)}, bf16[8,576,512]{2,1,0:T(8,128)(2,1)}, u32[]{:S(2)}, u32[]{:S(2)}) collective-permute-start(bf16[8,576,512]{2,1,0:T(8,128)(2,1)S(1)} %constant_dynamic-update-slice_fusion.34.own_ref), channel_id=1, source_target_pairs={{0,1},{1,0},{2,6},{3,7},{4,5},{5,4},{6,2},{7,3},{8,9},{9,8},{10,14... | collective-permute-start | bytes 14155784 | tf_op jit(solution)/shard_map/ppermute | solution.py:42
  187.8 22.6 %collective-permute-start.20 = (bf16[2,288,512]{2,1,0:T(8,128)(2,1)}, bf16[2,288,512]{2,1,0:T(8,128)(2,1)}, u32[]{:S(2)}, u32[]{:S(2)}) collective-permute-start(bf16[2,288,512]{2,1,0:T(8,128)(2,1)} %get-tuple-element.203), channel_id=1, source_target_pairs={{0,24},{1,25},{2,26},{3,27},{4,28},{5,29},{6,30},{7,31},{8,0},{9,1... | collective-permute-start | bytes 1769480 | tf_op jit(solution)/shard_map/ppermute | solution.py:42
  195.8 33.6 %collective-permute-start.19 = (bf16[2,288,512]{2,1,0:T(8,128)(2,1)}, bf16[2,288,512]{2,1,0:T(8,128)(2,1)}, u32[]{:S(2)}, u32[]{:S(2)}) collective-permute-start(bf16[2,288,512]{2,1,0:T(8,128)(2,1)} %get-tuple-element.203), channel_id=1, source_target_pairs={{0,16},{1,17},{2,18},{3,19},{4,20},{5,21},{6,22},{7,23},{8,24},{9,... | collective-permute-start | bytes 1769480 | tf_op jit(solution)/shard_map/ppermute | solution.py:42
  200.1 29.3 %collective-permute-start.18 = (bf16[2,288,512]{2,1,0:T(8,128)(2,1)}, bf16[2,288,512]{2,1,0:T(8,128)(2,1)}, u32[]{:S(2)}, u32[]{:S(2)}) collective-permute-start(bf16[2,288,512]{2,1,0:T(8,128)(2,1)} %get-tuple-element.203), channel_id=1, source_target_pairs={{0,8},{1,9},{2,10},{3,11},{4,12},{5,13},{6,14},{7,15},{8,16},{9,17... | collective-permute-start | bytes 1769480 | tf_op jit(solution)/shard_map/ppermute | solution.py:42
  242.7 50.4 %collective-permute-start.22 = (bf16[16,576,512]{2,1,0:T(8,128)(2,1)}, bf16[16,576,512]{2,1,0:T(8,128)(2,1)}, u32[]{:S(2)}, u32[]{:S(2)}) collective-permute-start(bf16[16,576,512]{2,1,0:T(8,128)(2,1)} %shard_map.232), channel_id=1, source_target_pairs={{0,2},{1,3},{2,0},{3,1},{4,6},{5,7},{6,4},{7,5},{8,10},{9,11},{10,... | collective-permute-start | bytes 28311560 | tf_op jit(solution)/shard_map/ppermute | solution.py:42
  256.8 25.4 %collective-permute-start.21 = (bf16[8,256,512]{2,1,0:T(8,128)(2,1)S(1)}, bf16[8,256,512]{2,1,0:T(8,128)(2,1)}, u32[]{:S(2)}, u32[]{:S(2)}) collective-permute-start(bf16[8,256,512]{2,1,0:T(8,128)(2,1)S(1)} %constant_dynamic-update-slice_fusion.36.own_ref), channel_id=1, source_target_pairs={{0,1},{1,0},{2,6},{3,7},{4,5},{5,4},{6,2},{7,3},{8,9},{9,8},{10,14... | collective-permute-start | bytes 6291464 | tf_op jit(solution)/shard_map/ppermute | solution.py:42
  282.2 37.4 %collective-permute-start.23 = (bf16[4,576,512]{2,1,0:T(8,128)(2,1)S(1)}, bf16[4,576,512]{2,1,0:T(8,128)(2,1)}, u32[]{:S(2)}, u32[]{:S(2)}) collective-permute-start(bf16[4,576,512]{2,1,0:T(8,128)(2,1)S(1)} %pad_maximum_fusion.2), channel_id=1, source_target_pairs={{0,4},{1,5},{2,3},{3,2},{4,0},{5,1},{6,7},{7,6},{8,12},{9,13},{10,... | collective-permute-start | bytes 7077896 | tf_op jit(solution)/shard_map/ppermute | solution.py:42
  324.7 53.5 %collective-permute-start.25 = (bf16[8,576,512]{2,1,0:T(8,128)(2,1)}, bf16[8,576,512]{2,1,0:T(8,128)(2,1)S(1)}, u32[]{:S(2)}, u32[]{:S(2)}) collective-permute-start(bf16[8,576,512]{2,1,0:T(8,128)(2,1)} %constant_dynamic-update-slice_fusion.38.own_ref), channel_id=1, source_target_pairs={{0,1},{1,0},{2,6},{3,7},{4,5},{5,4},{6,2},{7,3},{8,9},{9,8},{10,14... | collective-permute-start | bytes 14155784 | tf_op jit(solution)/shard_map/ppermute | solution.py:42
  393.9 25.8 %collective-permute-start.26 = (bf16[16,576,512]{2,1,0:T(8,128)(2,1)}, bf16[16,576,512]{2,1,0:T(8,128)(2,1)}, u32[]{:S(2)}, u32[]{:S(2)}) collective-permute-start(bf16[16,576,512]{2,1,0:T(8,128)(2,1)} %shard_map.238), channel_id=1, source_target_pairs={{0,2},{1,3},{2,0},{3,1},{4,6},{5,7},{6,4},{7,5},{8,10},{9,11},{10,... | collective-permute-start | bytes 28311560 | tf_op jit(solution)/shard_map/ppermute | solution.py:42
  399.7 48.9 %collective-permute-start.28 = (bf16[1,512,1024]{2,1,0:T(8,128)(2,1)S(1)}, bf16[1,512,1024]{2,1,0:T(8,128)(2,1)}, u32[]{:S(2)}, u32[]{:S(2)}) collective-permute-start(bf16[1,512,1024]{2,1,0:T(8,128)(2,1)S(1)} %broadcast_select_fusion.6), channel_id=1, source_target_pairs={{0,1},{1,0},{2,3},{3,2},{4,5},{5,4},{6,7},{7,6},{8,9},{9,8},{10,11... | collective-permute-start | bytes 3145736 | tf_op jit(solution)/shard_map/ppermute | solution.py:1173
  447.0 69.9 %collective-permute-start.27 = (bf16[1,512,1024]{2,1,0:T(8,128)(2,1)S(1)}, bf16[1,512,1024]{2,1,0:T(8,128)(2,1)S(1)}, u32[]{:S(2)}, u32[]{:S(2)}) collective-permute-start(bf16[1,512,1024]{2,1,0:T(8,128)(2,1)S(1)} %broadcast_select_fusion.10), channel_id=1, source_target_pairs={{0,1},{1,0},{2,3},{3,2},{4,5},{5,4},{6,7},{7,6},{8,9},{9,8},{10,11... | collective-permute-start | bytes 3145736 | tf_op jit(solution)/shard_map/ppermute | solution.py:1173
  518.7 74.3 %reduce-scatter.11.cloned.1.call-start = ((), (), s32[]{:S(2)}) async-start(), calls=%async_computation.9 | async-start | bytes 14155776 | tf_op jit(solution)/shard_map/reduce_scatter | solution.py:175
  539.3 129.8 %reduce-scatter.13.cloned.1.call-start = ((), (), s32[]{:S(2)}) async-start(), calls=%async_computation.10 | async-start | bytes 6291456 | tf_op jit(solution)/shard_map/reduce_scatter | solution.py:175
  539.4 53.6 %collective-permute-start.29 = (bf16[8,576,512]{2,1,0:T(8,128)(2,1)}, bf16[8,576,512]{2,1,0:T(8,128)(2,1)}, u32[]{:S(2)}, u32[]{:S(2)}) collective-permute-start(bf16[8,576,512]{2,1,0:T(8,128)(2,1)} %bitcast.350), channel_id=1, source_target_pairs={{0,1},{1,0},{2,6},{3,7},{4,5},{5,4},{6,2},{7,3},{8,9},{9,8},{10,14... | collective-permute-start | bytes 14155784 | tf_op jit(solution)/shard_map/ppermute | solution.py:42
  598.5 96.8 %reduce-scatter.17.cloned.1.call-start = ((), (), s32[]{:S(2)}) async-start(), calls=%async_computation.12 | async-start | bytes 6291456 | tf_op jit(solution)/shard_map/reduce_scatter | solution.py:175
  598.5 68.4 %collective-permute-start.30 = (bf16[4,576,512]{2,1,0:T(8,128)(2,1)}, bf16[4,576,512]{2,1,0:T(8,128)(2,1)S(1)}, u32[]{:S(2)}, u32[]{:S(2)}) collective-permute-start(bf16[4,576,512]{2,1,0:T(8,128)(2,1)} %get-tuple-element.397), channel_id=1, source_target_pairs={{0,4},{1,5},{2,3},{3,2},{4,0},{5,1},{6,7},{7,6},{8,12},{9,13},{10,... | collective-permute-start | bytes 7077896 | tf_op jit(solution)/shard_map/ppermute | solution.py:42
  669.1 33.8 %reduce-scatter.15.cloned.1.call-start = ((), (), s32[]{:S(2)}) async-start(), calls=%async_computation.11 | async-start | bytes 14155776 | tf_op jit(solution)/shard_map/reduce_scatter | solution.py:175
  669.7 100.2 %reduce-scatter.19.cloned.1.call-start = ((), (), s32[]{:S(2)}) async-start(), calls=%async_computation.13 | async-start | bytes 14155776 | tf_op jit(solution)/shard_map/reduce_scatter | solution.py:175
  669.7 25.6 %collective-permute-start.31 = (bf16[8,256,512]{2,1,0:T(8,128)(2,1)}, bf16[8,256,512]{2,1,0:T(8,128)(2,1)}, u32[]{:S(2)}, u32[]{:S(2)}) collective-permute-start(bf16[8,256,512]{2,1,0:T(8,128)(2,1)} %bitcast.351), channel_id=1, source_target_pairs={{0,1},{1,0},{2,6},{3,7},{4,5},{5,4},{6,2},{7,3},{8,9},{9,8},{10,14... | collective-permute-start | bytes 6291464 | tf_op jit(solution)/shard_map/ppermute | solution.py:42
  672.0 28.5 %collective-permute-start.32 = (bf16[576,512]{1,0:T(8,128)(2,1)S(1)}, bf16[576,512]{1,0:T(8,128)(2,1)S(1)}, u32[]{:S(2)}, u32[]{:S(2)}) collective-permute-start(bf16[576,512]{1,0:T(8,128)(2,1)S(1)} %get-tuple-element.415), channel_id=1, source_target_pairs={{0,24},{1,25},{2,26},{3,27},{4,28},{5,29},{6,30},{7,31},{8,0},{9,1... | collective-permute-start | bytes 1769480 | tf_op jit(solution)/shard_map/ppermute | solution.py:42
  702.9 103.5 %reduce-scatter.21.cloned.1.call-start = ((), (), s32[]{:S(2)}) async-start(), calls=%async_computation.14 | async-start | bytes 6291456 | tf_op jit(solution)/shard_map/reduce_scatter | solution.py:175
  702.9 67.0 %collective-permute-start.33 = (bf16[8,576,512]{2,1,0:T(8,128)(2,1)}, bf16[8,576,512]{2,1,0:T(8,128)(2,1)}, u32[]{:S(2)}, u32[]{:S(2)}) collective-permute-start(bf16[8,576,512]{2,1,0:T(8,128)(2,1)} %bitcast.349), channel_id=1, source_target_pairs={{0,1},{1,0},{2,6},{3,7},{4,5},{5,4},{6,2},{7,3},{8,9},{9,8},{10,14... | collective-permute-start | bytes 14155784 | tf_op jit(solution)/shard_map/ppermute | solution.py:42
  704.7 41.9 %collective-permute-start.35 = (bf16[576,512]{1,0:T(8,128)(2,1)}, bf16[576,512]{1,0:T(8,128)(2,1)S(1)}, u32[]{:S(2)}, u32[]{:S(2)}) collective-permute-start(bf16[576,512]{1,0:T(8,128)(2,1)} %get-tuple-element.413), channel_id=1, source_target_pairs={{0,8},{1,9},{2,10},{3,11},{4,12},{5,13},{6,14},{7,15},{8,16},{9,17... | collective-permute-start | bytes 1769480 | tf_op jit(solution)/shard_map/ppermute | solution.py:42
  706.0 41.3 %collective-permute-start.34 = (bf16[576,512]{1,0:T(8,128)(2,1)}, bf16[576,512]{1,0:T(8,128)(2,1)S(1)}, u32[]{:S(2)}, u32[]{:S(2)}) collective-permute-start(bf16[576,512]{1,0:T(8,128)(2,1)} %get-tuple-element.414), channel_id=1, source_target_pairs={{0,16},{1,17},{2,18},{3,19},{4,20},{5,21},{6,22},{7,23},{8,24},{9,... | collective-permute-start | bytes 1769480 | tf_op jit(solution)/shard_map/ppermute | solution.py:42
  708.2 67.3 %collective-permute-start.38 = (bf16[4,256,512]{2,1,0:T(8,128)(2,1)}, bf16[4,256,512]{2,1,0:T(8,128)(2,1)S(1)}, u32[]{:S(2)}, u32[]{:S(2)}) collective-permute-start(bf16[4,256,512]{2,1,0:T(8,128)(2,1)} %get-tuple-element.403), channel_id=1, source_target_pairs={{0,4},{1,5},{2,3},{3,2},{4,0},{5,1},{6,7},{7,6},{8,12},{9,13},{10,... | collective-permute-start | bytes 3145736 | tf_op jit(solution)/shard_map/ppermute | solution.py:42
  778.0 59.3 %reduce-scatter.23.cloned.1.call-start = ((), (), s32[]{:S(2)}) async-start(), calls=%async_computation.15 | async-start | bytes 6291456 | tf_op jit(solution)/shard_map/reduce_scatter | solution.py:175
  778.0 28.4 %collective-permute-start.39 = (bf16[4,576,512]{2,1,0:T(8,128)(2,1)}, bf16[4,576,512]{2,1,0:T(8,128)(2,1)}, u32[]{:S(2)}, u32[]{:S(2)}) collective-permute-start(bf16[4,576,512]{2,1,0:T(8,128)(2,1)} %get-tuple-element.315), channel_id=1, source_target_pairs={{0,4},{1,5},{2,3},{3,2},{4,0},{5,1},{6,7},{7,6},{8,12},{9,13},{10,... | collective-permute-start | bytes 7077896 | tf_op jit(solution)/shard_map/ppermute | solution.py:42
  780.4 29.7 %collective-permute-start.42 = (bf16[256,512]{1,0:T(8,128)(2,1)}, bf16[256,512]{1,0:T(8,128)(2,1)}, u32[]{:S(2)}, u32[]{:S(2)}) collective-permute-start(bf16[256,512]{1,0:T(8,128)(2,1)} %get-tuple-element.427), channel_id=1, source_target_pairs={{0,8},{1,9},{2,10},{3,11},{4,12},{5,13},{6,14},{7,15},{8,16},{9,17... | collective-permute-start | bytes 786440 | tf_op jit(solution)/shard_map/ppermute | solution.py:42
  781.6 28.5 %collective-permute-start.41 = (bf16[256,512]{1,0:T(8,128)(2,1)}, bf16[256,512]{1,0:T(8,128)(2,1)}, u32[]{:S(2)}, u32[]{:S(2)}) collective-permute-start(bf16[256,512]{1,0:T(8,128)(2,1)} %get-tuple-element.428), channel_id=1, source_target_pairs={{0,16},{1,17},{2,18},{3,19},{4,20},{5,21},{6,22},{7,23},{8,24},{9,... | collective-permute-start | bytes 786440 | tf_op jit(solution)/shard_map/ppermute | solution.py:42
  783.8 26.3 %collective-permute-start.40 = (bf16[256,512]{1,0:T(8,128)(2,1)}, bf16[256,512]{1,0:T(8,128)(2,1)}, u32[]{:S(2)}, u32[]{:S(2)}) collective-permute-start(bf16[256,512]{1,0:T(8,128)(2,1)} %get-tuple-element.429), channel_id=1, source_target_pairs={{0,24},{1,25},{2,26},{3,27},{4,28},{5,29},{6,30},{7,31},{8,0},{9,1... | collective-permute-start | bytes 786440 | tf_op jit(solution)/shard_map/ppermute | solution.py:42
  810.2 102.7 %all-reduce.2.cloned.1.call-start = ((), (), s32[]{:S(2)}) async-start(), calls=%async_computation.16 | async-start | bytes 262144 | tf_op jit(solution)/shard_map/psum | solution.py:215
  810.2 27.1 %collective-permute-start.43 = (bf16[8,256,512]{2,1,0:T(8,128)(2,1)}, bf16[8,256,512]{2,1,0:T(8,128)(2,1)}, u32[]{:S(2)}, u32[]{:S(2)}) collective-permute-start(bf16[8,256,512]{2,1,0:T(8,128)(2,1)} %bitcast.352), channel_id=1, source_target_pairs={{0,1},{1,0},{2,6},{3,7},{4,5},{5,4},{6,2},{7,3},{8,9},{9,8},{10,14... | collective-permute-start | bytes 6291464 | tf_op jit(solution)/shard_map/ppermute | solution.py:42
  813.0 28.1 %collective-permute-start.44 = (bf16[576,512]{1,0:T(8,128)(2,1)}, bf16[576,512]{1,0:T(8,128)(2,1)}, u32[]{:S(2)}, u32[]{:S(2)}) collective-permute-start(bf16[576,512]{1,0:T(8,128)(2,1)} %get-tuple-element.412), channel_id=1, source_target_pairs={{0,24},{1,25},{2,26},{3,27},{4,28},{5,29},{6,30},{7,31},{8,0},{9,1... | collective-permute-start | bytes 1769480 | tf_op jit(solution)/shard_map/ppermute | solution.py:42
  843.5 43.5 %collective-permute-start.53 = (bf16[576,512]{1,0:T(8,128)(2,1)}, bf16[576,512]{1,0:T(8,128)(2,1)}, u32[]{:S(2)}, u32[]{:S(2)}) collective-permute-start(bf16[576,512]{1,0:T(8,128)(2,1)} %get-tuple-element.411), channel_id=1, source_target_pairs={{0,16},{1,17},{2,18},{3,19},{4,20},{5,21},{6,22},{7,23},{8,24},{9,... | collective-permute-start | bytes 1769480 | tf_op jit(solution)/shard_map/ppermute | solution.py:42
  894.1 30.8 %collective-permute-start.56 = (f32[288,512]{1,0:T(8,128)}, f32[288,512]{1,0:T(8,128)}, u32[]{:S(2)}, u32[]{:S(2)}) collective-permute-start(f32[288,512]{1,0:T(8,128)} %slice_select_fusion.1), channel_id=1, source_target_pairs={{0,2},{1,3},{2,0},{3,1},{4,6},{5,7},{6,4},{7,5},{8,10},{9,11},{10,... | collective-permute-start | bytes 1769480 | tf_op jit(solution)/shard_map/ppermute | solution.py:42
  894.2 33.8 %collective-permute-start.55 = (f32[288,512]{1,0:T(8,128)}, f32[288,512]{1,0:T(8,128)}, u32[]{:S(2)}, u32[]{:S(2)}) collective-permute-start(f32[288,512]{1,0:T(8,128)} %slice_select_fusion.3), channel_id=1, source_target_pairs={{0,2},{1,3},{2,0},{3,1},{4,6},{5,7},{6,4},{7,5},{8,10},{9,11},{10,... | collective-permute-start | bytes 1769480 | tf_op jit(solution)/shard_map/ppermute | solution.py:42
  906.3 34.1 %collective-permute-start.46 = (bf16[1,512,1024]{2,1,0:T(8,128)(2,1)}, bf16[1,512,1024]{2,1,0:T(8,128)(2,1)S(1)}, u32[]{:S(2)}, u32[]{:S(2)}) collective-permute-start(bf16[1,512,1024]{2,1,0:T(8,128)(2,1)} %select_convert_fusion), channel_id=1, source_target_pairs={{0,1},{1,0},{2,3},{3,2},{4,5},{5,4},{6,7},{7,6},{8,9},{9,8},{10,11... | collective-permute-start | bytes 3145736 | tf_op jit(solution)/shard_map/ppermute | solution.py:1173
  (71 other events, 744.5 us)
Sparse Core Ops, SparseCore 0:
  518.8 16.1 reduce-scatter.8
  539.4 16.8 reduce-scatter.10
  598.6 11.7 reduce-scatter.12
  669.2 12.3 reduce-scatter.16
  683.7 19.0 reduce-scatter.14
  705.0 19.0 reduce-scatter.18
  778.1 20.5 reduce-scatter.20
  810.3 22.4 reduce-scatter.22
  858.9 53.9 all-reduce.1

commit v4 on v3

--- a/solution.py
+++ b/solution.py
@@ -200,19 +200,23 @@
         self.parts = [moved(line[step], along_z(-step)) for step in range(1, self.depth)]
         return self.parts
 
-    def end_z(self, core):
+    def total(self):
         total = self.line[0].astype(F32)
         for part in self.parts:
             total = total + part.astype(F32)
-        total = total.reshape((2, -1) + total.shape[1:])
-        kept = jnp.where(core == 0, total[0], total[1])
-        came = moved(jnp.where(core == 0, total[1], total[0]), to_core)
-        return jnp.where(core == 0, kept, came), jnp.where(core == 0, came, kept)
+        return total.reshape((2, -1) + total.shape[1:])
 
 
 def summed_z(array):
-    dp, _ = sizes()
-    return lax.psum(array, "dp", axis_index_groups=[list(range(i, dp, 4)) for i in range(4)])
+    depth = sizes()[0] // 4
+    if depth == 4:
+        for bit in (1, 2):
+            array = array + moved(array, lambda z, x, c, y, bit=bit: (z ^ bit, x, c, y))
+        return array
+    total = array
+    for step in range(1, depth):
+        total = total + moved(array, along_z(step))
+    return total
 
 
 def hop_y(array):
@@ -1514,22 +1518,29 @@
         line = last_chan.end_second(away)
         last_att.third(line, parts)
         last_chan.z(away, parts)
-        small = summed_z(tie(sums_xy, line))
         last_att.end_third()
-        last_att.second(last_chan.parts[0])
-        line = last_att.end_second()
+        small = summed_z(tie(sums_xy, last_chan.parts[:2]))
+        last_att.second(last_chan.parts[:2])
+        line = last_att.end_second(small)
         last_att.z()
-        small = tie(small, last_att.parts)
-        for move in (earlier_chan, earlier_att, last_chan):
-            move.parts = tie(move.parts, line)
+        came = [last_att.parts]
         if swapped:
             kept_runs, sent_runs = runs_cut(tie(grad, line))
-            came = partner_y(sent_runs.astype(BF))
-            grad = runs_joined(kept_runs, came.astype(F32))
-        for name in list(sums):
-            first, second = sums[name].end_z(core)
+            came.append(partner_y(sent_runs.astype(BF)))
+        small, came, *parts = tie((small, came, *[move.parts for move in sums.values()]))
+        if swapped:
+            grad = runs_joined(kept_runs, came[1].astype(F32))
+        for move, part in zip(sums.values(), parts):
+            move.parts = part
+        totals = [move.total() for move in sums.values()]
+        kept_all = [jnp.where(core == 0, total[0], total[1]) for total in totals]
+        sent_all = [jnp.where(core == 0, total[1], total[0]) for total in totals]
+        came_all = moved(jnp.concatenate(sent_all), to_core)
+        spots = spots_of(kept_all)
+        for name, mine, theirs in zip(list(sums), kept_all, cut_at(came_all, spots)):
+            first, second = jnp.where(core == 0, mine, theirs), jnp.where(core == 0, theirs, mine)
             spots = part_spots if name[0] == "chan" else [0, 2 * rows]
-            sums[name] = (cut_at(first, spots), cut_at(second, spots)) if name[0] == "chan" else ([first], [second])
+            sums[name] = cut_at(first, spots), cut_at(second, spots)
     else:
         small = lax.psum(small, BOTH)
     large = []

time: 964 us -> 953 us (0.989)
  other arithmetic: 77.5 us -> 67.2 us
    unnamed x145 -> x139, local copies, waits for them, and re-layouts: 18.3 us -> 20.6 us
    ppermute x52 -> x51, starting transfers between devices: 79.9 us -> 80.8 us  [moved(): return lax.ppermute(array, BOTH, pairs)]
    ppermute x52 -> x51, waiting for transfers between devices: 192 us -> 193 us  [moved(): return lax.ppermute(array, BOTH, pairs)]
  transfers between devices with their start and end apart: 66 -> 64, of which waited for: 24 -> 25; matrix products, arithmetic and copies ran while one was open for 10% -> 7% of each run, Pallas kernels for 47% -> 48%
where the time goes in v4:
time: 953 us; the launch traced here: 940 us
  Pallas kernels  479 us (50%)
  waiting for transfers between devices  237 us (25%)
  starting transfers between devices  88.2 us (9%)
  other arithmetic  67.2 us (7%)
  local copies, waits for them, and re-layouts  51.8 us (5%)
  between operations  15.9 us (2%)
    ppermute x51, waiting for transfers between devices, moved(): return lax.ppermute(array, BOTH, pairs)  193 us
    pallas_call x2, Pallas kernels, channel_back(): pl.pallas_call(body, grid=(2 * steps,), in_specs=[SCALAR, held(g.shape),...  133 us
    ppermute x51, starting transfers between devices, moved(): return lax.ppermute(array, BOTH, pairs)  80.8 us
    pallas_call x2, Pallas kernels, time_back(): pl.pallas_call(body, grid=(tiles,), in_specs=[SCALAR, block, fixed(fix.sh...  70.1 us
    pallas_call x4, Pallas kernels, arrange(): pl.pallas_call(body, grid_spec=pltpu.PrefetchScalarGridSpec(num_scalar_pr...  48.6 us
    pallas_call x2, Pallas kernels, channel_two(): pl.pallas_call(body, grid=(cut.steps,), in_specs=[held(s.shape), held(xk....  45.8 us
    ppermute x5, waiting for transfers between devices, partner_y(): return lax.ppermute(array, 'seq', [(0, 1), (1, 0)])  41.6 us
    pallas_call x2, Pallas kernels, out_back(): pl.pallas_call(body, grid=(tokens // tile,), in_specs=[SCALAR, block, fix...  40.4 us
  transfers between devices with their start and end apart: 64, of which 25 were waited for; matrix products, arithmetic and copies ran while one was open for 7% of the time, Pallas kernels for 48%

profile of v4, /device:TPU:1, one launch (start us, length us, event | category | flops | bytes accessed | tf_op | source)
XLA Modules:
  0.0 939.6 jit_solution(16447158182275305239)
XLA Ops:
  20.0 3.9 collective-permute-start.5
  24.4 17.0 %collective-permute-done = bf16[1,512,1024]{2,1,0:T(8,128)(2,1)S(1)} collective-permute-done((bf16[1,512,1024]{2,1,0:T(8,128)(2,1)S(1)}, bf16[1,512,1024]{2,1,0:T(8,128)(2,1)S(1)}, u32[]{:S(2)}, u32[]{:S(2)}) %collective-permute-start) | collective-permute-done | bytes 1048608 | tf_op jit(solution)/shard_map/ppermute | solution.py:1177
  48.9 14.6 %collective-permute-done.7 = bf16[2,288,512]{2,1,0:T(8,128)(2,1)S(1)} collective-permute-done((bf16[2,288,512]{2,1,0:T(8,128)(2,1)S(1)}, bf16[2,288,512]{2,1,0:T(8,128)(2,1)S(1)}, u32[]{:S(2)}, u32[]{:S(2)}) %collective-permute-start.7) | collective-permute-done | bytes 589856 | tf_op jit(solution)/shard_map/ppermute | solution.py:42
  68.7 21.9 %collective-permute-done.8.other_ref = bf16[8,256,512]{2,1,0:T(8,128)(2,1)} collective-permute-done((bf16[8,256,512]{2,1,0:T(8,128)(2,1)S(1)}, bf16[8,256,512]{2,1,0:T(8,128)(2,1)}, u32[]{:S(2)}, u32[]{:S(2)}) %collective-permute-start.8) | collective-permute-done | bytes 2097184 | tf_op jit(solution)/shard_map/ppermute | solution.py:42
  90.6 10.9 %shard_map.229 = bf16[16,256,512]{2,1,0:T(8,128)(2,1)} custom-call(s32[7,16]{1,0:T(8,128)} %dynamic-slice_bitcast_fusion.table_ref, bf16[8,256,512]{2,1,0:T(8,128)(2,1)} %copy-done.11, bf16[8,256,512]{2,1,0:T(8,128)(2,1)} %collective-permute-done.8.other_ref), custom_call_target="tpu_custom_call" | custom-call | flops 1 | bytes 1 | tf_op jit(solution)/shard_map/pallas_call | solution.py:117
  101.5 4.3 collective-permute-done.9
  112.3 24.6 %collective-permute-done.1 = s32[1,512]{1,0:T(1,128)S(1)} collective-permute-done((s32[1,512]{1,0:T(1,128)S(1)}, s32[1,512]{1,0:T(1,128)S(1)}, u32[]{:S(2)}, u32[]{:S(2)}) %collective-permute-start.1) | collective-permute-done | bytes 2080 | tf_op jit(solution)/shard_map/ppermute | solution.py:1177
  142.2 17.7 %shard_map.230 = (bf16[1024,1024]{1,0:T(8,128)(2,1)}, bf16[1024,1024]{1,0:T(8,128)(2,1)}, bf16[1024,1024]{1,0:T(8,128)(2,1)}, f32[1024,1024]{1,0:T(8,128)}, f32[...) custom-call(s32[1]{0:T(128)} %bitcast.core_ref, ...), custom_call_target="tpu_custom_call" | custom-call | flops 1 | bytes 1 | tf_op jit(solution)/shard_map/pallas_call | solution.py:401
  168.1 17.5 %shard_map.231 = (bf16[1024,1024]{1,0:T(8,128)(2,1)}, f32[1024,1024]{1,0:T(8,128)}, f32[1024,1024]{1,0:T(8,128)}, f32[1024,1024]{1,0:T(8,128)}) custom-call(s32[1]{0:T(128)} %bitcast.core_ref, bf16[1024,1024]{1,0:T(8,128)(2,1)} %maximum_bitcast_fusion.s_ref, f32[1024,1024]{1,0:T(8,128)} %get-tuple-element.195.k_ref, f32[1024,1024]{1,0:T(8,128)} %get-tuple-element.196.v_ref, ...), custom_call_target="tpu_custom_call" | custom-call | flops 1 | bytes 1 | tf_op jit(solution)/shard_map/pallas_call | solution.py:468
  187.8 8.0 collective-permute-start.20
  195.8 4.3 collective-permute-start.19
  201.5 8.9 collective-permute-done.20
  210.5 19.0 %collective-permute-done.19 = bf16[2,288,512]{2,1,0:T(8,128)(2,1)} collective-permute-done((bf16[2,288,512]{2,1,0:T(8,128)(2,1)}, bf16[2,288,512]{2,1,0:T(8,128)(2,1)}, u32[]{:S(2)}, u32[]{:S(2)}) %collective-permute-start.19) | collective-permute-done | bytes 589856 | tf_op jit(solution)/shard_map/ppermute | solution.py:42
  229.4 13.3 %shard_map.232 = bf16[16,576,512]{2,1,0:T(8,128)(2,1)} custom-call(s32[7,16]{1,0:T(8,128)} %dynamic-slice_bitcast_fusion.table_ref, bf16[8,576,512]{2,1,0:T(8,128)(2,1)} %copy-done.2, bf16[8,576,512]{2,1,0:T(8,128)(2,1)} %collective-permute-done.16.other_ref), custom_call_target="tpu_custom_call" | custom-call | flops 1 | bytes 1 | tf_op jit(solution)/shard_map/pallas_call | solution.py:117
  242.8 13.9 %collective-permute-done.17 = bf16[4,256,512]{2,1,0:T(8,128)(2,1)S(1)} collective-permute-done((bf16[4,256,512]{2,1,0:T(8,128)(2,1)S(1)}, bf16[4,256,512]{2,1,0:T(8,128)(2,1)S(1)}, u32[]{:S(2)}, u32[]{:S(2)}) %collective-permute-start.17) | collective-permute-done | bytes 1048608 | tf_op jit(solution)/shard_map/ppermute | solution.py:42
  258.9 19.6 %shard_map.233 = (bf16[1024,1024]{1,0:T(8,128)(2,1)}, bf16[1024,1024]{1,0:T(8,128)(2,1)}, f32[4,1,1024]{2,1,0:T(1,128)}, bf16[4,1024,512]{2,1,0:T(8,128)(2,1)}, f32[1024,1024]{1,0:T(8,128)}) custom-call(f32[1024,1024]{1,0:T(8,128)} %get-tuple-element.198.s_ref, f32[1,1024]{1,0:T(1,128)} %broadcast_1_before_ref_fix_ref.2.before_ref.fix_ref, ...), custom_call_target="tpu_custom_call" | custom-call | flops 1 | bytes 1 | tf_op jit(solution)/shard_map/pallas_call | solution.py:560
  282.2 10.9 %shard_map.234 = bf16[16,256,512]{2,1,0:T(8,128)(2,1)} custom-call(s32[7,16]{1,0:T(8,128)} %dynamic-slice_bitcast_fusion.table_ref, bf16[8,256,512]{2,1,0:T(8,128)(2,1)} %copy-done.12, bf16[8,256,512]{2,1,0:T(8,128)(2,1)} %collective-permute-done.21.other_ref), custom_call_target="tpu_custom_call" | custom-call | flops 1 | bytes 1 | tf_op jit(solution)/shard_map/pallas_call | solution.py:117
  296.4 23.3 %shard_map.235 = (bf16[4,1024,512]{2,1,0:T(8,128)(2,1)}, bf16[1024,1024]{1,0:T(8,128)(2,1)}, bf16[1024,1024]{1,0:T(8,128)(2,1)}, f32[1024,1024]{1,0:T(8,128)}) custom-call(f32[1024,1024]{1,0:T(8,128)} %get-tuple-element.198.s_ref, bf16[1024,1024]{1,0:T(8,128)(2,1)} %get-tuple-element.210.xk_ref, bf16[1024,1024]{1,0:T(8,128)(2,1)} %get-tuple-element.211.xr_ref, ...), custom_call_target="tpu_custom_call" | custom-call | flops 1 | bytes 1 | tf_op jit(solution)/shard_map/pallas_call | solution.py:609
  329.3 6.2 collective-permute-done.24
  337.5 17.8 %shard_map.236 = (bf16[1024,1024]{1,0:T(8,128)(2,1)}, bf16[1024,1024]{1,0:T(8,128)(2,1)}, bf16[1024,1024]{1,0:T(8,128)(2,1)}, f32[1024,1024]{1,0:T(8,128)}, f32[...) custom-call(s32[1]{0:T(128)} %bitcast.core_ref, ...), custom_call_target="tpu_custom_call" | custom-call | flops 1 | bytes 1 | tf_op jit(solution)/shard_map/pallas_call | solution.py:401
  355.3 18.3 %shard_map.237 = (bf16[1024,1024]{1,0:T(8,128)(2,1)}, f32[1024,1024]{1,0:T(8,128)}, f32[1024,1024]{1,0:T(8,128)}, f32[1024,1024]{1,0:T(8,128)}) custom-call(s32[1]{0:T(128)} %bitcast.core_ref, f32[1024,1024]{1,0:T(8,128)} %get-tuple-element.223.s_ref, f32[1024,1024]{1,0:T(8,128)} %get-tuple-element.224.k_ref, f32[1024,1024]{1,0:T(8,128)} %get-tuple-element.225.v_ref, ...), custom_call_target="tpu_custom_call" | custom-call | flops 1 | bytes 1 | tf_op jit(solution)/shard_map/pallas_call | solution.py:468
  373.6 4.6 collective-permute-done.25.other_ref
  380.4 13.5 %shard_map.238 = bf16[16,576,512]{2,1,0:T(8,128)(2,1)} custom-call(s32[7,16]{1,0:T(8,128)} %dynamic-slice_bitcast_fusion.table_ref, bf16[8,576,512]{2,1,0:T(8,128)(2,1)} %constant_dynamic-update-slice_fusion.38.own_ref, bf16[8,576,512]{2,1,0:T(8,128)(2,1)} %copy-done.10), custom_call_target="tpu_custom_call" | custom-call | flops 1 | bytes 1 | tf_op jit(solution)/shard_map/pallas_call | solution.py:117
  393.9 5.0 collective-permute-start.26
  399.7 19.9 %shard_map.239 = (bf16[1024,1024]{1,0:T(8,128)(2,1)}, bf16[1024,1024]{1,0:T(8,128)(2,1)}, f32[4,1,1024]{2,1,0:T(1,128)}, bf16[4,1024,512]{2,1,0:T(8,128)(2,1)}, f32[1024,1024]{1,0:T(8,128)}) custom-call(f32[1024,1024]{1,0:T(8,128)} %get-tuple-element.227.s_ref, f32[1,1024]{1,0:T(1,128)} %broadcast_1_before_ref_fix_ref.2.before_ref.fix_ref, ...), custom_call_target="tpu_custom_call" | custom-call | flops 1 | bytes 1 | tf_op jit(solution)/shard_map/pallas_call | solution.py:560
  422.8 22.5 %shard_map.240 = (bf16[4,1024,512]{2,1,0:T(8,128)(2,1)}, bf16[1024,1024]{1,0:T(8,128)(2,1)}, bf16[1024,1024]{1,0:T(8,128)(2,1)}, bf16[1024,1024]{1,0:T(8,128)(2,1)}) custom-call(f32[1024,1024]{1,0:T(8,128)} %get-tuple-element.227.s_ref, bf16[1024,1024]{1,0:T(8,128)(2,1)} %get-tuple-element.232.xk_ref, bf16[1024,1024]{1,0:T(8,128)(2,1)} %get-tuple-element.233.xr_ref, ...), custom_call_target="tpu_custom_call" | custom-call | flops 1 | bytes 1 | tf_op jit(solution)/shard_map/pallas_call | solution.py:609
  451.4 65.6 %shard_map.241 = (bf16[2,8,2,288,512]{4,3,2,1,0:T(8,128)(2,1)}, bf16[2,8,2,288,512]{4,3,2,1,0:T(8,128)(2,1)}, f32[1024,1024]{1,0:T(8,128)}, f32[1,1024]{1,0:T(1,128)}, f32[4,1024]{1,0:T(4,128)}) custom-call(s32[1]{0:T(128)} %bitcast.core_ref, bf16[1024,1024]{1,0:T(8,128)(2,1)} %maximum_bitcast_fusion.1.g_ref, ...), custom_call_target="tpu_custom_call" | custom-call | flops 1 | bytes 1 | tf_op jit(solution)/shard_map/pallas_call | solution.py:819
  518.8 20.5 %shard_map.242 = (bf16[1024,1024]{1,0:T(8,128)(2,1)}, bf16[1024,1024]{1,0:T(8,128)(2,1)}, f32[1024,1024]{1,0:T(8,128)}, f32[1024,1024]{1,0:T(8,128)}, f32[1,2,1024]{2,1,0:T(2,128)}) custom-call(s32[1]{0:T(128)} %bitcast.core_ref, f32[1024,1024]{1,0:T(8,128)} %get-tuple-element.246.g_ref, f32[1,1024]{1,0:T(1,128)} %broadcast_1_before_ref_fix_ref.2.before_ref.fix_ref, ...), custom_call_target="tpu_custom_call" | custom-call | flops 1 | bytes 1 | tf_op jit(solution)/shard_map/pallas_call | solution.py:896
  540.0 34.0 %shard_map.243 = (bf16[1024,1024]{1,0:T(8,128)(2,1)}, bf16[1024,1024]{1,0:T(8,128)(2,1)}, f32[1024,1024]{1,0:T(8,128)}, f32[1,1024]{1,0:T(1,128)}, f32[7,1024]{1,0:T(8,128)}) custom-call(s32[1]{0:T(128)} %bitcast.core_ref, f32[1024,1024]{1,0:T(8,128)} %get-tuple-element.246.g_ref, f32[1,1024]{1,0:T(1,128)} %broadcast_1_before_ref_fix_ref.2.before_ref.fix_ref, ...), custom_call_target="tpu_custom_call" | custom-call | flops 1 | bytes 1 | tf_op jit(solution)/shard_map/pallas_call | solution.py:989
  574.0 15.0 %shard_map.244 = (bf16[2,8,2,128,512]{4,3,2,1,0:T(8,128)(2,1)}, bf16[2,8,2,128,512]{4,3,2,1,0:T(8,128)(2,1)}) custom-call(s32[7,16]{1,0:T(8,128)} %dynamic-slice_bitcast_fusion.table_ref, bf16[1024,1024]{1,0:T(8,128)(2,1)} %get-tuple-element.259.refs_0_, bf16[1024,1024]{1,0:T(8,128)(2,1)} %get-tuple-element.260.refs_1_, ...), custom_call_target="tpu_custom_call" | custom-call | flops 1 | bytes 1 | tf_op jit(solution)/shard_map/pallas_call | solution.py:1090
  589.0 4.1 collective-permute-done.29
  593.1 5.4 add_convert_fusion.4
  599.2 67.8 %shard_map.245 = (bf16[2,8,2,288,512]{4,3,2,1,0:T(8,128)(2,1)}, bf16[2,8,2,288,512]{4,3,2,1,0:T(8,128)(2,1)}, f32[1024,1024]{1,0:T(8,128)}, f32[1,1024]{1,0:T(1,128)}, f32[4,1024]{1,0:T(4,128)}) custom-call(s32[1]{0:T(128)} %bitcast.core_ref, f32[1024,1024]{1,0:T(8,128)} %get-tuple-element.268.g_ref, ...), custom_call_target="tpu_custom_call" | custom-call | flops 1 | bytes 1 | tf_op jit(solution)/shard_map/pallas_call | solution.py:819
  671.9 19.9 %shard_map.246 = (bf16[1024,1024]{1,0:T(8,128)(2,1)}, bf16[1024,1024]{1,0:T(8,128)(2,1)}, f32[1024,1024]{1,0:T(8,128)}, f32[1024,1024]{1,0:T(8,128)}, f32[1,2,1024]{2,1,0:T(2,128)}) custom-call(s32[1]{0:T(128)} %bitcast.core_ref, f32[1024,1024]{1,0:T(8,128)} %get-tuple-element.283.g_ref, f32[1,1024]{1,0:T(1,128)} %broadcast_1_before_ref_fix_ref.2.before_ref.fix_ref, ...), custom_call_target="tpu_custom_call" | custom-call | flops 1 | bytes 1 | tf_op jit(solution)/shard_map/pallas_call | solution.py:896
  691.8 3.7 collective-permute-done.31
  695.4 5.2 add_convert_fusion.10
  710.5 36.1 %shard_map.247 = (bf16[1024,1024]{1,0:T(8,128)(2,1)}, bf16[1024,1024]{1,0:T(8,128)(2,1)}, f32[1024,1024]{1,0:T(8,128)}, f32[1,1024]{1,0:T(1,128)}, f32[7,1024]{1,0:T(8,128)}) custom-call(s32[1]{0:T(128)} %bitcast.core_ref, f32[1024,1024]{1,0:T(8,128)} %get-tuple-element.283.g_ref, f32[1,1024]{1,0:T(1,128)} %broadcast_1_before_ref_fix_ref.2.before_ref.fix_ref, ...), custom_call_target="tpu_custom_call" | custom-call | flops 1 | bytes 1 | tf_op jit(solution)/shard_map/pallas_call | solution.py:989
  751.4 15.0 %shard_map.248 = (bf16[2,8,2,128,512]{4,3,2,1,0:T(8,128)(2,1)}, bf16[2,8,2,128,512]{4,3,2,1,0:T(8,128)(2,1)}) custom-call(s32[7,16]{1,0:T(8,128)} %dynamic-slice_bitcast_fusion.table_ref, bf16[1024,1024]{1,0:T(8,128)(2,1)} %get-tuple-element.301.refs_0_, bf16[1024,1024]{1,0:T(8,128)(2,1)} %get-tuple-element.304.refs_1_, ...), custom_call_target="tpu_custom_call" | custom-call | flops 1 | bytes 1 | tf_op jit(solution)/shard_map/pallas_call | solution.py:1090
  766.6 4.2 collective-permute-done.37
  770.8 5.6 add_convert_fusion.2
  784.5 22.8 %collective-permute-done.39 = bf16[4,576,512]{2,1,0:T(8,128)(2,1)} collective-permute-done((bf16[4,576,512]{2,1,0:T(8,128)(2,1)}, bf16[4,576,512]{2,1,0:T(8,128)(2,1)}, u32[]{:S(2)}, u32[]{:S(2)}) %collective-permute-start.39) | collective-permute-done | bytes 2359328 | tf_op jit(solution)/shard_map/ppermute | solution.py:42
  807.3 3.7 add_convert_fusion
  816.2 20.9 %collective-permute-done.43 = bf16[8,256,512]{2,1,0:T(8,128)(2,1)} collective-permute-done((bf16[8,256,512]{2,1,0:T(8,128)(2,1)}, bf16[8,256,512]{2,1,0:T(8,128)(2,1)}, u32[]{:S(2)}, u32[]{:S(2)}) %collective-permute-start.43) | collective-permute-done | bytes 2097184 | tf_op jit(solution)/shard_map/ppermute | solution.py:42
  841.9 12.1 %collective-permute-start.47 = (f32[2,11,1024]{2,1,0:T(8,128)S(1)}, f32[2,11,1024]{2,1,0:T(8,128)S(1)}, u32[]{:S(2)}, u32[]{:S(2)}) collective-permute-start(f32[2,11,1024]{2,1,0:T(8,128)S(1)} %add.117), channel_id=1, source_target_pairs={{0,2},{1,3},{2,0},{3,1},{4,6},{5,7},{6,4},{7,5},{8,10},{9,11},{10,... | collective-permute-start | bytes 270344 | tf_op jit(solution)/shard_map/ppermute | solution.py:42
  864.5 5.9 collective-permute-done.49
  879.0 9.8 %collective-permute-done.51 = bf16[576,512]{1,0:T(8,128)(2,1)S(1)} collective-permute-done((bf16[576,512]{1,0:T(8,128)(2,1)S(1)}, bf16[576,512]{1,0:T(8,128)(2,1)S(1)}, u32[]{:S(2)}, u32[]{:S(2)}) %collective-permute-start.51) | collective-permute-done | bytes 589856 | tf_op jit(solution)/shard_map/ppermute | solution.py:42
  888.9 5.6 collective-permute-done.54
  894.5 12.5 %collective-permute-done.53 = bf16[256,512]{1,0:T(8,128)(2,1)S(1)} collective-permute-done((bf16[256,512]{1,0:T(8,128)(2,1)S(1)}, bf16[256,512]{1,0:T(8,128)(2,1)S(1)}, u32[]{:S(2)}, u32[]{:S(2)}) %collective-permute-start.53) | collective-permute-done | bytes 262176 | tf_op jit(solution)/shard_map/ppermute | solution.py:42
  (397 shorter events, 166.7 us)
Async XLA Ops:
  7.2 532.2 %reduce-scatter.9.cloned.1.call-start = ((), (), s32[]{:S(2)}) async-start(), calls=%async_computation.8 | async-start | bytes 14155776 | tf_op jit(solution)/shard_map/reduce_scatter | solution.py:175
  15.1 26.3 %collective-permute-start = (bf16[1,512,1024]{2,1,0:T(8,128)(2,1)S(1)}, bf16[1,512,1024]{2,1,0:T(8,128)(2,1)S(1)}, u32[]{:S(2)}, u32[]{:S(2)}) collective-permute-start(bf16[1,512,1024]{2,1,0:T(8,128)(2,1)S(1)} %broadcast_select_fusion.14), channel_id=1, source_target_pairs={{0,1},{1,0},{2,3},{3,2},{4,5},{5,4},{6,7},{7,6},{8,9},{9,8},{10,11... | collective-permute-start | bytes 3145736 | tf_op jit(solution)/shard_map/ppermute | solution.py:1177
  20.0 23.1 %collective-permute-start.5 = (bf16[2,128,512]{2,1,0:T(8,128)(2,1)S(1)}, bf16[2,128,512]{2,1,0:T(8,128)(2,1)S(1)}, u32[]{:S(2)}, u32[]{:S(2)}) collective-permute-start(bf16[2,128,512]{2,1,0:T(8,128)(2,1)S(1)} %get-tuple-element.439), channel_id=1, source_target_pairs={{0,24},{1,25},{2,26},{3,27},{4,28},{5,29},{6,30},{7,31},{8,0},{9,1... | collective-permute-start | bytes 786440 | tf_op jit(solution)/shard_map/ppermute | solution.py:42
  23.9 22.1 %collective-permute-start.4 = (bf16[2,128,512]{2,1,0:T(8,128)(2,1)S(1)}, bf16[2,128,512]{2,1,0:T(8,128)(2,1)S(1)}, u32[]{:S(2)}, u32[]{:S(2)}) collective-permute-start(bf16[2,128,512]{2,1,0:T(8,128)(2,1)S(1)} %get-tuple-element.439), channel_id=1, source_target_pairs={{0,16},{1,17},{2,18},{3,19},{4,20},{5,21},{6,22},{7,23},{8,24},{9,... | collective-permute-start | bytes 786440 | tf_op jit(solution)/shard_map/ppermute | solution.py:42
  23.9 22.1 %collective-permute-start.3 = (bf16[2,128,512]{2,1,0:T(8,128)(2,1)S(1)}, bf16[2,128,512]{2,1,0:T(8,128)(2,1)S(1)}, u32[]{:S(2)}, u32[]{:S(2)}) collective-permute-start(bf16[2,128,512]{2,1,0:T(8,128)(2,1)S(1)} %get-tuple-element.439), channel_id=1, source_target_pairs={{0,8},{1,9},{2,10},{3,11},{4,12},{5,13},{6,14},{7,15},{8,16},{9,17... | collective-permute-start | bytes 786440 | tf_op jit(solution)/shard_map/ppermute | solution.py:42
  64.5 26.1 %collective-permute-start.8 = (bf16[8,256,512]{2,1,0:T(8,128)(2,1)S(1)}, bf16[8,256,512]{2,1,0:T(8,128)(2,1)}, u32[]{:S(2)}, u32[]{:S(2)}) collective-permute-start(bf16[8,256,512]{2,1,0:T(8,128)(2,1)S(1)} %constant_dynamic-update-slice_fusion.32.own_ref), channel_id=1, source_target_pairs={{0,1},{1,0},{2,6},{3,7},{4,5},{5,4},{6,2},{7,3},{8,9},{9,8},{10,14... | collective-permute-start | bytes 6291464 | tf_op jit(solution)/shard_map/ppermute | solution.py:42
  66.8 34.8 %collective-permute-start.10 = (bf16[2,288,512]{2,1,0:T(8,128)(2,1)S(1)}, bf16[2,288,512]{2,1,0:T(8,128)(2,1)}, u32[]{:S(2)}, u32[]{:S(2)}) collective-permute-start(bf16[2,288,512]{2,1,0:T(8,128)(2,1)S(1)} %get-tuple-element.185), channel_id=1, source_target_pairs={{0,24},{1,25},{2,26},{3,27},{4,28},{5,29},{6,30},{7,31},{8,0},{9,1... | collective-permute-start | bytes 1769480 | tf_op jit(solution)/shard_map/ppermute | solution.py:42
  67.5 38.4 %collective-permute-start.9 = (bf16[2,288,512]{2,1,0:T(8,128)(2,1)S(1)}, bf16[2,288,512]{2,1,0:T(8,128)(2,1)}, u32[]{:S(2)}, u32[]{:S(2)}) collective-permute-start(bf16[2,288,512]{2,1,0:T(8,128)(2,1)S(1)} %get-tuple-element.185), channel_id=1, source_target_pairs={{0,16},{1,17},{2,18},{3,19},{4,20},{5,21},{6,22},{7,23},{8,24},{9,... | collective-permute-start | bytes 1769480 | tf_op jit(solution)/shard_map/ppermute | solution.py:42
  105.9 35.8 %collective-permute-start.11 = (bf16[16,256,512]{2,1,0:T(8,128)(2,1)}, bf16[16,256,512]{2,1,0:T(8,128)(2,1)}, u32[]{:S(2)}, u32[]{:S(2)}) collective-permute-start(bf16[16,256,512]{2,1,0:T(8,128)(2,1)} %shard_map.229), channel_id=1, source_target_pairs={{0,2},{1,3},{2,0},{3,1},{4,6},{5,7},{6,4},{7,5},{8,10},{9,11},{10,... | collective-permute-start | bytes 12582920 | tf_op jit(solution)/shard_map/ppermute | solution.py:42
  108.7 51.2 %collective-permute-start.12 = (bf16[4,576,512]{2,1,0:T(8,128)(2,1)S(1)}, bf16[4,576,512]{2,1,0:T(8,128)(2,1)}, u32[]{:S(2)}, u32[]{:S(2)}) collective-permute-start(bf16[4,576,512]{2,1,0:T(8,128)(2,1)S(1)} %pad_maximum_fusion.1), channel_id=1, source_target_pairs={{0,4},{1,5},{2,3},{3,2},{4,0},{5,1},{6,7},{7,6},{8,12},{9,13},{10,... | collective-permute-start | bytes 7077896 | tf_op jit(solution)/shard_map/ppermute | solution.py:42
  108.8 28.1 %collective-permute-start.1 = (s32[1,512]{1,0:T(1,128)S(1)}, s32[1,512]{1,0:T(1,128)S(1)}, u32[]{:S(2)}, u32[]{:S(2)}) collective-permute-start(s32[1,512]{1,0:T(1,128)S(1)} %broadcast_select_fusion.20), channel_id=1, source_target_pairs={{0,1},{1,0},{2,3},{3,2},{4,5},{5,4},{6,7},{7,6},{8,9},{9,8},{10,11... | collective-permute-start | bytes 6152 | tf_op jit(solution)/shard_map/ppermute | solution.py:1177
  163.6 65.9 %collective-permute-start.16 = (bf16[8,576,512]{2,1,0:T(8,128)(2,1)S(1)}, bf16[8,576,512]{2,1,0:T(8,128)(2,1)}, u32[]{:S(2)}, u32[]{:S(2)}) collective-permute-start(bf16[8,576,512]{2,1,0:T(8,128)(2,1)S(1)} %constant_dynamic-update-slice_fusion.34.own_ref), channel_id=1, source_target_pairs={{0,1},{1,0},{2,6},{3,7},{4,5},{5,4},{6,2},{7,3},{8,9},{9,8},{10,14... | collective-permute-start | bytes 14155784 | tf_op jit(solution)/shard_map/ppermute | solution.py:42
  187.8 22.6 %collective-permute-start.20 = (bf16[2,288,512]{2,1,0:T(8,128)(2,1)}, bf16[2,288,512]{2,1,0:T(8,128)(2,1)}, u32[]{:S(2)}, u32[]{:S(2)}) collective-permute-start(bf16[2,288,512]{2,1,0:T(8,128)(2,1)} %get-tuple-element.207), channel_id=1, source_target_pairs={{0,24},{1,25},{2,26},{3,27},{4,28},{5,29},{6,30},{7,31},{8,0},{9,1... | collective-permute-start | bytes 1769480 | tf_op jit(solution)/shard_map/ppermute | solution.py:42
  195.8 33.6 %collective-permute-start.19 = (bf16[2,288,512]{2,1,0:T(8,128)(2,1)}, bf16[2,288,512]{2,1,0:T(8,128)(2,1)}, u32[]{:S(2)}, u32[]{:S(2)}) collective-permute-start(bf16[2,288,512]{2,1,0:T(8,128)(2,1)} %get-tuple-element.207), channel_id=1, source_target_pairs={{0,16},{1,17},{2,18},{3,19},{4,20},{5,21},{6,22},{7,23},{8,24},{9,... | collective-permute-start | bytes 1769480 | tf_op jit(solution)/shard_map/ppermute | solution.py:42
  200.1 29.3 %collective-permute-start.18 = (bf16[2,288,512]{2,1,0:T(8,128)(2,1)}, bf16[2,288,512]{2,1,0:T(8,128)(2,1)}, u32[]{:S(2)}, u32[]{:S(2)}) collective-permute-start(bf16[2,288,512]{2,1,0:T(8,128)(2,1)} %get-tuple-element.207), channel_id=1, source_target_pairs={{0,8},{1,9},{2,10},{3,11},{4,12},{5,13},{6,14},{7,15},{8,16},{9,17... | collective-permute-start | bytes 1769480 | tf_op jit(solution)/shard_map/ppermute | solution.py:42
  242.8 50.4 %collective-permute-start.22 = (bf16[16,576,512]{2,1,0:T(8,128)(2,1)}, bf16[16,576,512]{2,1,0:T(8,128)(2,1)}, u32[]{:S(2)}, u32[]{:S(2)}) collective-permute-start(bf16[16,576,512]{2,1,0:T(8,128)(2,1)} %shard_map.232), channel_id=1, source_target_pairs={{0,2},{1,3},{2,0},{3,1},{4,6},{5,7},{6,4},{7,5},{8,10},{9,11},{10,... | collective-permute-start | bytes 28311560 | tf_op jit(solution)/shard_map/ppermute | solution.py:42
  256.9 25.4 %collective-permute-start.21 = (bf16[8,256,512]{2,1,0:T(8,128)(2,1)S(1)}, bf16[8,256,512]{2,1,0:T(8,128)(2,1)}, u32[]{:S(2)}, u32[]{:S(2)}) collective-permute-start(bf16[8,256,512]{2,1,0:T(8,128)(2,1)S(1)} %constant_dynamic-update-slice_fusion.36.own_ref), channel_id=1, source_target_pairs={{0,1},{1,0},{2,6},{3,7},{4,5},{5,4},{6,2},{7,3},{8,9},{9,8},{10,14... | collective-permute-start | bytes 6291464 | tf_op jit(solution)/shard_map/ppermute | solution.py:42
  282.2 37.5 %collective-permute-start.23 = (bf16[4,576,512]{2,1,0:T(8,128)(2,1)S(1)}, bf16[4,576,512]{2,1,0:T(8,128)(2,1)}, u32[]{:S(2)}, u32[]{:S(2)}) collective-permute-start(bf16[4,576,512]{2,1,0:T(8,128)(2,1)S(1)} %pad_maximum_fusion.2), channel_id=1, source_target_pairs={{0,4},{1,5},{2,3},{3,2},{4,0},{5,1},{6,7},{7,6},{8,12},{9,13},{10,... | collective-permute-start | bytes 7077896 | tf_op jit(solution)/shard_map/ppermute | solution.py:42
  324.7 53.5 %collective-permute-start.25 = (bf16[8,576,512]{2,1,0:T(8,128)(2,1)}, bf16[8,576,512]{2,1,0:T(8,128)(2,1)S(1)}, u32[]{:S(2)}, u32[]{:S(2)}) collective-permute-start(bf16[8,576,512]{2,1,0:T(8,128)(2,1)} %constant_dynamic-update-slice_fusion.38.own_ref), channel_id=1, source_target_pairs={{0,1},{1,0},{2,6},{3,7},{4,5},{5,4},{6,2},{7,3},{8,9},{9,8},{10,14... | collective-permute-start | bytes 14155784 | tf_op jit(solution)/shard_map/ppermute | solution.py:42
  393.9 25.7 %collective-permute-start.26 = (bf16[16,576,512]{2,1,0:T(8,128)(2,1)}, bf16[16,576,512]{2,1,0:T(8,128)(2,1)}, u32[]{:S(2)}, u32[]{:S(2)}) collective-permute-start(bf16[16,576,512]{2,1,0:T(8,128)(2,1)} %shard_map.238), channel_id=1, source_target_pairs={{0,2},{1,3},{2,0},{3,1},{4,6},{5,7},{6,4},{7,5},{8,10},{9,11},{10,... | collective-permute-start | bytes 28311560 | tf_op jit(solution)/shard_map/ppermute | solution.py:42
  399.6 48.8 %collective-permute-start.28 = (bf16[1,512,1024]{2,1,0:T(8,128)(2,1)S(1)}, bf16[1,512,1024]{2,1,0:T(8,128)(2,1)}, u32[]{:S(2)}, u32[]{:S(2)}) collective-permute-start(bf16[1,512,1024]{2,1,0:T(8,128)(2,1)S(1)} %broadcast_select_fusion.6), channel_id=1, source_target_pairs={{0,1},{1,0},{2,3},{3,2},{4,5},{5,4},{6,7},{7,6},{8,9},{9,8},{10,11... | collective-permute-start | bytes 3145736 | tf_op jit(solution)/shard_map/ppermute | solution.py:1177
  447.0 70.0 %collective-permute-start.27 = (bf16[1,512,1024]{2,1,0:T(8,128)(2,1)S(1)}, bf16[1,512,1024]{2,1,0:T(8,128)(2,1)S(1)}, u32[]{:S(2)}, u32[]{:S(2)}) collective-permute-start(bf16[1,512,1024]{2,1,0:T(8,128)(2,1)S(1)} %broadcast_select_fusion.10), channel_id=1, source_target_pairs={{0,1},{1,0},{2,3},{3,2},{4,5},{5,4},{6,7},{7,6},{8,9},{9,8},{10,11... | collective-permute-start | bytes 3145736 | tf_op jit(solution)/shard_map/ppermute | solution.py:1177
  518.7 74.4 %reduce-scatter.11.cloned.1.call-start = ((), (), s32[]{:S(2)}) async-start(), calls=%async_computation.9 | async-start | bytes 14155776 | tf_op jit(solution)/shard_map/reduce_scatter | solution.py:175
  539.4 129.8 %reduce-scatter.13.cloned.1.call-start = ((), (), s32[]{:S(2)}) async-start(), calls=%async_computation.10 | async-start | bytes 6291456 | tf_op jit(solution)/shard_map/reduce_scatter | solution.py:175
  539.4 53.6 %collective-permute-start.29 = (bf16[8,576,512]{2,1,0:T(8,128)(2,1)}, bf16[8,576,512]{2,1,0:T(8,128)(2,1)}, u32[]{:S(2)}, u32[]{:S(2)}) collective-permute-start(bf16[8,576,512]{2,1,0:T(8,128)(2,1)} %bitcast.350), channel_id=1, source_target_pairs={{0,1},{1,0},{2,6},{3,7},{4,5},{5,4},{6,2},{7,3},{8,9},{9,8},{10,14... | collective-permute-start | bytes 14155784 | tf_op jit(solution)/shard_map/ppermute | solution.py:42
  598.6 96.9 %reduce-scatter.17.cloned.1.call-start = ((), (), s32[]{:S(2)}) async-start(), calls=%async_computation.12 | async-start | bytes 6291456 | tf_op jit(solution)/shard_map/reduce_scatter | solution.py:175
  598.6 68.5 %collective-permute-start.30 = (bf16[4,576,512]{2,1,0:T(8,128)(2,1)}, bf16[4,576,512]{2,1,0:T(8,128)(2,1)S(1)}, u32[]{:S(2)}, u32[]{:S(2)}) collective-permute-start(bf16[4,576,512]{2,1,0:T(8,128)(2,1)} %get-tuple-element.405), channel_id=1, source_target_pairs={{0,4},{1,5},{2,3},{3,2},{4,0},{5,1},{6,7},{7,6},{8,12},{9,13},{10,... | collective-permute-start | bytes 7077896 | tf_op jit(solution)/shard_map/ppermute | solution.py:42
  669.2 33.7 %reduce-scatter.15.cloned.1.call-start = ((), (), s32[]{:S(2)}) async-start(), calls=%async_computation.11 | async-start | bytes 14155776 | tf_op jit(solution)/shard_map/reduce_scatter | solution.py:175
  669.8 101.0 %reduce-scatter.19.cloned.1.call-start = ((), (), s32[]{:S(2)}) async-start(), calls=%async_computation.13 | async-start | bytes 14155776 | tf_op jit(solution)/shard_map/reduce_scatter | solution.py:175
  669.9 25.6 %collective-permute-start.31 = (bf16[8,256,512]{2,1,0:T(8,128)(2,1)}, bf16[8,256,512]{2,1,0:T(8,128)(2,1)}, u32[]{:S(2)}, u32[]{:S(2)}) collective-permute-start(bf16[8,256,512]{2,1,0:T(8,128)(2,1)} %bitcast.351), channel_id=1, source_target_pairs={{0,1},{1,0},{2,6},{3,7},{4,5},{5,4},{6,2},{7,3},{8,9},{9,8},{10,14... | collective-permute-start | bytes 6291464 | tf_op jit(solution)/shard_map/ppermute | solution.py:42
  671.9 28.8 %collective-permute-start.32 = (bf16[576,512]{1,0:T(8,128)(2,1)}, bf16[576,512]{1,0:T(8,128)(2,1)S(1)}, u32[]{:S(2)}, u32[]{:S(2)}) collective-permute-start(bf16[576,512]{1,0:T(8,128)(2,1)} %get-tuple-element.427), channel_id=1, source_target_pairs={{0,24},{1,25},{2,26},{3,27},{4,28},{5,29},{6,30},{7,31},{8,0},{9,1... | collective-permute-start | bytes 1769480 | tf_op jit(solution)/shard_map/ppermute | solution.py:42
  703.0 104.3 %reduce-scatter.21.cloned.1.call-start = ((), (), s32[]{:S(2)}) async-start(), calls=%async_computation.14 | async-start | bytes 6291456 | tf_op jit(solution)/shard_map/reduce_scatter | solution.py:175
  703.0 67.7 %collective-permute-start.33 = (bf16[8,576,512]{2,1,0:T(8,128)(2,1)}, bf16[8,576,512]{2,1,0:T(8,128)(2,1)}, u32[]{:S(2)}, u32[]{:S(2)}) collective-permute-start(bf16[8,576,512]{2,1,0:T(8,128)(2,1)} %bitcast.349), channel_id=1, source_target_pairs={{0,1},{1,0},{2,6},{3,7},{4,5},{5,4},{6,2},{7,3},{8,9},{9,8},{10,14... | collective-permute-start | bytes 14155784 | tf_op jit(solution)/shard_map/ppermute | solution.py:42
  705.4 46.0 %collective-permute-start.35 = (bf16[576,512]{1,0:T(8,128)(2,1)S(1)}, bf16[576,512]{1,0:T(8,128)(2,1)S(1)}, u32[]{:S(2)}, u32[]{:S(2)}) collective-permute-start(bf16[576,512]{1,0:T(8,128)(2,1)S(1)} %get-tuple-element.425), channel_id=1, source_target_pairs={{0,8},{1,9},{2,10},{3,11},{4,12},{5,13},{6,14},{7,15},{8,16},{9,17... | collective-permute-start | bytes 1769480 | tf_op jit(solution)/shard_map/ppermute | solution.py:42
  706.6 44.8 %collective-permute-start.34 = (bf16[576,512]{1,0:T(8,128)(2,1)S(1)}, bf16[576,512]{1,0:T(8,128)(2,1)S(1)}, u32[]{:S(2)}, u32[]{:S(2)}) collective-permute-start(bf16[576,512]{1,0:T(8,128)(2,1)S(1)} %get-tuple-element.426), channel_id=1, source_target_pairs={{0,16},{1,17},{2,18},{3,19},{4,20},{5,21},{6,22},{7,23},{8,24},{9,... | collective-permute-start | bytes 1769480 | tf_op jit(solution)/shard_map/ppermute | solution.py:42
  709.3 67.1 %collective-permute-start.38 = (bf16[4,256,512]{2,1,0:T(8,128)(2,1)}, bf16[4,256,512]{2,1,0:T(8,128)(2,1)S(1)}, u32[]{:S(2)}, u32[]{:S(2)}) collective-permute-start(bf16[4,256,512]{2,1,0:T(8,128)(2,1)} %get-tuple-element.411), channel_id=1, source_target_pairs={{0,4},{1,5},{2,3},{3,2},{4,0},{5,1},{6,7},{7,6},{8,12},{9,13},{10,... | collective-permute-start | bytes 3145736 | tf_op jit(solution)/shard_map/ppermute | solution.py:42
  778.9 58.2 %reduce-scatter.23.cloned.1.call-start = ((), (), s32[]{:S(2)}) async-start(), calls=%async_computation.15 | async-start | bytes 6291456 | tf_op jit(solution)/shard_map/reduce_scatter | solution.py:175
  778.9 28.4 %collective-permute-start.39 = (bf16[4,576,512]{2,1,0:T(8,128)(2,1)}, bf16[4,576,512]{2,1,0:T(8,128)(2,1)}, u32[]{:S(2)}, u32[]{:S(2)}) collective-permute-start(bf16[4,576,512]{2,1,0:T(8,128)(2,1)} %get-tuple-element.319), channel_id=1, source_target_pairs={{0,4},{1,5},{2,3},{3,2},{4,0},{5,1},{6,7},{7,6},{8,12},{9,13},{10,... | collective-permute-start | bytes 7077896 | tf_op jit(solution)/shard_map/ppermute | solution.py:42
  781.2 29.8 %collective-permute-start.42 = (bf16[256,512]{1,0:T(8,128)(2,1)}, bf16[256,512]{1,0:T(8,128)(2,1)}, u32[]{:S(2)}, u32[]{:S(2)}) collective-permute-start(bf16[256,512]{1,0:T(8,128)(2,1)} %get-tuple-element.443), channel_id=1, source_target_pairs={{0,8},{1,9},{2,10},{3,11},{4,12},{5,13},{6,14},{7,15},{8,16},{9,17... | collective-permute-start | bytes 786440 | tf_op jit(solution)/shard_map/ppermute | solution.py:42
  781.2 29.8 %collective-permute-start.41 = (bf16[256,512]{1,0:T(8,128)(2,1)}, bf16[256,512]{1,0:T(8,128)(2,1)}, u32[]{:S(2)}, u32[]{:S(2)}) collective-permute-start(bf16[256,512]{1,0:T(8,128)(2,1)} %get-tuple-element.444), channel_id=1, source_target_pairs={{0,16},{1,17},{2,18},{3,19},{4,20},{5,21},{6,22},{7,23},{8,24},{9,... | collective-permute-start | bytes 786440 | tf_op jit(solution)/shard_map/ppermute | solution.py:42
  783.2 27.9 %collective-permute-start.40 = (bf16[256,512]{1,0:T(8,128)(2,1)}, bf16[256,512]{1,0:T(8,128)(2,1)}, u32[]{:S(2)}, u32[]{:S(2)}) collective-permute-start(bf16[256,512]{1,0:T(8,128)(2,1)} %get-tuple-element.445), channel_id=1, source_target_pairs={{0,24},{1,25},{2,26},{3,27},{4,28},{5,29},{6,30},{7,31},{8,0},{9,1... | collective-permute-start | bytes 786440 | tf_op jit(solution)/shard_map/ppermute | solution.py:42
  811.1 26.0 %collective-permute-start.43 = (bf16[8,256,512]{2,1,0:T(8,128)(2,1)}, bf16[8,256,512]{2,1,0:T(8,128)(2,1)}, u32[]{:S(2)}, u32[]{:S(2)}) collective-permute-start(bf16[8,256,512]{2,1,0:T(8,128)(2,1)} %bitcast.352), channel_id=1, source_target_pairs={{0,1},{1,0},{2,6},{3,7},{4,5},{5,4},{6,2},{7,3},{8,9},{9,8},{10,14... | collective-permute-start | bytes 6291464 | tf_op jit(solution)/shard_map/ppermute | solution.py:42
  814.0 26.2 %collective-permute-start.45 = (bf16[576,512]{1,0:T(8,128)(2,1)}, bf16[576,512]{1,0:T(8,128)(2,1)}, u32[]{:S(2)}, u32[]{:S(2)}) collective-permute-start(bf16[576,512]{1,0:T(8,128)(2,1)} %get-tuple-element.423), channel_id=1, source_target_pairs={{0,16},{1,17},{2,18},{3,19},{4,20},{5,21},{6,22},{7,23},{8,24},{9,... | collective-permute-start | bytes 1769480 | tf_op jit(solution)/shard_map/ppermute | solution.py:42
  814.9 25.3 %collective-permute-start.44 = (bf16[576,512]{1,0:T(8,128)(2,1)}, bf16[576,512]{1,0:T(8,128)(2,1)}, u32[]{:S(2)}, u32[]{:S(2)}) collective-permute-start(bf16[576,512]{1,0:T(8,128)(2,1)} %get-tuple-element.424), channel_id=1, source_target_pairs={{0,24},{1,25},{2,26},{3,27},{4,28},{5,29},{6,30},{7,31},{8,0},{9,1... | collective-permute-start | bytes 1769480 | tf_op jit(solution)/shard_map/ppermute | solution.py:42
  840.1 30.3 %collective-permute-start.46 = (bf16[4,256,512]{2,1,0:T(8,128)(2,1)S(1)}, bf16[4,256,512]{2,1,0:T(8,128)(2,1)S(1)}, u32[]{:S(2)}, u32[]{:S(2)}) collective-permute-start(bf16[4,256,512]{2,1,0:T(8,128)(2,1)S(1)} %get-tuple-element.331), channel_id=1, source_target_pairs={{0,4},{1,5},{2,3},{3,2},{4,0},{5,1},{6,7},{7,6},{8,12},{9,13},{10,... | collective-permute-start | bytes 3145736 | tf_op jit(solution)/shard_map/ppermute | solution.py:42
  870.9 36.0 %collective-permute-start.50 = (bf16[1,512,1024]{2,1,0:T(8,128)(2,1)S(1)}, bf16[1,512,1024]{2,1,0:T(8,128)(2,1)S(1)}, u32[]{:S(2)}, u32[]{:S(2)}) collective-permute-start(bf16[1,512,1024]{2,1,0:T(8,128)(2,1)S(1)} %select_convert_fusion), channel_id=1, source_target_pairs={{0,1},{1,0},{2,3},{3,2},{4,5},{5,4},{6,7},{7,6},{8,9},{9,8},{10,11... | collective-permute-start | bytes 3145736 | tf_op jit(solution)/shard_map/ppermute | solution.py:1177
  873.6 33.4 %collective-permute-start.53 = (bf16[256,512]{1,0:T(8,128)(2,1)S(1)}, bf16[256,512]{1,0:T(8,128)(2,1)S(1)}, u32[]{:S(2)}, u32[]{:S(2)}) collective-permute-start(bf16[256,512]{1,0:T(8,128)(2,1)S(1)} %get-tuple-element.441), channel_id=1, source_target_pairs={{0,16},{1,17},{2,18},{3,19},{4,20},{5,21},{6,22},{7,23},{8,24},{9,... | collective-permute-start | bytes 786440 | tf_op jit(solution)/shard_map/ppermute | solution.py:42
  876.7 30.2 %collective-permute-start.52 = (bf16[256,512]{1,0:T(8,128)(2,1)S(1)}, bf16[256,512]{1,0:T(8,128)(2,1)S(1)}, u32[]{:S(2)}, u32[]{:S(2)}) collective-permute-start(bf16[256,512]{1,0:T(8,128)(2,1)S(1)} %get-tuple-element.442), channel_id=1, source_target_pairs={{0,24},{1,25},{2,26},{3,27},{4,28},{5,29},{6,30},{7,31},{8,0},{9,1... | collective-permute-start | bytes 786440 | tf_op jit(solution)/shard_map/ppermute | solution.py:42
  (66 other events, 738.2 us)
Sparse Core Ops, SparseCore 0:
  518.9 16.2 reduce-scatter.8
  539.5 16.9 reduce-scatter.10
  598.7 11.8 reduce-scatter.12
  669.3 12.3 reduce-scatter.16
  683.8 19.0 reduce-scatter.14
  705.1 19.0 reduce-scatter.18
  779.0 19.0 reduce-scatter.20
  811.2 20.9 reduce-scatter.22

commit v5 on v4

--- a/solution.py
+++ b/solution.py
@@ -512,7 +512,7 @@
 
 def hidden_step(x_ref, lookup_ref, content_ref, act_ref, total_ref, first):
     tokens = x_ref.shape[0]
-    tile = min(256, tokens)
+    tile = min(512, tokens)
     _, dp, rows, width = lookup_ref.shape
     seq, group, grain, columns = content_ref.shape
     up = lookup_ref[0].reshape(dp * rows, width)
@@ -735,7 +735,7 @@
 
         def work(act_ref, lookup_ref, content_ref, first):
             up = lookup_ref[0].reshape(dp * cut.rows, cut.width)
-            size = min(256, tokens)
+            size = min(512, tokens)
             for t in range(0, tokens, size):
                 rows = slice(t, t + size)
                 act = act_ref[0, rows, :].astype(F32)

time: 953 us -> 946 us (level)
  no operation moved by 1% of the time
where the time goes in v5:
time: 946 us; the launch traced here: 932 us
  Pallas kernels  471 us (50%)
  waiting for transfers between devices  238 us (25%)
  starting transfers between devices  88 us (9%)
  other arithmetic  67.2 us (7%)
  local copies, waits for them, and re-layouts  51.9 us (5%)
  between operations  15.9 us (2%)
    ppermute x51, waiting for transfers between devices, moved(): return lax.ppermute(array, BOTH, pairs)  194 us
    pallas_call x2, Pallas kernels, channel_back(): pl.pallas_call(body, grid=(2 * steps,), in_specs=[SCALAR, held(g.shape),...  130 us
    ppermute x51, starting transfers between devices, moved(): return lax.ppermute(array, BOTH, pairs)  80.6 us
    pallas_call x2, Pallas kernels, time_back(): pl.pallas_call(body, grid=(tiles,), in_specs=[SCALAR, block, fixed(fix.sh...  70.1 us
    pallas_call x4, Pallas kernels, arrange(): pl.pallas_call(body, grid_spec=pltpu.PrefetchScalarGridSpec(num_scalar_pr...  48.6 us
    pallas_call x2, Pallas kernels, channel_two(): pl.pallas_call(body, grid=(cut.steps,), in_specs=[held(s.shape), held(xk....  43.1 us
    ppermute x5, waiting for transfers between devices, partner_y(): return lax.ppermute(array, 'seq', [(0, 1), (1, 0)])  41.6 us
    pallas_call x2, Pallas kernels, out_back(): pl.pallas_call(body, grid=(tokens // tile,), in_specs=[SCALAR, block, fix...  40.4 us
  transfers between devices with their start and end apart: 64, of which 25 were waited for; matrix products, arithmetic and copies ran while one was open for 7% of the time, Pallas kernels for 48%

profile of v5, /device:TPU:1, one launch (start us, length us, event | category | flops | bytes accessed | tf_op | source)
XLA Modules:
  0.0 932.5 jit_solution(7532463244387888941)
XLA Ops:
  20.0 3.9 collective-permute-start.5
  24.4 17.0 %collective-permute-done = bf16[1,512,1024]{2,1,0:T(8,128)(2,1)S(1)} collective-permute-done((bf16[1,512,1024]{2,1,0:T(8,128)(2,1)S(1)}, bf16[1,512,1024]{2,1,0:T(8,128)(2,1)S(1)}, u32[]{:S(2)}, u32[]{:S(2)}) %collective-permute-start) | collective-permute-done | bytes 1048608 | tf_op jit(solution)/shard_map/ppermute | solution.py:1177
  48.9 14.6 %collective-permute-done.7 = bf16[2,288,512]{2,1,0:T(8,128)(2,1)S(1)} collective-permute-done((bf16[2,288,512]{2,1,0:T(8,128)(2,1)S(1)}, bf16[2,288,512]{2,1,0:T(8,128)(2,1)S(1)}, u32[]{:S(2)}, u32[]{:S(2)}) %collective-permute-start.7) | collective-permute-done | bytes 589856 | tf_op jit(solution)/shard_map/ppermute | solution.py:42
  68.7 21.9 %collective-permute-done.8.other_ref = bf16[8,256,512]{2,1,0:T(8,128)(2,1)} collective-permute-done((bf16[8,256,512]{2,1,0:T(8,128)(2,1)S(1)}, bf16[8,256,512]{2,1,0:T(8,128)(2,1)}, u32[]{:S(2)}, u32[]{:S(2)}) %collective-permute-start.8) | collective-permute-done | bytes 2097184 | tf_op jit(solution)/shard_map/ppermute | solution.py:42
  90.6 10.9 %shard_map.229 = bf16[16,256,512]{2,1,0:T(8,128)(2,1)} custom-call(s32[7,16]{1,0:T(8,128)} %dynamic-slice_bitcast_fusion.table_ref, bf16[8,256,512]{2,1,0:T(8,128)(2,1)} %copy-done.11, bf16[8,256,512]{2,1,0:T(8,128)(2,1)} %collective-permute-done.8.other_ref), custom_call_target="tpu_custom_call" | custom-call | flops 1 | bytes 1 | tf_op jit(solution)/shard_map/pallas_call | solution.py:117
  101.5 4.3 collective-permute-done.9
  112.3 24.6 %collective-permute-done.1 = s32[1,512]{1,0:T(1,128)S(1)} collective-permute-done((s32[1,512]{1,0:T(1,128)S(1)}, s32[1,512]{1,0:T(1,128)S(1)}, u32[]{:S(2)}, u32[]{:S(2)}) %collective-permute-start.1) | collective-permute-done | bytes 2080 | tf_op jit(solution)/shard_map/ppermute | solution.py:1177
  142.2 17.7 %shard_map.230 = (bf16[1024,1024]{1,0:T(8,128)(2,1)}, bf16[1024,1024]{1,0:T(8,128)(2,1)}, bf16[1024,1024]{1,0:T(8,128)(2,1)}, f32[1024,1024]{1,0:T(8,128)}, f32[...) custom-call(s32[1]{0:T(128)} %bitcast.core_ref, ...), custom_call_target="tpu_custom_call" | custom-call | flops 1 | bytes 1 | tf_op jit(solution)/shard_map/pallas_call | solution.py:401
  168.1 17.5 %shard_map.231 = (bf16[1024,1024]{1,0:T(8,128)(2,1)}, f32[1024,1024]{1,0:T(8,128)}, f32[1024,1024]{1,0:T(8,128)}, f32[1024,1024]{1,0:T(8,128)}) custom-call(s32[1]{0:T(128)} %bitcast.core_ref, bf16[1024,1024]{1,0:T(8,128)(2,1)} %maximum_bitcast_fusion.s_ref, f32[1024,1024]{1,0:T(8,128)} %get-tuple-element.195.k_ref, f32[1024,1024]{1,0:T(8,128)} %get-tuple-element.196.v_ref, ...), custom_call_target="tpu_custom_call" | custom-call | flops 1 | bytes 1 | tf_op jit(solution)/shard_map/pallas_call | solution.py:468
  187.8 8.0 collective-permute-start.20
  195.8 4.3 collective-permute-start.19
  201.5 8.9 collective-permute-done.20
  210.5 19.0 %collective-permute-done.19 = bf16[2,288,512]{2,1,0:T(8,128)(2,1)} collective-permute-done((bf16[2,288,512]{2,1,0:T(8,128)(2,1)}, bf16[2,288,512]{2,1,0:T(8,128)(2,1)}, u32[]{:S(2)}, u32[]{:S(2)}) %collective-permute-start.19) | collective-permute-done | bytes 589856 | tf_op jit(solution)/shard_map/ppermute | solution.py:42
  229.4 13.3 %shard_map.232 = bf16[16,576,512]{2,1,0:T(8,128)(2,1)} custom-call(s32[7,16]{1,0:T(8,128)} %dynamic-slice_bitcast_fusion.table_ref, bf16[8,576,512]{2,1,0:T(8,128)(2,1)} %copy-done.2, bf16[8,576,512]{2,1,0:T(8,128)(2,1)} %collective-permute-done.16.other_ref), custom_call_target="tpu_custom_call" | custom-call | flops 1 | bytes 1 | tf_op jit(solution)/shard_map/pallas_call | solution.py:117
  242.8 13.9 %collective-permute-done.17 = bf16[4,256,512]{2,1,0:T(8,128)(2,1)S(1)} collective-permute-done((bf16[4,256,512]{2,1,0:T(8,128)(2,1)S(1)}, bf16[4,256,512]{2,1,0:T(8,128)(2,1)S(1)}, u32[]{:S(2)}, u32[]{:S(2)}) %collective-permute-start.17) | collective-permute-done | bytes 1048608 | tf_op jit(solution)/shard_map/ppermute | solution.py:42
  258.9 18.5 %shard_map.233 = (bf16[1024,1024]{1,0:T(8,128)(2,1)}, bf16[1024,1024]{1,0:T(8,128)(2,1)}, f32[4,1,1024]{2,1,0:T(1,128)}, bf16[4,1024,512]{2,1,0:T(8,128)(2,1)}, f32[1024,1024]{1,0:T(8,128)}) custom-call(f32[1024,1024]{1,0:T(8,128)} %get-tuple-element.198.s_ref, f32[1,1024]{1,0:T(1,128)} %broadcast_1_before_ref_fix_ref.2.before_ref.fix_ref, ...), custom_call_target="tpu_custom_call" | custom-call | flops 1 | bytes 1 | tf_op jit(solution)/shard_map/pallas_call | solution.py:560
  282.2 10.9 %shard_map.234 = bf16[16,256,512]{2,1,0:T(8,128)(2,1)} custom-call(s32[7,16]{1,0:T(8,128)} %dynamic-slice_bitcast_fusion.table_ref, bf16[8,256,512]{2,1,0:T(8,128)(2,1)} %copy-done.12, bf16[8,256,512]{2,1,0:T(8,128)(2,1)} %collective-permute-done.21.other_ref), custom_call_target="tpu_custom_call" | custom-call | flops 1 | bytes 1 | tf_op jit(solution)/shard_map/pallas_call | solution.py:117
  296.4 21.9 %shard_map.235 = (bf16[4,1024,512]{2,1,0:T(8,128)(2,1)}, bf16[1024,1024]{1,0:T(8,128)(2,1)}, bf16[1024,1024]{1,0:T(8,128)(2,1)}, f32[1024,1024]{1,0:T(8,128)}) custom-call(f32[1024,1024]{1,0:T(8,128)} %get-tuple-element.198.s_ref, bf16[1024,1024]{1,0:T(8,128)(2,1)} %get-tuple-element.210.xk_ref, bf16[1024,1024]{1,0:T(8,128)(2,1)} %get-tuple-element.211.xr_ref, ...), custom_call_target="tpu_custom_call" | custom-call | flops 1 | bytes 1 | tf_op jit(solution)/shard_map/pallas_call | solution.py:609
  327.8 6.2 collective-permute-done.24
  336.0 18.0 %shard_map.236 = (bf16[1024,1024]{1,0:T(8,128)(2,1)}, bf16[1024,1024]{1,0:T(8,128)(2,1)}, bf16[1024,1024]{1,0:T(8,128)(2,1)}, f32[1024,1024]{1,0:T(8,128)}, f32[...) custom-call(s32[1]{0:T(128)} %bitcast.core_ref, ...), custom_call_target="tpu_custom_call" | custom-call | flops 1 | bytes 1 | tf_op jit(solution)/shard_map/pallas_call | solution.py:401
  354.0 18.3 %shard_map.237 = (bf16[1024,1024]{1,0:T(8,128)(2,1)}, f32[1024,1024]{1,0:T(8,128)}, f32[1024,1024]{1,0:T(8,128)}, f32[1024,1024]{1,0:T(8,128)}) custom-call(s32[1]{0:T(128)} %bitcast.core_ref, f32[1024,1024]{1,0:T(8,128)} %get-tuple-element.223.s_ref, f32[1024,1024]{1,0:T(8,128)} %get-tuple-element.224.k_ref, f32[1024,1024]{1,0:T(8,128)} %get-tuple-element.225.v_ref, ...), custom_call_target="tpu_custom_call" | custom-call | flops 1 | bytes 1 | tf_op jit(solution)/shard_map/pallas_call | solution.py:468
  372.4 4.4 collective-permute-done.25.other_ref
  379.0 13.5 %shard_map.238 = bf16[16,576,512]{2,1,0:T(8,128)(2,1)} custom-call(s32[7,16]{1,0:T(8,128)} %dynamic-slice_bitcast_fusion.table_ref, bf16[8,576,512]{2,1,0:T(8,128)(2,1)} %constant_dynamic-update-slice_fusion.38.own_ref, bf16[8,576,512]{2,1,0:T(8,128)(2,1)} %copy-done.10), custom_call_target="tpu_custom_call" | custom-call | flops 1 | bytes 1 | tf_op jit(solution)/shard_map/pallas_call | solution.py:117
  392.4 5.0 collective-permute-start.26
  398.2 18.9 %shard_map.239 = (bf16[1024,1024]{1,0:T(8,128)(2,1)}, bf16[1024,1024]{1,0:T(8,128)(2,1)}, f32[4,1,1024]{2,1,0:T(1,128)}, bf16[4,1024,512]{2,1,0:T(8,128)(2,1)}, f32[1024,1024]{1,0:T(8,128)}) custom-call(f32[1024,1024]{1,0:T(8,128)} %get-tuple-element.227.s_ref, f32[1,1024]{1,0:T(1,128)} %broadcast_1_before_ref_fix_ref.2.before_ref.fix_ref, ...), custom_call_target="tpu_custom_call" | custom-call | flops 1 | bytes 1 | tf_op jit(solution)/shard_map/pallas_call | solution.py:560
  420.3 21.3 %shard_map.240 = (bf16[4,1024,512]{2,1,0:T(8,128)(2,1)}, bf16[1024,1024]{1,0:T(8,128)(2,1)}, bf16[1024,1024]{1,0:T(8,128)(2,1)}, bf16[1024,1024]{1,0:T(8,128)(2,1)}) custom-call(f32[1024,1024]{1,0:T(8,128)} %get-tuple-element.227.s_ref, bf16[1024,1024]{1,0:T(8,128)(2,1)} %get-tuple-element.232.xk_ref, bf16[1024,1024]{1,0:T(8,128)(2,1)} %get-tuple-element.233.xr_ref, ...), custom_call_target="tpu_custom_call" | custom-call | flops 1 | bytes 1 | tf_op jit(solution)/shard_map/pallas_call | solution.py:609
  447.6 63.9 %shard_map.241 = (bf16[2,8,2,288,512]{4,3,2,1,0:T(8,128)(2,1)}, bf16[2,8,2,288,512]{4,3,2,1,0:T(8,128)(2,1)}, f32[1024,1024]{1,0:T(8,128)}, f32[1,1024]{1,0:T(1,128)}, f32[4,1024]{1,0:T(4,128)}) custom-call(s32[1]{0:T(128)} %bitcast.core_ref, bf16[1024,1024]{1,0:T(8,128)(2,1)} %maximum_bitcast_fusion.1.g_ref, ...), custom_call_target="tpu_custom_call" | custom-call | flops 1 | bytes 1 | tf_op jit(solution)/shard_map/pallas_call | solution.py:819
  513.3 20.5 %shard_map.242 = (bf16[1024,1024]{1,0:T(8,128)(2,1)}, bf16[1024,1024]{1,0:T(8,128)(2,1)}, f32[1024,1024]{1,0:T(8,128)}, f32[1024,1024]{1,0:T(8,128)}, f32[1,2,1024]{2,1,0:T(2,128)}) custom-call(s32[1]{0:T(128)} %bitcast.core_ref, f32[1024,1024]{1,0:T(8,128)} %get-tuple-element.246.g_ref, f32[1,1024]{1,0:T(1,128)} %broadcast_1_before_ref_fix_ref.2.before_ref.fix_ref, ...), custom_call_target="tpu_custom_call" | custom-call | flops 1 | bytes 1 | tf_op jit(solution)/shard_map/pallas_call | solution.py:896
  534.5 33.9 %shard_map.243 = (bf16[1024,1024]{1,0:T(8,128)(2,1)}, bf16[1024,1024]{1,0:T(8,128)(2,1)}, f32[1024,1024]{1,0:T(8,128)}, f32[1,1024]{1,0:T(1,128)}, f32[7,1024]{1,0:T(8,128)}) custom-call(s32[1]{0:T(128)} %bitcast.core_ref, f32[1024,1024]{1,0:T(8,128)} %get-tuple-element.246.g_ref, f32[1,1024]{1,0:T(1,128)} %broadcast_1_before_ref_fix_ref.2.before_ref.fix_ref, ...), custom_call_target="tpu_custom_call" | custom-call | flops 1 | bytes 1 | tf_op jit(solution)/shard_map/pallas_call | solution.py:989
  568.5 15.0 %shard_map.244 = (bf16[2,8,2,128,512]{4,3,2,1,0:T(8,128)(2,1)}, bf16[2,8,2,128,512]{4,3,2,1,0:T(8,128)(2,1)}) custom-call(s32[7,16]{1,0:T(8,128)} %dynamic-slice_bitcast_fusion.table_ref, bf16[1024,1024]{1,0:T(8,128)(2,1)} %get-tuple-element.259.refs_0_, bf16[1024,1024]{1,0:T(8,128)(2,1)} %get-tuple-element.260.refs_1_, ...), custom_call_target="tpu_custom_call" | custom-call | flops 1 | bytes 1 | tf_op jit(solution)/shard_map/pallas_call | solution.py:1090
  583.4 4.2 collective-permute-done.29
  587.6 5.4 add_convert_fusion.4
  593.8 66.1 %shard_map.245 = (bf16[2,8,2,288,512]{4,3,2,1,0:T(8,128)(2,1)}, bf16[2,8,2,288,512]{4,3,2,1,0:T(8,128)(2,1)}, f32[1024,1024]{1,0:T(8,128)}, f32[1,1024]{1,0:T(1,128)}, f32[4,1024]{1,0:T(4,128)}) custom-call(s32[1]{0:T(128)} %bitcast.core_ref, f32[1024,1024]{1,0:T(8,128)} %get-tuple-element.268.g_ref, ...), custom_call_target="tpu_custom_call" | custom-call | flops 1 | bytes 1 | tf_op jit(solution)/shard_map/pallas_call | solution.py:819
  664.7 19.9 %shard_map.246 = (bf16[1024,1024]{1,0:T(8,128)(2,1)}, bf16[1024,1024]{1,0:T(8,128)(2,1)}, f32[1024,1024]{1,0:T(8,128)}, f32[1024,1024]{1,0:T(8,128)}, f32[1,2,1024]{2,1,0:T(2,128)}) custom-call(s32[1]{0:T(128)} %bitcast.core_ref, f32[1024,1024]{1,0:T(8,128)} %get-tuple-element.283.g_ref, f32[1,1024]{1,0:T(1,128)} %broadcast_1_before_ref_fix_ref.2.before_ref.fix_ref, ...), custom_call_target="tpu_custom_call" | custom-call | flops 1 | bytes 1 | tf_op jit(solution)/shard_map/pallas_call | solution.py:896
  684.6 3.7 collective-permute-done.31
  688.2 5.2 add_convert_fusion.10
  703.4 36.1 %shard_map.247 = (bf16[1024,1024]{1,0:T(8,128)(2,1)}, bf16[1024,1024]{1,0:T(8,128)(2,1)}, f32[1024,1024]{1,0:T(8,128)}, f32[1,1024]{1,0:T(1,128)}, f32[7,1024]{1,0:T(8,128)}) custom-call(s32[1]{0:T(128)} %bitcast.core_ref, f32[1024,1024]{1,0:T(8,128)} %get-tuple-element.283.g_ref, f32[1,1024]{1,0:T(1,128)} %broadcast_1_before_ref_fix_ref.2.before_ref.fix_ref, ...), custom_call_target="tpu_custom_call" | custom-call | flops 1 | bytes 1 | tf_op jit(solution)/shard_map/pallas_call | solution.py:989
  744.3 15.0 %shard_map.248 = (bf16[2,8,2,128,512]{4,3,2,1,0:T(8,128)(2,1)}, bf16[2,8,2,128,512]{4,3,2,1,0:T(8,128)(2,1)}) custom-call(s32[7,16]{1,0:T(8,128)} %dynamic-slice_bitcast_fusion.table_ref, bf16[1024,1024]{1,0:T(8,128)(2,1)} %get-tuple-element.301.refs_0_, bf16[1024,1024]{1,0:T(8,128)(2,1)} %get-tuple-element.304.refs_1_, ...), custom_call_target="tpu_custom_call" | custom-call | flops 1 | bytes 1 | tf_op jit(solution)/shard_map/pallas_call | solution.py:1090
  759.4 4.2 collective-permute-done.37
  763.7 5.6 add_convert_fusion.2
  777.3 22.8 %collective-permute-done.39 = bf16[4,576,512]{2,1,0:T(8,128)(2,1)} collective-permute-done((bf16[4,576,512]{2,1,0:T(8,128)(2,1)}, bf16[4,576,512]{2,1,0:T(8,128)(2,1)}, u32[]{:S(2)}, u32[]{:S(2)}) %collective-permute-start.39) | collective-permute-done | bytes 2359328 | tf_op jit(solution)/shard_map/ppermute | solution.py:42
  800.2 3.7 add_convert_fusion
  809.1 20.8 %collective-permute-done.43 = bf16[8,256,512]{2,1,0:T(8,128)(2,1)} collective-permute-done((bf16[8,256,512]{2,1,0:T(8,128)(2,1)}, bf16[8,256,512]{2,1,0:T(8,128)(2,1)}, u32[]{:S(2)}, u32[]{:S(2)}) %collective-permute-start.43) | collective-permute-done | bytes 2097184 | tf_op jit(solution)/shard_map/ppermute | solution.py:42
  834.9 11.9 %collective-permute-start.47 = (f32[2,11,1024]{2,1,0:T(8,128)S(1)}, f32[2,11,1024]{2,1,0:T(8,128)S(1)}, u32[]{:S(2)}, u32[]{:S(2)}) collective-permute-start(f32[2,11,1024]{2,1,0:T(8,128)S(1)} %add.117), channel_id=1, source_target_pairs={{0,2},{1,3},{2,0},{3,1},{4,6},{5,7},{6,4},{7,5},{8,10},{9,11},{10,... | collective-permute-start | bytes 270344 | tf_op jit(solution)/shard_map/ppermute | solution.py:42
  857.3 5.9 collective-permute-done.49
  871.9 9.8 %collective-permute-done.51 = bf16[576,512]{1,0:T(8,128)(2,1)S(1)} collective-permute-done((bf16[576,512]{1,0:T(8,128)(2,1)S(1)}, bf16[576,512]{1,0:T(8,128)(2,1)S(1)}, u32[]{:S(2)}, u32[]{:S(2)}) %collective-permute-start.51) | collective-permute-done | bytes 589856 | tf_op jit(solution)/shard_map/ppermute | solution.py:42
  881.7 5.6 collective-permute-done.54
  887.3 12.5 %collective-permute-done.53 = bf16[256,512]{1,0:T(8,128)(2,1)S(1)} collective-permute-done((bf16[256,512]{1,0:T(8,128)(2,1)S(1)}, bf16[256,512]{1,0:T(8,128)(2,1)S(1)}, u32[]{:S(2)}, u32[]{:S(2)}) %collective-permute-start.53) | collective-permute-done | bytes 262176 | tf_op jit(solution)/shard_map/ppermute | solution.py:42
  (397 shorter events, 168.1 us)
Async XLA Ops:
  7.2 526.7 %reduce-scatter.9.cloned.1.call-start = ((), (), s32[]{:S(2)}) async-start(), calls=%async_computation.8 | async-start | bytes 14155776 | tf_op jit(solution)/shard_map/reduce_scatter | solution.py:175
  15.1 26.3 %collective-permute-start = (bf16[1,512,1024]{2,1,0:T(8,128)(2,1)S(1)}, bf16[1,512,1024]{2,1,0:T(8,128)(2,1)S(1)}, u32[]{:S(2)}, u32[]{:S(2)}) collective-permute-start(bf16[1,512,1024]{2,1,0:T(8,128)(2,1)S(1)} %broadcast_select_fusion.14), channel_id=1, source_target_pairs={{0,1},{1,0},{2,3},{3,2},{4,5},{5,4},{6,7},{7,6},{8,9},{9,8},{10,11... | collective-permute-start | bytes 3145736 | tf_op jit(solution)/shard_map/ppermute | solution.py:1177
  20.0 23.1 %collective-permute-start.5 = (bf16[2,128,512]{2,1,0:T(8,128)(2,1)S(1)}, bf16[2,128,512]{2,1,0:T(8,128)(2,1)S(1)}, u32[]{:S(2)}, u32[]{:S(2)}) collective-permute-start(bf16[2,128,512]{2,1,0:T(8,128)(2,1)S(1)} %get-tuple-element.439), channel_id=1, source_target_pairs={{0,24},{1,25},{2,26},{3,27},{4,28},{5,29},{6,30},{7,31},{8,0},{9,1... | collective-permute-start | bytes 786440 | tf_op jit(solution)/shard_map/ppermute | solution.py:42
  23.9 22.1 %collective-permute-start.4 = (bf16[2,128,512]{2,1,0:T(8,128)(2,1)S(1)}, bf16[2,128,512]{2,1,0:T(8,128)(2,1)S(1)}, u32[]{:S(2)}, u32[]{:S(2)}) collective-permute-start(bf16[2,128,512]{2,1,0:T(8,128)(2,1)S(1)} %get-tuple-element.439), channel_id=1, source_target_pairs={{0,16},{1,17},{2,18},{3,19},{4,20},{5,21},{6,22},{7,23},{8,24},{9,... | collective-permute-start | bytes 786440 | tf_op jit(solution)/shard_map/ppermute | solution.py:42
  23.9 22.1 %collective-permute-start.3 = (bf16[2,128,512]{2,1,0:T(8,128)(2,1)S(1)}, bf16[2,128,512]{2,1,0:T(8,128)(2,1)S(1)}, u32[]{:S(2)}, u32[]{:S(2)}) collective-permute-start(bf16[2,128,512]{2,1,0:T(8,128)(2,1)S(1)} %get-tuple-element.439), channel_id=1, source_target_pairs={{0,8},{1,9},{2,10},{3,11},{4,12},{5,13},{6,14},{7,15},{8,16},{9,17... | collective-permute-start | bytes 786440 | tf_op jit(solution)/shard_map/ppermute | solution.py:42
  64.5 26.1 %collective-permute-start.8 = (bf16[8,256,512]{2,1,0:T(8,128)(2,1)S(1)}, bf16[8,256,512]{2,1,0:T(8,128)(2,1)}, u32[]{:S(2)}, u32[]{:S(2)}) collective-permute-start(bf16[8,256,512]{2,1,0:T(8,128)(2,1)S(1)} %constant_dynamic-update-slice_fusion.32.own_ref), channel_id=1, source_target_pairs={{0,1},{1,0},{2,6},{3,7},{4,5},{5,4},{6,2},{7,3},{8,9},{9,8},{10,14... | collective-permute-start | bytes 6291464 | tf_op jit(solution)/shard_map/ppermute | solution.py:42
  66.8 34.8 %collective-permute-start.10 = (bf16[2,288,512]{2,1,0:T(8,128)(2,1)S(1)}, bf16[2,288,512]{2,1,0:T(8,128)(2,1)}, u32[]{:S(2)}, u32[]{:S(2)}) collective-permute-start(bf16[2,288,512]{2,1,0:T(8,128)(2,1)S(1)} %get-tuple-element.185), channel_id=1, source_target_pairs={{0,24},{1,25},{2,26},{3,27},{4,28},{5,29},{6,30},{7,31},{8,0},{9,1... | collective-permute-start | bytes 1769480 | tf_op jit(solution)/shard_map/ppermute | solution.py:42
  67.5 38.4 %collective-permute-start.9 = (bf16[2,288,512]{2,1,0:T(8,128)(2,1)S(1)}, bf16[2,288,512]{2,1,0:T(8,128)(2,1)}, u32[]{:S(2)}, u32[]{:S(2)}) collective-permute-start(bf16[2,288,512]{2,1,0:T(8,128)(2,1)S(1)} %get-tuple-element.185), channel_id=1, source_target_pairs={{0,16},{1,17},{2,18},{3,19},{4,20},{5,21},{6,22},{7,23},{8,24},{9,... | collective-permute-start | bytes 1769480 | tf_op jit(solution)/shard_map/ppermute | solution.py:42
  105.9 35.8 %collective-permute-start.11 = (bf16[16,256,512]{2,1,0:T(8,128)(2,1)}, bf16[16,256,512]{2,1,0:T(8,128)(2,1)}, u32[]{:S(2)}, u32[]{:S(2)}) collective-permute-start(bf16[16,256,512]{2,1,0:T(8,128)(2,1)} %shard_map.229), channel_id=1, source_target_pairs={{0,2},{1,3},{2,0},{3,1},{4,6},{5,7},{6,4},{7,5},{8,10},{9,11},{10,... | collective-permute-start | bytes 12582920 | tf_op jit(solution)/shard_map/ppermute | solution.py:42
  108.7 51.2 %collective-permute-start.12 = (bf16[4,576,512]{2,1,0:T(8,128)(2,1)S(1)}, bf16[4,576,512]{2,1,0:T(8,128)(2,1)}, u32[]{:S(2)}, u32[]{:S(2)}) collective-permute-start(bf16[4,576,512]{2,1,0:T(8,128)(2,1)S(1)} %pad_maximum_fusion.1), channel_id=1, source_target_pairs={{0,4},{1,5},{2,3},{3,2},{4,0},{5,1},{6,7},{7,6},{8,12},{9,13},{10,... | collective-permute-start | bytes 7077896 | tf_op jit(solution)/shard_map/ppermute | solution.py:42
  108.8 28.1 %collective-permute-start.1 = (s32[1,512]{1,0:T(1,128)S(1)}, s32[1,512]{1,0:T(1,128)S(1)}, u32[]{:S(2)}, u32[]{:S(2)}) collective-permute-start(s32[1,512]{1,0:T(1,128)S(1)} %broadcast_select_fusion.20), channel_id=1, source_target_pairs={{0,1},{1,0},{2,3},{3,2},{4,5},{5,4},{6,7},{7,6},{8,9},{9,8},{10,11... | collective-permute-start | bytes 6152 | tf_op jit(solution)/shard_map/ppermute | solution.py:1177
  163.6 65.9 %collective-permute-start.16 = (bf16[8,576,512]{2,1,0:T(8,128)(2,1)S(1)}, bf16[8,576,512]{2,1,0:T(8,128)(2,1)}, u32[]{:S(2)}, u32[]{:S(2)}) collective-permute-start(bf16[8,576,512]{2,1,0:T(8,128)(2,1)S(1)} %constant_dynamic-update-slice_fusion.34.own_ref), channel_id=1, source_target_pairs={{0,1},{1,0},{2,6},{3,7},{4,5},{5,4},{6,2},{7,3},{8,9},{9,8},{10,14... | collective-permute-start | bytes 14155784 | tf_op jit(solution)/shard_map/ppermute | solution.py:42
  187.8 22.6 %collective-permute-start.20 = (bf16[2,288,512]{2,1,0:T(8,128)(2,1)}, bf16[2,288,512]{2,1,0:T(8,128)(2,1)}, u32[]{:S(2)}, u32[]{:S(2)}) collective-permute-start(bf16[2,288,512]{2,1,0:T(8,128)(2,1)} %get-tuple-element.207), channel_id=1, source_target_pairs={{0,24},{1,25},{2,26},{3,27},{4,28},{5,29},{6,30},{7,31},{8,0},{9,1... | collective-permute-start | bytes 1769480 | tf_op jit(solution)/shard_map/ppermute | solution.py:42
  195.8 33.6 %collective-permute-start.19 = (bf16[2,288,512]{2,1,0:T(8,128)(2,1)}, bf16[2,288,512]{2,1,0:T(8,128)(2,1)}, u32[]{:S(2)}, u32[]{:S(2)}) collective-permute-start(bf16[2,288,512]{2,1,0:T(8,128)(2,1)} %get-tuple-element.207), channel_id=1, source_target_pairs={{0,16},{1,17},{2,18},{3,19},{4,20},{5,21},{6,22},{7,23},{8,24},{9,... | collective-permute-start | bytes 1769480 | tf_op jit(solution)/shard_map/ppermute | solution.py:42
  200.1 29.3 %collective-permute-start.18 = (bf16[2,288,512]{2,1,0:T(8,128)(2,1)}, bf16[2,288,512]{2,1,0:T(8,128)(2,1)}, u32[]{:S(2)}, u32[]{:S(2)}) collective-permute-start(bf16[2,288,512]{2,1,0:T(8,128)(2,1)} %get-tuple-element.207), channel_id=1, source_target_pairs={{0,8},{1,9},{2,10},{3,11},{4,12},{5,13},{6,14},{7,15},{8,16},{9,17... | collective-permute-start | bytes 1769480 | tf_op jit(solution)/shard_map/ppermute | solution.py:42
  242.8 50.4 %collective-permute-start.22 = (bf16[16,576,512]{2,1,0:T(8,128)(2,1)}, bf16[16,576,512]{2,1,0:T(8,128)(2,1)}, u32[]{:S(2)}, u32[]{:S(2)}) collective-permute-start(bf16[16,576,512]{2,1,0:T(8,128)(2,1)} %shard_map.232), channel_id=1, source_target_pairs={{0,2},{1,3},{2,0},{3,1},{4,6},{5,7},{6,4},{7,5},{8,10},{9,11},{10,... | collective-permute-start | bytes 28311560 | tf_op jit(solution)/shard_map/ppermute | solution.py:42
  256.9 25.4 %collective-permute-start.21 = (bf16[8,256,512]{2,1,0:T(8,128)(2,1)S(1)}, bf16[8,256,512]{2,1,0:T(8,128)(2,1)}, u32[]{:S(2)}, u32[]{:S(2)}) collective-permute-start(bf16[8,256,512]{2,1,0:T(8,128)(2,1)S(1)} %constant_dynamic-update-slice_fusion.36.own_ref), channel_id=1, source_target_pairs={{0,1},{1,0},{2,6},{3,7},{4,5},{5,4},{6,2},{7,3},{8,9},{9,8},{10,14... | collective-permute-start | bytes 6291464 | tf_op jit(solution)/shard_map/ppermute | solution.py:42
  282.2 36.0 %collective-permute-start.23 = (bf16[4,576,512]{2,1,0:T(8,128)(2,1)S(1)}, bf16[4,576,512]{2,1,0:T(8,128)(2,1)}, u32[]{:S(2)}, u32[]{:S(2)}) collective-permute-start(bf16[4,576,512]{2,1,0:T(8,128)(2,1)S(1)} %pad_maximum_fusion.2), channel_id=1, source_target_pairs={{0,4},{1,5},{2,3},{3,2},{4,0},{5,1},{6,7},{7,6},{8,12},{9,13},{10,... | collective-permute-start | bytes 7077896 | tf_op jit(solution)/shard_map/ppermute | solution.py:42
  323.3 53.5 %collective-permute-start.25 = (bf16[8,576,512]{2,1,0:T(8,128)(2,1)}, bf16[8,576,512]{2,1,0:T(8,128)(2,1)S(1)}, u32[]{:S(2)}, u32[]{:S(2)}) collective-permute-start(bf16[8,576,512]{2,1,0:T(8,128)(2,1)} %constant_dynamic-update-slice_fusion.38.own_ref), channel_id=1, source_target_pairs={{0,1},{1,0},{2,6},{3,7},{4,5},{5,4},{6,2},{7,3},{8,9},{9,8},{10,14... | collective-permute-start | bytes 14155784 | tf_op jit(solution)/shard_map/ppermute | solution.py:42
  392.4 24.7 %collective-permute-start.26 = (bf16[16,576,512]{2,1,0:T(8,128)(2,1)}, bf16[16,576,512]{2,1,0:T(8,128)(2,1)}, u32[]{:S(2)}, u32[]{:S(2)}) collective-permute-start(bf16[16,576,512]{2,1,0:T(8,128)(2,1)} %shard_map.238), channel_id=1, source_target_pairs={{0,2},{1,3},{2,0},{3,1},{4,6},{5,7},{6,4},{7,5},{8,10},{9,11},{10,... | collective-permute-start | bytes 28311560 | tf_op jit(solution)/shard_map/ppermute | solution.py:42
  398.1 46.5 %collective-permute-start.28 = (bf16[1,512,1024]{2,1,0:T(8,128)(2,1)S(1)}, bf16[1,512,1024]{2,1,0:T(8,128)(2,1)}, u32[]{:S(2)}, u32[]{:S(2)}) collective-permute-start(bf16[1,512,1024]{2,1,0:T(8,128)(2,1)S(1)} %broadcast_select_fusion.6), channel_id=1, source_target_pairs={{0,1},{1,0},{2,3},{3,2},{4,5},{5,4},{6,7},{7,6},{8,9},{9,8},{10,11... | collective-permute-start | bytes 3145736 | tf_op jit(solution)/shard_map/ppermute | solution.py:1177
  443.2 68.3 %collective-permute-start.27 = (bf16[1,512,1024]{2,1,0:T(8,128)(2,1)S(1)}, bf16[1,512,1024]{2,1,0:T(8,128)(2,1)S(1)}, u32[]{:S(2)}, u32[]{:S(2)}) collective-permute-start(bf16[1,512,1024]{2,1,0:T(8,128)(2,1)S(1)} %broadcast_select_fusion.10), channel_id=1, source_target_pairs={{0,1},{1,0},{2,3},{3,2},{4,5},{5,4},{6,7},{7,6},{8,9},{9,8},{10,11... | collective-permute-start | bytes 3145736 | tf_op jit(solution)/shard_map/ppermute | solution.py:1177
  513.3 74.4 %reduce-scatter.11.cloned.1.call-start = ((), (), s32[]{:S(2)}) async-start(), calls=%async_computation.9 | async-start | bytes 14155776 | tf_op jit(solution)/shard_map/reduce_scatter | solution.py:175
  533.9 128.1 %reduce-scatter.13.cloned.1.call-start = ((), (), s32[]{:S(2)}) async-start(), calls=%async_computation.10 | async-start | bytes 6291456 | tf_op jit(solution)/shard_map/reduce_scatter | solution.py:175
  534.0 53.6 %collective-permute-start.29 = (bf16[8,576,512]{2,1,0:T(8,128)(2,1)}, bf16[8,576,512]{2,1,0:T(8,128)(2,1)}, u32[]{:S(2)}, u32[]{:S(2)}) collective-permute-start(bf16[8,576,512]{2,1,0:T(8,128)(2,1)} %bitcast.350), channel_id=1, source_target_pairs={{0,1},{1,0},{2,6},{3,7},{4,5},{5,4},{6,2},{7,3},{8,9},{9,8},{10,14... | collective-permute-start | bytes 14155784 | tf_op jit(solution)/shard_map/ppermute | solution.py:42
  593.1 95.2 %reduce-scatter.17.cloned.1.call-start = ((), (), s32[]{:S(2)}) async-start(), calls=%async_computation.12 | async-start | bytes 6291456 | tf_op jit(solution)/shard_map/reduce_scatter | solution.py:175
  593.1 66.8 %collective-permute-start.30 = (bf16[4,576,512]{2,1,0:T(8,128)(2,1)}, bf16[4,576,512]{2,1,0:T(8,128)(2,1)S(1)}, u32[]{:S(2)}, u32[]{:S(2)}) collective-permute-start(bf16[4,576,512]{2,1,0:T(8,128)(2,1)} %get-tuple-element.405), channel_id=1, source_target_pairs={{0,4},{1,5},{2,3},{3,2},{4,0},{5,1},{6,7},{7,6},{8,12},{9,13},{10,... | collective-permute-start | bytes 7077896 | tf_op jit(solution)/shard_map/ppermute | solution.py:42
  662.0 33.8 %reduce-scatter.15.cloned.1.call-start = ((), (), s32[]{:S(2)}) async-start(), calls=%async_computation.11 | async-start | bytes 14155776 | tf_op jit(solution)/shard_map/reduce_scatter | solution.py:175
  662.6 101.0 %reduce-scatter.19.cloned.1.call-start = ((), (), s32[]{:S(2)}) async-start(), calls=%async_computation.13 | async-start | bytes 14155776 | tf_op jit(solution)/shard_map/reduce_scatter | solution.py:175
  662.7 25.6 %collective-permute-start.31 = (bf16[8,256,512]{2,1,0:T(8,128)(2,1)}, bf16[8,256,512]{2,1,0:T(8,128)(2,1)}, u32[]{:S(2)}, u32[]{:S(2)}) collective-permute-start(bf16[8,256,512]{2,1,0:T(8,128)(2,1)} %bitcast.351), channel_id=1, source_target_pairs={{0,1},{1,0},{2,6},{3,7},{4,5},{5,4},{6,2},{7,3},{8,9},{9,8},{10,14... | collective-permute-start | bytes 6291464 | tf_op jit(solution)/shard_map/ppermute | solution.py:42
  664.7 28.8 %collective-permute-start.32 = (bf16[576,512]{1,0:T(8,128)(2,1)}, bf16[576,512]{1,0:T(8,128)(2,1)S(1)}, u32[]{:S(2)}, u32[]{:S(2)}) collective-permute-start(bf16[576,512]{1,0:T(8,128)(2,1)} %get-tuple-element.427), channel_id=1, source_target_pairs={{0,24},{1,25},{2,26},{3,27},{4,28},{5,29},{6,30},{7,31},{8,0},{9,1... | collective-permute-start | bytes 1769480 | tf_op jit(solution)/shard_map/ppermute | solution.py:42
  695.8 104.3 %reduce-scatter.21.cloned.1.call-start = ((), (), s32[]{:S(2)}) async-start(), calls=%async_computation.14 | async-start | bytes 6291456 | tf_op jit(solution)/shard_map/reduce_scatter | solution.py:175
  695.9 67.7 %collective-permute-start.33 = (bf16[8,576,512]{2,1,0:T(8,128)(2,1)}, bf16[8,576,512]{2,1,0:T(8,128)(2,1)}, u32[]{:S(2)}, u32[]{:S(2)}) collective-permute-start(bf16[8,576,512]{2,1,0:T(8,128)(2,1)} %bitcast.349), channel_id=1, source_target_pairs={{0,1},{1,0},{2,6},{3,7},{4,5},{5,4},{6,2},{7,3},{8,9},{9,8},{10,14... | collective-permute-start | bytes 14155784 | tf_op jit(solution)/shard_map/ppermute | solution.py:42
  698.2 46.0 %collective-permute-start.35 = (bf16[576,512]{1,0:T(8,128)(2,1)S(1)}, bf16[576,512]{1,0:T(8,128)(2,1)S(1)}, u32[]{:S(2)}, u32[]{:S(2)}) collective-permute-start(bf16[576,512]{1,0:T(8,128)(2,1)S(1)} %get-tuple-element.425), channel_id=1, source_target_pairs={{0,8},{1,9},{2,10},{3,11},{4,12},{5,13},{6,14},{7,15},{8,16},{9,17... | collective-permute-start | bytes 1769480 | tf_op jit(solution)/shard_map/ppermute | solution.py:42
  699.4 44.8 %collective-permute-start.34 = (bf16[576,512]{1,0:T(8,128)(2,1)S(1)}, bf16[576,512]{1,0:T(8,128)(2,1)S(1)}, u32[]{:S(2)}, u32[]{:S(2)}) collective-permute-start(bf16[576,512]{1,0:T(8,128)(2,1)S(1)} %get-tuple-element.426), channel_id=1, source_target_pairs={{0,16},{1,17},{2,18},{3,19},{4,20},{5,21},{6,22},{7,23},{8,24},{9,... | collective-permute-start | bytes 1769480 | tf_op jit(solution)/shard_map/ppermute | solution.py:42
  702.2 67.0 %collective-permute-start.38 = (bf16[4,256,512]{2,1,0:T(8,128)(2,1)}, bf16[4,256,512]{2,1,0:T(8,128)(2,1)S(1)}, u32[]{:S(2)}, u32[]{:S(2)}) collective-permute-start(bf16[4,256,512]{2,1,0:T(8,128)(2,1)} %get-tuple-element.411), channel_id=1, source_target_pairs={{0,4},{1,5},{2,3},{3,2},{4,0},{5,1},{6,7},{7,6},{8,12},{9,13},{10,... | collective-permute-start | bytes 3145736 | tf_op jit(solution)/shard_map/ppermute | solution.py:42
  771.7 58.1 %reduce-scatter.23.cloned.1.call-start = ((), (), s32[]{:S(2)}) async-start(), calls=%async_computation.15 | async-start | bytes 6291456 | tf_op jit(solution)/shard_map/reduce_scatter | solution.py:175
  771.8 28.4 %collective-permute-start.39 = (bf16[4,576,512]{2,1,0:T(8,128)(2,1)}, bf16[4,576,512]{2,1,0:T(8,128)(2,1)}, u32[]{:S(2)}, u32[]{:S(2)}) collective-permute-start(bf16[4,576,512]{2,1,0:T(8,128)(2,1)} %get-tuple-element.319), channel_id=1, source_target_pairs={{0,4},{1,5},{2,3},{3,2},{4,0},{5,1},{6,7},{7,6},{8,12},{9,13},{10,... | collective-permute-start | bytes 7077896 | tf_op jit(solution)/shard_map/ppermute | solution.py:42
  774.1 29.8 %collective-permute-start.42 = (bf16[256,512]{1,0:T(8,128)(2,1)}, bf16[256,512]{1,0:T(8,128)(2,1)}, u32[]{:S(2)}, u32[]{:S(2)}) collective-permute-start(bf16[256,512]{1,0:T(8,128)(2,1)} %get-tuple-element.443), channel_id=1, source_target_pairs={{0,8},{1,9},{2,10},{3,11},{4,12},{5,13},{6,14},{7,15},{8,16},{9,17... | collective-permute-start | bytes 786440 | tf_op jit(solution)/shard_map/ppermute | solution.py:42
  774.1 29.8 %collective-permute-start.41 = (bf16[256,512]{1,0:T(8,128)(2,1)}, bf16[256,512]{1,0:T(8,128)(2,1)}, u32[]{:S(2)}, u32[]{:S(2)}) collective-permute-start(bf16[256,512]{1,0:T(8,128)(2,1)} %get-tuple-element.444), channel_id=1, source_target_pairs={{0,16},{1,17},{2,18},{3,19},{4,20},{5,21},{6,22},{7,23},{8,24},{9,... | collective-permute-start | bytes 786440 | tf_op jit(solution)/shard_map/ppermute | solution.py:42
  776.0 27.9 %collective-permute-start.40 = (bf16[256,512]{1,0:T(8,128)(2,1)}, bf16[256,512]{1,0:T(8,128)(2,1)}, u32[]{:S(2)}, u32[]{:S(2)}) collective-permute-start(bf16[256,512]{1,0:T(8,128)(2,1)} %get-tuple-element.445), channel_id=1, source_target_pairs={{0,24},{1,25},{2,26},{3,27},{4,28},{5,29},{6,30},{7,31},{8,0},{9,1... | collective-permute-start | bytes 786440 | tf_op jit(solution)/shard_map/ppermute | solution.py:42
  803.9 25.9 %collective-permute-start.43 = (bf16[8,256,512]{2,1,0:T(8,128)(2,1)}, bf16[8,256,512]{2,1,0:T(8,128)(2,1)}, u32[]{:S(2)}, u32[]{:S(2)}) collective-permute-start(bf16[8,256,512]{2,1,0:T(8,128)(2,1)} %bitcast.352), channel_id=1, source_target_pairs={{0,1},{1,0},{2,6},{3,7},{4,5},{5,4},{6,2},{7,3},{8,9},{9,8},{10,14... | collective-permute-start | bytes 6291464 | tf_op jit(solution)/shard_map/ppermute | solution.py:42
  806.8 26.4 %collective-permute-start.45 = (bf16[576,512]{1,0:T(8,128)(2,1)}, bf16[576,512]{1,0:T(8,128)(2,1)}, u32[]{:S(2)}, u32[]{:S(2)}) collective-permute-start(bf16[576,512]{1,0:T(8,128)(2,1)} %get-tuple-element.423), channel_id=1, source_target_pairs={{0,16},{1,17},{2,18},{3,19},{4,20},{5,21},{6,22},{7,23},{8,24},{9,... | collective-permute-start | bytes 1769480 | tf_op jit(solution)/shard_map/ppermute | solution.py:42
  807.7 25.5 %collective-permute-start.44 = (bf16[576,512]{1,0:T(8,128)(2,1)}, bf16[576,512]{1,0:T(8,128)(2,1)}, u32[]{:S(2)}, u32[]{:S(2)}) collective-permute-start(bf16[576,512]{1,0:T(8,128)(2,1)} %get-tuple-element.424), channel_id=1, source_target_pairs={{0,24},{1,25},{2,26},{3,27},{4,28},{5,29},{6,30},{7,31},{8,0},{9,1... | collective-permute-start | bytes 1769480 | tf_op jit(solution)/shard_map/ppermute | solution.py:42
  833.2 30.0 %collective-permute-start.46 = (bf16[4,256,512]{2,1,0:T(8,128)(2,1)S(1)}, bf16[4,256,512]{2,1,0:T(8,128)(2,1)S(1)}, u32[]{:S(2)}, u32[]{:S(2)}) collective-permute-start(bf16[4,256,512]{2,1,0:T(8,128)(2,1)S(1)} %get-tuple-element.331), channel_id=1, source_target_pairs={{0,4},{1,5},{2,3},{3,2},{4,0},{5,1},{6,7},{7,6},{8,12},{9,13},{10,... | collective-permute-start | bytes 3145736 | tf_op jit(solution)/shard_map/ppermute | solution.py:42
  863.8 36.0 %collective-permute-start.50 = (bf16[1,512,1024]{2,1,0:T(8,128)(2,1)S(1)}, bf16[1,512,1024]{2,1,0:T(8,128)(2,1)S(1)}, u32[]{:S(2)}, u32[]{:S(2)}) collective-permute-start(bf16[1,512,1024]{2,1,0:T(8,128)(2,1)S(1)} %select_convert_fusion), channel_id=1, source_target_pairs={{0,1},{1,0},{2,3},{3,2},{4,5},{5,4},{6,7},{7,6},{8,9},{9,8},{10,11... | collective-permute-start | bytes 3145736 | tf_op jit(solution)/shard_map/ppermute | solution.py:1177
  866.4 33.4 %collective-permute-start.53 = (bf16[256,512]{1,0:T(8,128)(2,1)S(1)}, bf16[256,512]{1,0:T(8,128)(2,1)S(1)}, u32[]{:S(2)}, u32[]{:S(2)}) collective-permute-start(bf16[256,512]{1,0:T(8,128)(2,1)S(1)} %get-tuple-element.441), channel_id=1, source_target_pairs={{0,16},{1,17},{2,18},{3,19},{4,20},{5,21},{6,22},{7,23},{8,24},{9,... | collective-permute-start | bytes 786440 | tf_op jit(solution)/shard_map/ppermute | solution.py:42
  869.6 30.2 %collective-permute-start.52 = (bf16[256,512]{1,0:T(8,128)(2,1)S(1)}, bf16[256,512]{1,0:T(8,128)(2,1)S(1)}, u32[]{:S(2)}, u32[]{:S(2)}) collective-permute-start(bf16[256,512]{1,0:T(8,128)(2,1)S(1)} %get-tuple-element.442), channel_id=1, source_target_pairs={{0,24},{1,25},{2,26},{3,27},{4,28},{5,29},{6,30},{7,31},{8,0},{9,1... | collective-permute-start | bytes 786440 | tf_op jit(solution)/shard_map/ppermute | solution.py:42
  (66 other events, 734.4 us)
Sparse Core Ops, SparseCore 0:
  513.4 16.2 reduce-scatter.8
  534.0 16.9 reduce-scatter.10
  593.2 11.8 reduce-scatter.12
  662.2 12.3 reduce-scatter.16
  676.7 19.0 reduce-scatter.14
  697.9 19.0 reduce-scatter.18
  771.9 19.1 reduce-scatter.20
  804.1 21.0 reduce-scatter.22
